TPU v7x, 32 devices: a whole 2x2x4 slice. The times are simulated.
32 devices in a mesh: row: 8 (over z, x), col: 4 (over y, core).
Axes of the slice: x: 2, y: 2, z: 4, core: 2. Of those that a mesh axis runs over, the one named last changes fastest.
Arguments:
- tokens: bfloat16 [64, 320, 768], P(('row', 'col')), may hold values from -6 to 6
- w_in_x: bfloat16 [768, 1536], P('row', 'col'), may hold values from -0.21875 to 0.21875
- w_in_z: bfloat16 [768, 1536], P('row', 'col'), may hold values from -0.21875 to 0.21875
- conv_w: bfloat16 [4, 1536], P(None, ('row', 'col')), may hold values from -3 to 3
- conv_b: bfloat16 [1536], P(('row', 'col')), may hold values from -0.5 to 0.5
- w_xproj: bfloat16 [1536, 80], P('row', 'col'), may hold values from -0.15625 to 0.15625
- w_dt: bfloat16 [48, 1536], P('row', 'col'), may hold values from -0.875 to 0.875
- dt_bias: bfloat16 [1536], P(('row', 'col')), may hold values from -7 to -3
- a_log: bfloat16 [16, 1536], P(None, ('row', 'col')), may hold values from 0 to 2.765625
- d_skip: bfloat16 [1536], P(('row', 'col')), may hold values from 0.5 to 1.5
- w_out: bfloat16 [1536, 768], P('row', 'col'), may hold values from -0.15625 to 0.15625
- gain_mix: bfloat16 [768], P(('row', 'col')), may hold values from 0.5 to 1.5
- gain_moe: bfloat16 [768], P(('row', 'col')), may hold values from 0.5 to 1.5
- w_router: bfloat16 [768, 32], P('row', 'col'), may hold values from -0.109375 to 0.109375
- w_up: bfloat16 [32, 768, 3072], P('row', None, 'col'), may hold values from -0.21875 to 0.21875
- w_down: bfloat16 [32, 3072, 768], P('row', 'col'), may hold values from -3.5 to 3.5
- routes: int32 [64, 320, 1], P(('row', 'col')), may hold values from 0 to 31
- lengths: int32 [64], P(('row', 'col')), may hold values from 128 to 320, as said below
- cotangent: float32 [64, 320, 768], P(('row', 'col')), may hold values from -6 to 6
Outputs:
- mixed_out: bfloat16 [64, 320, 768], P(('row', 'col'))
- grad_tokens: float32 [64, 320, 768], P(('row', 'col'))
- grad_w_in_x: float32 [768, 1536], P('row', 'col')
- grad_w_in_z: float32 [768, 1536], P('row', 'col')
- grad_conv_w: float32 [4, 1536], P(None, ('row', 'col'))
- grad_conv_b: float32 [1536], P(('row', 'col'))
- grad_w_xproj: float32 [1536, 80], P('row', 'col')
- grad_w_dt: float32 [48, 1536], P('row', 'col')
- grad_dt_bias: float32 [1536], P(('row', 'col'))
- grad_a_log: float32 [16, 1536], P(None, ('row', 'col'))
- grad_d_skip: float32 [1536], P(('row', 'col'))
- grad_w_out: float32 [1536, 768], P('row', 'col')
- grad_gain_mix: float32 [768], P(('row', 'col'))
- grad_gain_moe: float32 [768], P(('row', 'col'))
- grad_w_router: float32 [768, 32], P('row', 'col')
- grad_w_up: float32 [32, 768, 3072], P('row', None, 'col')
- grad_w_down: float32 [32, 3072, 768], P('row', 'col')
Inputs may be any that keep to these rules, and one draw needn't show every extreme that they name: `lengths`: each sequence's number of real tokens; the slots after them are padding.
All inputs are finite; a program needn't handle non-finite values.
Results may differ from a plain program's by a relative error of at most 0.014.
Values may be sent and summed in bfloat16 or wider, within the bound.
No kernel may reach another device: no remote copies, remote signals or barrier semaphores. Data moves between devices by JAX's collectives and lax.ppermute only.
A program may use at most 320 MiB of HBM per device.

v0:
```python
import functools
import jax
import jax.numpy as jnp
from jax import lax
from jax.sharding import PartitionSpec as P
from jax.experimental import pallas as pl
from jax.experimental.pallas import tpu as pltpu
NS=16
F32=jnp.float32
SLOT_OF=[4*((i>>2)&1)+2*(1-((i>>1)&1))+(1-(i&1)) for i in range(8)]
def merge8(rows):
    idx=lax.broadcasted_iota(jnp.int32,(8,128),0)
    m4=idx<4; m2=(idx&2)!=0; m1=(idx&1)!=0
    p=[None]*8
    for i in range(8): p[SLOT_OF[i]]=rows[i]
    r=[jnp.where(m4,p[k],p[k+4])+pltpu.roll(jnp.where(m4,p[k+4],p[k]),4,0) for k in range(4)]
    def half(x,y,m,d):
        return jnp.where(m,x+pltpu.roll(x,d,0),y+pltpu.roll(y,8-d,0))
    v=[half(r[k],r[k+2],m2,2) for k in range(2)]
    return half(v[0],v[1],m1,1)
def softplus(v):
    e=jnp.exp(-jnp.abs(v))
    return jnp.maximum(v,0.)+jnp.log1p(e)
def spread(dst,src,T):
    for j in range(T):
        dst[j]=jnp.broadcast_to(src[0,0,:,j:j+1],(NS,128))
def fold(x): return x[0:8]+x[8:16]

def fwd_kernel(T,Q,u_ref,dtp_ref,bT_ref,cT_ref,bias_ref,a2_ref,skip_ref,y_ref,st_ref,state,bx,cx,dl,du):
    DI=u_ref.shape[-1]
    @pl.when(pl.program_id(1)==0)
    def _(): state[...]=jnp.zeros_like(state)
    st_ref[0,0]=state[...]
    spread(bx,bT_ref,T); spread(cx,cT_ref,T)
    d=softplus(dtp_ref[0]+bias_ref[...][None])
    dl[...]=d
    du[...]=d*u_ref[0]
    def grp(g,_):
        base=pl.multiple_of(g*(Q*128),128)
        lanes=[pl.ds(base+q*128,128) for q in range(Q)]
        a=[a2_ref[:,ln] for ln in lanes]
        sk=[skip_ref[:,ln] for ln in lanes]
        def tb(i,s):
            s=list(s)
            rows=[[] for _ in range(Q)]
            for k in range(8):
                t=i*8+k
                b=bx[t]; c=cx[t]
                for q in range(Q):
                    dd=dl[i,k:k+1,lanes[q]]; dub=du[i,k:k+1,lanes[q]]
                    s[q]=jnp.exp2(dd*a[q])*s[q]+b*dub
                    rows[q].append(fold(s[q]*c))
            for q in range(Q):
                y_ref[0,i,:,lanes[q]]=merge8(rows[q])+sk[q]*u_ref[0,i,:,lanes[q]]
            return tuple(s)
        s=lax.fori_loop(0,T//8,tb,tuple(state[:,ln] for ln in lanes))
        for q in range(Q): state[:,lanes[q]]=s[q]
        return 0
    lax.fori_loop(0,DI//(Q*128),grp,0)

def rows8(x):
    S,L,DI=x.shape
    return x.reshape(S,L//8,8,DI)
def scan_fwd(u,dtp,bT,cT,bias,a2,skip,Q=3):
    S,L,DI=u.shape
    C,T=bT.shape[1],bT.shape[3]
    row=lambda s,c:(s,c,0,0)
    big=pl.BlockSpec((1,T//8,8,DI),row)
    small=pl.BlockSpec((1,1,NS,T),row)
    par=lambda n:pl.BlockSpec((n,DI),lambda s,c:(0,0))
    y,st=pl.pallas_call(functools.partial(fwd_kernel,T,Q),
        grid=(S,C),
        in_specs=[big,big,small,small,par(1),par(NS),par(1)],
        out_specs=[big,pl.BlockSpec((1,1,NS,DI),row)],
        out_shape=[jax.ShapeDtypeStruct((S,L//8,8,DI),F32),jax.ShapeDtypeStruct((S,C,NS,DI),F32)],
        scratch_shapes=[pltpu.VMEM((NS,DI),F32),pltpu.VMEM((T,NS,128),F32),pltpu.VMEM((T,NS,128),F32),
                        pltpu.VMEM((T//8,8,DI),F32),pltpu.VMEM((T//8,8,DI),F32)],
        compiler_params=pltpu.CompilerParams(vmem_limit_bytes=32<<20),
    )(rows8(u),rows8(dtp),bT,cT,bias,a2,skip)
    return y.reshape(S,L,DI),st

def bwd_kernel(T,Q,Q2,u_ref,dtp_ref,gs_ref,bT_ref,cT_ref,st_ref,bias_ref,an_ref,skip_ref,
               guc_ref,gdt_ref,gb_ref,gc_ref,gal_ref,gbias_ref,gskip_ref,
               carry,bx,cx,dl,du,hs,ds,gbp,gcp):
    DI=u_ref.shape[-1]
    s_id,c_id=pl.program_id(0),pl.program_id(1)
    @pl.when(c_id==0)
    def _(): carry[...]=jnp.zeros_like(carry)
    @pl.when((c_id==0)&(s_id==0))
    def _():
        gal_ref[...]=jnp.zeros_like(gal_ref)
        gbias_ref[...]=jnp.zeros_like(gbias_ref)
        gskip_ref[...]=jnp.zeros_like(gskip_ref)
    spread(bx,bT_ref,T); spread(cx,cT_ref,T)
    d=softplus(dtp_ref[0]+bias_ref[...][None])
    dl[...]=d
    du[...]=d*u_ref[0]
    gbp[...]=jnp.zeros_like(gbp)
    gcp[...]=jnp.zeros_like(gcp)
    W=Q*128
    def grp(g,_):
        base=pl.multiple_of(g*W,128)
        lanes=[pl.ds(base+q*128,128) for q in range(Q)]
        loc=[slice(q*128,q*128+128) for q in range(Q)]
        an=[an_ref[:,ln] for ln in lanes]
        a2=[x*1.4426950408889634 for x in an]
        def tb(i,s):
            s=list(s)
            for k in range(8):
                t=i*8+k
                b=bx[t]; gc=gcp[t]
                for q in range(Q):
                    dd=dl[i,k:k+1,lanes[q]]; dub=du[i,k:k+1,lanes[q]]; gsr=gs_ref[0,i,k:k+1,lanes[q]]
                    dec=jnp.exp2(dd*a2[q])
                    h=dec*s[q]
                    ds[t,:,loc[q]]=dec
                    hs[t,:,loc[q]]=h
                    s[q]=h+b*dub
                    gc=gc+s[q]*gsr
                gcp[t]=gc
            return tuple(s)
        lax.fori_loop(0,T//8,tb,tuple(st_ref[0,0,:,ln] for ln in lanes))
        for q0 in range(0,Q,Q2):
            qs=range(q0,q0+Q2)
            sk={q:skip_ref[:,lanes[q]] for q in qs}
            def rb(j,cr):
                i=T//8-1-j
                g_,ga={q:cr[0][q-q0] for q in qs},{q:cr[1][q-q0] for q in qs}
                gbs,gsk=cr[2],cr[3]
                m1={q:[None]*8 for q in qs}; m2={q:[None]*8 for q in qs}
                for k in range(7,-1,-1):
                    t=i*8+k
                    b=bx[t]; c=cx[t]; gb=gbp[t]
                    for q in qs:
                        dd=dl[i,k:k+1,lanes[q]]; dub=du[i,k:k+1,lanes[q]]; gsr=gs_ref[0,i,k:k+1,lanes[q]]
                        dec=ds[t,:,loc[q]]; h=hs[t,:,loc[q]]
                        gg=gsr*c+g_[q]
                        g_[q]=gg*dec
                        qq=gg*h
                        m1[q][k]=fold(gg*b)
                        m2[q][k]=fold(qq*an[q])
                        ga[q]=ga[q]+qq*dd
                        gb=gb+gg*dub
                    gbp[t]=gb
                for q in qs:
                    s1=merge8(m1[q]); s2=merge8(m2[q])
                    u8=u_ref[0,i,:,lanes[q]]; d8=dl[i,:,lanes[q]]; gs8=gs_ref[0,i,:,lanes[q]]
                    guc_ref[0,i,:,lanes[q]]=d8*s1+sk[q]*gs8
                    gd=(s2+u8*s1)*jax.nn.sigmoid(dtp_ref[0,i,:,lanes[q]]+bias_ref[:,lanes[q]])
                    gdt_ref[0,i,:,lanes[q]]=gd
                    gbs=gbs[:q-q0]+(gbs[q-q0]+gd,)+gbs[q-q0+1:]
                    gsk=gsk[:q-q0]+(gsk[q-q0]+gs8*u8,)+gsk[q-q0+1:]
                return (tuple(g_[q] for q in qs),tuple(ga[q] for q in qs),gbs,gsk)
            z8=tuple(jnp.zeros((8,128),F32) for q in qs)
            cr=lax.fori_loop(0,T//8,rb,(tuple(carry[:,lanes[q]] for q in qs),tuple(jnp.zeros((NS,128),F32) for q in qs),z8,z8))
            for q in qs:
                carry[:,lanes[q]]=cr[0][q-q0]
                gal_ref[:,lanes[q]]+=cr[1][q-q0]*an[q]
                gbias_ref[:,lanes[q]]+=cr[2][q-q0]
                gskip_ref[:,lanes[q]]+=cr[3][q-q0]
        return 0
    lax.fori_loop(0,DI//W,grp,0)
    ones=jnp.ones((8,128),F32)
    nt=(((1,),(1,)),((),()))
    gb_ref[0,0]=lax.dot_general(ones,gbp[...].reshape(T*NS,128),nt,precision=lax.Precision.HIGHEST,preferred_element_type=F32)
    gc_ref[0,0]=lax.dot_general(ones,gcp[...].reshape(T*NS,128),nt,precision=lax.Precision.HIGHEST,preferred_element_type=F32)

def scan_bwd(u,dtp,gs,bT,cT,st,bias,an,skip,Q=3,Q2=1):
    S,L,DI=u.shape
    C,T=bT.shape[1],bT.shape[3]
    row=lambda s,c:(s,C-1-c,0,0)
    big=pl.BlockSpec((1,T//8,8,DI),row)
    small=pl.BlockSpec((1,1,NS,T),row)
    par=lambda n:pl.BlockSpec((n,DI),lambda s,c:(0,0))
    red=pl.BlockSpec((1,1,8,T*NS),row)
    guc,gdt,gb,gc,gal,gbias,gskip=pl.pallas_call(functools.partial(bwd_kernel,T,Q,Q2),
        grid=(S,C),
        in_specs=[big,big,big,small,small,pl.BlockSpec((1,1,NS,DI),row),par(1),par(NS),par(1)],
        out_specs=[big,big,red,red,par(NS),par(8),par(8)],
        out_shape=[jax.ShapeDtypeStruct((S,L//8,8,DI),F32)]*2+[jax.ShapeDtypeStruct((S,C,8,T*NS),F32)]*2+
                  [jax.ShapeDtypeStruct((NS,DI),F32)]+[jax.ShapeDtypeStruct((8,DI),F32)]*2,
        scratch_shapes=[pltpu.VMEM((NS,DI),F32),pltpu.VMEM((T,NS,128),F32),pltpu.VMEM((T,NS,128),F32),
                        pltpu.VMEM((T//8,8,DI),F32),pltpu.VMEM((T//8,8,DI),F32),
                        pltpu.VMEM((T,NS,Q*128),F32),pltpu.VMEM((T,NS,Q*128),F32),
                        pltpu.VMEM((T,NS,128),F32),pltpu.VMEM((T,NS,128),F32)],
        compiler_params=pltpu.CompilerParams(vmem_limit_bytes=40<<20),
    )(rows8(u),rows8(dtp),rows8(gs),bT,cT,st,bias,an,skip)
    gb=gb[:,:,0].reshape(S,L,NS); gc=gc[:,:,0].reshape(S,L,NS)
    return guc.reshape(S,L,DI),gdt.reshape(S,L,DI),gb,gc,gal,jnp.sum(gbias,0),jnp.sum(gskip,0)


R = 48
QB = 64
CAP = 13
BF = jnp.bfloat16
epsilon = 1e-05
highest = lax.Precision.HIGHEST
root_half = 0.7071067811865476
inv_root_two_pi = 0.3989422804014327
log2e = 1.4426950408889634


def mm(a, b, dims=((1,), (0,)), **kw):
    return lax.dot_general(a, b, (dims, ((), ())), preferred_element_type=F32, **kw)


def swap(x, axis, bit):
    n = lax.axis_size(axis)
    return lax.ppermute(x, axis, [(i, i ^ bit) for i in range(n)])


def bits_of(axis):
    n = lax.axis_size(axis)
    return [1 << k for k in range(n.bit_length() - 1)]


def gather_steps():
    row, col = bits_of("row"), bits_of("col")
    return [("row", b) for b in row[1:] + row[:1]] + [("col", b) for b in col[::-1]]


def bit_set(axis, bit):
    return (lax.axis_index(axis) & bit) != 0


def gather_blocks(x):
    rows, cols = lax.axis_size("row"), lax.axis_size("col")
    dims = {}
    out = x
    order = []
    for axis, bit in gather_steps():
        other = swap(out, axis, bit)
        up = bit_set(axis, bit)
        out = jnp.where(up, jnp.stack([other, out]), jnp.stack([out, other]))
        order.insert(0, (axis, bit))
    n = len(order)
    wanted = [("row", b) for b in bits_of("row")[::-1]] + [("col", b) for b in bits_of("col")[::-1]]
    perm = [order.index(w) for w in wanted] + list(range(n, n + x.ndim))
    out = out.reshape((2,) * n + x.shape).transpose(perm)
    return out.reshape((rows, cols) + x.shape)


def reduce_blocks(x):
    block = x.shape[2:]
    row, col = bits_of("row"), bits_of("col")
    names = [("row", b) for b in row[::-1]] + [("col", b) for b in col[::-1]]
    x = x.reshape((2,) * len(names) + block)
    for axis, bit in gather_steps()[::-1]:
        d = names.index((axis, bit))
        names.pop(d)
        mine = bit_set(axis, bit).astype(jnp.int32)
        keep = lax.dynamic_index_in_dim(x, mine, d, keepdims=False)
        give = lax.dynamic_index_in_dim(x, 1 - mine, d, keepdims=False).astype(BF)
        x = keep + swap(give, axis, bit).astype(F32)
    return x


def gelu_parts(v):
    phi = 0.5 * (1.0 + lax.erf(v * root_half))
    return v * phi, phi + v * jnp.exp(-0.5 * v * v) * inv_root_two_pi


def to_chunks(b):
    s, length, n = b.shape
    return b.reshape(s, length // QB, QB, n).swapaxes(2, 3)


def on_device(tokens, w_in_x, w_in_z, conv_w, conv_b, w_xproj, w_dt, dt_bias, a_log, d_skip, w_out,
              gain_mix, gain_moe, w_router, w_up, w_down, routes, lengths, cotangent):
    rows, cols = lax.axis_size("row"), lax.axis_size("col")
    parts = rows * cols
    my_row = lax.axis_index("row")
    seqs, length, width = tokens.shape
    experts_here = w_up.shape[0]
    experts_all = experts_here * rows
    inner = w_in_x.shape[1] * cols
    count = seqs * length
    xp = w_xproj.shape[1] * cols
    share = inner // parts

    small = jnp.concatenate([conv_w, conv_b[None], dt_bias[None], a_log, d_skip[None],
                             jnp.concatenate([gain_mix, gain_moe])[None]], axis=0)
    flat = [w_xproj.reshape(-1), w_dt.reshape(-1), w_router.reshape(-1), small.reshape(-1)]
    sizes = [f.shape[0] for f in flat]
    lanes = w_in_x.shape[1]
    extra = -(-sum(sizes) // (8 * lanes)) * 8
    flat = jnp.pad(jnp.concatenate(flat), (0, extra * lanes - sum(sizes))).reshape(extra, lanes)
    here = w_in_x.shape[0]
    first = gather_blocks(jnp.concatenate([w_in_x, flat], axis=0))
    second = gather_blocks(jnp.concatenate([w_in_z.reshape(-1, lanes), w_out.reshape(-1, lanes)], axis=0))
    def whole(blocks):
        return blocks.transpose(0, 2, 1, 3).reshape(blocks.shape[0] * blocks.shape[2], -1)
    full_x = whole(first[:, :, :here])
    rest = first[:, :, here:].reshape(rows, cols, extra * lanes)
    cut = [0]
    for n in sizes:
        cut.append(cut[-1] + n)
    full_xproj = whole(rest[:, :, cut[0]:cut[1]].reshape((rows, cols) + w_xproj.shape))
    full_dt = whole(rest[:, :, cut[1]:cut[2]].reshape((rows, cols) + w_dt.shape))
    full_router = whole(rest[:, :, cut[2]:cut[3]].reshape((rows, cols) + w_router.shape))
    small = rest[:, :, cut[3]:cut[4]].reshape((parts,) + small.shape).transpose(1, 0, 2).astype(F32)
    chan = small[:-1].reshape(-1, inner)
    taps = conv_w.shape[0]
    conv_w_f, conv_b_f, dt_bias_f = chan[:taps], chan[taps], chan[taps + 1]
    a_log_f, d_skip_f = chan[taps + 2:taps + 2 + NS], chan[taps + 2 + NS]
    gain_mix_f = small[-1, :, :gain_mix.shape[0]].reshape(width)
    gain_moe_f = small[-1, :, gain_mix.shape[0]:].reshape(width)
    full_z = whole(second[:, :, :w_in_z.shape[0]])
    full_out = whole(second[:, :, w_in_z.shape[0]:].reshape((rows, cols) + w_out.shape))
    a_neg = -jnp.exp(a_log_f)

    flat_route = routes.reshape(count)
    live = (jnp.arange(length, dtype=jnp.int32)[None, :] < lengths[:, None]).reshape(count)
    live_f = live.astype(F32)[:, None]
    route_onehot = flat_route[:, None] == jnp.arange(experts_all, dtype=jnp.int32)
    hits = (route_onehot & live[:, None]).astype(BF).reshape(seqs, length, experts_all)
    before = jnp.arange(length)[:, None] > jnp.arange(length)[None, :]
    earlier = jnp.einsum("pq,sqe->spe", before.astype(BF), hits, preferred_element_type=F32)
    slot = jnp.sum(earlier * hits.astype(F32), axis=-1).astype(jnp.int32).reshape(count)
    kept = live & (slot < CAP)
    seq_of = jnp.arange(count, dtype=jnp.int32) // length
    per_row = experts_here * seqs * CAP
    target = (((flat_route // experts_here) ^ my_row) * per_row
              + (flat_route % experts_here) * (seqs * CAP) + seq_of * CAP + slot)
    target = jnp.where(kept, target, rows * per_row)
    route_f = route_onehot.astype(F32)

    x = tokens.astype(F32).reshape(count, width)
    rms1 = lax.rsqrt(jnp.mean(x * x, axis=-1, keepdims=True) + epsilon)
    hat1 = x * rms1
    normed_mix = (hat1 * gain_mix_f).astype(BF)
    inner_x = mm(normed_mix, full_x).reshape(seqs, length, inner)
    padded = jnp.pad(inner_x, ((0, 0), (taps - 1, 0), (0, 0)))
    conv_out = conv_b_f
    for k in range(taps):
        conv_out = conv_out + conv_w_f[k] * padded[:, k:k + length]
    conv_sig = jax.nn.sigmoid(conv_out)
    u_value = conv_out * conv_sig
    u_low = u_value.astype(BF).reshape(count, inner)
    projected = mm(u_low, full_xproj)
    dt_low = projected[:, :R].astype(BF)
    dt_pre = mm(dt_low, full_dt).reshape(seqs, length, inner)
    bT = to_chunks(projected[:, R:R + NS].reshape(seqs, length, NS))
    cT = to_chunks(projected[:, R + NS:].reshape(seqs, length, NS))
    ssm_out, starts = scan_fwd(u_value, dt_pre, bT, cT, dt_bias_f[None], a_neg * log2e, d_skip_f[None])
    ssm_out = ssm_out.reshape(count, inner)
    gate_z = mm(normed_mix, full_z)
    gate_sig = jax.nn.sigmoid(gate_z)
    gate_silu = gate_z * gate_sig
    gated = (ssm_out * gate_silu).astype(BF)
    hidden = x + mm(gated, full_out)

    rms2 = lax.rsqrt(jnp.mean(hidden * hidden, axis=-1, keepdims=True) + epsilon)
    hat2 = hidden * rms2
    normed_moe = hat2 * gain_moe_f
    router_f = full_router.astype(F32)
    route_probs = jax.nn.softmax(mm(normed_moe, router_f, precision=highest), axis=-1)
    gate_prob = jnp.sum(route_probs * route_f, axis=-1, keepdims=True)

    grad_y = live_f * cotangent.reshape(count, width)
    both = jnp.concatenate([normed_moe.astype(BF), (grad_y * gate_prob).astype(BF)], axis=1)
    place = jnp.arange(rows * per_row, dtype=jnp.int32)[:, None] == target[None, :]
    place = place.astype(BF)
    outgoing = mm(place, both).astype(BF)
    arrived = [outgoing[:per_row]]
    for k in range(1, rows):
        arrived.append(swap(outgoing[k * per_row:(k + 1) * per_row], "row", k))
    arrived = jnp.stack(arrived)
    for bit in bits_of("col")[::-1]:
        arrived = jnp.concatenate([arrived, swap(arrived, "col", bit)], axis=0)
    sources = rows * cols
    arrived = arrived.reshape(sources, experts_here, seqs * CAP, 2 * width).transpose(1, 0, 2, 3)
    arrived = arrived.reshape(experts_here, sources * seqs * CAP, 2 * width)
    expert_in, grad_eo = arrived[..., :width], arrived[..., width:]

    def bmm(a, b, da, db):
        return lax.dot_general(a, b, (((da,), (db,)), ((0,), (0,))), preferred_element_type=F32)
    pre_act = bmm(expert_in, w_up, 2, 1)
    act, slope = gelu_parts(pre_act)
    act = act.astype(BF)
    expert_out = bmm(act, w_down, 2, 1)
    grad_pre = (bmm(grad_eo, w_down, 2, 2) * slope).astype(BF)
    grad_ei = bmm(grad_pre, w_up, 2, 2)
    grad_w_up = bmm(expert_in, grad_pre, 1, 1)
    grad_w_down = bmm(act, grad_eo, 1, 1)
    back = jnp.concatenate([expert_out, grad_ei], axis=-1)
    back = back.reshape(experts_here, sources, seqs * CAP, 2 * width).transpose(1, 0, 2, 3)
    back = back.reshape(sources, per_row, 2 * width)
    for bit in bits_of("col"):
        half = back.shape[0] // 2
        back = back[:half] + swap(back[half:].astype(BF), "col", bit).astype(F32)
    back = back.astype(BF)
    home = [back[0]]
    for k in range(1, rows):
        home.append(swap(back[k], "row", k))
    home = jnp.concatenate(home, axis=0)
    tok = mm(place, home, ((0,), (0,)))
    expert_tok, grad_sent = tok[:, :width], tok[:, width:]

    mixed_out = (live_f * (hidden + gate_prob * expert_tok)).astype(BF)
    grad_gate = jnp.sum(grad_y * expert_tok, axis=-1, keepdims=True)
    grad_logits = grad_gate * gate_prob * (route_f - route_probs)
    grad_router = mm(normed_moe, grad_logits, ((0,), (0,)), precision=highest)
    grad_normed = grad_sent + mm(grad_logits, router_f, ((1,), (1,)), precision=highest)
    grad_gain_moe = jnp.sum(grad_normed * hat2, axis=0)
    scaled = grad_normed * gain_moe_f
    grad_hidden = grad_y + rms2 * (scaled - hat2 * jnp.mean(scaled * hat2, axis=-1, keepdims=True))
    grad_mixed = grad_hidden.astype(BF)

    grad_out = mm(gated, grad_mixed, ((0,), (0,)))
    grad_gated = mm(grad_mixed, full_out, ((1,), (1,)))
    grad_ssm = grad_gated * gate_silu
    grad_z = (grad_gated * ssm_out * (gate_sig * (1.0 + gate_z * (1.0 - gate_sig)))).astype(BF)
    guc, gdt, gb, gc, grad_a_log, grad_dt_bias, grad_d_skip = scan_bwd(
        u_value, dt_pre, grad_ssm.reshape(seqs, length, inner), bT, cT, starts,
        dt_bias_f[None], a_neg, d_skip_f[None])
    gdt = gdt.reshape(count, inner).astype(BF)
    grad_dt = mm(dt_low, gdt, ((0,), (0,)))
    grad_proj = jnp.concatenate([mm(gdt, full_dt, ((1,), (1,))), gb.reshape(count, NS), gc.reshape(count, NS)],
                                axis=1).astype(BF)
    grad_xproj = mm(u_low, grad_proj, ((0,), (0,)))
    grad_u = guc.reshape(count, inner) + mm(grad_proj, full_xproj, ((1,), (1,)))
    grad_conv = grad_u.reshape(seqs, length, inner) * (conv_sig * (1.0 + conv_out * (1.0 - conv_sig)))
    grad_conv_b = jnp.sum(grad_conv, axis=(0, 1))
    grad_conv_w = jnp.stack([jnp.sum(grad_conv * padded[:, k:k + length], axis=(0, 1)) for k in range(taps)])
    after = jnp.pad(grad_conv, ((0, 0), (0, taps - 1), (0, 0)))
    grad_inner = sum(conv_w_f[k] * after[:, taps - 1 - k:taps - 1 - k + length] for k in range(taps))
    grad_inner = grad_inner.reshape(count, inner).astype(BF)
    grad_in_x = mm(normed_mix, grad_inner, ((0,), (0,)))
    grad_in_z = mm(normed_mix, grad_z, ((0,), (0,)))
    grad_nm = mm(grad_inner, full_x, ((1,), (1,))) + mm(grad_z, full_z, ((1,), (1,)))
    grad_gain_mix = jnp.sum(grad_nm * hat1, axis=0)
    scaled = grad_nm * gain_mix_f
    grad_tokens = grad_hidden + rms1 * (scaled - hat1 * jnp.mean(scaled * hat1, axis=-1, keepdims=True))

    def blocks(g, like):
        r, c = like.shape
        return g.reshape(rows, r, cols, c).transpose(0, 2, 1, 3)
    grad_z_block = reduce_blocks(blocks(grad_in_z, w_in_z))
    grad_out_block = reduce_blocks(blocks(grad_out, w_out).reshape(rows, cols, -1, lanes)).reshape(w_out.shape)
    gsmall = jnp.concatenate([grad_conv_w, grad_conv_b[None], grad_dt_bias[None], grad_a_log, grad_d_skip[None]], axis=0)
    ggain = jnp.concatenate([grad_gain_mix.reshape(parts, 1, -1), grad_gain_moe.reshape(parts, 1, -1)], axis=2)
    gsmall = jnp.concatenate([gsmall.reshape(-1, parts, share).transpose(1, 0, 2), ggain], axis=1)
    gflat = jnp.concatenate([blocks(grad_xproj, w_xproj).reshape(rows, cols, -1),
                             blocks(grad_dt, w_dt).reshape(rows, cols, -1),
                             blocks(grad_router, w_router).reshape(rows, cols, -1),
                             gsmall.reshape(rows, cols, -1)], axis=2)
    gflat = jnp.pad(gflat, ((0, 0), (0, 0), (0, extra * lanes - sum(sizes)))).reshape(rows, cols, extra, lanes)
    done = reduce_blocks(jnp.concatenate([blocks(grad_in_x, w_in_x), gflat], axis=2))
    grad_x_block = done[:here]
    done = done[here:].reshape(-1)
    sm = done[cut[3]:cut[4]].reshape(-1, share)
    gm = gain_mix.shape[0]
    return (
        mixed_out.reshape(tokens.shape),
        grad_tokens.reshape(tokens.shape),
        grad_x_block,
        grad_z_block,
        sm[:taps],
        sm[taps],
        done[cut[0]:cut[1]].reshape(w_xproj.shape),
        done[cut[1]:cut[2]].reshape(w_dt.shape),
        sm[taps + 1],
        sm[taps + 2:taps + 2 + NS],
        sm[taps + 2 + NS],
        grad_out_block,
        sm[-1, :gm],
        sm[-1, gm:],
        done[cut[2]:cut[3]].reshape(w_router.shape),
        grad_w_up,
        grad_w_down,
    )


def solution(mesh):
    tok = P(("row", "col"), None, None)
    mat = P("row", "col")
    vec = P(("row", "col"))
    chan = P(None, ("row", "col"))
    up, down = P("row", None, "col"), P("row", "col", None)
    return jax.shard_map(
        on_device,
        mesh=mesh,
        in_specs=(tok, mat, mat, chan, vec, mat, mat, vec, chan, vec, mat, vec, vec, mat, up, down, tok, vec, tok),
        out_specs=(tok, tok, mat, mat, chan, vec, mat, mat, vec, chan, vec, mat, vec, vec, mat, up, down),
        check_vma=False,
    )
```

profile of v0, /device:TPU:0, one launch (start us, length us, event | category | flops | bytes accessed | tf_op | source)
XLA Modules:
  0.0 962.6 jit_solution(13391106144373146906)
XLA Ops:
  20.3 13.7 %collective-permute-done.1 = bf16[2,120,384]{2,1,0:T(8,128)(2,1)S(1)} collective-permute-done((bf16[2,120,384]{2,1,0:T(8,128)(2,1)S(1)}, bf16[2,120,384]{2,1,0:T(8,128)(2,1)S(1)}, u32[]{:S(2)}, u32[]{:S(2)}) %collective-permute-start.1) | collective-permute-done | bytes 184352 | tf_op jit(solution)/shard_map/ppermute | solution.py:209
  46.0 8.8 collective-permute-done.7
  63.2 20.2 %collective-permute-done.8 = bf16[2,2,2,192,384]{4,3,0,2,1:T(8,128)(2,1)} collective-permute-done((bf16[2,2,2,192,384]{4,3,0,2,1:T(8,128)(2,1)}, bf16[2,2,2,192,384]{4,3,0,2,1:T(8,128)(2,1)}, u32[]{:S(2)}, u32[]{:S(2)}) %collective-permute-start.8) | collective-permute-done | bytes 1179680 | tf_op jit(solution)/shard_map/ppermute | solution.py:209
  127.1 30.2 %shard_map.314 = (f32[2,40,8,1536]{3,2,1,0:T(8,128)S(1)}, f32[2,5,16,1536]{3,2,1,0:T(8,128)S(1)}) custom-call(f32[2,40,8,1536]{3,2,1,0:T(8,128)S(1)} %fusion.60.u_ref, f32[2,40,8,1536]{3,2,1,0:T(8,128)S(1)} %fusion.78.dtp_ref, f32[2,5,16,64]{3,2,1,0:T(8,128)S(1)} %get-tuple-element.272.bT_ref, f32[2,5,16,64]{3,2,1,0:T(8,128)S(1)} %get-tuple-element.271.cT_ref, ...), custom_call_target="tpu_custom_call" | custom-call | tf_op jit(solution)/shard_map/pallas_call | solution.py:71
  164.8 5.6 reshape.1315
  170.4 5.5 copy.595
  175.9 6.5 reshape.1316
  198.6 7.6 collective-permute-start.16
  211.3 10.0 %collective-permute-done.10 = bf16[104,1536]{1,0:T(8,128)(2,1)S(1)} collective-permute-done((bf16[104,1536]{1,0:T(8,128)(2,1)S(1)}, bf16[104,1536]{1,0:T(8,128)(2,1)S(1)}, u32[]{:S(2)}, u32[]{:S(2)}) %collective-permute-start.10) | collective-permute-done | bytes 319520 | tf_op jit(solution)/shard_map/ppermute | solution.py:209
  222.2 18.9 %collective-permute-done.11 = bf16[104,1536]{1,0:T(8,128)(2,1)S(1)} collective-permute-done((bf16[104,1536]{1,0:T(8,128)(2,1)S(1)}, bf16[104,1536]{1,0:T(8,128)(2,1)S(1)}, u32[]{:S(2)}, u32[]{:S(2)}) %collective-permute-start.11) | collective-permute-done | bytes 319520 | tf_op jit(solution)/shard_map/ppermute | solution.py:209
  244.3 20.5 %collective-permute-done.12 = bf16[104,1536]{1,0:T(8,128)(2,1)S(1)} collective-permute-done((bf16[104,1536]{1,0:T(8,128)(2,1)S(1)}, bf16[104,1536]{1,0:T(8,128)(2,1)S(1)}, u32[]{:S(2)}, u32[]{:S(2)}) %collective-permute-start.12) | collective-permute-done | bytes 319520 | tf_op jit(solution)/shard_map/ppermute | solution.py:209
  270.5 54.7 %collective-permute-done.17 = bf16[8,104,1536]{2,1,0:T(8,128)(2,1)S(1)} collective-permute-done((bf16[8,104,1536]{2,1,0:T(8,128)(2,1)S(1)}, bf16[8,104,1536]{2,1,0:T(8,128)(2,1)S(1)}, u32[]{:S(2)}, u32[]{:S(2)}) %collective-permute-start.17) | collective-permute-done | bytes 2555936 | tf_op jit(solution)/shard_map/ppermute | solution.py:209
  352.3 6.4 copy.599
  358.7 55.7 %concatenate.331 = bf16[32,4,26,1536]{3,0,2,1:T(8,128)(2,1)} concatenate(bf16[1,4,26,1536]{3,0,2,1:T(2,128)(2,1)} %concatenate.350, bf16[1,4,26,1536]{3,0,2,1:T(2,128)(2,1)} %concatenate.351, bf16[1,4,26,1536]{3,0,2,1:T(2,128)(2,1)} %concatenate.352, bf16[1,4,26,1536]{3,0,2,1:T(2,128)(2,1)} %concatenate.353, bf16[1,4,26,1536]{3,0,2,1:T(2,128)(2,1)} %concatenate.354, ...), dimensions={0} | concatenate | bytes 20447232 | tf_op jit(solution)/shard_map/concatenate | solution.py:370
  414.4 11.0 %copy.608 = bf16[4,32,26,1536]{3,0,2,1:T(4,128)(2,1)S(1)} copy(bf16[4,32,26,1536]{3,1,2,0:T(8,128)(2,1)} %bitcast.420) | data formatting | bytes 20447232 | tf_op jit(solution)/shard_map/transpose | solution.py:372
  429.1 8.4 multiply_convert_fusion
  437.6 10.8 %fusion.5 = bf16[4,832,768]{2,1,0:T(8,128)(2,1)} fusion(f32[4,832,768]{2,1,0:T(8,128)} %get-tuple-element.268, bf16[4,768,768]{2,1,0:T(8,128)(2,1)S(1)} %bitcast.518, bf16[4,832,768]{2,0,1:T(4,128)(2,1)S(1)} %get-tuple-element.209), kind=kOutput, calls=%fused_computation.7 | convolution fusion | flops 3951427584 | bytes 25165824 | tf_op jit(solution)/shard_map/dot_general | solution.py:377
  448.4 7.6 fusion.134
  456.0 9.1 fusion.133
  465.1 6.4 pad_maximum_fusion
  471.5 32.5 %copy.611 = f32[4,832,1536]{2,0,1:T(4,128)} copy(f32[4,832,1536]{2,1,0:T(8,128)S(1)} %pad_maximum_fusion) | data formatting | bytes 40894464 | tf_op jit(solution)/shard_map/concatenate | solution.py:386
  504.1 8.0 slice.430
  512.0 6.3 copy.613
  518.9 9.6 slice.346
  528.4 13.6 %copy.612 = f32[16,4,26,1536]{3,0,2,1:T(8,128)} copy(f32[16,4,26,1536]{3,1,2,0:T(4,128)} %slice.346) | data formatting | bytes 20447232 | tf_op jit(solution)/shard_map/slice | solution.py:391
  542.0 12.1 %bitcast_add_fusion = f32[16,104,1536]{2,0,1:T(8,128)} fusion(f32[16,4,26,1536]{3,0,2,1:T(8,128)} %copy.612, bf16[16,104,1536]{2,0,1:T(8,128)(2,1)} %collective-permute-done.19), kind=kLoop, calls=%fused_computation.9 | loop fusion | flops 5111808 | bytes 25559040 | tf_op jit(solution)/shard_map/add | solution.py:391
  569.1 11.0 %fusion.7 = f32[4,768,768]{2,1,0:T(8,128)} fusion(bf16[4,832,768]{2,1,0:T(8,128)(2,1)} %get-tuple-element.267, bf16[4,832,768]{2,0,1:T(4,128)(2,1)} %copy-done.35), kind=kOutput, calls=%fused_computation.18 | convolution fusion | flops 3925868544 | bytes 19660800 | tf_op jit(solution)/shard_map/dot_general | solution.py:377
  580.1 11.0 %fusion.11 = f32[4,768,768]{2,1,0:T(8,128)} fusion(bf16[4,832,768]{2,1,0:T(8,128)(2,1)} %fusion.5, bf16[4,832,768]{2,0,1:T(4,128)(2,1)} %copy-done.34), kind=kOutput, calls=%fused_computation.22 | convolution fusion | flops 3925868544 | bytes 19660800 | tf_op jit(solution)/shard_map/dot_general | solution.py:377
  591.1 25.0 %collective-permute-done.20 = bf16[8,104,1536]{2,0,1:T(8,128)(2,1)} collective-permute-done((bf16[8,104,1536]{2,0,1:T(8,128)(2,1)}, bf16[8,104,1536]{2,0,1:T(8,128)(2,1)}, u32[]{:S(2)}, u32[]{:S(2)}) %collective-permute-start.20) | collective-permute-done | bytes 2555936 | tf_op jit(solution)/shard_map/ppermute | solution.py:209
  618.8 4.9 fusion.127
  633.5 12.1 %collective-permute-done.22 = bf16[104,1536]{1,0:T(8,128)(2,1)S(1)} collective-permute-done((bf16[104,1536]{1,0:T(8,128)(2,1)S(1)}, bf16[104,1536]{1,0:T(8,128)(2,1)S(1)}, u32[]{:S(2)}, u32[]{:S(2)}) %collective-permute-start.22) | collective-permute-done | bytes 319520 | tf_op jit(solution)/shard_map/ppermute | solution.py:209
  650.2 16.1 %collective-permute-done.24 = bf16[104,1536]{1,0:T(8,128)(2,1)S(1)} collective-permute-done((bf16[104,1536]{1,0:T(8,128)(2,1)S(1)}, bf16[104,1536]{1,0:T(8,128)(2,1)S(1)}, u32[]{:S(2)}, u32[]{:S(2)}) %collective-permute-start.24) | collective-permute-done | bytes 319520 | tf_op jit(solution)/shard_map/ppermute | solution.py:209
  666.3 7.9 collective-permute-done.25
  682.5 4.5 fusion.64
  688.9 4.9 fusion.17
  693.8 83.6 %shard_map.315 = (f32[2,40,8,1536]{3,2,1,0:T(8,128)S(1)}, f32[2,40,8,1536]{3,2,1,0:T(8,128)S(1)}, f32[2,5,8,1024]{3,2,1,0:T(8,128)S(1)}, f32[2,5,8,1024]{3,2,1,0...) custom-call(f32[2,40,8,1536]{3,2,1,0:T(8,128)S(1)} %copy-done.2, ...), custom_call_target="tpu_custom_call" | custom-call | tf_op jit(solution)/shard_map/pallas_call | solution.py:176
  792.0 4.4 multiply_reduce_fusion
  799.3 7.0 add_convert_fusion
  821.3 8.3 reshape.1335
  829.7 6.6 copy.700
  836.3 7.1 reshape_reshape.26
  885.4 11.8 %collective-permute-done.39 = bf16[2,2,2,96,384]{4,3,2,1,0:T(8,128)(2,1)S(1)} collective-permute-done((bf16[2,2,2,96,384]{4,3,2,1,0:T(8,128)(2,1)S(1)}, bf16[2,2,2,96,384]{4,3,2,1,0:T(8,128)(2,1)S(1)}, u32[]{:S(2)}, u32[]{:S(2)}) %collective-permute-start.39) | collective-permute-done | bytes 589856 | tf_op jit(solution)/shard_map/ppermute | solution.py:209
  897.8 12.0 %collective-permute-done.34 = bf16[2,2,2,96,384]{4,3,1,0,2:T(8,128)(2,1)S(1)} collective-permute-done((bf16[2,2,2,96,384]{4,3,1,0,2:T(8,128)(2,1)S(1)}, bf16[2,2,2,96,384]{4,3,1,0,2:T(8,128)(2,1)S(1)}, u32[]{:S(2)}, u32[]{:S(2)}) %collective-permute-start.34) | collective-permute-done | bytes 589856 | tf_op jit(solution)/shard_map/ppermute | solution.py:209
  910.6 11.0 %collective-permute-start.41 = (bf16[2,96,384]{2,1,0:T(8,128)(2,1)S(1)}, bf16[2,96,384]{2,1,0:T(8,128)(2,1)S(1)}, u32[]{:S(2)}, u32[]{:S(2)}) collective-permute-start(bf16[2,96,384]{2,1,0:T(8,128)(2,1)S(1)} %fusion.77), channel_id=1, source_target_pairs={{0,16},{4,20},{8,24},{12,28},{16,0},{20,4},{24,8},{28,12},{1,17},{... | collective-permute-start | bytes 442376 | tf_op jit(solution)/shard_map/ppermute | solution.py:209
  921.7 5.8 collective-permute-start.36
  929.1 8.0 collective-permute-start.42
  937.3 7.6 collective-permute-start.31
  944.9 7.4 collective-permute-done.31
  (517 shorter events, 282.2 us)
Async XLA Ops:
  7.2 8.0 collective-permute-start
  12.2 6.3 collective-permute-start.5
  13.8 87.2 %copy-start.74 = (f32[2,320]{1,0:T(2,128)}, f32[2,320]{1,0:T(2,128)S(1)}, u32[]{:S(2)}) copy-start(f32[2,320]{1,0:T(2,128)S(1)} %add_rsqrt_fusion.1) | copy-start | bytes 7684
  15.3 18.7 %collective-permute-start.1 = (bf16[2,120,384]{2,1,0:T(8,128)(2,1)S(1)}, bf16[2,120,384]{2,1,0:T(8,128)(2,1)S(1)}, u32[]{:S(2)}, u32[]{:S(2)}) collective-permute-start(bf16[2,120,384]{2,1,0:T(8,128)(2,1)S(1)} %maximum_select_fusion.12), channel_id=1, source_target_pairs={{0,16},{4,20},{8,24},{12,28},{16,0},{20,4},{24,8},{28,12},{1,17},{... | collective-permute-start | bytes 552968 | tf_op jit(solution)/shard_map/ppermute | solution.py:209
  18.5 20.5 %collective-permute-start.6 = (bf16[2,192,384]{2,1,0:T(8,128)(2,1)S(1)}, bf16[2,192,384]{2,1,0:T(8,128)(2,1)S(1)}, u32[]{:S(2)}, u32[]{:S(2)}) collective-permute-start(bf16[2,192,384]{2,1,0:T(8,128)(2,1)S(1)} %maximum_select_fusion.10), channel_id=1, source_target_pairs={{0,16},{4,20},{8,24},{12,28},{16,0},{20,4},{24,8},{28,12},{1,17},{... | collective-permute-start | bytes 884744 | tf_op jit(solution)/shard_map/ppermute | solution.py:209
  34.0 9.6 collective-permute-start.2
  39.1 15.7 %collective-permute-start.7 = (bf16[2,2,192,384]{3,2,1,0:T(8,128)(2,1)S(1)}, bf16[2,2,192,384]{3,2,1,0:T(8,128)(2,1)S(1)}, u32[]{:S(2)}, u32[]{:S(2)}) collective-permute-start(bf16[2,2,192,384]{3,2,1,0:T(8,128)(2,1)S(1)} %maximum_select_fusion.8), channel_id=1, source_target_pairs={{0,4},{4,0},{8,12},{12,8},{16,20},{20,16},{24,28},{28,24},{1,5},{5... | collective-permute-start | bytes 1769480 | tf_op jit(solution)/shard_map/ppermute | solution.py:209
  43.8 14.7 %collective-permute-start.3 = (bf16[2,2,2,120,384]{4,3,0,2,1:T(8,128)(2,1)S(1)}, bf16[2,2,2,120,384]{4,3,0,2,1:T(8,128)(2,1)S(1)}, u32[]{:S(2)}, u32[]{:S(2)}) collective-permute-start(bf16[2,2,2,120,384]{4,3,0,2,1:T(8,128)(2,1)S(1)} %maximum_select_fusion.7), channel_id=1, source_target_pairs={{0,2},{1,3},{2,0},{3,1},{4,6},{5,7},{6,4},{7,5},{8,10},{9,11},{10,... | collective-permute-start | bytes 2211848 | tf_op jit(solution)/shard_map/ppermute | solution.py:209
  56.0 27.4 %collective-permute-start.8 = (bf16[2,2,2,192,384]{4,3,0,2,1:T(8,128)(2,1)}, bf16[2,2,2,192,384]{4,3,0,2,1:T(8,128)(2,1)}, u32[]{:S(2)}, u32[]{:S(2)}) collective-permute-start(bf16[2,2,2,192,384]{4,3,0,2,1:T(8,128)(2,1)} %maximum_select_fusion.6), channel_id=1, source_target_pairs={{0,2},{1,3},{2,0},{3,1},{4,6},{5,7},{6,4},{7,5},{8,10},{9,11},{10,... | collective-permute-start | bytes 3538952 | tf_op jit(solution)/shard_map/ppermute | solution.py:209
  60.7 29.5 %collective-permute-start.4 = (bf16[2,2,2,2,120,384]{5,4,1,3,2,0:T(8,128)(2,1)}, bf16[2,2,2,2,120,384]{5,4,1,3,2,0:T(8,128)(2,1)}, u32[]{:S(2)}, u32[]{:S(2)}) collective-permute-start(bf16[2,2,2,2,120,384]{5,4,1,3,2,0:T(8,128)(2,1)} %maximum_select_fusion.4), channel_id=1, source_target_pairs={{0,1},{1,0},{2,3},{3,2},{4,5},{5,4},{6,7},{7,6},{8,9},{9,8},{10,11... | collective-permute-start | bytes 4423688 | tf_op jit(solution)/shard_map/ppermute | solution.py:209
  61.3 135.0 %copy-start.77 = (s32[640]{0:T(1024)}, s32[640]{0:T(1024)S(1)}, u32[]{:S(2)}) copy-start(s32[640]{0:T(1024)S(1)} %fusion.109) | copy-start | bytes 7684
  86.8 70.5 %collective-permute-start.9 = (bf16[2,2,2,2,192,384]{5,4,1,3,2,0:T(8,128)(2,1)}, bf16[2,2,2,2,192,384]{5,4,1,3,2,0:T(8,128)(2,1)}, u32[]{:S(2)}, u32[]{:S(2)}) collective-permute-start(bf16[2,2,2,2,192,384]{5,4,1,3,2,0:T(8,128)(2,1)} %maximum_select_fusion.2), channel_id=1, source_target_pairs={{0,1},{1,0},{2,3},{3,2},{4,5},{5,4},{6,7},{7,6},{8,9},{9,8},{10,11... | collective-permute-start | bytes 7077896 | tf_op jit(solution)/shard_map/ppermute | solution.py:209
  198.6 69.6 %collective-permute-start.16 = (bf16[104,1536]{1,0:T(8,128)(2,1)S(1)}, bf16[104,1536]{1,0:T(8,128)(2,1)S(1)}, u32[]{:S(2)}, u32[]{:S(2)}) collective-permute-start(bf16[104,1536]{1,0:T(8,128)(2,1)S(1)} %get-tuple-element.227), channel_id=1, source_target_pairs={{0,28},{4,24},{8,20},{12,16},{16,12},{20,8},{24,4},{28,0},{1,29},{... | collective-permute-start | bytes 958472 | tf_op jit(solution)/shard_map/ppermute | solution.py:209
  206.2 61.2 %collective-permute-start.15 = (bf16[104,1536]{1,0:T(8,128)(2,1)S(1)}, bf16[104,1536]{1,0:T(8,128)(2,1)S(1)}, u32[]{:S(2)}, u32[]{:S(2)}) collective-permute-start(bf16[104,1536]{1,0:T(8,128)(2,1)S(1)} %get-tuple-element.228), channel_id=1, source_target_pairs={{0,24},{4,28},{8,16},{12,20},{16,8},{20,12},{24,0},{28,4},{1,25},{... | collective-permute-start | bytes 958472 | tf_op jit(solution)/shard_map/ppermute | solution.py:209
  206.2 60.3 %collective-permute-start.14 = (bf16[104,1536]{1,0:T(8,128)(2,1)S(1)}, bf16[104,1536]{1,0:T(8,128)(2,1)S(1)}, u32[]{:S(2)}, u32[]{:S(2)}) collective-permute-start(bf16[104,1536]{1,0:T(8,128)(2,1)S(1)} %get-tuple-element.229), channel_id=1, source_target_pairs={{0,20},{4,16},{8,28},{12,24},{16,4},{20,0},{24,12},{28,8},{1,21},{... | collective-permute-start | bytes 958472 | tf_op jit(solution)/shard_map/ppermute | solution.py:209
  206.2 59.5 %collective-permute-start.13 = (bf16[104,1536]{1,0:T(8,128)(2,1)S(1)}, bf16[104,1536]{1,0:T(8,128)(2,1)S(1)}, u32[]{:S(2)}, u32[]{:S(2)}) collective-permute-start(bf16[104,1536]{1,0:T(8,128)(2,1)S(1)} %get-tuple-element.230), channel_id=1, source_target_pairs={{0,16},{4,20},{8,24},{12,28},{16,0},{20,4},{24,8},{28,12},{1,17},{... | collective-permute-start | bytes 958472 | tf_op jit(solution)/shard_map/ppermute | solution.py:209
  209.2 12.1 %collective-permute-start.10 = (bf16[104,1536]{1,0:T(8,128)(2,1)S(1)}, bf16[104,1536]{1,0:T(8,128)(2,1)S(1)}, u32[]{:S(2)}, u32[]{:S(2)}) collective-permute-start(bf16[104,1536]{1,0:T(8,128)(2,1)S(1)} %get-tuple-element.233), channel_id=1, source_target_pairs={{0,4},{4,0},{8,12},{12,8},{16,20},{20,16},{24,28},{28,24},{1,5},{5... | collective-permute-start | bytes 958472 | tf_op jit(solution)/shard_map/ppermute | solution.py:209
  221.3 19.7 %collective-permute-start.11 = (bf16[104,1536]{1,0:T(8,128)(2,1)S(1)}, bf16[104,1536]{1,0:T(8,128)(2,1)S(1)}, u32[]{:S(2)}, u32[]{:S(2)}) collective-permute-start(bf16[104,1536]{1,0:T(8,128)(2,1)S(1)} %get-tuple-element.232), channel_id=1, source_target_pairs={{0,8},{4,12},{8,0},{12,4},{16,24},{20,28},{24,16},{28,20},{1,9},{5... | collective-permute-start | bytes 958472 | tf_op jit(solution)/shard_map/ppermute | solution.py:209
  241.1 23.8 %collective-permute-start.12 = (bf16[104,1536]{1,0:T(8,128)(2,1)S(1)}, bf16[104,1536]{1,0:T(8,128)(2,1)S(1)}, u32[]{:S(2)}, u32[]{:S(2)}) collective-permute-start(bf16[104,1536]{1,0:T(8,128)(2,1)S(1)} %get-tuple-element.231), channel_id=1, source_target_pairs={{0,12},{4,8},{8,4},{12,0},{16,28},{20,24},{24,20},{28,16},{1,13},{... | collective-permute-start | bytes 958472 | tf_op jit(solution)/shard_map/ppermute | solution.py:209
  264.8 60.4 %copy-start.57 = (bf16[104,1536]{1,0:T(8,128)(2,1)}, bf16[104,1536]{1,0:T(8,128)(2,1)S(1)}, u32[]{:S(2)}) copy-start(bf16[104,1536]{1,0:T(8,128)(2,1)S(1)} %collective-permute-done.12) | copy-start | bytes 958468
  265.7 59.5 %copy-start.54 = (bf16[104,1536]{1,0:T(8,128)(2,1)}, bf16[104,1536]{1,0:T(8,128)(2,1)S(1)}, u32[]{:S(2)}) copy-start(bf16[104,1536]{1,0:T(8,128)(2,1)S(1)} %collective-permute-done.13) | copy-start | bytes 958468
  266.5 58.7 %copy-start.53 = (bf16[104,1536]{1,0:T(8,128)(2,1)}, bf16[104,1536]{1,0:T(8,128)(2,1)S(1)}, u32[]{:S(2)}) copy-start(bf16[104,1536]{1,0:T(8,128)(2,1)S(1)} %collective-permute-done.14) | copy-start | bytes 958468
  269.0 56.2 %collective-permute-start.17 = (bf16[8,104,1536]{2,1,0:T(8,128)(2,1)S(1)}, bf16[8,104,1536]{2,1,0:T(8,128)(2,1)S(1)}, u32[]{:S(2)}, u32[]{:S(2)}) collective-permute-start(bf16[8,104,1536]{2,1,0:T(8,128)(2,1)S(1)} %get-tuple-element.241), channel_id=1, source_target_pairs={{0,2},{1,3},{2,0},{3,1},{4,6},{5,7},{6,4},{7,5},{8,10},{9,11},{10,... | collective-permute-start | bytes 7667720 | tf_op jit(solution)/shard_map/ppermute | solution.py:209
  327.5 24.7 %collective-permute-start.18 = (bf16[16,104,1536]{2,1,0:T(8,128)(2,1)}, bf16[16,104,1536]{2,1,0:T(8,128)(2,1)}, u32[]{:S(2)}, u32[]{:S(2)}) collective-permute-start(bf16[16,104,1536]{2,1,0:T(8,128)(2,1)} %constant_dynamic-update-slice_fusion.4), channel_id=1, source_target_pairs={{0,1},{1,0},{2,3},{3,2},{4,5},{5,4},{6,7},{7,6},{8,9},{9,8},{10,11... | collective-permute-start | bytes 15335432 | tf_op jit(solution)/shard_map/ppermute | solution.py:209
  518.4 23.7 %collective-permute-start.19 = (bf16[16,104,1536]{2,0,1:T(8,128)(2,1)}, bf16[16,104,1536]{2,0,1:T(8,128)(2,1)}, u32[]{:S(2)}, u32[]{:S(2)}) collective-permute-start(bf16[16,104,1536]{2,0,1:T(8,128)(2,1)} %bitcast.77), channel_id=1, source_target_pairs={{0,1},{1,0},{2,3},{3,2},{4,5},{5,4},{6,7},{7,6},{8,9},{9,8},{10,11... | collective-permute-start | bytes 15335432 | tf_op jit(solution)/shard_map/ppermute | solution.py:209
  558.4 57.7 %collective-permute-start.20 = (bf16[8,104,1536]{2,0,1:T(8,128)(2,1)}, bf16[8,104,1536]{2,0,1:T(8,128)(2,1)}, u32[]{:S(2)}, u32[]{:S(2)}) collective-permute-start(bf16[8,104,1536]{2,0,1:T(8,128)(2,1)} %slice.431), channel_id=1, source_target_pairs={{0,2},{1,3},{2,0},{3,1},{4,6},{5,7},{6,4},{7,5},{8,10},{9,11},{10,... | collective-permute-start | bytes 7667720 | tf_op jit(solution)/shard_map/ppermute | solution.py:209
  624.0 8.7 collective-permute-start.21
  625.7 19.9 %collective-permute-start.22 = (bf16[104,1536]{1,0:T(8,128)(2,1)S(1)}, bf16[104,1536]{1,0:T(8,128)(2,1)S(1)}, u32[]{:S(2)}, u32[]{:S(2)}) collective-permute-start(bf16[104,1536]{1,0:T(8,128)(2,1)S(1)} %bitcast.507), channel_id=1, source_target_pairs={{0,8},{4,12},{8,0},{12,4},{16,24},{20,28},{24,16},{28,20},{1,9},{5... | collective-permute-start | bytes 958472 | tf_op jit(solution)/shard_map/ppermute | solution.py:209
  625.7 24.5 %collective-permute-start.23 = (bf16[104,1536]{1,0:T(8,128)(2,1)S(1)}, bf16[104,1536]{1,0:T(8,128)(2,1)S(1)}, u32[]{:S(2)}, u32[]{:S(2)}) collective-permute-start(bf16[104,1536]{1,0:T(8,128)(2,1)S(1)} %bitcast.504), channel_id=1, source_target_pairs={{0,12},{4,8},{8,4},{12,0},{16,28},{20,24},{24,20},{28,16},{1,13},{... | collective-permute-start | bytes 958472 | tf_op jit(solution)/shard_map/ppermute | solution.py:209
  627.5 38.8 %collective-permute-start.24 = (bf16[104,1536]{1,0:T(8,128)(2,1)S(1)}, bf16[104,1536]{1,0:T(8,128)(2,1)S(1)}, u32[]{:S(2)}, u32[]{:S(2)}) collective-permute-start(bf16[104,1536]{1,0:T(8,128)(2,1)S(1)} %bitcast.503), channel_id=1, source_target_pairs={{0,16},{4,20},{8,24},{12,28},{16,0},{20,4},{24,8},{28,12},{1,17},{... | collective-permute-start | bytes 958472 | tf_op jit(solution)/shard_map/ppermute | solution.py:209
  627.5 46.7 %collective-permute-start.25 = (bf16[104,1536]{1,0:T(8,128)(2,1)S(1)}, bf16[104,1536]{1,0:T(8,128)(2,1)S(1)}, u32[]{:S(2)}, u32[]{:S(2)}) collective-permute-start(bf16[104,1536]{1,0:T(8,128)(2,1)S(1)} %bitcast.502), channel_id=1, source_target_pairs={{0,20},{4,16},{8,28},{12,24},{16,4},{20,0},{24,12},{28,8},{1,21},{... | collective-permute-start | bytes 958472 | tf_op jit(solution)/shard_map/ppermute | solution.py:209
  632.6 41.6 %collective-permute-start.26 = (bf16[104,1536]{1,0:T(8,128)(2,1)S(1)}, bf16[104,1536]{1,0:T(8,128)(2,1)S(1)}, u32[]{:S(2)}, u32[]{:S(2)}) collective-permute-start(bf16[104,1536]{1,0:T(8,128)(2,1)S(1)} %bitcast.506), channel_id=1, source_target_pairs={{0,24},{4,28},{8,16},{12,20},{16,8},{20,12},{24,0},{28,4},{1,25},{... | collective-permute-start | bytes 958472 | tf_op jit(solution)/shard_map/ppermute | solution.py:209
  645.6 28.7 %collective-permute-start.27 = (bf16[104,1536]{1,0:T(8,128)(2,1)S(1)}, bf16[104,1536]{1,0:T(8,128)(2,1)S(1)}, u32[]{:S(2)}, u32[]{:S(2)}) collective-permute-start(bf16[104,1536]{1,0:T(8,128)(2,1)S(1)} %bitcast.505), channel_id=1, source_target_pairs={{0,28},{4,24},{8,20},{12,16},{16,12},{20,8},{24,4},{28,0},{1,29},{... | collective-permute-start | bytes 958472 | tf_op jit(solution)/shard_map/ppermute | solution.py:209
  846.2 33.0 %collective-permute-start.38 = (bf16[2,2,2,2,96,384]{5,4,3,2,1,0:T(8,128)(2,1)}, bf16[2,2,2,2,96,384]{5,4,3,2,1,0:T(8,128)(2,1)}, u32[]{:S(2)}, u32[]{:S(2)}) collective-permute-start(bf16[2,2,2,2,96,384]{5,4,3,2,1,0:T(8,128)(2,1)} %fusion.47), channel_id=1, source_target_pairs={{0,1},{1,0},{2,3},{3,2},{4,5},{5,4},{6,7},{7,6},{8,9},{9,8},{10,11... | collective-permute-start | bytes 3538952 | tf_op jit(solution)/shard_map/ppermute | solution.py:209
  872.2 10.3 %collective-permute-start.33 = (bf16[2,2,2,2,96,384]{5,4,1,0,2,3:T(8,128)(2,1)S(1)}, bf16[2,2,2,2,96,384]{5,4,1,0,2,3:T(8,128)(2,1)S(1)}, u32[]{:S(2)}, u32[]{:S(2)}) collective-permute-start(bf16[2,2,2,2,96,384]{5,4,1,0,2,3:T(8,128)(2,1)S(1)} %fusion.48), channel_id=1, source_target_pairs={{0,1},{1,0},{2,3},{3,2},{4,5},{5,4},{6,7},{7,6},{8,9},{9,8},{10,11... | collective-permute-start | bytes 3538952 | tf_op jit(solution)/shard_map/ppermute | solution.py:209
  875.9 7.6 collective-permute-start.28
  880.9 16.3 %collective-permute-start.39 = (bf16[2,2,2,96,384]{4,3,2,1,0:T(8,128)(2,1)S(1)}, bf16[2,2,2,96,384]{4,3,2,1,0:T(8,128)(2,1)S(1)}, u32[]{:S(2)}, u32[]{:S(2)}) collective-permute-start(bf16[2,2,2,96,384]{4,3,2,1,0:T(8,128)(2,1)S(1)} %fusion.62), channel_id=1, source_target_pairs={{0,2},{1,3},{2,0},{3,1},{4,6},{5,7},{6,4},{7,5},{8,10},{9,11},{10,... | collective-permute-start | bytes 1769480 | tf_op jit(solution)/shard_map/ppermute | solution.py:209
  882.9 26.9 %collective-permute-start.34 = (bf16[2,2,2,96,384]{4,3,1,0,2:T(8,128)(2,1)S(1)}, bf16[2,2,2,96,384]{4,3,1,0,2:T(8,128)(2,1)S(1)}, u32[]{:S(2)}, u32[]{:S(2)}) collective-permute-start(bf16[2,2,2,96,384]{4,3,1,0,2:T(8,128)(2,1)S(1)} %fusion.61), channel_id=1, source_target_pairs={{0,2},{1,3},{2,0},{3,1},{4,6},{5,7},{6,4},{7,5},{8,10},{9,11},{10,... | collective-permute-start | bytes 1769480 | tf_op jit(solution)/shard_map/ppermute | solution.py:209
  883.8 43.6 %collective-permute-start.29 = (bf16[2,2,2,120,384]{4,3,1,0,2:T(8,128)(2,1)S(1)}, bf16[2,2,2,120,384]{4,3,1,0,2:T(8,128)(2,1)S(1)}, u32[]{:S(2)}, u32[]{:S(2)}) collective-permute-start(bf16[2,2,2,120,384]{4,3,1,0,2:T(8,128)(2,1)S(1)} %fusion.57), channel_id=1, source_target_pairs={{0,2},{1,3},{2,0},{3,1},{4,6},{5,7},{6,4},{7,5},{8,10},{9,11},{10,... | collective-permute-start | bytes 2211848 | tf_op jit(solution)/shard_map/ppermute | solution.py:209
  897.4 13.1 %collective-permute-start.40 = (bf16[2,2,96,384]{3,2,1,0:T(8,128)(2,1)S(1)}, bf16[2,2,96,384]{3,2,1,0:T(8,128)(2,1)S(1)}, u32[]{:S(2)}, u32[]{:S(2)}) collective-permute-start(bf16[2,2,96,384]{3,2,1,0:T(8,128)(2,1)S(1)} %fusion.73), channel_id=1, source_target_pairs={{0,4},{4,0},{8,12},{12,8},{16,20},{20,16},{24,28},{28,24},{1,5},{5... | collective-permute-start | bytes 884744 | tf_op jit(solution)/shard_map/ppermute | solution.py:209
  910.0 11.6 %collective-permute-start.35 = (bf16[2,2,96,384]{3,2,1,0:T(8,128)(2,1)S(1)}, bf16[2,2,96,384]{3,2,1,0:T(8,128)(2,1)S(1)}, u32[]{:S(2)}, u32[]{:S(2)}) collective-permute-start(bf16[2,2,96,384]{3,2,1,0:T(8,128)(2,1)S(1)} %fusion.72), channel_id=1, source_target_pairs={{0,4},{4,0},{8,12},{12,8},{16,20},{20,16},{24,28},{28,24},{1,5},{5... | collective-permute-start | bytes 884744 | tf_op jit(solution)/shard_map/ppermute | solution.py:209
  910.6 18.4 %collective-permute-start.41 = (bf16[2,96,384]{2,1,0:T(8,128)(2,1)S(1)}, bf16[2,96,384]{2,1,0:T(8,128)(2,1)S(1)}, u32[]{:S(2)}, u32[]{:S(2)}) collective-permute-start(bf16[2,96,384]{2,1,0:T(8,128)(2,1)S(1)} %fusion.77), channel_id=1, source_target_pairs={{0,16},{4,20},{8,24},{12,28},{16,0},{20,4},{24,8},{28,12},{1,17},{... | collective-permute-start | bytes 442376 | tf_op jit(solution)/shard_map/ppermute | solution.py:209
  921.7 15.4 %collective-permute-start.36 = (bf16[2,96,384]{2,1,0:T(8,128)(2,1)S(1)}, bf16[2,96,384]{2,1,0:T(8,128)(2,1)S(1)}, u32[]{:S(2)}, u32[]{:S(2)}) collective-permute-start(bf16[2,96,384]{2,1,0:T(8,128)(2,1)S(1)} %fusion.76), channel_id=1, source_target_pairs={{0,16},{4,20},{8,24},{12,28},{16,0},{20,4},{24,8},{28,12},{1,17},{... | collective-permute-start | bytes 442376 | tf_op jit(solution)/shard_map/ppermute | solution.py:209
  927.7 9.5 collective-permute-start.30
  929.1 15.8 %collective-permute-start.42 = (bf16[96,384]{1,0:T(8,128)(2,1)S(1)}, bf16[96,384]{1,0:T(8,128)(2,1)S(1)}, u32[]{:S(2)}, u32[]{:S(2)}) collective-permute-start(bf16[96,384]{1,0:T(8,128)(2,1)S(1)} %fusion.85), channel_id=1, source_target_pairs={{0,8},{4,12},{8,0},{12,4},{16,24},{20,28},{24,16},{28,20},{1,9},{5... | collective-permute-start | bytes 221192 | tf_op jit(solution)/shard_map/ppermute | solution.py:209
  937.1 15.9 %collective-permute-start.37 = (bf16[96,384]{1,0:T(8,128)(2,1)S(1)}, bf16[96,384]{1,0:T(8,128)(2,1)S(1)}, u32[]{:S(2)}, u32[]{:S(2)}) collective-permute-start(bf16[96,384]{1,0:T(8,128)(2,1)S(1)} %fusion.84), channel_id=1, source_target_pairs={{0,8},{4,12},{8,0},{12,4},{16,24},{20,28},{24,16},{28,20},{1,9},{5... | collective-permute-start | bytes 221192 | tf_op jit(solution)/shard_map/ppermute | solution.py:209
  937.3 15.0 %collective-permute-start.31 = (bf16[2,120,384]{2,1,0:T(8,128)(2,1)S(1)}, bf16[2,120,384]{2,1,0:T(8,128)(2,1)S(1)}, u32[]{:S(2)}, u32[]{:S(2)}) collective-permute-start(bf16[2,120,384]{2,1,0:T(8,128)(2,1)S(1)} %fusion.75), channel_id=1, source_target_pairs={{0,16},{4,20},{8,24},{12,28},{16,0},{20,4},{24,8},{28,12},{1,17},{... | collective-permute-start | bytes 552968 | tf_op jit(solution)/shard_map/ppermute | solution.py:209
  952.4 4.6 collective-permute-start.32
  (88 other events, 782.7 us)
where the time goes:
time: 977 us; the launch traced here: 963 us
  local copies, waits for them, and re-layouts  339 us (35%)
  waiting for transfers between devices  251 us (26%)
  Pallas kernels  114 us (12%)
  matrix products  105 us (11%)
  starting transfers between devices  83.8 us (9%)
  other arithmetic  67 us (7%)
    ppermute x43, waiting for transfers between devices, swap(): return lax.ppermute(x, axis, [(i, i ^ bit) for i in range(n)])  251 us
    ppermute x43, starting transfers between devices, swap(): return lax.ppermute(x, axis, [(i, i ^ bit) for i in range(n)])  83.8 us
    pallas_call x1, Pallas kernels, scan_bwd(): pl.pallas_call(functools.partial(bwd_kernel, T, Q, Q2), grid=(S, C), in_s...  83.6 us
    concatenate x10, local copies, waits for them, and re-layouts, on_device(): arrived = jnp.concatenate([arrived, swap(arrived, 'col', bit)], axis=0)  78.3 us
    dot_general x6, matrix products, bmm(): lax.dot_general(a, b, (((da,), (db,)), ((0,), (0,))), preferred_element_t...  57.9 us
    dot_general x20, matrix products, mm(): lax.dot_general(a, b, (dims, ((), ())), preferred_element_type=F32, **kw)  47.3 us
    slice x5, local copies, waits for them, and re-layouts, on_device(): back = back[:half] + swap(back[half:].astype(BF), 'col', bit).astype(F32)  41.7 us
    unnamed x223, local copies, waits for them, and re-layouts  39.4 us
  transfers between devices with their start and end apart: 43, of which 20 were waited for; matrix products, arithmetic and copies ran while one was open for 18% of the time, Pallas kernels for 3%

commit v1 on v0

--- a/solution.py
+++ b/solution.py
@@ -214,50 +214,205 @@
     return [1 << k for k in range(n.bit_length() - 1)]
 
 
-def gather_steps():
+def exchange(x, mask):
+    rm, cm = mask
+    if rm == 0:
+        return swap(x, "col", cm)
+    if cm == 0:
+        return swap(x, "row", rm)
+    rows, cols = lax.axis_size("row"), lax.axis_size("col")
+    pairs = [(r * cols + c, (r ^ rm) * cols + (c ^ cm)) for r in range(rows) for c in range(cols)]
+    return lax.ppermute(x, ("row", "col"), pairs)
+
+
+def combos(bits):
+    out = [(0, 0)]
+    for rb, cb in bits:
+        out = out + [(r | rb, c | cb) for r, c in out]
+    return out
+
+
+def stages():
     row, col = bits_of("row"), bits_of("col")
-    return [("row", b) for b in row[1:] + row[:1]] + [("col", b) for b in col[::-1]]
-
-
-def bit_set(axis, bit):
-    return (lax.axis_index(axis) & bit) != 0
-
-
-def gather_blocks(x):
+    far = combos([(b, 0) for b in row[1:]])
+    plane = combos([(row[0], 0)] + [(0, b) for b in col[1:]])
+    return far, plane, (0, col[0])
+
+
+def add(a, b):
+    return (a[0] ^ b[0], a[1] ^ b[1])
+
+
+def gather_list(x):
+    far, plane, core = stages()
+    mine = jnp.stack([x] + [exchange(x, m) for m in far[1:]])
+    near = [([add(f, m) for f in far], mine if m == (0, 0) else exchange(mine, m)) for m in plane]
+    return near + [([add(m, core) for m in ms], exchange(b, core)) for ms, b in near]
+
+
+def assemble_kernel(masks, moves, count_in, *refs):
+    r0, c0 = refs[0][0], refs[0][1]
+    ins, outs = refs[1:1 + count_in], refs[1 + count_in:]
+    for buf, ms in zip(ins, masks):
+        for i, (rm, cm) in enumerate(ms):
+            for (row, count, lanes), out, place in moves:
+                place(outs[out], r0 ^ rm, c0 ^ cm, buf[i, row:row + count, :lanes])
+
+
+def put_block(out, r, c, block):
+    n, m = block.shape
+    out[pl.ds(pl.multiple_of(r * n, n), n), pl.ds(pl.multiple_of(c * m, m), m)] = block
+
+
+def put_pair(out, r, c, block):
+    out[r, c] = block
+
+
+def take_blocks(gathered):
     rows, cols = lax.axis_size("row"), lax.axis_size("col")
-    dims = {}
-    out = x
-    order = []
-    for axis, bit in gather_steps():
-        other = swap(out, axis, bit)
-        up = bit_set(axis, bit)
-        out = jnp.where(up, jnp.stack([other, out]), jnp.stack([out, other]))
-        order.insert(0, (axis, bit))
-    n = len(order)
-    wanted = [("row", b) for b in bits_of("row")[::-1]] + [("col", b) for b in bits_of("col")[::-1]]
-    perm = [order.index(w) for w in wanted] + list(range(n, n + x.ndim))
-    out = out.reshape((2,) * n + x.shape).transpose(perm)
-    return out.reshape((rows, cols) + x.shape)
-
-
-def reduce_blocks(x):
-    block = x.shape[2:]
-    row, col = bits_of("row"), bits_of("col")
-    names = [("row", b) for b in row[::-1]] + [("col", b) for b in col[::-1]]
-    x = x.reshape((2,) * len(names) + block)
-    for axis, bit in gather_steps()[::-1]:
-        d = names.index((axis, bit))
-        names.pop(d)
-        mine = bit_set(axis, bit).astype(jnp.int32)
-        keep = lax.dynamic_index_in_dim(x, mine, d, keepdims=False)
-        give = lax.dynamic_index_in_dim(x, 1 - mine, d, keepdims=False).astype(BF)
-        x = keep + swap(give, axis, bit).astype(F32)
-    return x
+    order = [r * cols + c for ms, _ in gathered for r, c in ms]
+    entry = jnp.asarray([order.index(i) for i in range(rows * cols)], jnp.int32)
+    me = lax.axis_index("row") * cols + lax.axis_index("col")
+    stacked = jnp.concatenate([b for _, b in gathered], axis=0)
+    out = jnp.take(stacked, entry[jnp.arange(rows * cols, dtype=jnp.int32) ^ me], axis=0)
+    return out.reshape((rows, cols) + stacked.shape[1:])
+
+
+def assemble(gathered, moves, shapes):
+    masks = [ms for ms, _ in gathered]
+    bufs = [b for _, b in gathered]
+    if any(lanes % 128 for (_, _, lanes), _, _ in moves):
+        every = take_blocks(gathered)
+        cut = [every[:, :, row:row + count, :lanes] for (row, count, lanes), _, _ in moves]
+        return [v if place is put_pair else v.transpose(0, 2, 1, 3).reshape(shape)
+                for v, shape, (_, _, place) in zip(cut, shapes, moves)]
+    me = jnp.stack([lax.axis_index("row"), lax.axis_index("col")]).astype(jnp.int32)
+    vmem = pl.BlockSpec(memory_space=pltpu.VMEM)
+    return pl.pallas_call(
+        functools.partial(assemble_kernel, masks, moves, len(bufs)),
+        in_specs=[pl.BlockSpec(memory_space=pltpu.SMEM)] + [vmem] * len(bufs),
+        out_specs=[vmem] * len(shapes),
+        out_shape=[jax.ShapeDtypeStruct(s, BF) for s in shapes],
+        compiler_params=pltpu.CompilerParams(vmem_limit_bytes=32 << 20),
+        cost_estimate=pl.CostEstimate(flops=0, bytes_accessed=4 * sum(b.size for b in bufs), transcendentals=0),
+    )(me, *bufs)
+
+
+def reduce_list(parts):
+    far, plane, core = stages()
+    rows, cols = lax.axis_size("row"), lax.axis_size("col")
+    r0 = lax.axis_index("row")
+    near = [k for k in range(cols) if not k & core[1]]
+    give = exchange(jnp.stack([parts[k | core[1]] for k in near]), core)
+    sums = {k: parts[k].astype(F32) + give[i].astype(F32) for i, k in enumerate(near)}
+    block = parts[0].shape[1:]
+
+    def rows_of(k, rm):
+        view = sums[k].reshape((rows // 2, 2) + block)
+        return lax.dynamic_index_in_dim(view, (r0 ^ rm) & 1, 1, keepdims=False)
+    total = rows_of(0, 0)
+    for rm, cm in plane[1:]:
+        total = total + exchange(rows_of(cm, rm).astype(BF), (rm, cm)).astype(F32)
+    done = lax.dynamic_index_in_dim(total, r0 >> 1, 0, keepdims=False)
+    for rm, cm in far[1:]:
+        piece = lax.dynamic_index_in_dim(total, (r0 ^ rm) >> 1, 0, keepdims=False)
+        done = done + exchange(piece.astype(BF), (rm, cm)).astype(F32)
+    return done
+
+
+def column_kernel(count, s_ref, *refs):
+    total = mm(refs[0][...], refs[1][...], ((0,), (0,)))
+    for k in range(1, count):
+        total = total + mm(refs[2 * k][...], refs[2 * k + 1][...], ((0,), (0,)))
+    refs[-1][0] = total.astype(BF)
+
+
+def column_blocks(pairs, cols, my_col):
+    n, m = pairs[0][0].shape
+    w = pairs[0][1].shape[1] // cols
+    count = len(pairs)
+    if w % 128:
+        total = sum(mm(a, b, ((0,), (0,))) for a, b in pairs).astype(BF).reshape(m, cols, w).transpose(1, 0, 2)
+        return jnp.take(total, jnp.arange(cols, dtype=jnp.int32) ^ my_col, axis=0)
+    return pl.pallas_call(
+        functools.partial(column_kernel, count),
+        grid_spec=pltpu.PrefetchScalarGridSpec(
+            num_scalar_prefetch=1, grid=(cols,),
+            in_specs=[pl.BlockSpec((n, m), lambda k, s: (0, 0)), pl.BlockSpec((n, w), lambda k, s: (0, s[0] ^ k))] * count,
+            out_specs=pl.BlockSpec((1, m, w), lambda k, s: (k, 0, 0))),
+        out_shape=jax.ShapeDtypeStruct((cols, m, w), BF),
+        compiler_params=pltpu.CompilerParams(vmem_limit_bytes=32 << 20),
+        cost_estimate=pl.CostEstimate(flops=2 * count * n * m * w * cols, bytes_accessed=2 * (count * (n * m + n * w * cols) + m * w * cols), transcendentals=0),
+    )(my_col.reshape(1), *[v for p in pairs for v in p])
 
 
 def gelu_parts(v):
     phi = 0.5 * (1.0 + lax.erf(v * root_half))
     return v * phi, phi + v * jnp.exp(-0.5 * v * v) * inv_root_two_pi
+
+
+def expert_kernel(cols, *refs):
+    both, up, down = refs[:cols], refs[cols], refs[cols + 1]
+    outs, acts, gps = refs[cols + 2:2 * cols + 2], refs[2 * cols + 2], refs[2 * cols + 3]
+    width = up.shape[1]
+    n = both[0].shape[1]
+    rows = jnp.concatenate([b[0] for b in both], axis=0)
+    act, slope = gelu_parts(mm(rows[:, :width], up[0]))
+    act = act.astype(BF)
+    acts[0] = act
+    gp = (mm(rows[:, width:], down[0], ((1,), (1,))) * slope).astype(BF)
+    gps[0] = gp
+    out = mm(act, down[0]).astype(BF)
+    gin = mm(gp, up[0], ((1,), (1,))).astype(BF)
+    for c in range(cols):
+        outs[c][0, :, :width] = out[c * n:(c + 1) * n]
+        outs[c][0, :, width:] = gin[c * n:(c + 1) * n]
+
+
+def weights_kernel(cols, sets, *refs):
+    up, down = refs[-2:]
+    step = cols + 2
+    gu = gd = None
+    width = up.shape[1]
+    for s in range(sets):
+        both, act, gp = refs[s * step:s * step + cols], refs[s * step + cols][0], refs[s * step + cols + 1][0]
+        rows = jnp.concatenate([b[0] for b in both], axis=0)
+        a = mm(rows[:, :width], gp, ((0,), (0,)))
+        b = mm(act, rows[:, width:], ((0,), (0,)))
+        gu, gd = (a, b) if gu is None else (gu + a, gd + b)
+    up[0] = gu
+    down[0] = gd
+
+
+def per_expert(kernel, ins, shapes, flops):
+    tok = lambda a: pl.BlockSpec((1,) + a.shape[1:], lambda e: (e, 0, 0))
+    size = sum(a.size * 2 for a in ins) + sum(s.size * s.dtype.itemsize for s in shapes)
+    return list(pl.pallas_call(
+        kernel, grid=(ins[0].shape[0],),
+        in_specs=[tok(a) for a in ins], out_specs=[tok(s) for s in shapes], out_shape=shapes,
+        compiler_params=pltpu.CompilerParams(vmem_limit_bytes=56 << 20),
+        cost_estimate=pl.CostEstimate(flops=flops, bytes_accessed=size, transcendentals=0),
+    )(*ins))
+
+
+def expert_both(bufs, up, down):
+    cols = len(bufs)
+    experts, d, f = up.shape
+    n = bufs[0].shape[1]
+    shapes = ([jax.ShapeDtypeStruct((experts, n, 2 * d), BF)] * cols
+              + [jax.ShapeDtypeStruct((experts, n * cols, f), BF)] * 2)
+    outs = per_expert(functools.partial(expert_kernel, cols), bufs + [up, down], shapes, 8 * experts * cols * n * d * f)
+    return outs[:cols], outs[cols:]
+
+
+def expert_weights(sets, d, f):
+    cols = len(sets[0]) - 2
+    experts, n, _ = sets[0][0].shape
+    if len(sets) > 1 and len(sets) * cols > 8:
+        return [sum(v) for v in zip(*[expert_weights([s], d, f) for s in sets])]
+    shapes = [jax.ShapeDtypeStruct((experts, d, f), F32), jax.ShapeDtypeStruct((experts, f, d), F32)]
+    return per_expert(functools.partial(weights_kernel, cols, len(sets)), [v for s in sets for v in s], shapes,
+                      4 * experts * cols * n * d * f * len(sets))
 
 
 def to_chunks(b):
@@ -269,7 +424,7 @@
               gain_mix, gain_moe, w_router, w_up, w_down, routes, lengths, cotangent):
     rows, cols = lax.axis_size("row"), lax.axis_size("col")
     parts = rows * cols
-    my_row = lax.axis_index("row")
+    my_col = lax.axis_index("col")
     seqs, length, width = tokens.shape
     experts_here = w_up.shape[0]
     experts_all = experts_here * rows
@@ -283,15 +438,24 @@
     flat = [w_xproj.reshape(-1), w_dt.reshape(-1), w_router.reshape(-1), small.reshape(-1)]
     sizes = [f.shape[0] for f in flat]
     lanes = w_in_x.shape[1]
-    extra = -(-sum(sizes) // (8 * lanes)) * 8
+    extra = -(-sum(sizes) // (16 * lanes)) * 16
     flat = jnp.pad(jnp.concatenate(flat), (0, extra * lanes - sum(sizes))).reshape(extra, lanes)
-    here = w_in_x.shape[0]
-    first = gather_blocks(jnp.concatenate([w_in_x, flat], axis=0))
-    second = gather_blocks(jnp.concatenate([w_in_z.reshape(-1, lanes), w_out.reshape(-1, lanes)], axis=0))
+    here, out_rows, out_lanes = w_in_x.shape[0], w_out.shape[0], w_out.shape[1]
+    wide = -(-out_lanes // 128) * 128
+    first = gather_list(jnp.concatenate([w_in_x, flat], axis=0))
+    full_x, rest = assemble(first, [((0, here, lanes), 0, put_block), ((here, extra, lanes), 1, put_pair)],
+                            [(width, inner), (rows, cols, extra, lanes)])
+    far_end = first[len(first) // 2 - 1][1]
+    late_z, late_o, _ = lax.optimization_barrier((w_in_z, jnp.pad(w_out, ((0, 0), (0, wide - out_lanes))), far_end))
+    (full_z,) = assemble(gather_list(late_z), [((0, here, lanes), 0, put_block)], [(width, inner)])
+    (wide_out,) = assemble(gather_list(late_o), [((0, out_rows, wide), 0, put_block)], [(inner, cols * wide)])
+    lane_of = jnp.arange(cols * wide, dtype=jnp.int32)
+    narrow = jnp.where(lane_of % wide < out_lanes, lane_of // wide * out_lanes + lane_of % wide, -1)
+    narrow = (narrow[:, None] == jnp.arange(width, dtype=jnp.int32)[None, :]).astype(BF)
+    full_out = mm(wide_out, narrow).astype(BF)
     def whole(blocks):
         return blocks.transpose(0, 2, 1, 3).reshape(blocks.shape[0] * blocks.shape[2], -1)
-    full_x = whole(first[:, :, :here])
-    rest = first[:, :, here:].reshape(rows, cols, extra * lanes)
+    rest = rest.reshape(rows, cols, extra * lanes)
     cut = [0]
     for n in sizes:
         cut.append(cut[-1] + n)
@@ -305,155 +469,165 @@
     a_log_f, d_skip_f = chan[taps + 2:taps + 2 + NS], chan[taps + 2 + NS]
     gain_mix_f = small[-1, :, :gain_mix.shape[0]].reshape(width)
     gain_moe_f = small[-1, :, gain_mix.shape[0]:].reshape(width)
-    full_z = whole(second[:, :, :w_in_z.shape[0]])
-    full_out = whole(second[:, :, w_in_z.shape[0]:].reshape((rows, cols) + w_out.shape))
     a_neg = -jnp.exp(a_log_f)
 
-    flat_route = routes.reshape(count)
-    live = (jnp.arange(length, dtype=jnp.int32)[None, :] < lengths[:, None]).reshape(count)
-    live_f = live.astype(F32)[:, None]
-    route_onehot = flat_route[:, None] == jnp.arange(experts_all, dtype=jnp.int32)
-    hits = (route_onehot & live[:, None]).astype(BF).reshape(seqs, length, experts_all)
-    before = jnp.arange(length)[:, None] > jnp.arange(length)[None, :]
-    earlier = jnp.einsum("pq,sqe->spe", before.astype(BF), hits, preferred_element_type=F32)
-    slot = jnp.sum(earlier * hits.astype(F32), axis=-1).astype(jnp.int32).reshape(count)
-    kept = live & (slot < CAP)
-    seq_of = jnp.arange(count, dtype=jnp.int32) // length
-    per_row = experts_here * seqs * CAP
-    target = (((flat_route // experts_here) ^ my_row) * per_row
-              + (flat_route % experts_here) * (seqs * CAP) + seq_of * CAP + slot)
-    target = jnp.where(kept, target, rows * per_row)
-    route_f = route_onehot.astype(F32)
-
-    x = tokens.astype(F32).reshape(count, width)
-    rms1 = lax.rsqrt(jnp.mean(x * x, axis=-1, keepdims=True) + epsilon)
-    hat1 = x * rms1
-    normed_mix = (hat1 * gain_mix_f).astype(BF)
-    inner_x = mm(normed_mix, full_x).reshape(seqs, length, inner)
-    padded = jnp.pad(inner_x, ((0, 0), (taps - 1, 0), (0, 0)))
-    conv_out = conv_b_f
-    for k in range(taps):
-        conv_out = conv_out + conv_w_f[k] * padded[:, k:k + length]
-    conv_sig = jax.nn.sigmoid(conv_out)
-    u_value = conv_out * conv_sig
-    u_low = u_value.astype(BF).reshape(count, inner)
-    projected = mm(u_low, full_xproj)
-    dt_low = projected[:, :R].astype(BF)
-    dt_pre = mm(dt_low, full_dt).reshape(seqs, length, inner)
-    bT = to_chunks(projected[:, R:R + NS].reshape(seqs, length, NS))
-    cT = to_chunks(projected[:, R + NS:].reshape(seqs, length, NS))
-    ssm_out, starts = scan_fwd(u_value, dt_pre, bT, cT, dt_bias_f[None], a_neg * log2e, d_skip_f[None])
-    ssm_out = ssm_out.reshape(count, inner)
-    gate_z = mm(normed_mix, full_z)
-    gate_sig = jax.nn.sigmoid(gate_z)
-    gate_silu = gate_z * gate_sig
-    gated = (ssm_out * gate_silu).astype(BF)
-    hidden = x + mm(gated, full_out)
-
-    rms2 = lax.rsqrt(jnp.mean(hidden * hidden, axis=-1, keepdims=True) + epsilon)
-    hat2 = hidden * rms2
-    normed_moe = hat2 * gain_moe_f
+    shifted = jnp.where(lane_of % wide < out_lanes, (lane_of // wide ^ my_col) * out_lanes + lane_of % wide, -1)
+    shifted = (jnp.arange(width, dtype=jnp.int32)[:, None] == shifted[None, :]).astype(BF)
     router_f = full_router.astype(F32)
-    route_probs = jax.nn.softmax(mm(normed_moe, router_f, precision=highest), axis=-1)
-    gate_prob = jnp.sum(route_probs * route_f, axis=-1, keepdims=True)
-
-    grad_y = live_f * cotangent.reshape(count, width)
-    both = jnp.concatenate([normed_moe.astype(BF), (grad_y * gate_prob).astype(BF)], axis=1)
-    place = jnp.arange(rows * per_row, dtype=jnp.int32)[:, None] == target[None, :]
-    place = place.astype(BF)
-    outgoing = mm(place, both).astype(BF)
-    arrived = [outgoing[:per_row]]
-    for k in range(1, rows):
-        arrived.append(swap(outgoing[k * per_row:(k + 1) * per_row], "row", k))
-    arrived = jnp.stack(arrived)
-    for bit in bits_of("col")[::-1]:
-        arrived = jnp.concatenate([arrived, swap(arrived, "col", bit)], axis=0)
-    sources = rows * cols
-    arrived = arrived.reshape(sources, experts_here, seqs * CAP, 2 * width).transpose(1, 0, 2, 3)
-    arrived = arrived.reshape(experts_here, sources * seqs * CAP, 2 * width)
-    expert_in, grad_eo = arrived[..., :width], arrived[..., width:]
-
-    def bmm(a, b, da, db):
-        return lax.dot_general(a, b, (((da,), (db,)), ((0,), (0,))), preferred_element_type=F32)
-    pre_act = bmm(expert_in, w_up, 2, 1)
-    act, slope = gelu_parts(pre_act)
-    act = act.astype(BF)
-    expert_out = bmm(act, w_down, 2, 1)
-    grad_pre = (bmm(grad_eo, w_down, 2, 2) * slope).astype(BF)
-    grad_ei = bmm(grad_pre, w_up, 2, 2)
-    grad_w_up = bmm(expert_in, grad_pre, 1, 1)
-    grad_w_down = bmm(act, grad_eo, 1, 1)
-    back = jnp.concatenate([expert_out, grad_ei], axis=-1)
-    back = back.reshape(experts_here, sources, seqs * CAP, 2 * width).transpose(1, 0, 2, 3)
-    back = back.reshape(sources, per_row, 2 * width)
-    for bit in bits_of("col"):
-        half = back.shape[0] // 2
-        back = back[:half] + swap(back[half:].astype(BF), "col", bit).astype(F32)
-    back = back.astype(BF)
-    home = [back[0]]
-    for k in range(1, rows):
-        home.append(swap(back[k], "row", k))
-    home = jnp.concatenate(home, axis=0)
-    tok = mm(place, home, ((0,), (0,)))
-    expert_tok, grad_sent = tok[:, :width], tok[:, width:]
-
-    mixed_out = (live_f * (hidden + gate_prob * expert_tok)).astype(BF)
-    grad_gate = jnp.sum(grad_y * expert_tok, axis=-1, keepdims=True)
-    grad_logits = grad_gate * gate_prob * (route_f - route_probs)
-    grad_router = mm(normed_moe, grad_logits, ((0,), (0,)), precision=highest)
-    grad_normed = grad_sent + mm(grad_logits, router_f, ((1,), (1,)), precision=highest)
-    grad_gain_moe = jnp.sum(grad_normed * hat2, axis=0)
-    scaled = grad_normed * gain_moe_f
-    grad_hidden = grad_y + rms2 * (scaled - hat2 * jnp.mean(scaled * hat2, axis=-1, keepdims=True))
-    grad_mixed = grad_hidden.astype(BF)
-
-    grad_out = mm(gated, grad_mixed, ((0,), (0,)))
-    grad_gated = mm(grad_mixed, full_out, ((1,), (1,)))
-    grad_ssm = grad_gated * gate_silu
-    grad_z = (grad_gated * ssm_out * (gate_sig * (1.0 + gate_z * (1.0 - gate_sig)))).astype(BF)
-    guc, gdt, gb, gc, grad_a_log, grad_dt_bias, grad_d_skip = scan_bwd(
-        u_value, dt_pre, grad_ssm.reshape(seqs, length, inner), bT, cT, starts,
-        dt_bias_f[None], a_neg, d_skip_f[None])
-    gdt = gdt.reshape(count, inner).astype(BF)
-    grad_dt = mm(dt_low, gdt, ((0,), (0,)))
-    grad_proj = jnp.concatenate([mm(gdt, full_dt, ((1,), (1,))), gb.reshape(count, NS), gc.reshape(count, NS)],
-                                axis=1).astype(BF)
-    grad_xproj = mm(u_low, grad_proj, ((0,), (0,)))
-    grad_u = guc.reshape(count, inner) + mm(grad_proj, full_xproj, ((1,), (1,)))
-    grad_conv = grad_u.reshape(seqs, length, inner) * (conv_sig * (1.0 + conv_out * (1.0 - conv_sig)))
-    grad_conv_b = jnp.sum(grad_conv, axis=(0, 1))
-    grad_conv_w = jnp.stack([jnp.sum(grad_conv * padded[:, k:k + length], axis=(0, 1)) for k in range(taps)])
-    after = jnp.pad(grad_conv, ((0, 0), (0, taps - 1), (0, 0)))
-    grad_inner = sum(conv_w_f[k] * after[:, taps - 1 - k:taps - 1 - k + length] for k in range(taps))
-    grad_inner = grad_inner.reshape(count, inner).astype(BF)
-    grad_in_x = mm(normed_mix, grad_inner, ((0,), (0,)))
-    grad_in_z = mm(normed_mix, grad_z, ((0,), (0,)))
-    grad_nm = mm(grad_inner, full_x, ((1,), (1,))) + mm(grad_z, full_z, ((1,), (1,)))
-    grad_gain_mix = jnp.sum(grad_nm * hat1, axis=0)
-    scaled = grad_nm * gain_mix_f
-    grad_tokens = grad_hidden + rms1 * (scaled - hat1 * jnp.mean(scaled * hat1, axis=-1, keepdims=True))
+
+    message = -(-experts_here * CAP // 8) * 8
+    group = -(-rows * CAP // 16) * 16
+    at = jnp.arange(experts_here * group, dtype=jnp.int32)
+    there = at % group
+    source = jnp.where(there < rows * CAP, there // CAP * message + at // group * CAP + there % CAP, -1)
+    sort = (source[:, None] == jnp.arange(rows * message, dtype=jnp.int32)[None, :]).astype(BF)
+
+    def forward(s, x, route, n_live, grad):
+        out = {}
+        route = route.reshape(length)
+        live = jnp.arange(length, dtype=jnp.int32) < n_live
+        live_f = live.astype(F32)[:, None]
+        onehot = route[:, None] == jnp.arange(experts_all, dtype=jnp.int32)
+        hits = (onehot & live[:, None]).astype(BF)
+        before = jnp.arange(length)[:, None] > jnp.arange(length)[None, :]
+        slot = jnp.sum(mm(before.astype(BF), hits) * hits.astype(F32), axis=-1).astype(jnp.int32)
+        target = route // experts_here * message + route % experts_here * CAP + slot
+        target = jnp.where(live & (slot < CAP), target, rows * message)
+        place = (jnp.arange(rows * message, dtype=jnp.int32)[:, None] == target[None, :]).astype(BF)
+        route_f = onehot.astype(F32)
+
+        x = x.astype(F32)
+        rms1 = lax.rsqrt(jnp.mean(x * x, axis=-1, keepdims=True) + epsilon)
+        normed_mix = (x * rms1 * gain_mix_f).astype(BF)
+        inner_x = mm(normed_mix, full_x)
+        padded = jnp.pad(inner_x, ((taps - 1, 0), (0, 0)))
+        conv_out = conv_b_f
+        for k in range(taps):
+            conv_out = conv_out + conv_w_f[k] * padded[k:k + length]
+        u_value = conv_out * jax.nn.sigmoid(conv_out)
+        u_low = u_value.astype(BF)
+        projected = mm(u_low, full_xproj)
+        dt_low = projected[:, :R].astype(BF)
+        dt_pre = mm(dt_low, full_dt)
+        bT = to_chunks(projected[None, :, R:R + NS])
+        cT = to_chunks(projected[None, :, R + NS:])
+        ssm_out, starts = scan_fwd(u_value[None], dt_pre[None], bT, cT, dt_bias_f[None], a_neg * log2e, d_skip_f[None])
+        ssm_out = ssm_out[0]
+        gate_z = mm(normed_mix, full_z)
+        gated = (ssm_out * (gate_z * jax.nn.sigmoid(gate_z))).astype(BF)
+        hidden = x + mm(gated, full_out)
+        rms2 = lax.rsqrt(jnp.mean(hidden * hidden, axis=-1, keepdims=True) + epsilon)
+        normed_moe = hidden * rms2 * gain_moe_f
+        probs = jax.nn.softmax(mm(normed_moe, router_f, precision=highest), axis=-1)
+        gate_prob = jnp.sum(probs * route_f, axis=-1, keepdims=True)
+        grad_y = live_f * grad
+        both = jnp.concatenate([normed_moe.astype(BF), (grad_y * gate_prob).astype(BF)], axis=1)
+        outgoing = mm(place, both).astype(BF)
+        kept = dict(x=x, rms1=rms1, normed_mix=normed_mix, inner_x=inner_x, conv_out=conv_out, u_value=u_value, u_low=u_low,
+                    dt_low=dt_low, dt_pre=dt_pre, bT=bT, cT=cT, ssm_out=ssm_out, starts=starts, gate_z=gate_z, gated=gated,
+                    hidden=hidden, rms2=rms2, normed_moe=normed_moe, probs=probs, gate_prob=gate_prob, grad_y=grad_y,
+                    place=place, route_f=route_f, live_f=live_f)
+        return outgoing, kept
+
+    def to_experts(outgoing):
+        got = lax.all_to_all(outgoing, "row", split_axis=0, concat_axis=0, tiled=True)
+        bufs = [mm(sort, got).astype(BF).reshape(experts_here, group, 2 * width)]
+        for bit in bits_of("col")[::-1]:
+            bufs = bufs + [swap(v, "col", bit) for v in bufs]
+        return bufs
+
+    def from_experts(bufs):
+        for bit in bits_of("col"):
+            half = len(bufs) // 2
+            bufs = [(a.astype(F32) + swap(b, "col", bit).astype(F32)).astype(BF) for a, b in zip(bufs[:half], bufs[half:])]
+        got = mm(sort, bufs[0].reshape(experts_here * group, 2 * width), ((0,), (0,))).astype(BF)
+        return lax.all_to_all(got, "row", split_axis=0, concat_axis=0, tiled=True)
+
+    def backward(k, home):
+        tok = mm(k["place"], home, ((0,), (0,)))
+        expert_tok, grad_sent = tok[:, :width], tok[:, width:]
+        g = {}
+        hat2 = k["hidden"] * k["rms2"]
+        mixed_out = (k["live_f"] * (k["hidden"] + k["gate_prob"] * expert_tok)).astype(BF)
+        grad_gate = jnp.sum(k["grad_y"] * expert_tok, axis=-1, keepdims=True)
+        grad_logits = grad_gate * k["gate_prob"] * (k["route_f"] - k["probs"])
+        g["router"] = mm(k["normed_moe"], grad_logits, ((0,), (0,)), precision=highest)
+        grad_normed = grad_sent + mm(grad_logits, router_f, ((1,), (1,)), precision=highest)
+        g["gain_moe"] = jnp.sum(grad_normed * hat2, axis=0)
+        scaled = grad_normed * gain_moe_f
+        grad_hidden = k["grad_y"] + k["rms2"] * (scaled - hat2 * jnp.mean(scaled * hat2, axis=-1, keepdims=True))
+        grad_mixed = grad_hidden.astype(BF)
+        spread_mixed = mm(grad_mixed, shifted).astype(BF)
+        grad_gated = mm(grad_mixed, full_out, ((1,), (1,)))
+        gate_sig = jax.nn.sigmoid(k["gate_z"])
+        grad_ssm = grad_gated * (k["gate_z"] * gate_sig)
+        grad_z = (grad_gated * k["ssm_out"] * (gate_sig * (1.0 + k["gate_z"] * (1.0 - gate_sig)))).astype(BF)
+        guc, gdt, gb, gc, g["a_log"], g["dt_bias"], g["d_skip"] = scan_bwd(
+            k["u_value"][None], k["dt_pre"][None], grad_ssm[None], k["bT"], k["cT"], k["starts"], dt_bias_f[None], a_neg, d_skip_f[None])
+        gdt = gdt[0].astype(BF)
+        g["dt"] = mm(k["dt_low"], gdt, ((0,), (0,)))
+        grad_proj = jnp.concatenate([mm(gdt, full_dt, ((1,), (1,))), gb[0], gc[0]], axis=1).astype(BF)
+        g["xproj"] = mm(k["u_low"], grad_proj, ((0,), (0,)))
+        grad_u = guc[0] + mm(grad_proj, full_xproj, ((1,), (1,)))
+        sig = jax.nn.sigmoid(k["conv_out"])
+        grad_conv = grad_u * (sig * (1.0 + k["conv_out"] * (1.0 - sig)))
+        g["conv_b"] = jnp.sum(grad_conv, axis=0)
+        padded = jnp.pad(k["inner_x"], ((taps - 1, 0), (0, 0)))
+        g["conv_w"] = jnp.stack([jnp.sum(grad_conv * padded[i:i + length], axis=0) for i in range(taps)])
+        after = jnp.pad(grad_conv, ((0, taps - 1), (0, 0)))
+        grad_inner = sum(conv_w_f[i] * after[taps - 1 - i:taps - 1 - i + length] for i in range(taps)).astype(BF)
+        grad_nm = mm(grad_inner, full_x, ((1,), (1,))) + mm(grad_z, full_z, ((1,), (1,)))
+        hat1 = k["x"] * k["rms1"]
+        g["gain_mix"] = jnp.sum(grad_nm * hat1, axis=0)
+        scaled = grad_nm * gain_mix_f
+        grad_tokens = grad_hidden + k["rms1"] * (scaled - hat1 * jnp.mean(scaled * hat1, axis=-1, keepdims=True))
+        return mixed_out, grad_tokens, g, spread_mixed, grad_z, grad_inner
+
+    states, arrivals, last = [], [], None
+    for s in range(seqs):
+        x = tokens[s]
+        if last is not None:
+            x, last = lax.optimization_barrier((x, last))
+            arrivals.append(to_experts(last))
+        last, kept = forward(s, x, routes[s], lengths[s], cotangent[s])
+        states.append(kept)
+    arrivals.append(to_experts(last))
+    homes, sets = [], []
+    for bufs in arrivals:
+        outs, more = expert_both(bufs, w_up, w_down)
+        sets.append(bufs + more)
+        homes.append(from_experts(outs))
+    grad_w_up, grad_w_down = expert_weights(sets, width, w_up.shape[2])
+    results = [backward(k, h) for k, h in zip(states, homes)]
+    total = functools.reduce(lambda a, b: jax.tree.map(jnp.add, a, b), [r[2] for r in results])
+
+    grad_out = sum(mm(k["gated"], r[3], ((0,), (0,))) for k, r in zip(states, results)).astype(BF)
+    grad_out_block = reduce_list([grad_out[:, k * wide:(k + 1) * wide].reshape(rows, out_rows, wide) for k in range(cols)])
+    grad_out_block = grad_out_block[:, :out_lanes]
+    grad_in_z = column_blocks([(k["normed_mix"], r[4]) for k, r in zip(states, results)], cols, my_col)
+    grad_z_block = reduce_list([grad_in_z[k].reshape(rows, here, lanes) for k in range(cols)])
+    grad_in_x = column_blocks([(k["normed_mix"], r[5]) for k, r in zip(states, results)], cols, my_col)
 
     def blocks(g, like):
         r, c = like.shape
-        return g.reshape(rows, r, cols, c).transpose(0, 2, 1, 3)
-    grad_z_block = reduce_blocks(blocks(grad_in_z, w_in_z))
-    grad_out_block = reduce_blocks(blocks(grad_out, w_out).reshape(rows, cols, -1, lanes)).reshape(w_out.shape)
-    gsmall = jnp.concatenate([grad_conv_w, grad_conv_b[None], grad_dt_bias[None], grad_a_log, grad_d_skip[None]], axis=0)
-    ggain = jnp.concatenate([grad_gain_mix.reshape(parts, 1, -1), grad_gain_moe.reshape(parts, 1, -1)], axis=2)
-    gsmall = jnp.concatenate([gsmall.reshape(-1, parts, share).transpose(1, 0, 2), ggain], axis=1)
-    gflat = jnp.concatenate([blocks(grad_xproj, w_xproj).reshape(rows, cols, -1),
-                             blocks(grad_dt, w_dt).reshape(rows, cols, -1),
-                             blocks(grad_router, w_router).reshape(rows, cols, -1),
+        return g.astype(BF).reshape(rows, r, cols, c).transpose(0, 2, 1, 3).reshape(rows, cols, -1)
+    gsmall = jnp.concatenate([total["conv_w"], total["conv_b"][None], total["dt_bias"][None], total["a_log"],
+                              total["d_skip"][None]], axis=0).astype(BF)
+    ggain = jnp.concatenate([total["gain_mix"].reshape(parts, 1, -1), total["gain_moe"].reshape(parts, 1, -1)], axis=2)
+    gsmall = jnp.concatenate([gsmall.reshape(-1, parts, share).transpose(1, 0, 2), ggain.astype(BF)], axis=1)
+    gflat = jnp.concatenate([blocks(total["xproj"], w_xproj), blocks(total["dt"], w_dt), blocks(total["router"], w_router),
                              gsmall.reshape(rows, cols, -1)], axis=2)
     gflat = jnp.pad(gflat, ((0, 0), (0, 0), (0, extra * lanes - sum(sizes)))).reshape(rows, cols, extra, lanes)
-    done = reduce_blocks(jnp.concatenate([blocks(grad_in_x, w_in_x), gflat], axis=2))
+    done = reduce_list([jnp.concatenate([grad_in_x[k].reshape(rows, here, lanes),
+                                         lax.dynamic_index_in_dim(gflat, my_col ^ k, 1, keepdims=False)], axis=1)
+                        for k in range(cols)])
     grad_x_block = done[:here]
     done = done[here:].reshape(-1)
     sm = done[cut[3]:cut[4]].reshape(-1, share)
     gm = gain_mix.shape[0]
     return (
-        mixed_out.reshape(tokens.shape),
-        grad_tokens.reshape(tokens.shape),
+        jnp.stack([r[0] for r in results]),
+        jnp.stack([r[1] for r in results]),
         grad_x_block,
         grad_z_block,
         sm[:taps],

time: 977 us -> 643 us (0.66)
  local copies, waits for them, and re-layouts: 339 us -> 88.5 us
  waiting for transfers between devices: 251 us -> 166 us
  Pallas kernels: 114 us -> 170 us
  matrix products: 105 us -> 76.9 us
  other arithmetic: 67 us -> 52.1 us
    ppermute x43 -> x57, waiting for transfers between devices: 251 us -> 125 us  [swap(): return lax.ppermute(x, axis, [(i, i ^ bit) for i in range(n)])]
    concatenate x25 -> x7, local copies, waits for them, and re-layouts: 118 us -> 0.97 us  [the longest x3 0.77 us: on_device(): jnp.concatenate([total['conv_w'], total['conv_b'][None], total['dt_bias']...]
    pallas_call x0 -> x8, Pallas kernels: none -> 58.2 us  [the longest x3 45.1 us: per_expert(): pl.pallas_call(kernel, grid=(ins[0].shape[0],), in_specs=[tok(a) for a in...]
    dot_general x7 -> x0, matrix products: 58.1 us -> none  [the longest x6 57.9 us: bmm(): lax.dot_general(a, b, (((da,), (db,)), ((0,), (0,))), preferred_element_t...]
    slice x13 -> x14, local copies, waits for them, and re-layouts: 53.7 us -> 11.5 us  [the longest x3 3.02 us: reduce_list(): give[i].astype(F32)]
    ppermute x43 -> x57, starting transfers between devices: 83.8 us -> 45.7 us  [swap(): return lax.ppermute(x, axis, [(i, i ^ bit) for i in range(n)])]
    dot_general x20 -> x43, matrix products: 47.3 us -> 76.9 us  [mm(): lax.dot_general(a, b, (dims, ((), ())), preferred_element_type=F32, **kw)]
    reshape x14 -> x10, local copies, waits for them, and re-layouts: 34.5 us -> 6.71 us  [the longest x9 6.49 us: blocks(): g.astype(BF).reshape(rows, r, cols, c).transpose(0, 2, 1, 3)]
  transfers between devices with their start and end apart: 43 -> 67, of which waited for: 20 -> 24; matrix products, arithmetic and copies ran while one was open for 18% -> 18% of each run, Pallas kernels for 3% -> 12%
where the time goes in v1:
time: 643 us; the launch traced here: 636 us
  Pallas kernels  170 us (26%)
  waiting for transfers between devices  166 us (26%)
  local copies, waits for them, and re-layouts  88.5 us (14%)
  starting transfers between devices  78.2 us (12%)
  matrix products  76.9 us (12%)
  other arithmetic  52.1 us (8%)
    ppermute x57, waiting for transfers between devices, swap(): return lax.ppermute(x, axis, [(i, i ^ bit) for i in range(n)])  125 us
    pallas_call x2, Pallas kernels, scan_bwd(): pl.pallas_call(functools.partial(bwd_kernel, T, Q, Q2), grid=(S, C), in_s...  81.9 us
    dot_general x43, matrix products, mm(): lax.dot_general(a, b, (dims, ((), ())), preferred_element_type=F32, **kw)  76.9 us
    ppermute x57, starting transfers between devices, swap(): return lax.ppermute(x, axis, [(i, i ^ bit) for i in range(n)])  45.7 us
    pallas_call x3, Pallas kernels, per_expert(): pl.pallas_call(kernel, grid=(ins[0].shape[0],), in_specs=[tok(a) for a in...  45.1 us
    unnamed x337, local copies, waits for them, and re-layouts  38 us
    pallas_call x2, Pallas kernels, scan_fwd(): pl.pallas_call(functools.partial(fwd_kernel, T, Q), grid=(S, C), in_specs...  30.2 us
    ppermute x6, waiting for transfers between devices, exchange(): return lax.ppermute(x, ('row', 'col'), pairs)  24.4 us
  transfers between devices with their start and end apart: 67, of which 24 were waited for; matrix products, arithmetic and copies ran while one was open for 18% of the time, Pallas kernels for 12%

profile of v1, /device:TPU:0, one launch (start us, length us, event | category | flops | bytes accessed | tf_op | source)
XLA Modules:
  0.0 635.7 jit_solution(12787637160795854762)
XLA Ops:
  7.3 5.1 collective-permute-start.2
  21.2 2.7 collective-permute-start.5
  27.5 6.8 %collective-permute-done.5.refs_4_ = bf16[4,128,384]{2,1,0:T(8,128)(2,1)S(1)} collective-permute-done((bf16[4,128,384]{2,1,0:T(8,128)(2,1)S(1)}, bf16[4,128,384]{2,1,0:T(8,128)(2,1)S(1)}, u32[]{:S(2)}, u32[]{:S(2)}) %collective-permute-start.5) | collective-permute-done | bytes 393248 | tf_op jit(solution)/shard_map/ppermute | solution.py:225
  34.3 3.7 collective-permute-start.12
  41.0 3.5 collective-permute-start.22
  48.8 6.8 %collective-permute-done.21 = bf16[192,256]{1,0:T(8,128)(2,1)S(1)} collective-permute-done((bf16[192,256]{1,0:T(8,128)(2,1)S(1)}, bf16[192,256]{1,0:T(8,128)(2,1)S(1)}, u32[]{:S(2)}, u32[]{:S(2)}) %collective-permute-start.21) | collective-permute-done | bytes 98336 | tf_op jit(solution)/shard_map/ppermute | solution.py:209
  55.7 4.6 collective-permute-done.20
  75.0 3.8 reshape.681
  82.5 2.6 fusion.260
  107.1 15.1 %shard_map.315 = (f32[1,40,8,1536]{3,2,1,0:T(8,128)S(1)}, f32[1,5,16,1536]{3,2,1,0:T(8,128)S(1)}) custom-call(f32[1,40,8,1536]{3,2,1,0:T(8,128)S(1)} %get-tuple-element.160.u_ref, f32[1,40,8,1536]{3,2,1,0:T(8,128)S(1)} %convolution_bitcast_fusion.1.dtp_ref, f32[1,5,16,64]{3,2,1,0:T(8,128)S(1)} %bitcast.342, f32[1,5,16,64]{3,2,1,0:T(8,128)S(1)} %bitcast.344, ...), custom_call_target="tpu_custom_call" | custom-call | tf_op jit(solution)/shard_map/pallas_call | solution.py:71
  130.8 3.2 convolution_convert_fusion
  139.5 4.5 all-to-all-start
  147.8 2.6 fusion.261
  156.6 15.1 %shard_map.319 = (f32[1,40,8,1536]{3,2,1,0:T(8,128)S(1)}, f32[1,5,16,1536]{3,2,1,0:T(8,128)S(1)}) custom-call(f32[1,40,8,1536]{3,2,1,0:T(8,128)S(1)} %copy-done.2, f32[1,40,8,1536]{3,2,1,0:T(8,128)S(1)} %convolution_bitcast_fusion.dtp_ref, f32[1,5,16,64]{3,2,1,0:T(8,128)S(1)} %bitcast.346, f32[1,5,16,64]{3,2,1,0:T(8,128)S(1)} %bitcast.348, ...), custom_call_target="tpu_custom_call" | custom-call | tf_op jit(solution)/shard_map/pallas_call | solution.py:71
  179.4 3.4 convolution_convert_fusion.5
  185.2 6.2 all-to-all-start.2
  191.5 23.8 %collective-permute-done.30.refs_1_ = bf16[4,112,1536]{2,1,0:T(8,128)(2,1)} collective-permute-done((bf16[4,112,1536]{2,1,0:T(8,128)(2,1)}, bf16[4,112,1536]{2,1,0:T(8,128)(2,1)}, u32[]{:S(2)}, u32[]{:S(2)}) %collective-permute-start.30) | collective-permute-done | bytes 1376288 | tf_op jit(solution)/shard_map/ppermute | solution.py:209
  215.3 8.6 %all-to-all-done.2 = bf16[8,56,1536]{2,1,0:T(8,128)(2,1)} async-done(((bf16[8,56,1536]{2,1,0:T(8,128)(2,1)}), bf16[8,56,1536]{2,1,0:T(8,128)(2,1)}, u32[]{:S(2)}, u32[]{:S(2)}) %all-to-all-start.2) | async-done | bytes 1376288 | tf_op jit(solution)/shard_map/all_to_all | solution.py:533
  223.9 3.4 convolution_convert_fusion.2
  228.9 13.7 %shard_map.318 = (bf16[4,112,1536]{2,1,0:T(8,128)(2,1)}, bf16[4,112,1536]{2,1,0:T(8,128)(2,1)}, bf16[4,112,1536]{2,1,0:T(8,128)(2,1)}, bf16[4,112,1536]{2,1,0:T(...) custom-call(bf16[4,112,1536]{2,1,0:T(8,128)(2,1)} %bitcast.35.refs_0_, ...), custom_call_target="tpu_custom_call" | custom-call | flops 8455716864 | bytes 25952256 | tf_op jit(solution)/shard_map/pallas_call | solution.py:390
  243.2 14.8 %collective-permute-done.36.refs_1_.refs_7_ = bf16[4,112,1536]{2,1,0:T(8,128)(2,1)} collective-permute-done((bf16[4,112,1536]{2,1,0:T(8,128)(2,1)}, bf16[4,112,1536]{2,1,0:T(8,128)(2,1)}, u32[]{:S(2)}, u32[]{:S(2)}) %collective-permute-start.36) | collective-permute-done | bytes 1376288 | tf_op jit(solution)/shard_map/ppermute | solution.py:209
  258.6 2.8 add_convert_fusion.5
  263.5 13.7 %shard_map.320 = (bf16[4,112,1536]{2,1,0:T(8,128)(2,1)}, bf16[4,112,1536]{2,1,0:T(8,128)(2,1)}, bf16[4,112,1536]{2,1,0:T(8,128)(2,1)}, bf16[4,112,1536]{2,1,0:T(...) custom-call(bf16[4,112,1536]{2,1,0:T(8,128)(2,1)} %bitcast.50.refs_0_.refs_6_, ...), custom_call_target="tpu_custom_call" | custom-call | flops 8455716864 | bytes 25952256 | tf_op jit(solution)/shard_map/pallas_call | solution.py:390
  277.8 15.9 %collective-permute-done.35 = bf16[4,112,1536]{2,1,0:T(8,128)(2,1)S(1)} collective-permute-done((bf16[4,112,1536]{2,1,0:T(8,128)(2,1)}, bf16[4,112,1536]{2,1,0:T(8,128)(2,1)S(1)}, u32[]{:S(2)}, u32[]{:S(2)}) %collective-permute-start.35) | collective-permute-done | bytes 1376288 | tf_op jit(solution)/shard_map/ppermute | solution.py:209
  296.2 5.3 all-to-all-start.1
  305.5 29.3 %collective-permute-done.41 = bf16[4,112,1536]{2,1,0:T(8,128)(2,1)S(1)} collective-permute-done((bf16[4,112,1536]{2,1,0:T(8,128)(2,1)S(1)}, bf16[4,112,1536]{2,1,0:T(8,128)(2,1)S(1)}, u32[]{:S(2)}, u32[]{:S(2)}) %collective-permute-start.41) | collective-permute-done | bytes 1376288 | tf_op jit(solution)/shard_map/ppermute | solution.py:209
  338.8 6.3 all-to-all-start.3
  346.4 17.7 %shard_map.325 = (f32[4,768,768]{2,1,0:T(8,128)}, f32[4,768,768]{2,1,0:T(8,128)}) custom-call(bf16[4,112,1536]{2,1,0:T(8,128)(2,1)} %bitcast.35.refs_0_, bf16[4,112,1536]{2,1,0:T(8,128)(2,1)} %collective-permute-done.30.refs_1_, bf16[4,112,1536]{2,1,0:T(8,128)(2,1)} %collective-permute-done.31.refs_2_, ...), custom_call_target="tpu_custom_call" | custom-call | flops 8455716864 | bytes 40894464 | tf_op jit(solution)/shard_map/pallas_call | solution.py:390
  364.1 3.3 fusion.85
  367.5 8.5 %all-to-all-done.3 = bf16[8,56,1536]{2,1,0:T(8,128)(2,1)} async-done(((bf16[8,56,1536]{2,1,0:T(8,128)(2,1)}), bf16[8,56,1536]{2,1,0:T(8,128)(2,1)}, u32[]{:S(2)}, u32[]{:S(2)}) %all-to-all-start.3) | async-done | bytes 1376288 | tf_op jit(solution)/shard_map/all_to_all | solution.py:544
  378.6 2.7 multiply_reduce_fusion.13
  399.2 4.2 shard_map.324
  404.9 41.0 %shard_map.322 = (f32[1,40,8,1536]{3,2,1,0:T(8,128)S(1)}, f32[1,40,8,1536]{3,2,1,0:T(8,128)S(1)}, f32[1,5,8,1024]{3,2,1,0:T(8,128)S(1)}, f32[1,5,8,1024]{3,2,1,0...) custom-call(f32[1,40,8,1536]{3,2,1,0:T(8,128)S(1)} %copy-done.3, ...), custom_call_target="tpu_custom_call" | custom-call | tf_op jit(solution)/shard_map/pallas_call | solution.py:176
  453.7 40.9 %shard_map.321 = (f32[1,40,8,1536]{3,2,1,0:T(8,128)S(1)}, f32[1,40,8,1536]{3,2,1,0:T(8,128)S(1)}, f32[1,5,8,1024]{3,2,1,0:T(8,128)S(1)}, f32[1,5,8,1024]{3,2,1,0...) custom-call(f32[1,40,8,1536]{3,2,1,0:T(8,128)S(1)} %get-tuple-element.160.u_ref, ...), custom_call_target="tpu_custom_call" | custom-call | tf_op jit(solution)/shard_map/pallas_call | solution.py:176
  498.0 3.2 fusion.105
  505.6 3.9 multiply_reduce_fusion.3
  510.5 4.3 shard_map.323
  530.8 3.2 reshape.694
  541.9 6.3 fusion.35
  548.2 6.5 %add_convert_fusion = bf16[1536,1024]{1,0:T(8,128)(2,1)} fusion(f32[1536,1024]{1,0:T(8,128)} %fusion.35, bf16[320,1536]{1,0:T(8,128)(2,1)} %copy-done.159, s32[1024]{0:T(1024)S(1)} %copy-done.153, f32[320,768]{1,0:T(8,128)S(1)} %copy-done.61), kind=kOutput, calls=%fused_computation | convolution fusion | flops 1514455040 | bytes 11407360 | tf_op jit(solution)/shard_map/dot_general | solution.py:204
  564.2 5.1 collective-permute-done.52
  569.2 5.4 collective-permute-done.51
  576.3 3.2 collective-permute-start.53
  593.9 5.7 collective-permute-done.45
  600.8 7.3 %collective-permute-done.44 = bf16[4,128,384]{2,1,0:T(8,128)(2,1)S(1)} collective-permute-done((bf16[4,128,384]{2,1,0:T(8,128)(2,1)S(1)}, bf16[4,128,384]{2,1,0:T(8,128)(2,1)S(1)}, u32[]{:S(2)}, u32[]{:S(2)}) %collective-permute-start.44) | collective-permute-done | bytes 393248 | tf_op jit(solution)/shard_map/ppermute | solution.py:209
  609.7 6.8 %collective-permute-done.59 = bf16[4,192,256]{2,1,0:T(8,128)(2,1)S(1)} collective-permute-done((bf16[4,192,256]{2,1,0:T(8,128)(2,1)S(1)}, bf16[4,192,256]{2,1,0:T(8,128)(2,1)S(1)}, u32[]{:S(2)}, u32[]{:S(2)}) %collective-permute-start.59) | collective-permute-done | bytes 393248 | tf_op jit(solution)/shard_map/ppermute | solution.py:225
  616.5 7.2 %collective-permute-done.58 = bf16[4,192,256]{2,1,0:T(8,128)(2,1)S(1)} collective-permute-done((bf16[4,192,256]{2,1,0:T(8,128)(2,1)S(1)}, bf16[4,192,256]{2,1,0:T(8,128)(2,1)S(1)}, u32[]{:S(2)}, u32[]{:S(2)}) %collective-permute-start.58) | collective-permute-done | bytes 393248 | tf_op jit(solution)/shard_map/ppermute | solution.py:209
  625.7 3.0 collective-permute-start.60
  (689 shorter events, 215.4 us)
Async XLA Ops:
  7.3 13.9 %collective-permute-start.2 = (bf16[128,384]{1,0:T(8,128)(2,1)S(1)}, bf16[128,384]{1,0:T(8,128)(2,1)S(1)}, u32[]{:S(2)}, u32[]{:S(2)}) collective-permute-start(bf16[128,384]{1,0:T(8,128)(2,1)S(1)} %constant_dynamic-update-slice_fusion), channel_id=1, source_target_pairs={{0,24},{4,28},{8,16},{12,20},{16,8},{20,12},{24,0},{28,4},{1,25},{... | collective-permute-start | bytes 294920 | tf_op jit(solution)/shard_map/ppermute | solution.py:209
  21.2 13.1 %collective-permute-start.5 = (bf16[4,128,384]{2,1,0:T(8,128)(2,1)S(1)}, bf16[4,128,384]{2,1,0:T(8,128)(2,1)S(1)}, u32[]{:S(2)}, u32[]{:S(2)}) collective-permute-start(bf16[4,128,384]{2,1,0:T(8,128)(2,1)S(1)} %pad_maximum_fusion.6.refs_1_), channel_id=1, source_target_pairs={{0,6},{1,7},{2,4},{3,5},{4,2},{5,3},{6,0},{7,1},{8,14},{9,15},{10,... | collective-permute-start | bytes 1179656 | tf_op jit(solution)/shard_map/ppermute | solution.py:225
  24.5 16.5 %collective-permute-start.3 = (bf16[4,128,384]{2,1,0:T(8,128)(2,1)S(1)}, bf16[4,128,384]{2,1,0:T(8,128)(2,1)S(1)}, u32[]{:S(2)}, u32[]{:S(2)}) collective-permute-start(bf16[4,128,384]{2,1,0:T(8,128)(2,1)S(1)} %pad_maximum_fusion.6.refs_1_), channel_id=1, source_target_pairs={{0,4},{4,0},{8,12},{12,8},{16,20},{20,16},{24,28},{28,24},{1,5},{5... | collective-permute-start | bytes 1179656 | tf_op jit(solution)/shard_map/ppermute | solution.py:209
  25.0 16.0 %collective-permute-start.4 = (bf16[4,128,384]{2,1,0:T(8,128)(2,1)S(1)}, bf16[4,128,384]{2,1,0:T(8,128)(2,1)S(1)}, u32[]{:S(2)}, u32[]{:S(2)}) collective-permute-start(bf16[4,128,384]{2,1,0:T(8,128)(2,1)S(1)} %pad_maximum_fusion.6.refs_1_), channel_id=1, source_target_pairs={{0,2},{1,3},{2,0},{3,1},{4,6},{5,7},{6,4},{7,5},{8,10},{9,11},{10,... | collective-permute-start | bytes 1179656 | tf_op jit(solution)/shard_map/ppermute | solution.py:209
  41.0 21.7 %collective-permute-start.6 = (bf16[4,128,384]{2,1,0:T(8,128)(2,1)S(1)}, bf16[4,128,384]{2,1,0:T(8,128)(2,1)S(1)}, u32[]{:S(2)}, u32[]{:S(2)}) collective-permute-start(bf16[4,128,384]{2,1,0:T(8,128)(2,1)S(1)} %pad_maximum_fusion.6.refs_1_), channel_id=1, source_target_pairs={{0,1},{1,0},{2,3},{3,2},{4,5},{5,4},{6,7},{7,6},{8,9},{9,8},{10,11... | collective-permute-start | bytes 1179656 | tf_op jit(solution)/shard_map/ppermute | solution.py:209
  44.5 21.0 %collective-permute-start.9 = (bf16[4,128,384]{2,1,0:T(8,128)(2,1)S(1)}, bf16[4,128,384]{2,1,0:T(8,128)(2,1)S(1)}, u32[]{:S(2)}, u32[]{:S(2)}) collective-permute-start(bf16[4,128,384]{2,1,0:T(8,128)(2,1)S(1)} %collective-permute-done.5.refs_4_), channel_id=1, source_target_pairs={{0,1},{1,0},{2,3},{3,2},{4,5},{5,4},{6,7},{7,6},{8,9},{9,8},{10,11... | collective-permute-start | bytes 1179656 | tf_op jit(solution)/shard_map/ppermute | solution.py:209
  44.7 18.4 %collective-permute-start.7 = (bf16[4,128,384]{2,1,0:T(8,128)(2,1)S(1)}, bf16[4,128,384]{2,1,0:T(8,128)(2,1)S(1)}, u32[]{:S(2)}, u32[]{:S(2)}) collective-permute-start(bf16[4,128,384]{2,1,0:T(8,128)(2,1)S(1)} %collective-permute-done.3.refs_2_), channel_id=1, source_target_pairs={{0,1},{1,0},{2,3},{3,2},{4,5},{5,4},{6,7},{7,6},{8,9},{9,8},{10,11... | collective-permute-start | bytes 1179656 | tf_op jit(solution)/shard_map/ppermute | solution.py:209
  45.0 20.5 %collective-permute-start.8 = (bf16[4,128,384]{2,1,0:T(8,128)(2,1)S(1)}, bf16[4,128,384]{2,1,0:T(8,128)(2,1)}, u32[]{:S(2)}, u32[]{:S(2)}) collective-permute-start(bf16[4,128,384]{2,1,0:T(8,128)(2,1)S(1)} %collective-permute-done.4.refs_3_), channel_id=1, source_target_pairs={{0,1},{1,0},{2,3},{3,2},{4,5},{5,4},{6,7},{7,6},{8,9},{9,8},{10,11... | collective-permute-start | bytes 1179656 | tf_op jit(solution)/shard_map/ppermute | solution.py:209
  60.2 44.2 %collective-permute-start.13 = (bf16[4,96,384]{2,1,0:T(8,128)(2,1)S(1)}, bf16[4,96,384]{2,1,0:T(8,128)(2,1)}, u32[]{:S(2)}, u32[]{:S(2)}) collective-permute-start(bf16[4,96,384]{2,1,0:T(8,128)(2,1)S(1)} %pad_maximum_fusion.8.refs_1_), channel_id=1, source_target_pairs={{0,4},{4,0},{8,12},{12,8},{16,20},{20,16},{24,28},{28,24},{1,5},{5... | collective-permute-start | bytes 884744 | tf_op jit(solution)/shard_map/ppermute | solution.py:209
  62.7 42.2 %collective-permute-start.14 = (bf16[4,96,384]{2,1,0:T(8,128)(2,1)S(1)}, bf16[4,96,384]{2,1,0:T(8,128)(2,1)}, u32[]{:S(2)}, u32[]{:S(2)}) collective-permute-start(bf16[4,96,384]{2,1,0:T(8,128)(2,1)S(1)} %pad_maximum_fusion.8.refs_1_), channel_id=1, source_target_pairs={{0,2},{1,3},{2,0},{3,1},{4,6},{5,7},{6,4},{7,5},{8,10},{9,11},{10,... | collective-permute-start | bytes 884744 | tf_op jit(solution)/shard_map/ppermute | solution.py:209
  63.9 42.6 %collective-permute-start.15 = (bf16[4,96,384]{2,1,0:T(8,128)(2,1)S(1)}, bf16[4,96,384]{2,1,0:T(8,128)(2,1)}, u32[]{:S(2)}, u32[]{:S(2)}) collective-permute-start(bf16[4,96,384]{2,1,0:T(8,128)(2,1)S(1)} %pad_maximum_fusion.8.refs_1_), channel_id=1, source_target_pairs={{0,6},{1,7},{2,4},{3,5},{4,2},{5,3},{6,0},{7,1},{8,14},{9,15},{10,... | collective-permute-start | bytes 884744 | tf_op jit(solution)/shard_map/ppermute | solution.py:225
  65.5 41.0 %collective-permute-start.16 = (bf16[4,96,384]{2,1,0:T(8,128)(2,1)S(1)}, bf16[4,96,384]{2,1,0:T(8,128)(2,1)}, u32[]{:S(2)}, u32[]{:S(2)}) collective-permute-start(bf16[4,96,384]{2,1,0:T(8,128)(2,1)S(1)} %pad_maximum_fusion.8.refs_1_), channel_id=1, source_target_pairs={{0,1},{1,0},{2,3},{3,2},{4,5},{5,4},{6,7},{7,6},{8,9},{9,8},{10,11... | collective-permute-start | bytes 884744 | tf_op jit(solution)/shard_map/ppermute | solution.py:209
  66.3 40.7 %collective-permute-start.23 = (bf16[4,192,256]{2,1,0:T(8,128)(2,1)S(1)}, bf16[4,192,256]{2,1,0:T(8,128)(2,1)}, u32[]{:S(2)}, u32[]{:S(2)}) collective-permute-start(bf16[4,192,256]{2,1,0:T(8,128)(2,1)S(1)} %pad_maximum_fusion.7.refs_1_), channel_id=1, source_target_pairs={{0,4},{4,0},{8,12},{12,8},{16,20},{20,16},{24,28},{28,24},{1,5},{5... | collective-permute-start | bytes 1179656 | tf_op jit(solution)/shard_map/ppermute | solution.py:209
  104.4 19.7 %collective-permute-start.24 = (bf16[4,192,256]{2,1,0:T(8,128)(2,1)S(1)}, bf16[4,192,256]{2,1,0:T(8,128)(2,1)S(1)}, u32[]{:S(2)}, u32[]{:S(2)}) collective-permute-start(bf16[4,192,256]{2,1,0:T(8,128)(2,1)S(1)} %pad_maximum_fusion.7.refs_1_), channel_id=1, source_target_pairs={{0,2},{1,3},{2,0},{3,1},{4,6},{5,7},{6,4},{7,5},{8,10},{9,11},{10,... | collective-permute-start | bytes 1179656 | tf_op jit(solution)/shard_map/ppermute | solution.py:209
  104.9 19.3 %collective-permute-start.25 = (bf16[4,192,256]{2,1,0:T(8,128)(2,1)S(1)}, bf16[4,192,256]{2,1,0:T(8,128)(2,1)S(1)}, u32[]{:S(2)}, u32[]{:S(2)}) collective-permute-start(bf16[4,192,256]{2,1,0:T(8,128)(2,1)S(1)} %pad_maximum_fusion.7.refs_1_), channel_id=1, source_target_pairs={{0,6},{1,7},{2,4},{3,5},{4,2},{5,3},{6,0},{7,1},{8,14},{9,15},{10,... | collective-permute-start | bytes 1179656 | tf_op jit(solution)/shard_map/ppermute | solution.py:225
  106.5 18.2 %collective-permute-start.17 = (bf16[4,96,384]{2,1,0:T(8,128)(2,1)}, bf16[4,96,384]{2,1,0:T(8,128)(2,1)S(1)}, u32[]{:S(2)}, u32[]{:S(2)}) collective-permute-start(bf16[4,96,384]{2,1,0:T(8,128)(2,1)} %collective-permute-done.13.refs_2_), channel_id=1, source_target_pairs={{0,1},{1,0},{2,3},{3,2},{4,5},{5,4},{6,7},{7,6},{8,9},{9,8},{10,11... | collective-permute-start | bytes 884744 | tf_op jit(solution)/shard_map/ppermute | solution.py:209
  106.5 18.2 %collective-permute-start.18 = (bf16[4,96,384]{2,1,0:T(8,128)(2,1)}, bf16[4,96,384]{2,1,0:T(8,128)(2,1)S(1)}, u32[]{:S(2)}, u32[]{:S(2)}) collective-permute-start(bf16[4,96,384]{2,1,0:T(8,128)(2,1)} %collective-permute-done.14.refs_3_), channel_id=1, source_target_pairs={{0,1},{1,0},{2,3},{3,2},{4,5},{5,4},{6,7},{7,6},{8,9},{9,8},{10,11... | collective-permute-start | bytes 884744 | tf_op jit(solution)/shard_map/ppermute | solution.py:209
  107.0 18.2 %collective-permute-start.19 = (bf16[4,96,384]{2,1,0:T(8,128)(2,1)}, bf16[4,96,384]{2,1,0:T(8,128)(2,1)S(1)}, u32[]{:S(2)}, u32[]{:S(2)}) collective-permute-start(bf16[4,96,384]{2,1,0:T(8,128)(2,1)} %collective-permute-done.15.refs_4_), channel_id=1, source_target_pairs={{0,1},{1,0},{2,3},{3,2},{4,5},{5,4},{6,7},{7,6},{8,9},{9,8},{10,11... | collective-permute-start | bytes 884744 | tf_op jit(solution)/shard_map/ppermute | solution.py:209
  139.5 39.8 %all-to-all-start = ((bf16[8,56,1536]{2,1,0:T(8,128)(2,1)}), bf16[8,56,1536]{2,1,0:T(8,128)(2,1)}, u32[]{:S(2)}, u32[]{:S(2)}) async-start(bf16[8,56,1536]{2,1,0:T(8,128)(2,1)} %bitcast.377), calls=%async_computation | async-start | bytes 2752512 | tf_op jit(solution)/shard_map/all_to_all | solution.py:533
  182.8 32.5 %collective-permute-start.30 = (bf16[4,112,1536]{2,1,0:T(8,128)(2,1)}, bf16[4,112,1536]{2,1,0:T(8,128)(2,1)}, u32[]{:S(2)}, u32[]{:S(2)}) collective-permute-start(bf16[4,112,1536]{2,1,0:T(8,128)(2,1)} %bitcast.35.refs_0_), channel_id=1, source_target_pairs={{0,2},{1,3},{2,0},{3,1},{4,6},{5,7},{6,4},{7,5},{8,10},{9,11},{10,... | collective-permute-start | bytes 4128776 | tf_op jit(solution)/shard_map/ppermute | solution.py:209
  185.2 38.7 %all-to-all-start.2 = ((bf16[8,56,1536]{2,1,0:T(8,128)(2,1)}), bf16[8,56,1536]{2,1,0:T(8,128)(2,1)}, u32[]{:S(2)}, u32[]{:S(2)}) async-start(bf16[8,56,1536]{2,1,0:T(8,128)(2,1)} %bitcast.379), calls=%async_computation.2 | async-start | bytes 2752512 | tf_op jit(solution)/shard_map/all_to_all | solution.py:533
  191.4 37.5 %collective-permute-start.31 = (bf16[4,112,1536]{2,1,0:T(8,128)(2,1)}, bf16[4,112,1536]{2,1,0:T(8,128)(2,1)}, u32[]{:S(2)}, u32[]{:S(2)}) collective-permute-start(bf16[4,112,1536]{2,1,0:T(8,128)(2,1)} %bitcast.35.refs_0_), channel_id=1, source_target_pairs={{0,1},{1,0},{2,3},{3,2},{4,5},{5,4},{6,7},{7,6},{8,9},{9,8},{10,11... | collective-permute-start | bytes 4128776 | tf_op jit(solution)/shard_map/ppermute | solution.py:209
  215.3 13.6 %collective-permute-start.32 = (bf16[4,112,1536]{2,1,0:T(8,128)(2,1)}, bf16[4,112,1536]{2,1,0:T(8,128)(2,1)}, u32[]{:S(2)}, u32[]{:S(2)}) collective-permute-start(bf16[4,112,1536]{2,1,0:T(8,128)(2,1)} %collective-permute-done.30.refs_1_), channel_id=1, source_target_pairs={{0,1},{1,0},{2,3},{3,2},{4,5},{5,4},{6,7},{7,6},{8,9},{9,8},{10,11... | collective-permute-start | bytes 4128776 | tf_op jit(solution)/shard_map/ppermute | solution.py:209
  227.3 30.8 %collective-permute-start.36 = (bf16[4,112,1536]{2,1,0:T(8,128)(2,1)}, bf16[4,112,1536]{2,1,0:T(8,128)(2,1)}, u32[]{:S(2)}, u32[]{:S(2)}) collective-permute-start(bf16[4,112,1536]{2,1,0:T(8,128)(2,1)} %bitcast.50.refs_0_.refs_6_), channel_id=1, source_target_pairs={{0,2},{1,3},{2,0},{3,1},{4,6},{5,7},{6,4},{7,5},{8,10},{9,11},{10,... | collective-permute-start | bytes 4128776 | tf_op jit(solution)/shard_map/ppermute | solution.py:209
  242.6 15.9 %collective-permute-start.34 = (bf16[4,112,1536]{2,1,0:T(8,128)(2,1)}, bf16[4,112,1536]{2,1,0:T(8,128)(2,1)S(1)}, u32[]{:S(2)}, u32[]{:S(2)}) collective-permute-start(bf16[4,112,1536]{2,1,0:T(8,128)(2,1)} %get-tuple-element.64), channel_id=1, source_target_pairs={{0,1},{1,0},{2,3},{3,2},{4,5},{5,4},{6,7},{7,6},{8,9},{9,8},{10,11... | collective-permute-start | bytes 4128776 | tf_op jit(solution)/shard_map/ppermute | solution.py:209
  242.7 20.2 %collective-permute-start.37 = (bf16[4,112,1536]{2,1,0:T(8,128)(2,1)}, bf16[4,112,1536]{2,1,0:T(8,128)(2,1)}, u32[]{:S(2)}, u32[]{:S(2)}) collective-permute-start(bf16[4,112,1536]{2,1,0:T(8,128)(2,1)} %bitcast.50.refs_0_.refs_6_), channel_id=1, source_target_pairs={{0,1},{1,0},{2,3},{3,2},{4,5},{5,4},{6,7},{7,6},{8,9},{9,8},{10,11... | collective-permute-start | bytes 4128776 | tf_op jit(solution)/shard_map/ppermute | solution.py:209
  258.1 19.7 %collective-permute-start.33 = (bf16[4,112,1536]{2,1,0:T(8,128)(2,1)}, bf16[4,112,1536]{2,1,0:T(8,128)(2,1)S(1)}, u32[]{:S(2)}, u32[]{:S(2)}) collective-permute-start(bf16[4,112,1536]{2,1,0:T(8,128)(2,1)} %get-tuple-element.62), channel_id=1, source_target_pairs={{0,1},{1,0},{2,3},{3,2},{4,5},{5,4},{6,7},{7,6},{8,9},{9,8},{10,11... | collective-permute-start | bytes 4128776 | tf_op jit(solution)/shard_map/ppermute | solution.py:209
  261.3 32.3 %collective-permute-start.35 = (bf16[4,112,1536]{2,1,0:T(8,128)(2,1)}, bf16[4,112,1536]{2,1,0:T(8,128)(2,1)S(1)}, u32[]{:S(2)}, u32[]{:S(2)}) collective-permute-start(bf16[4,112,1536]{2,1,0:T(8,128)(2,1)} %add_convert_fusion.5), channel_id=1, source_target_pairs={{0,2},{1,3},{2,0},{3,1},{4,6},{5,7},{6,4},{7,5},{8,10},{9,11},{10,... | collective-permute-start | bytes 4128776 | tf_op jit(solution)/shard_map/ppermute | solution.py:209
  277.2 24.4 %collective-permute-start.40 = (bf16[4,112,1536]{2,1,0:T(8,128)(2,1)}, bf16[4,112,1536]{2,1,0:T(8,128)(2,1)}, u32[]{:S(2)}, u32[]{:S(2)}) collective-permute-start(bf16[4,112,1536]{2,1,0:T(8,128)(2,1)} %get-tuple-element.70), channel_id=1, source_target_pairs={{0,1},{1,0},{2,3},{3,2},{4,5},{5,4},{6,7},{7,6},{8,9},{9,8},{10,11... | collective-permute-start | bytes 4128776 | tf_op jit(solution)/shard_map/ppermute | solution.py:209
  277.4 28.1 %collective-permute-start.39 = (bf16[4,112,1536]{2,1,0:T(8,128)(2,1)}, bf16[4,112,1536]{2,1,0:T(8,128)(2,1)}, u32[]{:S(2)}, u32[]{:S(2)}) collective-permute-start(bf16[4,112,1536]{2,1,0:T(8,128)(2,1)} %get-tuple-element.68), channel_id=1, source_target_pairs={{0,1},{1,0},{2,3},{3,2},{4,5},{5,4},{6,7},{7,6},{8,9},{9,8},{10,11... | collective-permute-start | bytes 4128776 | tf_op jit(solution)/shard_map/ppermute | solution.py:209
  296.2 42.6 %all-to-all-start.1 = ((bf16[8,56,1536]{2,1,0:T(8,128)(2,1)}), bf16[8,56,1536]{2,1,0:T(8,128)(2,1)}, u32[]{:S(2)}, u32[]{:S(2)}) async-start(bf16[8,56,1536]{2,1,0:T(8,128)(2,1)} %bitcast.378), calls=%async_computation.1 | async-start | bytes 2752512 | tf_op jit(solution)/shard_map/all_to_all | solution.py:544
  303.8 31.0 %collective-permute-start.41 = (bf16[4,112,1536]{2,1,0:T(8,128)(2,1)S(1)}, bf16[4,112,1536]{2,1,0:T(8,128)(2,1)S(1)}, u32[]{:S(2)}, u32[]{:S(2)}) collective-permute-start(bf16[4,112,1536]{2,1,0:T(8,128)(2,1)S(1)} %add_convert_fusion.2), channel_id=1, source_target_pairs={{0,2},{1,3},{2,0},{3,1},{4,6},{5,7},{6,4},{7,5},{8,10},{9,11},{10,... | collective-permute-start | bytes 4128776 | tf_op jit(solution)/shard_map/ppermute | solution.py:209
  338.8 37.2 %all-to-all-start.3 = ((bf16[8,56,1536]{2,1,0:T(8,128)(2,1)}), bf16[8,56,1536]{2,1,0:T(8,128)(2,1)}, u32[]{:S(2)}, u32[]{:S(2)}) async-start(bf16[8,56,1536]{2,1,0:T(8,128)(2,1)} %bitcast.376), calls=%async_computation.3 | async-start | bytes 2752512 | tf_op jit(solution)/shard_map/all_to_all | solution.py:544
  538.4 46.3 %collective-permute-start.42 = (bf16[2,8,128,384]{3,2,1,0:T(8,128)(2,1)}, bf16[2,8,128,384]{3,2,1,0:T(8,128)(2,1)}, u32[]{:S(2)}, u32[]{:S(2)}) collective-permute-start(bf16[2,8,128,384]{3,2,1,0:T(8,128)(2,1)} %pad_maximum_fusion.1), channel_id=1, source_target_pairs={{0,1},{1,0},{2,3},{3,2},{4,5},{5,4},{6,7},{7,6},{8,9},{9,8},{10,11... | collective-permute-start | bytes 4718600 | tf_op jit(solution)/shard_map/ppermute | solution.py:209
  541.5 15.3 %collective-permute-start.49 = (bf16[2,8,96,384]{3,2,1,0:T(8,128)(2,1)}, bf16[2,8,96,384]{3,2,1,0:T(8,128)(2,1)}, u32[]{:S(2)}, u32[]{:S(2)}) collective-permute-start(bf16[2,8,96,384]{3,2,1,0:T(8,128)(2,1)} %pad_maximum_fusion.3), channel_id=1, source_target_pairs={{0,1},{1,0},{2,3},{3,2},{4,5},{5,4},{6,7},{7,6},{8,9},{9,8},{10,11... | collective-permute-start | bytes 3538952 | tf_op jit(solution)/shard_map/ppermute | solution.py:209
  558.4 10.9 %collective-permute-start.52 = (bf16[4,96,384]{2,1,0:T(8,128)(2,1)S(1)}, bf16[4,96,384]{2,1,0:T(8,128)(2,1)S(1)}, u32[]{:S(2)}, u32[]{:S(2)}) collective-permute-start(bf16[4,96,384]{2,1,0:T(8,128)(2,1)S(1)} %get-tuple-element.208), channel_id=1, source_target_pairs={{0,6},{1,7},{2,4},{3,5},{4,2},{5,3},{6,0},{7,1},{8,14},{9,15},{10,... | collective-permute-start | bytes 884744 | tf_op jit(solution)/shard_map/ppermute | solution.py:225
  560.7 13.9 %collective-permute-start.51 = (bf16[4,96,384]{2,1,0:T(8,128)(2,1)S(1)}, bf16[4,96,384]{2,1,0:T(8,128)(2,1)S(1)}, u32[]{:S(2)}, u32[]{:S(2)}) collective-permute-start(bf16[4,96,384]{2,1,0:T(8,128)(2,1)S(1)} %get-tuple-element.207), channel_id=1, source_target_pairs={{0,2},{1,3},{2,0},{3,1},{4,6},{5,7},{6,4},{7,5},{8,10},{9,11},{10,... | collective-permute-start | bytes 884744 | tf_op jit(solution)/shard_map/ppermute | solution.py:209
  561.3 13.5 %collective-permute-start.50 = (bf16[4,96,384]{2,1,0:T(8,128)(2,1)S(1)}, bf16[4,96,384]{2,1,0:T(8,128)(2,1)S(1)}, u32[]{:S(2)}, u32[]{:S(2)}) collective-permute-start(bf16[4,96,384]{2,1,0:T(8,128)(2,1)S(1)} %fusion.123), channel_id=1, source_target_pairs={{0,4},{4,0},{8,12},{12,8},{16,20},{20,16},{24,28},{28,24},{1,5},{5... | collective-permute-start | bytes 884744 | tf_op jit(solution)/shard_map/ppermute | solution.py:209
  562.3 28.2 %collective-permute-start.56 = (bf16[2,8,192,256]{3,2,1,0:T(8,128)(2,1)S(1)}, bf16[2,8,192,256]{3,2,1,0:T(8,128)(2,1)S(1)}, u32[]{:S(2)}, u32[]{:S(2)}) collective-permute-start(bf16[2,8,192,256]{3,2,1,0:T(8,128)(2,1)S(1)} %pad_maximum_fusion.2), channel_id=1, source_target_pairs={{0,1},{1,0},{2,3},{3,2},{4,5},{5,4},{6,7},{7,6},{8,9},{9,8},{10,11... | collective-permute-start | bytes 4718600 | tf_op jit(solution)/shard_map/ppermute | solution.py:209
  586.6 13.0 %collective-permute-start.45 = (bf16[4,128,384]{2,1,0:T(8,128)(2,1)S(1)}, bf16[4,128,384]{2,1,0:T(8,128)(2,1)S(1)}, u32[]{:S(2)}, u32[]{:S(2)}) collective-permute-start(bf16[4,128,384]{2,1,0:T(8,128)(2,1)S(1)} %get-tuple-element.203), channel_id=1, source_target_pairs={{0,6},{1,7},{2,4},{3,5},{4,2},{5,3},{6,0},{7,1},{8,14},{9,15},{10,... | collective-permute-start | bytes 1179656 | tf_op jit(solution)/shard_map/ppermute | solution.py:225
  587.6 20.5 %collective-permute-start.44 = (bf16[4,128,384]{2,1,0:T(8,128)(2,1)S(1)}, bf16[4,128,384]{2,1,0:T(8,128)(2,1)S(1)}, u32[]{:S(2)}, u32[]{:S(2)}) collective-permute-start(bf16[4,128,384]{2,1,0:T(8,128)(2,1)S(1)} %get-tuple-element.202), channel_id=1, source_target_pairs={{0,2},{1,3},{2,0},{3,1},{4,6},{5,7},{6,4},{7,5},{8,10},{9,11},{10,... | collective-permute-start | bytes 1179656 | tf_op jit(solution)/shard_map/ppermute | solution.py:209
  589.6 18.5 %collective-permute-start.43 = (bf16[4,128,384]{2,1,0:T(8,128)(2,1)S(1)}, bf16[4,128,384]{2,1,0:T(8,128)(2,1)S(1)}, u32[]{:S(2)}, u32[]{:S(2)}) collective-permute-start(bf16[4,128,384]{2,1,0:T(8,128)(2,1)S(1)} %fusion.113), channel_id=1, source_target_pairs={{0,4},{4,0},{8,12},{12,8},{16,20},{20,16},{24,28},{28,24},{1,5},{5... | collective-permute-start | bytes 1179656 | tf_op jit(solution)/shard_map/ppermute | solution.py:209
  590.9 25.6 %collective-permute-start.59 = (bf16[4,192,256]{2,1,0:T(8,128)(2,1)S(1)}, bf16[4,192,256]{2,1,0:T(8,128)(2,1)S(1)}, u32[]{:S(2)}, u32[]{:S(2)}) collective-permute-start(bf16[4,192,256]{2,1,0:T(8,128)(2,1)S(1)} %get-tuple-element.194), channel_id=1, source_target_pairs={{0,6},{1,7},{2,4},{3,5},{4,2},{5,3},{6,0},{7,1},{8,14},{9,15},{10,... | collective-permute-start | bytes 1179656 | tf_op jit(solution)/shard_map/ppermute | solution.py:225
  591.9 31.8 %collective-permute-start.58 = (bf16[4,192,256]{2,1,0:T(8,128)(2,1)S(1)}, bf16[4,192,256]{2,1,0:T(8,128)(2,1)S(1)}, u32[]{:S(2)}, u32[]{:S(2)}) collective-permute-start(bf16[4,192,256]{2,1,0:T(8,128)(2,1)S(1)} %get-tuple-element.193), channel_id=1, source_target_pairs={{0,2},{1,3},{2,0},{3,1},{4,6},{5,7},{6,4},{7,5},{8,10},{9,11},{10,... | collective-permute-start | bytes 1179656 | tf_op jit(solution)/shard_map/ppermute | solution.py:209
  599.6 24.3 %collective-permute-start.57 = (bf16[4,192,256]{2,1,0:T(8,128)(2,1)S(1)}, bf16[4,192,256]{2,1,0:T(8,128)(2,1)S(1)}, u32[]{:S(2)}, u32[]{:S(2)}) collective-permute-start(bf16[4,192,256]{2,1,0:T(8,128)(2,1)S(1)} %fusion.116), channel_id=1, source_target_pairs={{0,4},{4,0},{8,12},{12,8},{16,20},{20,16},{24,28},{28,24},{1,5},{5... | collective-permute-start | bytes 1179656 | tf_op jit(solution)/shard_map/ppermute | solution.py:209
  608.3 17.4 %collective-permute-start.48 = (bf16[128,384]{1,0:T(8,128)(2,1)S(1)}, bf16[128,384]{1,0:T(8,128)(2,1)S(1)}, u32[]{:S(2)}, u32[]{:S(2)}) collective-permute-start(bf16[128,384]{1,0:T(8,128)(2,1)S(1)} %get-tuple-element.196), channel_id=1, source_target_pairs={{0,24},{4,28},{8,16},{12,20},{16,8},{20,12},{24,0},{28,4},{1,25},{... | collective-permute-start | bytes 294920 | tf_op jit(solution)/shard_map/ppermute | solution.py:209
  609.7 19.0 %collective-permute-start.47 = (bf16[128,384]{1,0:T(8,128)(2,1)S(1)}, bf16[128,384]{1,0:T(8,128)(2,1)S(1)}, u32[]{:S(2)}, u32[]{:S(2)}) collective-permute-start(bf16[128,384]{1,0:T(8,128)(2,1)S(1)} %get-tuple-element.197), channel_id=1, source_target_pairs={{0,16},{4,20},{8,24},{12,28},{16,0},{20,4},{24,8},{28,12},{1,17},{... | collective-permute-start | bytes 294920 | tf_op jit(solution)/shard_map/ppermute | solution.py:209
  616.5 12.2 %collective-permute-start.46 = (bf16[128,384]{1,0:T(8,128)(2,1)S(1)}, bf16[128,384]{1,0:T(8,128)(2,1)S(1)}, u32[]{:S(2)}, u32[]{:S(2)}) collective-permute-start(bf16[128,384]{1,0:T(8,128)(2,1)S(1)} %get-tuple-element.195), channel_id=1, source_target_pairs={{0,8},{4,12},{8,0},{12,4},{16,24},{20,28},{24,16},{28,20},{1,9},{5... | collective-permute-start | bytes 294920 | tf_op jit(solution)/shard_map/ppermute | solution.py:209
  (184 other events, 1770.7 us)

commit v2 on v1

v2 whole, which is shorter than its diff:
```python
import functools
import jax
import jax.numpy as jnp
from jax import lax
from jax.sharding import PartitionSpec as P
from jax.experimental import pallas as pl
from jax.experimental.pallas import tpu as pltpu
NS = 16
F32 = jnp.float32
SLOT_OF=[4*((i>>2)&1)+2*(1-((i>>1)&1))+(1-(i&1)) for i in range(8)]
def merge8(rows):
    idx=lax.broadcasted_iota(jnp.int32,(8,128),0)
    m4=idx<4; m2=(idx&2)!=0; m1=(idx&1)!=0
    p=[None]*8
    for i in range(8): p[SLOT_OF[i]]=rows[i]
    r=[jnp.where(m4,p[k],p[k+4])+pltpu.roll(jnp.where(m4,p[k+4],p[k]),4,0) for k in range(4)]
    def half(x,y,m,d):
        return jnp.where(m,x+pltpu.roll(x,d,0),y+pltpu.roll(y,8-d,0))
    v=[half(r[k],r[k+2],m2,2) for k in range(2)]
    return half(v[0],v[1],m1,1)
def mm(a, b, dims=((1,), (0,)), **kw):
    return lax.dot_general(a, b, (dims, ((), ())), preferred_element_type=F32, **kw)


NT = ((1,), (1,))
TN = ((0,), (0,))


def softplus(v):
    e = jnp.exp(-jnp.abs(v))
    tiny = e * (1.0 - e * (0.5 - e * (1.0 / 3.0 - e * 0.25)))
    return jnp.maximum(v, 0.0) + jnp.where(e < 0.01, tiny, jnp.log(1.0 + e))


def sigmoid_of_softplus(d):
    tiny = d * (1.0 - d * (0.5 - d * (1.0 / 6.0 - d * (1.0 / 24.0))))
    return jnp.where(d < 0.03, tiny, 1.0 - jnp.exp(-d))


def sigmoid(v):
    return 1.0 / (1.0 + jnp.exp(-v))


def spread(dst, src, T):
    for j in range(T):
        dst[j] = jnp.broadcast_to(src[:, j:j + 1], (NS, 128))


def fold(x):
    return x[0:8] + x[8:16]


def convolve(ext, w, b, T):
    taps = w.shape[0]
    out = b
    for k in range(taps):
        out = out + w[k:k + 1] * ext[9 - taps + k:9 - taps + k + T]
    return out


def mixer_kernel(T, Q, R, x_ref, gain_ref, wx_ref, xpT_ref, wdt_ref, par_ref, a2_ref,
                 nm_ref, in_ref, u_ref, dl_ref, pT_ref, y_ref, st_ref, state, bx, cx, du):
    c = pl.program_id(0)
    L, DI = nm_ref.shape[0], wx_ref.shape[1]
    taps = par_ref.shape[0] - 3

    @pl.when(c == 0)
    def _():
        state[...] = jnp.zeros_like(state)
        x = x_ref[...].astype(F32)
        nm = (x * lax.rsqrt(jnp.mean(x * x, axis=-1, keepdims=True) + 1e-05) * gain_ref[...]).astype(jnp.bfloat16)
        nm_ref[...] = nm
        in_ref[0:8] = jnp.zeros((8, DI), F32)
        in_ref[8:] = mm(nm, wx_ref[...])
    st_ref[0] = state[...]
    par = par_ref[...]
    skip = par[taps + 2:taps + 3]
    conv = convolve(in_ref[pl.ds(pl.multiple_of(c * T, 8), T + 8)], par[:taps], par[taps:taps + 1], T)
    u = conv * sigmoid(conv)
    u_ref[0] = u.reshape(T // 8, 8, DI)
    pT = mm(xpT_ref[...], u.astype(jnp.bfloat16), NT)
    pT_ref[0] = pT
    d = softplus(mm(pT[:R].astype(jnp.bfloat16), wdt_ref[...], TN) + par[taps + 1:taps + 2])
    dl_ref[0] = d.reshape(T // 8, 8, DI)
    du[...] = (d * u).reshape(T // 8, 8, DI)
    spread(bx, pT[R:R + NS], T)
    spread(cx, pT[R + NS:R + 2 * NS], T)

    def grp(g, _):
        base = pl.multiple_of(g * (Q * 128), 128)
        lanes = [pl.ds(base + q * 128, 128) for q in range(Q)]
        a = [a2_ref[:, ln] for ln in lanes]
        sk = [par_ref[taps + 2:taps + 3, ln] for ln in lanes]

        def tb(i, s):
            s = list(s)
            rows = [[] for _ in range(Q)]
            for k in range(8):
                t = i * 8 + k
                b = bx[t]
                cc = cx[t]
                for q in range(Q):
                    dd = dl_ref[0, i, k:k + 1, lanes[q]]
                    dub = du[i, k:k + 1, lanes[q]]
                    s[q] = jnp.exp2(dd * a[q]) * s[q] + b * dub
                    rows[q].append(fold(s[q] * cc))
            for q in range(Q):
                y_ref[0, i, :, lanes[q]] = merge8(rows[q]) + sk[q] * u_ref[0, i, :, lanes[q]]
            return tuple(s)
        s = lax.fori_loop(0, T // 8, tb, tuple(state[:, ln] for ln in lanes))
        for q in range(Q):
            state[:, lanes[q]] = s[q]
        return 0
    lax.fori_loop(0, DI // (Q * 128), grp, 0)


def whole_spec(a):
    return pl.BlockSpec(a.shape, lambda *_: (0,) * len(a.shape))


def sds(shape, dtype=F32):
    return jax.ShapeDtypeStruct(shape, dtype)


def mixer_forward(x, gain, wx, xpT, wdt, par, a2, T, Q=3):
    L, D = x.shape
    DI = wx.shape[1]
    C, XP, R = L // T, xpT.shape[0], wdt.shape[0]
    ins = [x, gain, wx, xpT, wdt, par, a2]
    rows = pl.BlockSpec((1, T // 8, 8, DI), lambda c: (c, 0, 0, 0))
    big = sds((C, T // 8, 8, DI))
    nm, inner = sds((L, D), jnp.bfloat16), sds((L + 8, DI))
    return pl.pallas_call(
        functools.partial(mixer_kernel, T, Q, R), grid=(C,),
        in_specs=[whole_spec(a) for a in ins],
        out_specs=[whole_spec(nm), whole_spec(inner), rows, rows, pl.BlockSpec((1, XP, T), lambda c: (c, 0, 0)), rows,
                   pl.BlockSpec((1, NS, DI), lambda c: (c, 0, 0))],
        out_shape=[nm, inner, big, big, sds((C, XP, T)), big, sds((C, NS, DI))],
        scratch_shapes=[pltpu.VMEM((NS, DI), F32), pltpu.VMEM((T, NS, 128), F32), pltpu.VMEM((T, NS, 128), F32),
                        pltpu.VMEM((T // 8, 8, DI), F32)],
        compiler_params=pltpu.CompilerParams(vmem_limit_bytes=48 << 20),
        cost_estimate=pl.CostEstimate(flops=40000000000, bytes_accessed=16 * L * DI, transcendentals=0),
    )(*ins)


def scan_back_kernel(T, Q, Q2, R, u_ref, dl_ref, gs_ref, in_ref, pT_ref, st_ref, xpT_ref, wdt_ref, par_ref, an_ref,
                     gi_ref, gxp_ref, gwd_ref, gpar_ref, carry, later, bx, cx, du, guc, gdt, hs, ds, gbp, gcp, sums):
    j = pl.program_id(0)
    c = pl.num_programs(0) - 1 - j
    DI = wdt_ref.shape[1]
    taps = par_ref.shape[0] - 3

    @pl.when(j == 0)
    def _():
        for ref in (carry, later, gxp_ref, gwd_ref, gpar_ref, sums):
            ref[...] = jnp.zeros_like(ref)
    pT = pT_ref[0]
    spread(bx, pT[R:R + NS], T)
    spread(cx, pT[R + NS:R + 2 * NS], T)
    du[...] = dl_ref[0] * u_ref[0]
    gbp[...] = jnp.zeros_like(gbp)
    gcp[...] = jnp.zeros_like(gcp)
    W = Q * 128

    def grp(g, _):
        base = pl.multiple_of(g * W, 128)
        lanes = [pl.ds(base + q * 128, 128) for q in range(Q)]
        loc = [slice(q * 128, q * 128 + 128) for q in range(Q)]
        an = [an_ref[:, ln] for ln in lanes]
        a2 = [v * 1.4426950408889634 for v in an]

        def tb(i, s):
            s = list(s)
            for k in range(8):
                t = i * 8 + k
                b = bx[t]
                gc = gcp[t]
                for q in range(Q):
                    dd = dl_ref[0, i, k:k + 1, lanes[q]]
                    dub = du[i, k:k + 1, lanes[q]]
                    gsr = gs_ref[0, i, k:k + 1, lanes[q]]
                    dec = jnp.exp2(dd * a2[q])
                    h = dec * s[q]
                    ds[t, :, loc[q]] = dec
                    hs[t, :, loc[q]] = h
                    s[q] = h + b * dub
                    gc = gc + s[q] * gsr
                gcp[t] = gc
            return tuple(s)
        lax.fori_loop(0, T // 8, tb, tuple(st_ref[0, :, ln] for ln in lanes))
        for q0 in range(0, Q, Q2):
            qs = range(q0, q0 + Q2)
            sk = {q: par_ref[taps + 2:taps + 3, lanes[q]] for q in qs}

            def rb(jj, cr):
                i = T // 8 - 1 - jj
                g_, ga = {q: cr[0][q - q0] for q in qs}, {q: cr[1][q - q0] for q in qs}
                gbs, gsk = list(cr[2]), list(cr[3])
                m1, m2 = {q: [None] * 8 for q in qs}, {q: [None] * 8 for q in qs}
                for k in range(7, -1, -1):
                    t = i * 8 + k
                    b = bx[t]
                    cc = cx[t]
                    gb = gbp[t]
                    for q in qs:
                        dd = dl_ref[0, i, k:k + 1, lanes[q]]
                        dub = du[i, k:k + 1, lanes[q]]
                        gsr = gs_ref[0, i, k:k + 1, lanes[q]]
                        gg = gsr * cc + g_[q]
                        g_[q] = gg * ds[t, :, loc[q]]
                        qq = gg * hs[t, :, loc[q]]
                        m1[q][k] = fold(gg * b)
                        m2[q][k] = fold(qq * an[q])
                        ga[q] = ga[q] + qq * dd
                        gb = gb + gg * dub
                    gbp[t] = gb
                for q in qs:
                    s1 = merge8(m1[q])
                    s2 = merge8(m2[q])
                    u8, d8, gs8 = u_ref[0, i, :, lanes[q]], dl_ref[0, i, :, lanes[q]], gs_ref[0, i, :, lanes[q]]
                    guc[i, :, lanes[q]] = d8 * s1 + sk[q] * gs8
                    gd = (s2 + u8 * s1) * sigmoid_of_softplus(d8)
                    gdt[i, :, lanes[q]] = gd
                    gbs[q - q0] = gbs[q - q0] + gd
                    gsk[q - q0] = gsk[q - q0] + gs8 * u8
                return (tuple(g_[q] for q in qs), tuple(ga[q] for q in qs), tuple(gbs), tuple(gsk))
            z8 = tuple(jnp.zeros((8, 128), F32) for q in qs)
            cr = lax.fori_loop(0, T // 8, rb, (tuple(carry[:, lanes[q]] for q in qs),
                                               tuple(jnp.zeros((NS, 128), F32) for q in qs), z8, z8))
            for q in qs:
                carry[:, lanes[q]] = cr[0][q - q0]
                gpar_ref[taps + 2:taps + 2 + NS, lanes[q]] += cr[1][q - q0] * an[q]
                sums[taps + 1, :, lanes[q]] += cr[2][q - q0]
                sums[taps + 2, :, lanes[q]] += cr[3][q - q0]
        return 0
    lax.fori_loop(0, DI // W, grp, 0)

    gbT = jnp.sum(gbp[...], axis=2).T
    gcT = jnp.sum(gcp[...], axis=2).T
    gd = gdt[...].reshape(T, DI).astype(jnp.bfloat16)
    gpT = jnp.concatenate([mm(wdt_ref[...], gd, NT), gbT, gcT], axis=0).astype(jnp.bfloat16)
    gwd_ref[...] += mm(pT[:R].astype(jnp.bfloat16), gd)
    gxp_ref[...] += mm(gpT, u_ref[0].reshape(T, DI).astype(jnp.bfloat16))
    gu = guc[...].reshape(T, DI) + mm(gpT, xpT_ref[...], TN)
    par = par_ref[...]
    ext = in_ref[pl.ds(pl.multiple_of(c * T, 8), T + 8)]
    conv = convolve(ext, par[:taps], par[taps:taps + 1], T)
    sig = sigmoid(conv)
    gconv = gu * (sig * (1.0 + conv * (1.0 - sig)))
    part = lambda v: jnp.sum(v.reshape(T // 8, 8, DI), axis=0)
    sums[taps] += part(gconv)
    for k in range(taps):
        sums[k] += part(gconv * ext[9 - taps + k:9 - taps + k + T])
    both = jnp.concatenate([gconv, later[...]], axis=0)
    gi = par[0:1] * both[taps - 1:taps - 1 + T]
    for k in range(1, taps):
        gi = gi + par[k:k + 1] * both[taps - 1 - k:taps - 1 - k + T]
    gi_ref[...] = gi.astype(jnp.bfloat16)
    later[...] = gconv[:8]

    @pl.when(c == 0)
    def _():
        for k in range(taps + 2):
            gpar_ref[k:k + 1] = jnp.sum(sums[k], axis=0, keepdims=True)
        gpar_ref[taps + 2 + NS:taps + 3 + NS] = jnp.sum(sums[taps + 2], axis=0, keepdims=True)


def scan_backward(u, dl, gs, inner, pT, st, xpT, wdt, par, an, Q=2, Q2=2):
    C, T8, _, DI = u.shape
    T = T8 * 8
    XP, R = xpT.shape[0], wdt.shape[0]
    n = par.shape[0] + NS
    rev = lambda *shape: pl.BlockSpec((1,) + shape, lambda j: (C - 1 - j,) + (0,) * len(shape))
    rows = rev(T8, 8, DI)
    outs = [sds((C * T, DI), jnp.bfloat16), sds((XP, DI)), sds((R, DI)), sds((n, DI))]
    V = lambda *s: pltpu.VMEM(s, F32)
    return pl.pallas_call(
        functools.partial(scan_back_kernel, T, Q, Q2, R), grid=(C,),
        in_specs=[rows, rows, rows, whole_spec(inner), rev(XP, T), rev(NS, DI)] + [whole_spec(a) for a in (xpT, wdt, par, an)],
        out_specs=[pl.BlockSpec((T, DI), lambda j: (C - 1 - j, 0))] + [whole_spec(o) for o in outs[1:]],
        out_shape=outs,
        scratch_shapes=[V(NS, DI), V(8, DI), V(T, NS, 128), V(T, NS, 128), V(T8, 8, DI), V(T8, 8, DI), V(T8, 8, DI),
                        V(T, NS, Q * 128), V(T, NS, Q * 128), V(T, NS, 128), V(T, NS, 128), V(par.shape[0], 8, DI)],
        compiler_params=pltpu.CompilerParams(vmem_limit_bytes=52 << 20),
        cost_estimate=pl.CostEstimate(flops=80000000000, bytes_accessed=16 * C * T * DI, transcendentals=0),
    )(u, dl, gs, inner, pT, st, xpT, wdt, par, an)


def one_call(kernel, ins, outs, scalars=(), flops=0):
    smem = pl.BlockSpec(memory_space=pltpu.SMEM)
    vmem = pl.BlockSpec(memory_space=pltpu.VMEM)
    size = sum(a.size * a.dtype.itemsize for a in list(ins) + list(outs))
    return pl.pallas_call(
        kernel,
        in_specs=[smem] * len(scalars) + [vmem] * len(ins), out_specs=[vmem] * len(outs), out_shape=list(outs),
        compiler_params=pltpu.CompilerParams(vmem_limit_bytes=56 << 20),
        cost_estimate=pl.CostEstimate(flops=flops, bytes_accessed=size, transcendentals=0),
    )(*scalars, *ins)


def route_kernel(cap, here, message, live_ref, x_ref, nm_ref, y_ref, wz_ref, wo_ref, gain_ref, wr_ref, route_ref, cot_ref,
                 z_ref, gated_ref, hid_ref, place_ref, out_ref, prob_ref, gate_ref):
    bf = jnp.bfloat16
    L = x_ref.shape[0]
    E = wr_ref.shape[1]
    z = mm(nm_ref[...], wz_ref[...])
    z_ref[...] = z
    gated = (y_ref[...] * (z * sigmoid(z))).astype(bf)
    gated_ref[...] = gated
    hid = x_ref[...].astype(F32) + mm(gated, wo_ref[...])
    hid_ref[...] = hid
    nmoe = hid * lax.rsqrt(jnp.mean(hid * hid, axis=-1, keepdims=True) + 1e-05) * gain_ref[...]
    logits = mm(nmoe, wr_ref[...], precision=lax.Precision.HIGHEST)
    e = jnp.exp(logits - jnp.max(logits, axis=-1, keepdims=True))
    probs = e / jnp.sum(e, axis=-1, keepdims=True)
    prob_ref[...] = probs
    route = route_ref[...]
    hot = route == lax.broadcasted_iota(jnp.int32, (L, E), 1)
    gate = jnp.sum(jnp.where(hot, probs, 0.0), axis=-1, keepdims=True)
    gate_ref[...] = gate
    live = lax.broadcasted_iota(jnp.int32, (L, 1), 0) < live_ref[0]
    hits = jnp.where(hot & live, 1.0, 0.0)
    before = lax.broadcasted_iota(jnp.int32, (L, L), 0) > lax.broadcasted_iota(jnp.int32, (L, L), 1)
    slot = jnp.sum(mm(jnp.where(before, 1.0, 0.0).astype(bf), hits.astype(bf)) * hits, axis=-1, keepdims=True).astype(jnp.int32)
    slots = place_ref.shape[1]
    target = route // here * message + route % here * cap + slot
    target = jnp.where(live & (slot < cap), target, slots)
    place = jnp.where(target == lax.broadcasted_iota(jnp.int32, (L, slots), 1), 1.0, 0.0).astype(bf)
    place_ref[...] = place
    D = hid.shape[1]
    gy = jnp.where(live, cot_ref[...], 0.0)
    out_ref[:, :D] = mm(place, nmoe.astype(bf), TN).astype(bf)
    out_ref[:, D:] = mm(place, (gy * gate).astype(bf), TN).astype(bf)


def unroute_kernel(live_ref, home_ref, place_ref, hid_ref, prob_ref, gate_ref, route_ref, cot_ref, gain_ref, wr_ref, wo_ref, sh_ref,
                   z_ref, y_ref, mix_ref, gh_ref, gs_ref, gz_ref, gm_ref, gr_ref, gg_ref):
    bf = jnp.bfloat16
    high = lax.Precision.HIGHEST
    hid, gain = hid_ref[...], gain_ref[...]
    L, D = hid.shape
    E = wr_ref.shape[1]
    tok = mm(place_ref[...], home_ref[...])
    etok, gsent = tok[:, :D], tok[:, D:]
    live = lax.broadcasted_iota(jnp.int32, (L, 1), 0) < live_ref[0]
    gate, probs = gate_ref[...], prob_ref[...]
    mix_ref[...] = jnp.where(live, hid + gate * etok, 0.0).astype(bf)
    gy = jnp.where(live, cot_ref[...], 0.0)
    ggate = jnp.sum(gy * etok, axis=-1, keepdims=True)
    hot = jnp.where(route_ref[...] == lax.broadcasted_iota(jnp.int32, (L, E), 1), 1.0, 0.0)
    glog = ggate * gate * (hot - probs)
    rms = lax.rsqrt(jnp.mean(hid * hid, axis=-1, keepdims=True) + 1e-05)
    hat = hid * rms
    gr_ref[...] = mm(hat * gain, glog, TN, precision=high)
    gnorm = gsent + mm(glog, wr_ref[...], NT, precision=high)
    gg_ref[...] = jnp.sum(gnorm * hat, axis=0, keepdims=True)
    scaled = gnorm * gain
    gh = gy + rms * (scaled - hat * jnp.mean(scaled * hat, axis=-1, keepdims=True))
    gh_ref[...] = gh
    gmix = gh.astype(bf)
    gm_ref[...] = mm(gmix, sh_ref[...]).astype(bf)
    ggated = mm(gmix, wo_ref[...], NT)
    z = z_ref[...]
    sig = sigmoid(z)
    gs_ref[...] = ggated * (z * sig)
    gz_ref[...] = (ggated * y_ref[...] * (sig * (1.0 + z * (1.0 - sig)))).astype(bf)


def token_kernel(gi_ref, gz_ref, wx_ref, wz_ref, x_ref, gh_ref, gain_ref, gt_ref, gg_ref):
    gnm = mm(gi_ref[...], wx_ref[...], NT) + mm(gz_ref[...], wz_ref[...], NT)
    x = x_ref[...].astype(F32)
    rms = lax.rsqrt(jnp.mean(x * x, axis=-1, keepdims=True) + 1e-05)
    hat = x * rms
    gg_ref[...] = jnp.sum(gnm * hat, axis=0, keepdims=True)
    scaled = gnm * gain_ref[...]
    gt_ref[...] = gh_ref[...] + rms * (scaled - hat * jnp.mean(scaled * hat, axis=-1, keepdims=True))


QB = 64
CAP = 13
BF = jnp.bfloat16
root_half = 0.7071067811865476
inv_root_two_pi = 0.3989422804014327
log2e = 1.4426950408889634


def swap(x, axis, bit):
    n = lax.axis_size(axis)
    return lax.ppermute(x, axis, [(i, i ^ bit) for i in range(n)])


def bits_of(axis):
    n = lax.axis_size(axis)
    return [1 << k for k in range(n.bit_length() - 1)]


def exchange(x, mask):
    rm, cm = mask
    if rm == 0:
        return swap(x, "col", cm)
    if cm == 0:
        return swap(x, "row", rm)
    rows, cols = lax.axis_size("row"), lax.axis_size("col")
    pairs = [(r * cols + c, (r ^ rm) * cols + (c ^ cm)) for r in range(rows) for c in range(cols)]
    return lax.ppermute(x, ("row", "col"), pairs)


def combos(bits):
    out = [(0, 0)]
    for rb, cb in bits:
        out = out + [(r | rb, c | cb) for r, c in out]
    return out


def stages():
    row, col = bits_of("row"), bits_of("col")
    far = combos([(b, 0) for b in row[1:]])
    plane = combos([(row[0], 0)] + [(0, b) for b in col[1:]])
    return far, plane, (0, col[0])


def add(a, b):
    return (a[0] ^ b[0], a[1] ^ b[1])


def gather_far(x):
    return jnp.stack([x] + [exchange(x, m) for m in stages()[0][1:]])


def gather_plane(mine):
    return [mine] + [exchange(mine, m) for m in stages()[1][1:]]


def gather_core(near):
    far, plane, core = stages()
    near = [([add(f, m) for f in far], b) for m, b in zip(plane, near)]
    return near + [([add(m, core) for m in ms], exchange(b, core)) for ms, b in near]


def gather_list(x):
    return gather_core(gather_plane(gather_far(x)))


def assemble_kernel(masks, moves, count_in, *refs):
    r0, c0 = refs[0][0], refs[0][1]
    ins, outs = refs[1:1 + count_in], refs[1 + count_in:]
    for buf, ms in zip(ins, masks):
        for i, (rm, cm) in enumerate(ms):
            for (row, count, lanes), out, place in moves:
                place(outs[out], r0 ^ rm, c0 ^ cm, buf[i, row:row + count, :lanes])


def put_block(out, r, c, block):
    n, m = block.shape
    out[pl.ds(pl.multiple_of(r * n, n), n), pl.ds(pl.multiple_of(c * m, m), m)] = block


def put_pair(out, r, c, block):
    out[r, c] = block


def take_blocks(gathered):
    rows, cols = lax.axis_size("row"), lax.axis_size("col")
    order = [r * cols + c for ms, _ in gathered for r, c in ms]
    entry = jnp.asarray([order.index(i) for i in range(rows * cols)], jnp.int32)
    me = lax.axis_index("row") * cols + lax.axis_index("col")
    stacked = jnp.concatenate([b for _, b in gathered], axis=0)
    out = jnp.take(stacked, entry[jnp.arange(rows * cols, dtype=jnp.int32) ^ me], axis=0)
    return out.reshape((rows, cols) + stacked.shape[1:])


def assemble(gathered, moves, shapes):
    masks = [ms for ms, _ in gathered]
    bufs = [b for _, b in gathered]
    if any(lanes % 128 for (_, _, lanes), _, _ in moves):
        every = take_blocks(gathered)
        cut = [every[:, :, row:row + count, :lanes] for (row, count, lanes), _, _ in moves]
        return [v if place is put_pair else v.transpose(0, 2, 1, 3).reshape(shape)
                for v, shape, (_, _, place) in zip(cut, shapes, moves)]
    me = jnp.stack([lax.axis_index("row"), lax.axis_index("col")]).astype(jnp.int32)
    vmem = pl.BlockSpec(memory_space=pltpu.VMEM)
    return pl.pallas_call(
        functools.partial(assemble_kernel, masks, moves, len(bufs)),
        in_specs=[pl.BlockSpec(memory_space=pltpu.SMEM)] + [vmem] * len(bufs),
        out_specs=[vmem] * len(shapes),
        out_shape=[jax.ShapeDtypeStruct(s, BF) for s in shapes],
        compiler_params=pltpu.CompilerParams(vmem_limit_bytes=32 << 20),
        cost_estimate=pl.CostEstimate(flops=0, bytes_accessed=4 * sum(b.size for b in bufs), transcendentals=0),
    )(me, *bufs)


def between(work, give, got):
    result = work(give)
    return lax.optimization_barrier((got, result))


def reduce_core(parts, work=None):
    far, plane, core = stages()
    near = [k for k in range(lax.axis_size("col")) if not k & core[1]]
    give = jnp.stack([parts[k | core[1]] for k in near])
    got = exchange(give, core)
    result = None
    if work:
        got, result = between(work, give, got)
    return [parts[k].astype(F32) + got[i].astype(F32) for i, k in enumerate(near)], result


def reduce_plane_give(sums):
    far, plane, core = stages()
    near = [k for k in range(lax.axis_size("col")) if not k & core[1]]
    rows, r0 = lax.axis_size("row"), lax.axis_index("row")

    def rows_of(k, rm):
        v = sums[near.index(k)]
        return lax.dynamic_index_in_dim(v.reshape((rows // 2, 2) + v.shape[1:]), (r0 ^ rm) & 1, 1, keepdims=False)
    return rows_of(0, 0), [rows_of(cm, rm).astype(BF) for rm, cm in plane[1:]]


def reduce_plane(own, give, work=None):
    got = [exchange(g, m) for g, m in zip(give, stages()[1][1:])]
    result = None
    if work:
        got, result = between(work, give, got)
    return functools.reduce(lambda t, v: t + v.astype(F32), got, own), result


def reduce_far(total, work=None):
    far = stages()[0]
    r0 = lax.axis_index("row")
    give = [lax.dynamic_index_in_dim(total, (r0 ^ rm) >> 1, 0, keepdims=False).astype(BF) for rm, _ in far[1:]]
    got = [exchange(g, m) for g, m in zip(give, far[1:])]
    result = None
    if work:
        got, result = between(work, give, got)
    done = lax.dynamic_index_in_dim(total, r0 >> 1, 0, keepdims=False)
    return functools.reduce(lambda t, v: t + v.astype(F32), got, done), result


def reduce_list(parts):
    own, give = reduce_plane_give(reduce_core(parts)[0])
    return reduce_far(reduce_plane(own, give)[0])[0]


def column_kernel(count, s_ref, *refs):
    total = mm(refs[0][...], refs[1][...], ((0,), (0,)))
    for k in range(1, count):
        total = total + mm(refs[2 * k][...], refs[2 * k + 1][...], ((0,), (0,)))
    refs[-1][0] = total.astype(BF)


def column_blocks(pairs, cols, my_col):
    n, m = pairs[0][0].shape
    w = pairs[0][1].shape[1] // cols
    count = len(pairs)
    if w % 128:
        total = sum(mm(a, b, ((0,), (0,))) for a, b in pairs).astype(BF).reshape(m, cols, w).transpose(1, 0, 2)
        return jnp.take(total, jnp.arange(cols, dtype=jnp.int32) ^ my_col, axis=0)
    return pl.pallas_call(
        functools.partial(column_kernel, count),
        grid_spec=pltpu.PrefetchScalarGridSpec(
            num_scalar_prefetch=1, grid=(cols,),
            in_specs=[pl.BlockSpec((n, m), lambda k, s: (0, 0)), pl.BlockSpec((n, w), lambda k, s: (0, s[0] ^ k))] * count,
            out_specs=pl.BlockSpec((1, m, w), lambda k, s: (k, 0, 0))),
        out_shape=jax.ShapeDtypeStruct((cols, m, w), BF),
        compiler_params=pltpu.CompilerParams(vmem_limit_bytes=32 << 20),
        cost_estimate=pl.CostEstimate(flops=2 * count * n * m * w * cols, bytes_accessed=2 * (count * (n * m + n * w * cols) + m * w * cols), transcendentals=0),
    )(my_col.reshape(1), *[v for p in pairs for v in p])


def gelu_parts(v):
    phi = 0.5 * (1.0 + lax.erf(v * root_half))
    return v * phi, phi + v * jnp.exp(-0.5 * v * v) * inv_root_two_pi


def expert_kernel(cols, *refs):
    both, up, down = refs[:cols], refs[cols], refs[cols + 1]
    outs, acts, gps = refs[cols + 2:2 * cols + 2], refs[2 * cols + 2], refs[2 * cols + 3]
    width = up.shape[1]
    n = both[0].shape[1]
    rows = jnp.concatenate([b[0] for b in both], axis=0)
    act, slope = gelu_parts(mm(rows[:, :width], up[0]))
    act = act.astype(BF)
    acts[0] = act
    gp = (mm(rows[:, width:], down[0], ((1,), (1,))) * slope).astype(BF)
    gps[0] = gp
    out = mm(act, down[0]).astype(BF)
    gin = mm(gp, up[0], ((1,), (1,))).astype(BF)
    for c in range(cols):
        outs[c][0, :, :width] = out[c * n:(c + 1) * n]
        outs[c][0, :, width:] = gin[c * n:(c + 1) * n]


def weights_kernel(cols, sets, *refs):
    up, down = refs[-2:]
    step = cols + 2
    gu = gd = None
    width = up.shape[1]
    for s in range(sets):
        both, act, gp = refs[s * step:s * step + cols], refs[s * step + cols][0], refs[s * step + cols + 1][0]
        rows = jnp.concatenate([b[0] for b in both], axis=0)
        a = mm(rows[:, :width], gp, ((0,), (0,)))
        b = mm(act, rows[:, width:], ((0,), (0,)))
        gu, gd = (a, b) if gu is None else (gu + a, gd + b)
    up[0] = gu
    down[0] = gd


def per_expert(kernel, ins, shapes, flops):
    tok = lambda a: pl.BlockSpec((1,) + a.shape[1:], lambda e: (e, 0, 0))
    size = sum(a.size * 2 for a in ins) + sum(s.size * s.dtype.itemsize for s in shapes)
    return list(pl.pallas_call(
        kernel, grid=(ins[0].shape[0],),
        in_specs=[tok(a) for a in ins], out_specs=[tok(s) for s in shapes], out_shape=shapes,
        compiler_params=pltpu.CompilerParams(vmem_limit_bytes=56 << 20),
        cost_estimate=pl.CostEstimate(flops=flops, bytes_accessed=size, transcendentals=0),
    )(*ins))


def expert_both(bufs, up, down):
    cols = len(bufs)
    experts, d, f = up.shape
    n = bufs[0].shape[1]
    shapes = ([jax.ShapeDtypeStruct((experts, n, 2 * d), BF)] * cols
              + [jax.ShapeDtypeStruct((experts, n * cols, f), BF)] * 2)
    outs = per_expert(functools.partial(expert_kernel, cols), bufs + [up, down], shapes, 8 * experts * cols * n * d * f)
    return outs[:cols], outs[cols:]


def expert_weights(sets, d, f):
    cols = len(sets[0]) - 2
    experts, n, _ = sets[0][0].shape
    if len(sets) > 1 and len(sets) * cols > 8:
        return [sum(v) for v in zip(*[expert_weights([s], d, f) for s in sets])]
    shapes = [jax.ShapeDtypeStruct((experts, d, f), F32), jax.ShapeDtypeStruct((experts, f, d), F32)]
    return per_expert(functools.partial(weights_kernel, cols, len(sets)), [v for s in sets for v in s], shapes,
                      4 * experts * cols * n * d * f * len(sets))


def up_to(n, m):
    return -(-n // m) * m


def tiles_fit(w_in_x, w_xproj, w_out, conv_w):
    lanes = w_in_x.shape[1]
    return (lanes % 128 == 0 and w_in_x.shape[0] % 32 == 0 and up_to(w_xproj.shape[0], 128) + 128 == lanes
            and w_xproj.shape[1] <= 32 and conv_w.shape[1] <= 128 and w_out.shape[0] % 16 == 0
            and up_to(w_out.shape[1], 128) == 256)


def one_hot(shape, match):
    i = lax.broadcasted_iota(jnp.int32, shape, 0)
    j = lax.broadcasted_iota(jnp.int32, shape, 1)
    return jnp.where(match(i, j), 1.0, 0.0).astype(BF)


def pack_kernel(wx, wdt, xp, cw, cb, db, al, ds, gx, gm, wo, wr, first, other, s_dt, s_xp, s_sm, s_out, s_r):
    n = wx.shape[0]
    for s in (s_dt, s_xp, s_sm, s_out, s_r):
        s[...] = jnp.zeros_like(s)
    first[:n] = wx[...]
    s_dt[:wdt.shape[0]] = wdt[...].astype(F32)
    first[n:n + 16] = s_dt[...].astype(BF)
    s_xp[:xp.shape[1], :xp.shape[0]] = xp[...].astype(F32).T
    wide = s_xp.shape[1]
    first[n + 16:, :wide] = s_xp[...].astype(BF)
    at = 0
    for v in (cw, cb, db, al, ds, gx, gm):
        s_sm[at:at + v.shape[0], :v.shape[1]] = v[...].astype(F32)
        at += v.shape[0]
    first[n + 16:, wide:] = s_sm[...].astype(BF)
    s_out[:, :wo.shape[1]] = wo[...].astype(F32)
    other[:wo.shape[0]] = s_out[...].astype(BF)
    s_r[:, :wr.shape[1]] = wr[...].astype(F32)
    half = wr.shape[0] // 2
    other[wo.shape[0]:, :128] = s_r[:half].astype(BF)
    other[wo.shape[0]:, 128:] = s_r[half:].astype(BF)


def pack_params(w_in_x, w_dt, w_xproj, conv_w, conv_b, dt_bias, a_log, d_skip, gain_mix, gain_moe, w_out, w_router):
    n, lanes = w_in_x.shape
    ins = [w_in_x, w_dt, w_xproj, conv_w, conv_b[None], dt_bias[None], a_log, d_skip[None], gain_mix[None], gain_moe[None],
           w_out, w_router]
    vmem = pl.BlockSpec(memory_space=pltpu.VMEM)
    V = lambda *s: pltpu.VMEM(s, F32)
    return pl.pallas_call(
        pack_kernel, in_specs=[vmem] * len(ins), out_specs=[vmem] * 2,
        out_shape=[sds((n + 48, lanes), BF), sds((w_out.shape[0] + w_router.shape[0] // 2, 256), BF)],
        scratch_shapes=[V(16, lanes), V(32, lanes - 128), V(32, 128), V(w_out.shape[0], 256), V(w_router.shape[0], 128)],
    )(*ins)


def each_block(masks, bufs, r0, c0):
    for buf, ms in zip(bufs, masks):
        for i, (rm, cm) in enumerate(ms):
            yield buf, i, r0 ^ rm, c0 ^ cm


def span(i, n):
    return pl.ds(pl.multiple_of(i * n, n), n)


def unpack_first(masks, dims, me, *refs):
    dt_rows, xp_cols, xp_rows, share, gshare, taps, rows, cols = dims
    count = len(masks)
    bufs = refs[:count]
    fx, dt, xpT, par, an, a2, gx, gm, w_dt, w_xp, w_sm = refs[count:]
    n = bufs[0].shape[1] - 48
    lanes = bufs[0].shape[2]
    wide = lanes - 128
    for buf, i, r, c in each_block(masks, bufs, me[0], me[1]):
        fx[span(r, n), span(c, lanes)] = buf[i, :n]
        w_dt[span(r, 16), span(c, lanes)] = buf[i, n:n + 16]
        w_xp[span(c, 32), span(r, wide)] = buf[i, n + 16:, :wide]
        w_sm[:, span(r * cols + c, 128)] = buf[i, n + 16:, wide:]
    pick = one_hot((dt.shape[0], 16 * rows), lambda i, j: (j % 16 < dt_rows) & (j // 16 * dt_rows + j % 16 == i))
    dt[...] = mm(pick, w_dt[...]).astype(BF)
    pick = one_hot((xpT.shape[0], 32 * cols), lambda i, j: (j % 32 < xp_cols) & (j // 32 * xp_cols + j % 32 == i))
    t = mm(pick, w_xp[...])
    xpT[...] = jnp.concatenate([t[:, r * wide:r * wide + xp_rows] for r in range(rows)], axis=1).astype(BF)
    sm = w_sm[...].astype(F32)
    chan = jnp.concatenate([sm[:, p * 128:p * 128 + share] for p in range(rows * cols)], axis=1)
    par[:taps + 2] = chan[:taps + 2]
    par[taps + 2:] = chan[taps + 2 + NS:taps + 3 + NS]
    neg = -jnp.exp(chan[taps + 2:taps + 2 + NS])
    an[...] = neg
    a2[...] = neg * log2e
    gains = jnp.concatenate([sm[taps + 3 + NS:taps + 5 + NS, p * 128:p * 128 + gshare] for p in range(rows * cols)], axis=1)
    gx[...] = gains[:1]
    gm[...] = gains[1:]


def unpack_other(masks, dims, me, *refs):
    out_rows, out_lanes, r_cols, cols = dims
    count = len(masks)
    bufs = refs[:count]
    fo, router, w_out, w_r = refs[count:]
    half = bufs[0].shape[1] - out_rows
    for buf, i, r, c in each_block(masks, bufs, me[0], me[1]):
        w_out[span(r, out_rows), span(c, 256)] = buf[i, :out_rows]
        w_r[pl.ds(pl.multiple_of(r * (2 * half), half), half), span(c, 128)] = buf[i, out_rows:, :128]
        w_r[pl.ds(pl.multiple_of(r * (2 * half) + half, half), half), span(c, 128)] = buf[i, out_rows:, 128:]
    wide = w_out[...]
    fo[...] = jnp.concatenate([wide[:, c * 256:c * 256 + out_lanes] for c in range(cols)], axis=1)
    pick = one_hot((128 * cols, router.shape[1]), lambda i, j: (i % 128 < r_cols) & (i // 128 * r_cols + i % 128 == j))
    router[...] = mm(w_r[...], pick)


def unpack_call(kernel, gathered, dims, outs, scratch):
    masks = [ms for ms, _ in gathered]
    bufs = [b for _, b in gathered]
    me = jnp.stack([lax.axis_index("row"), lax.axis_index("col")]).astype(jnp.int32)
    vmem = pl.BlockSpec(memory_space=pltpu.VMEM)
    return pl.pallas_call(
        functools.partial(kernel, masks, dims),
        in_specs=[pl.BlockSpec(memory_space=pltpu.SMEM)] + [vmem] * len(bufs), out_specs=[vmem] * len(outs), out_shape=outs,
        scratch_shapes=[pltpu.VMEM(s, BF) for s in scratch],
        compiler_params=pltpu.CompilerParams(vmem_limit_bytes=48 << 20),
        cost_estimate=pl.CostEstimate(flops=0, bytes_accessed=4 * sum(b.size for b in bufs), transcendentals=0),
    )(me, *bufs)


def grad_x_kernel(count, dims, s_ref, *refs):
    dt_rows, xp_cols, xp_rows, share, gshare, rows, cols = dims
    pairs = refs[:2 * count]
    gwd, gxp, gpar, gmix, gmoe = (refs[(2 + i) * count:(3 + i) * count] for i in range(5))
    out, w_dt, w_xp, w_sm = refs[7 * count:]
    k = pl.program_id(0)
    c = s_ref[0] ^ k
    n, lanes = out.shape[2] - 48, out.shape[3]
    wide = lanes - 128
    total = lambda vs: functools.reduce(lambda a, b: a + b, [v[...] for v in vs])

    @pl.when(k == 0)
    def _():
        g = total(gwd).astype(BF)
        put = one_hot((16 * rows, g.shape[0]), lambda j, i: (j % 16 < dt_rows) & (j // 16 * dt_rows + j % 16 == i))
        w_dt[...] = mm(put, g).astype(BF)
        g = total(gxp).astype(BF)
        put = one_hot((32 * cols, g.shape[0]), lambda j, i: (j % 32 < xp_cols) & (j // 32 * xp_cols + j % 32 == i))
        t = mm(put, g)
        gap = jnp.zeros((t.shape[0], wide - xp_rows), F32)
        w_xp[...] = jnp.concatenate([v for r in range(rows) for v in (t[:, r * xp_rows:(r + 1) * xp_rows], gap)], axis=1).astype(BF)
        w_sm[...] = jnp.zeros_like(w_sm)
        par, mix, moe = total(gpar), total(gmix), total(gmoe)
        m = par.shape[0]
        for p in range(rows * cols):
            w_sm[:m, p * 128:p * 128 + share] = par[:, p * share:(p + 1) * share]
            w_sm[m:m + 1, p * 128:p * 128 + gshare] = mix[:, p * gshare:(p + 1) * gshare]
            w_sm[m + 1:m + 2, p * 128:p * 128 + gshare] = moe[:, p * gshare:(p + 1) * gshare]
    g = mm(pairs[0][...], pairs[1][...], TN)
    for i in range(1, count):
        g = g + mm(pairs[2 * i][...], pairs[2 * i + 1][...], TN)
    out[0, :, :n] = g.astype(BF).reshape(rows, n, lanes)
    for r in range(rows):
        out[0, r, n:n + 16] = w_dt[r * 16:(r + 1) * 16, span(c, lanes)]
        out[0, r, n + 16:, :wide] = w_xp[span(c, 32), r * wide:(r + 1) * wide]
        out[0, r, n + 16:, wide:] = w_sm[:, span(r * cols + c, 128)].astype(BF)


def grad_x_blocks(pairs, smalls, dims, my_col):
    rows, cols = dims[-2:]
    count = len(pairs)
    n, m = pairs[0][0].shape
    lanes = pairs[0][1].shape[1] // cols
    flat = [v for p in pairs for v in p]
    specs = [pl.BlockSpec((n, m), lambda k, s: (0, 0)), pl.BlockSpec((n, lanes), lambda k, s: (0, s[0] ^ k))] * count
    more = [g[name] for name in ("dt", "xproj", "chan", "gain_mix", "gain_moe") for g in smalls]
    block = m // rows + 48
    return pl.pallas_call(
        functools.partial(grad_x_kernel, count, dims),
        grid_spec=pltpu.PrefetchScalarGridSpec(
            num_scalar_prefetch=1, grid=(cols,), in_specs=specs + [whole_spec(v) for v in more],
            out_specs=pl.BlockSpec((1, rows, block, lanes), lambda k, s: (k, 0, 0, 0)),
            scratch_shapes=[pltpu.VMEM((16 * rows, lanes * cols), BF), pltpu.VMEM((32 * cols, (lanes - 128) * rows), BF),
                            pltpu.VMEM((32, 128 * rows * cols), F32)]),
        out_shape=sds((cols, rows, block, lanes), BF),
        compiler_params=pltpu.CompilerParams(vmem_limit_bytes=48 << 20),
        cost_estimate=pl.CostEstimate(flops=2 * count * n * m * lanes * cols, bytes_accessed=1 << 23, transcendentals=0),
    )(my_col.reshape(1), *flat, *more)


def grad_out_kernel(count, r_cols, s_ref, *refs):
    pairs, routers, out = refs[:2 * count], refs[2 * count:3 * count], refs[3 * count]
    c = s_ref[0] ^ pl.program_id(0)
    rows = out.shape[1]
    g = mm(pairs[0][...], pairs[1][...], TN)
    r = routers[0][...]
    for i in range(1, count):
        g = g + mm(pairs[2 * i][...], pairs[2 * i + 1][...], TN)
        r = r + routers[i][...]
    n = g.shape[0] // rows
    out[0, :, :n] = g.astype(BF).reshape(rows, n, 256)
    put = one_hot((r.shape[1], 128), lambda i, j: (j < r_cols) & (i == c * r_cols + j))
    w = mm(r.astype(BF), put).astype(BF).reshape(rows, r.shape[0] // rows, 128)
    half = w.shape[1] // 2
    out[0, :, n:, :128] = w[:, :half]
    out[0, :, n:, 128:] = w[:, half:]


def grad_out_blocks(pairs, routers, rows, cols, r_cols, my_col):
    count = len(pairs)
    n, m = pairs[0][0].shape
    flat = [v for p in pairs for v in p]
    specs = [pl.BlockSpec((n, m), lambda k, s: (0, 0)), pl.BlockSpec((n, 256), lambda k, s: (0, k))] * count
    block = m // rows + routers[0].shape[0] // rows // 2
    return pl.pallas_call(
        functools.partial(grad_out_kernel, count, r_cols),
        grid_spec=pltpu.PrefetchScalarGridSpec(
            num_scalar_prefetch=1, grid=(cols,), in_specs=specs + [whole_spec(v) for v in routers],
            out_specs=pl.BlockSpec((1, rows, block, 256), lambda k, s: (k, 0, 0, 0))),
        out_shape=sds((cols, rows, block, 256), BF),
        compiler_params=pltpu.CompilerParams(vmem_limit_bytes=48 << 20),
        cost_estimate=pl.CostEstimate(flops=2 * count * n * m * 256 * cols, bytes_accessed=1 << 23, transcendentals=0),
    )(my_col.reshape(1), *flat, *routers)


def weights_part_kernel(cols, sets, lead, *refs):
    out = refs[-1]
    step = cols + 1
    total = None
    for s in range(sets):
        both, other = refs[s * step:s * step + cols], refs[s * step + cols][0]
        width = both[0].shape[2] // 2
        rows = jnp.concatenate([b[0, :, :width] if lead else b[0, :, width:] for b in both], axis=0)
        v = mm(rows, other, TN) if lead else mm(other, rows, TN)
        total = v if total is None else total + v
    out[0] = total


def expert_weights_part(sets, lead, d, f):
    cols = len(sets[0]) - 1
    experts, n, _ = sets[0][0].shape
    if len(sets) > 1 and len(sets) * cols > 8:
        return sum(expert_weights_part([s], lead, d, f) for s in sets)
    shape = (experts, d, f) if lead else (experts, f, d)
    return per_expert(functools.partial(weights_part_kernel, cols, len(sets), lead), [v for s in sets for v in s],
                      [sds(shape)], 2 * experts * cols * n * d * f * len(sets))[0]


def params_generic(w_in_x, w_in_z, conv_w, conv_b, w_xproj, w_dt, dt_bias, a_log, d_skip, w_out, gain_mix, gain_moe, w_router):
    rows, cols = lax.axis_size("row"), lax.axis_size("col")
    parts = rows * cols
    inner, width = w_in_x.shape[1] * cols, w_in_x.shape[0] * rows
    small = jnp.concatenate([conv_w, conv_b[None], dt_bias[None], a_log, d_skip[None],
                             jnp.concatenate([gain_mix, gain_moe])[None]], axis=0)
    flat = [w_xproj.reshape(-1), w_dt.reshape(-1), w_router.reshape(-1), small.reshape(-1)]
    sizes = [f.shape[0] for f in flat]
    lanes = w_in_x.shape[1]
    extra = -(-sum(sizes) // (16 * lanes)) * 16
    flat = jnp.pad(jnp.concatenate(flat), (0, extra * lanes - sum(sizes))).reshape(extra, lanes)
    here, out_rows, out_lanes = w_in_x.shape[0], w_out.shape[0], w_out.shape[1]
    wide = -(-out_lanes // 128) * 128
    first = gather_list(jnp.concatenate([w_in_x, flat], axis=0))
    full_x, rest = assemble(first, [((0, here, lanes), 0, put_block), ((here, extra, lanes), 1, put_pair)],
                            [(width, inner), (rows, cols, extra, lanes)])
    far_end = first[len(first) // 2 - 1][1]
    late_z, late_o, _ = lax.optimization_barrier((w_in_z, jnp.pad(w_out, ((0, 0), (0, wide - out_lanes))), far_end))
    (full_z,) = assemble(gather_list(late_z), [((0, here, lanes), 0, put_block)], [(width, inner)])
    (wide_out,) = assemble(gather_list(late_o), [((0, out_rows, wide), 0, put_block)], [(inner, cols * wide)])
    lane_of = jnp.arange(cols * wide, dtype=jnp.int32)
    narrow = jnp.where(lane_of % wide < out_lanes, lane_of // wide * out_lanes + lane_of % wide, -1)
    narrow = (narrow[:, None] == jnp.arange(width, dtype=jnp.int32)[None, :]).astype(BF)
    full_out = mm(wide_out, narrow).astype(BF)
    def whole(blocks):
        return blocks.transpose(0, 2, 1, 3).reshape(blocks.shape[0] * blocks.shape[2], -1)
    rest = rest.reshape(rows, cols, extra * lanes)
    cut = [0]
    for n in sizes:
        cut.append(cut[-1] + n)
    full_xpT = whole(rest[:, :, cut[0]:cut[1]].reshape((rows, cols) + w_xproj.shape)).T
    full_dt = whole(rest[:, :, cut[1]:cut[2]].reshape((rows, cols) + w_dt.shape))
    router_f = whole(rest[:, :, cut[2]:cut[3]].reshape((rows, cols) + w_router.shape)).astype(F32)
    small = rest[:, :, cut[3]:cut[4]].reshape((parts,) + small.shape).transpose(1, 0, 2).astype(F32)
    chan = small[:-1].reshape(-1, inner)
    taps = conv_w.shape[0]
    par = jnp.concatenate([chan[:taps + 2], chan[taps + 2 + NS:]], axis=0)
    a_neg = -jnp.exp(chan[taps + 2:taps + 2 + NS])
    a_two = a_neg * log2e
    gain_mix_f = small[-1, :, :gain_mix.shape[0]].reshape(1, width)
    gain_moe_f = small[-1, :, gain_mix.shape[0]:].reshape(1, width)
    return lambda done: (full_z, full_out, router_f, done), full_x, full_xpT, full_dt, par, a_neg, a_two, gain_mix_f, gain_moe_f


def params_tiled(w_in_x, w_in_z, conv_w, conv_b, w_xproj, w_dt, dt_bias, a_log, d_skip, w_out, gain_mix, gain_moe, w_router):
    rows, cols = lax.axis_size("row"), lax.axis_size("col")
    here, lanes = w_in_x.shape
    inner, width = lanes * cols, here * rows
    taps, share = conv_w.shape
    packed, other = pack_params(w_in_x, w_dt, w_xproj, conv_w, conv_b, dt_bias, a_log, d_skip, gain_mix, gain_moe, w_out, w_router)
    mine = gather_far(packed)
    late_z, other, _ = lax.optimization_barrier((w_in_z, other, mine))
    mine_z, mine_o = gather_far(late_z), gather_far(other)
    near = gather_plane(mine)
    mine_z, mine_o, _ = lax.optimization_barrier((mine_z, mine_o, near[-1]))
    near_z, near_o = gather_plane(mine_z), gather_plane(mine_o)
    first = gather_core(near)
    dims = (w_dt.shape[0], w_xproj.shape[1], w_xproj.shape[0], share, gain_mix.shape[0], taps, rows, cols)
    full_x, full_dt, full_xpT, par, a_neg, a_two, gx, gm = unpack_call(
        unpack_first, first, dims,
        [sds((width, inner), BF), sds((w_dt.shape[0] * rows, inner), BF), sds((w_xproj.shape[1] * cols, inner), BF),
         sds((taps + 3, inner)), sds((NS, inner)), sds((NS, inner)), sds((1, width)), sds((1, width))],
        [(16 * rows, inner), (32 * cols, (lanes - 128) * rows), (32, 128 * rows * cols)])

    def rest(done):
        z, o, done = lax.optimization_barrier((near_z, near_o, done))
        (full_z,) = assemble(gather_core(z), [((0, here, lanes), 0, put_block)], [(width, inner)])
        full_out, router_f = unpack_call(
            unpack_other, gather_core(o), (w_out.shape[0], w_out.shape[1], w_router.shape[1], cols),
            [sds((inner, width), BF), sds((width, w_router.shape[1] * cols))], [(inner, 256 * cols), (width, 128 * cols)])
        return full_z, full_out, router_f, done
    return rest, full_x, full_xpT, full_dt, par, a_neg, a_two, gx, gm


def grads_generic(nms, gateds, gs, total, w_in_x, w_in_z, w_xproj, w_dt, w_out, w_router, gain_mix, conv_w):
    rows, cols = lax.axis_size("row"), lax.axis_size("col")
    parts = rows * cols
    my_col = lax.axis_index("col")
    here, lanes = w_in_x.shape
    out_rows, out_lanes = w_out.shape
    wide = up_to(out_lanes, 128)
    share = conv_w.shape[1]
    sizes = [w_xproj.size, w_dt.size, w_router.size, (conv_w.shape[0] + 4 + NS) * share]
    extra = up_to(-(-sum(sizes) // lanes), 16)
    cut = [sum(sizes[:i]) for i in range(5)]
    grad_out = sum(mm(k[1], r["gm"], TN) for k, r in zip(zip(nms, gateds), gs)).astype(BF)
    grad_out_block = reduce_list([grad_out[:, k * wide:(k + 1) * wide].reshape(rows, out_rows, wide) for k in range(cols)])
    grad_out_block = grad_out_block[:, :out_lanes]
    grad_in_z = column_blocks([(k[0], r["gz"]) for k, r in zip(zip(nms, gateds), gs)], cols, my_col)
    grad_z_block = reduce_list([grad_in_z[k].reshape(rows, here, lanes) for k in range(cols)])
    grad_in_x = column_blocks([(k[0], r["gi"]) for k, r in zip(zip(nms, gateds), gs)], cols, my_col)

    def blocks(g, like):
        r, c = like.shape
        return g.astype(BF).reshape(rows, r, cols, c).transpose(0, 2, 1, 3).reshape(rows, cols, -1)
    gsmall = total["chan"].astype(BF)
    ggain = jnp.concatenate([total["gain_mix"].reshape(parts, 1, -1), total["gain_moe"].reshape(parts, 1, -1)], axis=2)
    gsmall = jnp.concatenate([gsmall.reshape(-1, parts, share).transpose(1, 0, 2), ggain.astype(BF)], axis=1)
    gflat = jnp.concatenate([blocks(total["xproj"].T, w_xproj), blocks(total["dt"], w_dt), blocks(total["router"], w_router),
                             gsmall.reshape(rows, cols, -1)], axis=2)
    gflat = jnp.pad(gflat, ((0, 0), (0, 0), (0, extra * lanes - sum(sizes)))).reshape(rows, cols, extra, lanes)
    done = reduce_list([jnp.concatenate([grad_in_x[k].reshape(rows, here, lanes),
                                         lax.dynamic_index_in_dim(gflat, my_col ^ k, 1, keepdims=False)], axis=1)
                        for k in range(cols)])
    grad_x_block = done[:here]
    done = done[here:].reshape(-1)
    sm = done[cut[3]:cut[4]].reshape(-1, share)
    gm = gain_mix.shape[0]
    small = (done[cut[0]:cut[1]].reshape(w_xproj.shape), done[cut[1]:cut[2]].reshape(w_dt.shape), sm[:-1], sm[-1, :gm], sm[-1, gm:],
             done[cut[2]:cut[3]].reshape(w_router.shape))
    return (grad_x_block, grad_z_block, grad_out_block), small


def on_device(tokens, w_in_x, w_in_z, conv_w, conv_b, w_xproj, w_dt, dt_bias, a_log, d_skip, w_out,
              gain_mix, gain_moe, w_router, w_up, w_down, routes, lengths, cotangent):
    rows, cols = lax.axis_size("row"), lax.axis_size("col")
    parts = rows * cols
    my_col = lax.axis_index("col")
    seqs, length, width = tokens.shape
    experts_here = w_up.shape[0]
    experts_all = experts_here * rows
    inner = w_in_x.shape[1] * cols
    count = seqs * length
    xp = w_xproj.shape[1] * cols
    share = inner // parts

    tiled = tiles_fit(w_in_x, w_xproj, w_out, conv_w)
    here, lanes = w_in_x.shape
    out_rows, out_lanes = w_out.shape
    wide = up_to(out_lanes, 128)
    taps = conv_w.shape[0]
    rest_of, full_x, full_xpT, full_dt, par, a_neg, a_two, gain_mix_f, gain_moe_f = (
        params_tiled if tiled else params_generic)(
            w_in_x, w_in_z, conv_w, conv_b, w_xproj, w_dt, dt_bias, a_log, d_skip, w_out, gain_mix, gain_moe, w_router)
    lane_of = jnp.arange(cols * wide, dtype=jnp.int32)
    shifted = jnp.where(lane_of % wide < out_lanes, (lane_of // wide ^ my_col) * out_lanes + lane_of % wide, -1)
    shifted = (jnp.arange(width, dtype=jnp.int32)[:, None] == shifted[None, :]).astype(BF)

    message = -(-experts_here * CAP // 8) * 8
    group = -(-rows * CAP // 16) * 16
    at = jnp.arange(experts_here * group, dtype=jnp.int32)
    there = at % group
    source = jnp.where(there < rows * CAP, there // CAP * message + at // group * CAP + there % CAP, -1)
    sort = (source[:, None] == jnp.arange(rows * message, dtype=jnp.int32)[None, :]).astype(BF)

    def mixer(x):
        nm, inner_x, u, dl, pT, ssm, starts = mixer_forward(x, gain_mix_f, full_x, full_xpT, full_dt, par, a_two, QB)
        return dict(x=x, nm=nm, inner=inner_x, u=u, dl=dl, pT=pT, ssm=ssm.reshape(length, inner), starts=starts)

    def router(k, route, n_live, grad):
        n_live = n_live.reshape(1)
        slots = rows * message
        z, gated, hidden, place, outgoing, probs, gate = one_call(
            functools.partial(route_kernel, CAP, experts_here, message),
            [k["x"], k["nm"], k["ssm"], full_z, full_out, gain_moe_f, router_f, route, grad],
            [sds((length, inner)), sds((length, inner), BF), sds((length, width)), sds((length, slots), BF),
             sds((slots, 2 * width), BF), sds((length, experts_all)), sds((length, 1))],
            [n_live], 6 * length * inner * width)
        kept = dict(k, z=z, gated=gated, hidden=hidden, place=place, probs=probs, gate=gate, route=route, n_live=n_live, cot=grad)
        return outgoing, kept

    def home(rows_out):
        return lax.all_to_all(rows_out, "row", split_axis=0, concat_axis=0, tiled=True)

    def arrive(got):
        return mm(sort, got).astype(BF).reshape(experts_here, group, 2 * width)

    def gather_cols(own):
        bufs = [own]
        for bit in bits_of("col")[::-1]:
            bufs = bufs + [swap(v, "col", bit) for v in bufs]
        return bufs

    def from_experts(bufs):
        for bit in bits_of("col"):
            half = len(bufs) // 2
            bufs = [(a.astype(F32) + swap(b, "col", bit).astype(F32)).astype(BF) for a, b in zip(bufs[:half], bufs[half:])]
        return mm(sort, bufs[0].reshape(experts_here * group, 2 * width), ((0,), (0,))).astype(BF)

    def unroute(k, back):
        mixed_out, gh, gs, gz, gm, g_router, g_moe = one_call(
            unroute_kernel,
            [back, k["place"], k["hidden"], k["probs"], k["gate"], k["route"], k["cot"], gain_moe_f, router_f, full_out, shifted,
             k["z"], k["ssm"]],
            [sds((length, width), BF), sds((length, width)), sds((length, inner)), sds((length, inner), BF),
             sds((length, cols * wide), BF), sds((width, experts_all)), sds((1, width))],
            [k["n_live"]], 6 * length * inner * width)
        return dict(mixed_out=mixed_out, gh=gh, gs=gs.reshape(k["u"].shape), gz=gz, gm=gm, router=g_router, gain_moe=g_moe)

    def unscan(k, gs):
        gi, g_xp, g_dt, g_chan = scan_backward(k["u"], k["dl"], gs, k["inner"], k["pT"], k["starts"], full_xpT, full_dt, par, a_neg)
        return dict(gi=gi, xproj=g_xp, dt=g_dt, chan=g_chan)

    def unproject(k, g):
        grad_tokens, g_mix = one_call(
            token_kernel, [g["gi"], g["gz"], full_x, full_z, k["x"], g["gh"], gain_mix_f], [sds((length, width)), sds((1, width))], (),
            4 * length * inner * width)
        return dict(tokens=grad_tokens, gain_mix=g_mix)

    after = lax.optimization_barrier
    ks, owns, last = [], [], None
    for s in range(seqs):
        x = tokens[s]
        if last is not None:
            x, last = after((x, last))
        k = mixer(x)
        if s == 0:
            full_z, full_out, router_f, k["ssm"] = rest_of(k["ssm"])
        if last is not None:
            own = arrive(home(last))
            k["ssm"], own = after((k["ssm"], own))
            owns.append(own)
        last, k = router(k, routes[s], lengths[s], cotangent[s])
        ks.append(k)
    got = home(last)
    sets, sent = [], []
    for s in range(seqs):
        if s == seqs - 1:
            if sets:
                got, outs = after((got, outs))
                sent[-1] = from_experts(outs)
            owns.append(arrive(got))
        bufs = gather_cols(owns[s])
        outs, more = expert_both(bufs, w_up, w_down)
        sets.append((bufs, more))
        sent.append(from_experts(outs))
    backs = [home(v) for v in sent]
    gs_ = []
    for s in range(seqs):
        g = unroute(ks[s], backs[s])
        gs_.append(g)
        if s + 1 < seqs:
            g["gs"], sent[s + 1] = after((g["gs"], sent[s + 1]))
            g.update(unscan(ks[s], g["gs"]))
            g["gi"], backs[s + 1] = after((g["gi"], backs[s + 1]))
    g = gs_[-1]
    nms, gateds = [k["nm"] for k in ks], [k["gated"] for k in ks]
    if tiled:
        out_parts = grad_out_blocks([(v, q["gm"]) for v, q in zip(gateds, gs_)], [q["router"] for q in gs_], rows, cols,
                                    w_router.shape[1], my_col)
        z_parts = column_blocks([(v, q["gz"]) for v, q in zip(nms, gs_)], cols, my_col)
        z_sums, first = reduce_core([z_parts[k].reshape(rows, here, lanes) for k in range(cols)],
                                    lambda give: unproject(ks[0], dict(gs_[0], gi=after((gs_[0]["gi"], give))[0])))
        out_sums, _ = reduce_core([out_parts[k] for k in range(cols)])
        z_own, z_give = reduce_plane_give(z_sums)
        out_own, out_give = reduce_plane_give(out_sums)
        g["gs"], z_give, out_give = after((g["gs"], z_give, out_give))
        g.update(unscan(ks[-1], g["gs"]))
        z_total, _ = reduce_plane(z_own, z_give)
        out_total, _ = reduce_plane(out_own, out_give)
        z_total, out_total, g["gi"] = after((z_total, out_total, g["gi"]))
        z_done, _ = reduce_far(z_total)
        out_done, _ = reduce_far(out_total)
        gs_[0].update(first)
        for s in range(1, seqs - 1):
            gs_[s].update(unproject(ks[s], gs_[s]))
        dims = (w_dt.shape[0], w_xproj.shape[1], w_xproj.shape[0], conv_w.shape[1], gain_mix.shape[0], rows, cols)
        g.update(unproject(ks[-1], g))
        x_parts = grad_x_blocks([(v, q["gi"]) for v, q in zip(nms, gs_)], gs_, dims, my_col)

        def weights(lead):
            def work(give):
                ins, _ = after(([b + [m[1 if lead else 0]] for b, m in sets], give))
                return expert_weights_part(ins, lead, width, w_up.shape[2])
            return work
        x_sums, _ = reduce_core([x_parts[k] for k in range(cols)])
        x_own, x_give = reduce_plane_give(x_sums)
        x_total, grad_w_up = reduce_plane(x_own, x_give, weights(True))
        done, grad_w_down = reduce_far(x_total, weights(False))
        xp = up_to(w_xproj.shape[0], 128)
        sm = done[here + 16:, xp:]
        share = conv_w.shape[1]
        gm = gain_mix.shape[0]
        chan = sm[:taps + 3 + NS, :share]
        half = w_router.shape[0] // 2
        router_done = jnp.concatenate([out_done[out_rows:, :w_router.shape[1]], out_done[out_rows:, 128:128 + w_router.shape[1]]], axis=0)
        small = (done[here + 16:here + 16 + w_xproj.shape[1], :w_xproj.shape[0]].T, done[here:here + w_dt.shape[0]], chan,
                 sm[taps + 3 + NS, :gm], sm[taps + 4 + NS, :gm], router_done)
        blocks = (done[:here], z_done, out_done[:out_rows, :out_lanes])
    else:
        g.update(unscan(ks[-1], g["gs"]))
        for k, q in zip(ks, gs_):
            q.update(unproject(k, q))
        names = ("xproj", "dt", "chan", "gain_mix", "gain_moe", "router")
        total = {n: sum(q[n] for q in gs_) for n in names}
        blocks, small = grads_generic(nms, gateds, gs_, total, w_in_x, w_in_z, w_xproj, w_dt, w_out, w_router, gain_mix, conv_w)
        grad_w_up = expert_weights_part([b + [m[1]] for b, m in sets], True, width, w_up.shape[2])
        grad_w_down = expert_weights_part([b + [m[0]] for b, m in sets], False, width, w_up.shape[2])
    g_xproj, g_dt, chan, g_mix, g_moe, g_router = small
    return (
        jnp.stack([q["mixed_out"] for q in gs_]),
        jnp.stack([q["tokens"] for q in gs_]),
        blocks[0],
        blocks[1],
        chan[:taps],
        chan[taps],
        g_xproj,
        g_dt,
        chan[taps + 1],
        chan[taps + 2:taps + 2 + NS],
        chan[taps + 2 + NS],
        blocks[2],
        g_mix,
        g_moe,
        g_router,
        grad_w_up,
        grad_w_down,
    )


def solution(mesh):
    tok = P(("row", "col"), None, None)
    mat = P("row", "col")
    vec = P(("row", "col"))
    chan = P(None, ("row", "col"))
    up, down = P("row", None, "col"), P("row", "col", None)
    return jax.shard_map(
        on_device,
        mesh=mesh,
        in_specs=(tok, mat, mat, chan, vec, mat, mat, vec, chan, vec, mat, vec, vec, mat, up, down, tok, vec, tok),
        out_specs=(tok, tok, mat, mat, chan, vec, mat, mat, vec, chan, vec, mat, vec, vec, mat, up, down),
        check_vma=False,
    )
```

time: 643 us -> 592 us (0.921)
  Pallas kernels: 170 us -> 264 us
  matrix products: 76.9 us -> 8.85 us
  local copies, waits for them, and re-layouts: 88.5 us -> 57.7 us
  waiting for transfers between devices: 166 us -> 139 us
  other arithmetic: 52.1 us -> 33.9 us
    pallas_call x4 -> x15, Pallas kernels: 112 us -> 208 us  [the longest x2 89.8 us: scan_backward(): pl.pallas_call(functools.partial(scan_back_kernel, T, Q, Q2, R), grid=(C,...]
    dot_general x43 -> x4, matrix products: 76.9 us -> 8.85 us  [mm(): lax.dot_general(a, b, (dims, ((), ())), preferred_element_type=F32, **kw)]
    ppermute x57, waiting for transfers between devices: 125 us -> 101 us  [swap(): return lax.ppermute(x, axis, [(i, i ^ bit) for i in range(n)])]
    ppermute x6, waiting for transfers between devices: 24.4 us -> 4.14 us  [exchange(): return lax.ppermute(x, ('row', 'col'), pairs)]
    reshape x26 -> x0, local copies, waits for them, and re-layouts: 17.4 us -> none  [the longest x9 6.49 us: blocks(): g.astype(BF).reshape(rows, r, cols, c).transpose(0, 2, 1, 3)]
    all_to_all x4, waiting for transfers between devices: 17.1 us -> 33.7 us  [home(): lax.all_to_all(rows_out, 'row', split_axis=0, concat_axis=0, tiled=True)]
    reduce_sum x13 -> x0, other arithmetic: 10.8 us -> none  [the longest x1 3.86 us: backward(): jnp.sum(grad_conv * padded[i:i + length], axis=0)]
    slice x34 -> x11, local copies, waits for them, and re-layouts: 16.7 us -> 9.05 us  [the longest x1 1.63 us: on_device(): out_sums, _ = reduce_core([out_parts[k] for k in range(cols)])]
  transfers between devices with their start and end apart: 67 -> 67, of which waited for: 24 -> 18; matrix products, arithmetic and copies ran while one was open for 18% -> 7% of each run, Pallas kernels for 12% -> 38%
where the time goes in v2:
time: 592 us; the launch traced here: 583 us
  Pallas kernels  264 us (45%)
  waiting for transfers between devices  139 us (23%)
  starting transfers between devices  77.9 us (13%)
  local copies, waits for them, and re-layouts  57.7 us (10%)
  other arithmetic  33.9 us (6%)
  matrix products  8.85 us (1%)
    ppermute x57, waiting for transfers between devices, swap(): return lax.ppermute(x, axis, [(i, i ^ bit) for i in range(n)])  101 us
    pallas_call x2, Pallas kernels, scan_backward(): pl.pallas_call(functools.partial(scan_back_kernel, T, Q, Q2, R), grid=(C,...  89.8 us
    pallas_call x6, Pallas kernels, one_call(): pl.pallas_call(kernel, in_specs=[smem] * len(scalars) + [vmem] * len(ins)...  56.7 us
    pallas_call x4, Pallas kernels, per_expert(): pl.pallas_call(kernel, grid=(ins[0].shape[0],), in_specs=[tok(a) for a in...  51.1 us
    ppermute x57, starting transfers between devices, swap(): return lax.ppermute(x, axis, [(i, i ^ bit) for i in range(n)])  51 us
    pallas_call x2, Pallas kernels, mixer_forward(): pl.pallas_call(functools.partial(mixer_kernel, T, Q, R), grid=(C,), in_sp...  42.3 us
    unnamed x160, local copies, waits for them, and re-layouts  34.3 us
    all_to_all x4, waiting for transfers between devices, home(): lax.all_to_all(rows_out, 'row', split_axis=0, concat_axis=0, tiled=True)  33.7 us
  transfers between devices with their start and end apart: 67, of which 18 were waited for; matrix products, arithmetic and copies ran while one was open for 7% of the time, Pallas kernels for 38%

profile of v2, /device:TPU:0, one launch (start us, length us, event | category | flops | bytes accessed | tf_op | source)
XLA Modules:
  0.0 583.4 jit_solution(8274732979837992170)
XLA Ops:
  5.3 5.0 collective-permute-start.2
  11.0 3.6 collective-permute-done.2
  14.5 5.3 collective-permute-done.1
  26.9 4.0 collective-permute-done.12
  34.9 5.0 collective-permute-done.10
  43.8 2.9 collective-permute-done.14
  57.6 2.5 shard_map.315
  61.3 21.2 %shard_map.316 = (bf16[320,768]{1,0:T(8,128)(2,1)S(1)}, f32[328,1536]{1,0:T(8,128)}, f32[5,8,8,1536]{3,2,1,0:T(8,128)S(1)}, f32[5,8,8,1536]{3,2,1,0:T(8,128)S(1)...) custom-call(bf16[320,768]{1,0:T(8,128)(2,1)S(1)} %get-tuple-element.359.x_ref, ...), custom_call_target="tpu_custom_call" | custom-call | flops 40000000000 | bytes 7864320 | tf_op jit(solution)/shard_map/pallas_call | solution.py:133
  91.0 2.9 slice_bitcast_fusion
  96.9 3.0 shard_map.318
  100.6 10.0 %shard_map.319 = (f32[320,1536]{1,0:T(8,128)}, bf16[320,1536]{1,0:T(8,128)(2,1)}, f32[320,768]{1,0:T(8,128)}, bf16[320,448]{1,0:T(8,128)(2,1)}, bf16[448,1536]{1...) custom-call(s32[1]{0:T(128)} %get-tuple-element.379.live_ref, bf16[320,768]{1,0:T(8,128)(2,1)} %copy-done.3, ...), custom_call_target="tpu_custom_call" | custom-call | flops 2264924160 | bytes 14390784 | tf_op jit(solution)/shard_map/pallas_call | solution.py:293
  110.6 4.9 all-to-all-start
  115.6 21.1 %shard_map.320 = (bf16[320,768]{1,0:T(8,128)(2,1)S(1)}, f32[328,1536]{1,0:T(8,128)}, f32[5,8,8,1536]{3,2,1,0:T(8,128)S(1)}, f32[5,8,8,1536]{3,2,1,0:T(8,128)S(1)...) custom-call(bf16[320,768]{1,0:T(8,128)(2,1)S(1)} %get-tuple-element.189.x_ref, ...), custom_call_target="tpu_custom_call" | custom-call | flops 40000000000 | bytes 7864320 | tf_op jit(solution)/shard_map/pallas_call | solution.py:133
  140.9 7.6 %all-to-all-done = bf16[8,56,1536]{2,1,0:T(8,128)(2,1)S(1)} async-done(((bf16[8,56,1536]{2,1,0:T(8,128)(2,1)}), bf16[8,56,1536]{2,1,0:T(8,128)(2,1)S(1)}, u32[]{:S(2)}, u32[]{:S(2)}) %all-to-all-start) | async-done | bytes 1376288 | tf_op jit(solution)/shard_map/all_to_all | solution.py:1042
  154.2 10.0 %shard_map.321 = (f32[320,1536]{1,0:T(8,128)}, bf16[320,1536]{1,0:T(8,128)(2,1)}, f32[320,768]{1,0:T(8,128)}, bf16[320,448]{1,0:T(8,128)(2,1)}, bf16[448,1536]{1...) custom-call(s32[1]{0:T(128)} %get-tuple-element.380.live_ref, bf16[320,768]{1,0:T(8,128)(2,1)} %copy-done.2, ...), custom_call_target="tpu_custom_call" | custom-call | flops 2264924160 | bytes 14390784 | tf_op jit(solution)/shard_map/pallas_call | solution.py:293
  164.2 4.5 all-to-all-start.1
  168.8 14.3 %collective-permute-done.30.refs_1_ = bf16[4,112,1536]{2,1,0:T(8,128)(2,1)} collective-permute-done((bf16[4,112,1536]{2,1,0:T(8,128)(2,1)S(1)}, bf16[4,112,1536]{2,1,0:T(8,128)(2,1)}, u32[]{:S(2)}, u32[]{:S(2)}) %collective-permute-start.30) | collective-permute-done | bytes 1376288 | tf_op jit(solution)/shard_map/ppermute | solution.py:389
  183.1 3.3 collective-permute-done.32.refs_3_
  187.5 13.7 %shard_map.322 = (bf16[4,112,1536]{2,1,0:T(8,128)(2,1)}, bf16[4,112,1536]{2,1,0:T(8,128)(2,1)}, bf16[4,112,1536]{2,1,0:T(8,128)(2,1)}, bf16[4,112,1536]{2,1,0:T(...) custom-call(bf16[4,112,1536]{2,1,0:T(8,128)(2,1)} %bitcast.178, ...), custom_call_target="tpu_custom_call" | custom-call | flops 8455716864 | bytes 25952256 | tf_op jit(solution)/shard_map/pallas_call | solution.py:611
  205.7 30.2 %collective-permute-done.36.refs_1_.refs_6_ = bf16[4,112,1536]{2,1,0:T(8,128)(2,1)S(1)} collective-permute-done((bf16[4,112,1536]{2,1,0:T(8,128)(2,1)S(1)}, bf16[4,112,1536]{2,1,0:T(8,128)(2,1)S(1)}, u32[]{:S(2)}, u32[]{:S(2)}) %collective-permute-start.36) | collective-permute-done | bytes 1376288 | tf_op jit(solution)/shard_map/ppermute | solution.py:389
  242.1 13.9 %shard_map.324 = (bf16[4,112,1536]{2,1,0:T(8,128)(2,1)}, bf16[4,112,1536]{2,1,0:T(8,128)(2,1)}, bf16[4,112,1536]{2,1,0:T(8,128)(2,1)}, bf16[4,112,1536]{2,1,0:T(...) custom-call(bf16[4,112,1536]{2,1,0:T(8,128)(2,1)} %bitcast.183, ...), custom_call_target="tpu_custom_call" | custom-call | flops 8455716864 | bytes 25952256 | tf_op jit(solution)/shard_map/pallas_call | solution.py:611
  256.2 14.1 %collective-permute-done.35 = bf16[4,112,1536]{2,1,0:T(8,128)(2,1)} collective-permute-done((bf16[4,112,1536]{2,1,0:T(8,128)(2,1)}, bf16[4,112,1536]{2,1,0:T(8,128)(2,1)}, u32[]{:S(2)}, u32[]{:S(2)}) %collective-permute-start.35) | collective-permute-done | bytes 1376288 | tf_op jit(solution)/shard_map/ppermute | solution.py:389
  274.7 5.1 all-to-all-start.2
  279.8 2.8 add_convert_fusion.1
  285.9 26.0 %all-to-all-done.2 = bf16[8,56,1536]{2,1,0:T(8,128)(2,1)S(1)} async-done(((bf16[8,56,1536]{2,1,0:T(8,128)(2,1)}), bf16[8,56,1536]{2,1,0:T(8,128)(2,1)S(1)}, u32[]{:S(2)}, u32[]{:S(2)}) %all-to-all-start.2) | async-done | bytes 1376288 | tf_op jit(solution)/shard_map/all_to_all | solution.py:1042
  313.0 12.1 %shard_map.323 = (bf16[320,768]{1,0:T(8,128)(2,1)}, f32[320,768]{1,0:T(8,128)}, f32[320,1536]{1,0:T(8,128)}, bf16[320,1536]{1,0:T(8,128)(2,1)}, bf16[320,1024]{1...) custom-call(s32[1]{0:T(128)} %get-tuple-element.379.live_ref, bf16[448,1536]{1,0:T(8,128)(2,1)} %bitcast.174, ...), custom_call_target="tpu_custom_call" | custom-call | flops 2264924160 | bytes 16818688 | tf_op jit(solution)/shard_map/pallas_call | solution.py:293
  329.5 4.0 all-to-all-start.3
  333.5 44.9 %shard_map.325 = (bf16[320,1536]{1,0:T(8,128)(2,1)}, f32[80,1536]{1,0:T(8,128)S(1)}, f32[48,1536]{1,0:T(8,128)S(1)}, f32[23,1536]{1,0:T(8,128)S(1)}) custom-call(f32[5,8,8,1536]{3,2,1,0:T(8,128)} %copy-done.38, f32[5,8,8,1536]{3,2,1,0:T(8,128)} %copy-done.39, f32[5,8,8,1536]{3,2,1,0:T(8,128)} %bitcast.228, f32[328,1536]{1,0:T(8,128)} %get-tuple-element.219.in_ref, ...), custom_call_target="tpu_custom_call" | custom-call | flops 80000000000 | bytes 7864320 | tf_op jit(solution)/shard_map/pallas_call | solution.py:277
  379.5 12.1 %shard_map.326 = (bf16[320,768]{1,0:T(8,128)(2,1)}, f32[320,768]{1,0:T(8,128)}, f32[320,1536]{1,0:T(8,128)}, bf16[320,1536]{1,0:T(8,128)(2,1)}, bf16[320,1024]{1...) custom-call(s32[1]{0:T(128)} %get-tuple-element.380.live_ref, bf16[448,1536]{1,0:T(8,128)(2,1)} %bitcast.175, ...), custom_call_target="tpu_custom_call" | custom-call | flops 2264924160 | bytes 16818688 | tf_op jit(solution)/shard_map/pallas_call | solution.py:293
  392.9 4.0 shard_map.327
  400.3 5.9 %shard_map.329 = bf16[4,8,240,256]{3,2,1,0:T(8,128)(2,1)} custom-call(s32[1]{0:T(128)} %bitcast.3.s_ref, bf16[320,1536]{1,0:T(8,128)(2,1)S(1)} %copy-done.10, bf16[320,1024]{1,0:T(8,128)(2,1)S(1)} %copy-done.14, bf16[320,1536]{1,0:T(8,128)(2,1)S(1)} %copy-done.11, bf16[320,1024]{1,0:T(8,128)(2,1)S(1)} %copy-done.15, f32[768,32]{1,0:T(8,128)S(1)} %copy-done.20, ...), custom_call_target="tpu_custom_call" | custom-call | flops 2013265920 | bytes 8388608 | tf_op jit(solution)/shard_map/pallas_call | solution.py:846
  409.3 6.2 %shard_map.328 = (f32[320,768]{1,0:T(8,128)}, f32[1,768]{1,0:T(1,128)}) custom-call(bf16[320,1536]{1,0:T(8,128)(2,1)} %get-tuple-element.234.gi_ref.refs_1_, bf16[320,1536]{1,0:T(8,128)(2,1)} %get-tuple-element.231.refs_1_.gz_ref, bf16[768,1536]{1,0:T(8,128)(2,1)} %get-tuple-element.164.wx_ref, bf16[768,1536]{1,0:T(8,128)(2,1)} %copy-done, ...), custom_call_target="tpu_custom_call" | custom-call | flops 1509949440 | bytes 9148416 | tf_op jit(solution)/shard_map/pallas_call | solution.py:293
  430.3 2.9 collective-permute-start.46
  433.8 2.9 collective-permute-start.49
  437.3 4.1 collective-permute-done.46
  444.2 45.0 %shard_map.330 = (bf16[320,1536]{1,0:T(8,128)(2,1)}, f32[80,1536]{1,0:T(8,128)S(1)}, f32[48,1536]{1,0:T(8,128)S(1)}, f32[23,1536]{1,0:T(8,128)S(1)}) custom-call(f32[5,8,8,1536]{3,2,1,0:T(8,128)} %copy-done.36, f32[5,8,8,1536]{3,2,1,0:T(8,128)} %copy-done.37, f32[5,8,8,1536]{3,2,1,0:T(8,128)} %bitcast.227, f32[328,1536]{1,0:T(8,128)} %get-tuple-element.256.in_ref, ...), custom_call_target="tpu_custom_call" | custom-call | flops 80000000000 | bytes 7864320 | tf_op jit(solution)/shard_map/pallas_call | solution.py:277
  495.1 2.6 fusion.2
  497.7 6.3 %shard_map.331 = (f32[320,768]{1,0:T(8,128)}, f32[1,768]{1,0:T(1,128)}) custom-call(bf16[320,1536]{1,0:T(8,128)(2,1)} %get-tuple-element.260.gi_ref.refs_3_, bf16[320,1536]{1,0:T(8,128)(2,1)} %get-tuple-element.232.refs_3_.gz_ref, bf16[768,1536]{1,0:T(8,128)(2,1)} %get-tuple-element.164.wx_ref, bf16[768,1536]{1,0:T(8,128)(2,1)} %copy-done, ...), custom_call_target="tpu_custom_call" | custom-call | flops 1509949440 | bytes 9148416 | tf_op jit(solution)/shard_map/pallas_call | solution.py:293
  504.7 5.6 shard_map.332
  515.8 3.4 collective-permute-start.59
  520.3 3.4 collective-permute-start.62
  523.7 2.8 pad_maximum_fusion.1
  526.4 5.5 collective-permute-done.58
  532.6 4.8 collective-permute-done.61
  546.0 11.8 %shard_map.333 = f32[4,768,768]{2,1,0:T(8,128)} custom-call(bf16[4,112,1536]{2,1,0:T(8,128)(2,1)} %bitcast.179, bf16[4,112,1536]{2,1,0:T(8,128)(2,1)} %collective-permute-done.30.refs_1_, bf16[4,112,1536]{2,1,0:T(8,128)(2,1)} %copy-done.53, bf16[4,112,1536]{2,1,0:T(8,128)(2,1)} %copy-done.54, bf16[4,448,768]{2,1,0:T(8,128)(2,1)} %get-tuple-element.279.refs_4_, ...), custom_call_target="tpu_custom_call" | custom-call | flops 4227858432 | bytes 25952256 | tf_op jit(solution)/shard_map/pallas_call | solution.py:611
  557.8 3.7 collective-permute-done.52
  562.9 2.9 collective-permute-start.55
  567.2 11.8 %shard_map.334 = f32[4,768,768]{2,1,0:T(8,128)} custom-call(bf16[4,112,1536]{2,1,0:T(8,128)(2,1)} %bitcast.180, bf16[4,112,1536]{2,1,0:T(8,128)(2,1)} %collective-permute-done.30.refs_1_, bf16[4,112,1536]{2,1,0:T(8,128)(2,1)} %copy-done.53, bf16[4,112,1536]{2,1,0:T(8,128)(2,1)} %copy-done.54, bf16[4,448,768]{2,1,0:T(8,128)(2,1)} %get-tuple-element.294.refs_4_, ...), custom_call_target="tpu_custom_call" | custom-call | flops 4227858432 | bytes 25952256 | tf_op jit(solution)/shard_map/pallas_call | solution.py:611
  (329 shorter events, 136.3 us)
Async XLA Ops:
  5.3 9.2 %collective-permute-start.2 = (bf16[144,384]{1,0:T(8,128)(2,1)}, bf16[144,384]{1,0:T(8,128)(2,1)S(1)}, u32[]{:S(2)}, u32[]{:S(2)}) collective-permute-start(bf16[144,384]{1,0:T(8,128)(2,1)} %get-tuple-element.162), channel_id=1, source_target_pairs={{0,24},{4,28},{8,16},{12,20},{16,8},{20,12},{24,0},{28,4},{1,25},{... | collective-permute-start | bytes 331784 | tf_op jit(solution)/shard_map/ppermute | solution.py:389
  10.3 9.5 %collective-permute-start.1 = (bf16[144,384]{1,0:T(8,128)(2,1)}, bf16[144,384]{1,0:T(8,128)(2,1)S(1)}, u32[]{:S(2)}, u32[]{:S(2)}) collective-permute-start(bf16[144,384]{1,0:T(8,128)(2,1)} %get-tuple-element.162), channel_id=1, source_target_pairs={{0,16},{4,20},{8,24},{12,28},{16,0},{20,4},{24,8},{28,12},{1,17},{... | collective-permute-start | bytes 331784 | tf_op jit(solution)/shard_map/ppermute | solution.py:389
  10.3 9.5 %collective-permute-start = (bf16[144,384]{1,0:T(8,128)(2,1)}, bf16[144,384]{1,0:T(8,128)(2,1)S(1)}, u32[]{:S(2)}, u32[]{:S(2)}) collective-permute-start(bf16[144,384]{1,0:T(8,128)(2,1)} %get-tuple-element.162), channel_id=1, source_target_pairs={{0,8},{4,12},{8,0},{12,4},{16,24},{20,28},{24,16},{28,20},{1,9},{5... | collective-permute-start | bytes 331784 | tf_op jit(solution)/shard_map/ppermute | solution.py:389
  20.8 25.9 %collective-permute-start.3 = (bf16[4,144,384]{2,1,0:T(8,128)(2,1)S(1)}, bf16[4,144,384]{2,1,0:T(8,128)(2,1)S(1)}, u32[]{:S(2)}, u32[]{:S(2)}) collective-permute-start(bf16[4,144,384]{2,1,0:T(8,128)(2,1)S(1)} %pad_maximum_fusion.6.refs_0_), channel_id=1, source_target_pairs={{0,4},{4,0},{8,12},{12,8},{16,20},{20,16},{24,28},{28,24},{1,5},{5... | collective-permute-start | bytes 1327112 | tf_op jit(solution)/shard_map/ppermute | solution.py:389
  22.4 24.8 %collective-permute-start.4 = (bf16[4,144,384]{2,1,0:T(8,128)(2,1)S(1)}, bf16[4,144,384]{2,1,0:T(8,128)(2,1)S(1)}, u32[]{:S(2)}, u32[]{:S(2)}) collective-permute-start(bf16[4,144,384]{2,1,0:T(8,128)(2,1)S(1)} %pad_maximum_fusion.6.refs_0_), channel_id=1, source_target_pairs={{0,2},{1,3},{2,0},{3,1},{4,6},{5,7},{6,4},{7,5},{8,10},{9,11},{10,... | collective-permute-start | bytes 1327112 | tf_op jit(solution)/shard_map/ppermute | solution.py:389
  23.9 23.4 %collective-permute-start.5 = (bf16[4,144,384]{2,1,0:T(8,128)(2,1)S(1)}, bf16[4,144,384]{2,1,0:T(8,128)(2,1)S(1)}, u32[]{:S(2)}, u32[]{:S(2)}) collective-permute-start(bf16[4,144,384]{2,1,0:T(8,128)(2,1)S(1)} %pad_maximum_fusion.6.refs_0_), channel_id=1, source_target_pairs={{0,6},{1,7},{2,4},{3,5},{4,2},{5,3},{6,0},{7,1},{8,14},{9,15},{10,... | collective-permute-start | bytes 1327112 | tf_op jit(solution)/shard_map/ppermute | solution.py:405
  26.9 8.0 %collective-permute-start.11 = (bf16[96,384]{1,0:T(8,128)(2,1)}, bf16[96,384]{1,0:T(8,128)(2,1)S(1)}, u32[]{:S(2)}, u32[]{:S(2)}) collective-permute-start(bf16[96,384]{1,0:T(8,128)(2,1)} %param.21), channel_id=1, source_target_pairs={{0,16},{4,20},{8,24},{12,28},{16,0},{20,4},{24,8},{28,12},{1,17},{... | collective-permute-start | bytes 221192 | tf_op jit(solution)/shard_map/ppermute | solution.py:389
  30.9 9.7 %collective-permute-start.15 = (bf16[240,256]{1,0:T(8,128)(2,1)}, bf16[240,256]{1,0:T(8,128)(2,1)S(1)}, u32[]{:S(2)}, u32[]{:S(2)}) collective-permute-start(bf16[240,256]{1,0:T(8,128)(2,1)} %get-tuple-element.172), channel_id=1, source_target_pairs={{0,24},{4,28},{8,16},{12,20},{16,8},{20,12},{24,0},{28,4},{1,25},{... | collective-permute-start | bytes 368648 | tf_op jit(solution)/shard_map/ppermute | solution.py:389
  48.7 12.1 %collective-permute-start.16 = (bf16[4,96,384]{2,1,0:T(8,128)(2,1)S(1)}, bf16[4,96,384]{2,1,0:T(8,128)(2,1)S(1)}, u32[]{:S(2)}, u32[]{:S(2)}) collective-permute-start(bf16[4,96,384]{2,1,0:T(8,128)(2,1)S(1)} %pad_maximum_fusion.7.refs_1_), channel_id=1, source_target_pairs={{0,4},{4,0},{8,12},{12,8},{16,20},{20,16},{24,28},{28,24},{1,5},{5... | collective-permute-start | bytes 884744 | tf_op jit(solution)/shard_map/ppermute | solution.py:389
  50.5 36.9 %collective-permute-start.17 = (bf16[4,96,384]{2,1,0:T(8,128)(2,1)S(1)}, bf16[4,96,384]{2,1,0:T(8,128)(2,1)}, u32[]{:S(2)}, u32[]{:S(2)}) collective-permute-start(bf16[4,96,384]{2,1,0:T(8,128)(2,1)S(1)} %pad_maximum_fusion.7.refs_1_), channel_id=1, source_target_pairs={{0,2},{1,3},{2,0},{3,1},{4,6},{5,7},{6,4},{7,5},{8,10},{9,11},{10,... | collective-permute-start | bytes 884744 | tf_op jit(solution)/shard_map/ppermute | solution.py:389
  52.0 35.4 %collective-permute-start.18 = (bf16[4,96,384]{2,1,0:T(8,128)(2,1)S(1)}, bf16[4,96,384]{2,1,0:T(8,128)(2,1)}, u32[]{:S(2)}, u32[]{:S(2)}) collective-permute-start(bf16[4,96,384]{2,1,0:T(8,128)(2,1)S(1)} %pad_maximum_fusion.7.refs_1_), channel_id=1, source_target_pairs={{0,6},{1,7},{2,4},{3,5},{4,2},{5,3},{6,0},{7,1},{8,14},{9,15},{10,... | collective-permute-start | bytes 884744 | tf_op jit(solution)/shard_map/ppermute | solution.py:405
  52.5 34.9 %collective-permute-start.19 = (bf16[4,240,256]{2,1,0:T(8,128)(2,1)S(1)}, bf16[4,240,256]{2,1,0:T(8,128)(2,1)S(1)}, u32[]{:S(2)}, u32[]{:S(2)}) collective-permute-start(bf16[4,240,256]{2,1,0:T(8,128)(2,1)S(1)} %pad_maximum_fusion.5.refs_0_), channel_id=1, source_target_pairs={{0,4},{4,0},{8,12},{12,8},{16,20},{20,16},{24,28},{28,24},{1,5},{5... | collective-permute-start | bytes 1474568 | tf_op jit(solution)/shard_map/ppermute | solution.py:389
  54.0 33.4 %collective-permute-start.20 = (bf16[4,240,256]{2,1,0:T(8,128)(2,1)S(1)}, bf16[4,240,256]{2,1,0:T(8,128)(2,1)S(1)}, u32[]{:S(2)}, u32[]{:S(2)}) collective-permute-start(bf16[4,240,256]{2,1,0:T(8,128)(2,1)S(1)} %pad_maximum_fusion.5.refs_0_), channel_id=1, source_target_pairs={{0,2},{1,3},{2,0},{3,1},{4,6},{5,7},{6,4},{7,5},{8,10},{9,11},{10,... | collective-permute-start | bytes 1474568 | tf_op jit(solution)/shard_map/ppermute | solution.py:389
  60.8 26.6 %collective-permute-start.21 = (bf16[4,240,256]{2,1,0:T(8,128)(2,1)S(1)}, bf16[4,240,256]{2,1,0:T(8,128)(2,1)S(1)}, u32[]{:S(2)}, u32[]{:S(2)}) collective-permute-start(bf16[4,240,256]{2,1,0:T(8,128)(2,1)S(1)} %pad_maximum_fusion.5.refs_0_), channel_id=1, source_target_pairs={{0,6},{1,7},{2,4},{3,5},{4,2},{5,3},{6,0},{7,1},{8,14},{9,15},{10,... | collective-permute-start | bytes 1474568 | tf_op jit(solution)/shard_map/ppermute | solution.py:405
  110.6 37.9 %all-to-all-start = ((bf16[8,56,1536]{2,1,0:T(8,128)(2,1)}), bf16[8,56,1536]{2,1,0:T(8,128)(2,1)S(1)}, u32[]{:S(2)}, u32[]{:S(2)}) async-start(bf16[8,56,1536]{2,1,0:T(8,128)(2,1)} %bitcast.198), calls=%async_computation | async-start | bytes 2752512 | tf_op jit(solution)/shard_map/all_to_all | solution.py:1042
  151.8 31.2 %collective-permute-start.30 = (bf16[4,112,1536]{2,1,0:T(8,128)(2,1)S(1)}, bf16[4,112,1536]{2,1,0:T(8,128)(2,1)}, u32[]{:S(2)}, u32[]{:S(2)}) collective-permute-start(bf16[4,112,1536]{2,1,0:T(8,128)(2,1)S(1)} %bitcast.176), channel_id=1, source_target_pairs={{0,2},{1,3},{2,0},{3,1},{4,6},{5,7},{6,4},{7,5},{8,10},{9,11},{10,... | collective-permute-start | bytes 4128776 | tf_op jit(solution)/shard_map/ppermute | solution.py:389
  164.2 37.0 %all-to-all-start.1 = ((bf16[8,56,1536]{2,1,0:T(8,128)(2,1)}), bf16[8,56,1536]{2,1,0:T(8,128)(2,1)}, u32[]{:S(2)}, u32[]{:S(2)}) async-start(bf16[8,56,1536]{2,1,0:T(8,128)(2,1)} %bitcast.196), calls=%async_computation.1 | async-start | bytes 2752512 | tf_op jit(solution)/shard_map/all_to_all | solution.py:1042
  168.7 14.4 %collective-permute-start.31 = (bf16[4,112,1536]{2,1,0:T(8,128)(2,1)S(1)}, bf16[4,112,1536]{2,1,0:T(8,128)(2,1)S(1)}, u32[]{:S(2)}, u32[]{:S(2)}) collective-permute-start(bf16[4,112,1536]{2,1,0:T(8,128)(2,1)S(1)} %bitcast.177), channel_id=1, source_target_pairs={{0,1},{1,0},{2,3},{3,2},{4,5},{5,4},{6,7},{7,6},{8,9},{9,8},{10,11... | collective-permute-start | bytes 4128776 | tf_op jit(solution)/shard_map/ppermute | solution.py:389
  203.6 32.3 %collective-permute-start.36 = (bf16[4,112,1536]{2,1,0:T(8,128)(2,1)S(1)}, bf16[4,112,1536]{2,1,0:T(8,128)(2,1)S(1)}, u32[]{:S(2)}, u32[]{:S(2)}) collective-permute-start(bf16[4,112,1536]{2,1,0:T(8,128)(2,1)S(1)} %bitcast.181), channel_id=1, source_target_pairs={{0,2},{1,3},{2,0},{3,1},{4,6},{5,7},{6,4},{7,5},{8,10},{9,11},{10,... | collective-permute-start | bytes 4128776 | tf_op jit(solution)/shard_map/ppermute | solution.py:389
  205.2 31.2 %collective-permute-start.34 = (bf16[4,112,1536]{2,1,0:T(8,128)(2,1)S(1)}, bf16[4,112,1536]{2,1,0:T(8,128)(2,1)S(1)}, u32[]{:S(2)}, u32[]{:S(2)}) collective-permute-start(bf16[4,112,1536]{2,1,0:T(8,128)(2,1)S(1)} %copy-done.76), channel_id=1, source_target_pairs={{0,1},{1,0},{2,3},{3,2},{4,5},{5,4},{6,7},{7,6},{8,9},{9,8},{10,11... | collective-permute-start | bytes 4128776 | tf_op jit(solution)/shard_map/ppermute | solution.py:389
  205.2 34.2 %collective-permute-start.37 = (bf16[4,112,1536]{2,1,0:T(8,128)(2,1)S(1)}, bf16[4,112,1536]{2,1,0:T(8,128)(2,1)S(1)}, u32[]{:S(2)}, u32[]{:S(2)}) collective-permute-start(bf16[4,112,1536]{2,1,0:T(8,128)(2,1)S(1)} %bitcast.182), channel_id=1, source_target_pairs={{0,1},{1,0},{2,3},{3,2},{4,5},{5,4},{6,7},{7,6},{8,9},{9,8},{10,11... | collective-permute-start | bytes 4128776 | tf_op jit(solution)/shard_map/ppermute | solution.py:389
  235.9 20.3 %collective-permute-start.33 = (bf16[4,112,1536]{2,1,0:T(8,128)(2,1)}, bf16[4,112,1536]{2,1,0:T(8,128)(2,1)}, u32[]{:S(2)}, u32[]{:S(2)}) collective-permute-start(bf16[4,112,1536]{2,1,0:T(8,128)(2,1)} %get-tuple-element.201), channel_id=1, source_target_pairs={{0,1},{1,0},{2,3},{3,2},{4,5},{5,4},{6,7},{7,6},{8,9},{9,8},{10,11... | collective-permute-start | bytes 4128776 | tf_op jit(solution)/shard_map/ppermute | solution.py:389
  237.9 32.4 %collective-permute-start.35 = (bf16[4,112,1536]{2,1,0:T(8,128)(2,1)}, bf16[4,112,1536]{2,1,0:T(8,128)(2,1)}, u32[]{:S(2)}, u32[]{:S(2)}) collective-permute-start(bf16[4,112,1536]{2,1,0:T(8,128)(2,1)} %add_convert_fusion.4), channel_id=1, source_target_pairs={{0,2},{1,3},{2,0},{3,1},{4,6},{5,7},{6,4},{7,5},{8,10},{9,11},{10,... | collective-permute-start | bytes 4128776 | tf_op jit(solution)/shard_map/ppermute | solution.py:389
  256.0 23.8 %collective-permute-start.40 = (bf16[4,112,1536]{2,1,0:T(8,128)(2,1)}, bf16[4,112,1536]{2,1,0:T(8,128)(2,1)}, u32[]{:S(2)}, u32[]{:S(2)}) collective-permute-start(bf16[4,112,1536]{2,1,0:T(8,128)(2,1)} %get-tuple-element.217), channel_id=1, source_target_pairs={{0,1},{1,0},{2,3},{3,2},{4,5},{5,4},{6,7},{7,6},{8,9},{9,8},{10,11... | collective-permute-start | bytes 4128776 | tf_op jit(solution)/shard_map/ppermute | solution.py:389
  274.7 37.3 %all-to-all-start.2 = ((bf16[8,56,1536]{2,1,0:T(8,128)(2,1)}), bf16[8,56,1536]{2,1,0:T(8,128)(2,1)S(1)}, u32[]{:S(2)}, u32[]{:S(2)}) async-start(bf16[8,56,1536]{2,1,0:T(8,128)(2,1)} %bitcast.197), calls=%async_computation.2 | async-start | bytes 2752512 | tf_op jit(solution)/shard_map/all_to_all | solution.py:1042
  279.7 45.4 %collective-permute-start.39 = (bf16[4,112,1536]{2,1,0:T(8,128)(2,1)}, bf16[4,112,1536]{2,1,0:T(8,128)(2,1)}, u32[]{:S(2)}, u32[]{:S(2)}) collective-permute-start(bf16[4,112,1536]{2,1,0:T(8,128)(2,1)} %get-tuple-element.215), channel_id=1, source_target_pairs={{0,1},{1,0},{2,3},{3,2},{4,5},{5,4},{6,7},{7,6},{8,9},{9,8},{10,11... | collective-permute-start | bytes 4128776 | tf_op jit(solution)/shard_map/ppermute | solution.py:389
  282.6 42.5 %collective-permute-start.41 = (bf16[4,112,1536]{2,1,0:T(8,128)(2,1)}, bf16[4,112,1536]{2,1,0:T(8,128)(2,1)}, u32[]{:S(2)}, u32[]{:S(2)}) collective-permute-start(bf16[4,112,1536]{2,1,0:T(8,128)(2,1)} %add_convert_fusion.1), channel_id=1, source_target_pairs={{0,2},{1,3},{2,0},{3,1},{4,6},{5,7},{6,4},{7,5},{8,10},{9,11},{10,... | collective-permute-start | bytes 4128776 | tf_op jit(solution)/shard_map/ppermute | solution.py:389
  329.5 48.8 %all-to-all-start.3 = ((bf16[8,56,1536]{2,1,0:T(8,128)(2,1)}), bf16[8,56,1536]{2,1,0:T(8,128)(2,1)S(1)}, u32[]{:S(2)}, u32[]{:S(2)}) async-start(bf16[8,56,1536]{2,1,0:T(8,128)(2,1)} %bitcast.199), calls=%async_computation.3 | async-start | bytes 2752512 | tf_op jit(solution)/shard_map/all_to_all | solution.py:1042
  399.4 16.1 %collective-permute-start.42 = (bf16[2,8,96,384]{3,2,1,0:T(8,128)(2,1)}, bf16[2,8,96,384]{3,2,1,0:T(8,128)(2,1)}, u32[]{:S(2)}, u32[]{:S(2)}) collective-permute-start(bf16[2,8,96,384]{3,2,1,0:T(8,128)(2,1)} %pad_maximum_fusion.3), channel_id=1, source_target_pairs={{0,1},{1,0},{2,3},{3,2},{4,5},{5,4},{6,7},{7,6},{8,9},{9,8},{10,11... | collective-permute-start | bytes 3538952 | tf_op jit(solution)/shard_map/ppermute | solution.py:389
  409.3 9.7 %collective-permute-start.43 = (bf16[2,8,240,256]{3,2,1,0:T(8,128)(2,1)}, bf16[2,8,240,256]{3,2,1,0:T(8,128)(2,1)}, u32[]{:S(2)}, u32[]{:S(2)}) collective-permute-start(bf16[2,8,240,256]{3,2,1,0:T(8,128)(2,1)} %pad_maximum_fusion), channel_id=1, source_target_pairs={{0,1},{1,0},{2,3},{3,2},{4,5},{5,4},{6,7},{7,6},{8,9},{9,8},{10,11... | collective-permute-start | bytes 5898248 | tf_op jit(solution)/shard_map/ppermute | solution.py:389
  430.3 11.0 %collective-permute-start.46 = (bf16[4,96,384]{2,1,0:T(8,128)(2,1)}, bf16[4,96,384]{2,1,0:T(8,128)(2,1)S(1)}, u32[]{:S(2)}, u32[]{:S(2)}) collective-permute-start(bf16[4,96,384]{2,1,0:T(8,128)(2,1)} %get-tuple-element.249), channel_id=1, source_target_pairs={{0,6},{1,7},{2,4},{3,5},{4,2},{5,3},{6,0},{7,1},{8,14},{9,15},{10,... | collective-permute-start | bytes 884744 | tf_op jit(solution)/shard_map/ppermute | solution.py:405
  433.3 59.5 %collective-permute-start.45 = (bf16[4,96,384]{2,1,0:T(8,128)(2,1)}, bf16[4,96,384]{2,1,0:T(8,128)(2,1)}, u32[]{:S(2)}, u32[]{:S(2)}) collective-permute-start(bf16[4,96,384]{2,1,0:T(8,128)(2,1)} %get-tuple-element.248), channel_id=1, source_target_pairs={{0,2},{1,3},{2,0},{3,1},{4,6},{5,7},{6,4},{7,5},{8,10},{9,11},{10,... | collective-permute-start | bytes 884744 | tf_op jit(solution)/shard_map/ppermute | solution.py:389
  433.8 59.0 %collective-permute-start.44 = (bf16[4,96,384]{2,1,0:T(8,128)(2,1)}, bf16[4,96,384]{2,1,0:T(8,128)(2,1)}, u32[]{:S(2)}, u32[]{:S(2)}) collective-permute-start(bf16[4,96,384]{2,1,0:T(8,128)(2,1)} %fusion.14), channel_id=1, source_target_pairs={{0,4},{4,0},{8,12},{12,8},{16,20},{20,16},{24,28},{28,24},{1,5},{5... | collective-permute-start | bytes 884744 | tf_op jit(solution)/shard_map/ppermute | solution.py:389
  433.8 61.2 %collective-permute-start.49 = (bf16[4,240,256]{1,2,0:T(8,128)(2,1)}, bf16[4,240,256]{1,2,0:T(8,128)(2,1)}, u32[]{:S(2)}, u32[]{:S(2)}) collective-permute-start(bf16[4,240,256]{1,2,0:T(8,128)(2,1)} %bitcast.207), channel_id=1, source_target_pairs={{0,6},{1,7},{2,4},{3,5},{4,2},{5,3},{6,0},{7,1},{8,14},{9,15},{10,... | collective-permute-start | bytes 1474568 | tf_op jit(solution)/shard_map/ppermute | solution.py:405
  436.7 58.3 %collective-permute-start.48 = (bf16[4,240,256]{1,2,0:T(8,128)(2,1)}, bf16[4,240,256]{1,2,0:T(8,128)(2,1)}, u32[]{:S(2)}, u32[]{:S(2)}) collective-permute-start(bf16[4,240,256]{1,2,0:T(8,128)(2,1)} %bitcast.206), channel_id=1, source_target_pairs={{0,2},{1,3},{2,0},{3,1},{4,6},{5,7},{6,4},{7,5},{8,10},{9,11},{10,... | collective-permute-start | bytes 1474568 | tf_op jit(solution)/shard_map/ppermute | solution.py:389
  441.4 53.7 %collective-permute-start.47 = (bf16[4,240,256]{1,2,0:T(8,128)(2,1)}, bf16[4,240,256]{1,2,0:T(8,128)(2,1)}, u32[]{:S(2)}, u32[]{:S(2)}) collective-permute-start(bf16[4,240,256]{1,2,0:T(8,128)(2,1)} %bitcast.205), channel_id=1, source_target_pairs={{0,4},{4,0},{8,12},{12,8},{16,20},{20,16},{24,28},{28,24},{1,5},{5... | collective-permute-start | bytes 1474568 | tf_op jit(solution)/shard_map/ppermute | solution.py:389
  513.4 25.5 %collective-permute-start.50 = (bf16[2,8,144,384]{3,2,1,0:T(8,128)(2,1)}, bf16[2,8,144,384]{3,2,1,0:T(8,128)(2,1)S(1)}, u32[]{:S(2)}, u32[]{:S(2)}) collective-permute-start(bf16[2,8,144,384]{3,2,1,0:T(8,128)(2,1)} %pad_maximum_fusion.2), channel_id=1, source_target_pairs={{0,1},{1,0},{2,3},{3,2},{4,5},{5,4},{6,7},{7,6},{8,9},{9,8},{10,11... | collective-permute-start | bytes 5308424 | tf_op jit(solution)/shard_map/ppermute | solution.py:389
  515.8 10.6 %collective-permute-start.59 = (bf16[96,384]{1,0:T(8,128)(2,1)S(1)}, bf16[96,384]{1,0:T(8,128)(2,1)S(1)}, u32[]{:S(2)}, u32[]{:S(2)}) collective-permute-start(bf16[96,384]{1,0:T(8,128)(2,1)S(1)} %get-tuple-element.366), channel_id=1, source_target_pairs={{0,24},{4,28},{8,16},{12,20},{16,8},{20,12},{24,0},{28,4},{1,25},{... | collective-permute-start | bytes 221192 | tf_op jit(solution)/shard_map/ppermute | solution.py:389
  519.2 12.7 %collective-permute-start.58 = (bf16[96,384]{1,0:T(8,128)(2,1)S(1)}, bf16[96,384]{1,0:T(8,128)(2,1)S(1)}, u32[]{:S(2)}, u32[]{:S(2)}) collective-permute-start(bf16[96,384]{1,0:T(8,128)(2,1)S(1)} %get-tuple-element.367), channel_id=1, source_target_pairs={{0,16},{4,20},{8,24},{12,28},{16,0},{20,4},{24,8},{28,12},{1,17},{... | collective-permute-start | bytes 221192 | tf_op jit(solution)/shard_map/ppermute | solution.py:389
  519.2 12.8 %collective-permute-start.57 = (bf16[96,384]{1,0:T(8,128)(2,1)S(1)}, bf16[96,384]{1,0:T(8,128)(2,1)S(1)}, u32[]{:S(2)}, u32[]{:S(2)}) collective-permute-start(bf16[96,384]{1,0:T(8,128)(2,1)S(1)} %get-tuple-element.365), channel_id=1, source_target_pairs={{0,8},{4,12},{8,0},{12,4},{16,24},{20,28},{24,16},{28,20},{1,9},{5... | collective-permute-start | bytes 221192 | tf_op jit(solution)/shard_map/ppermute | solution.py:389
  520.3 12.3 %collective-permute-start.62 = (bf16[240,256]{0,1:T(8,128)(2,1)S(1)}, bf16[240,256]{0,1:T(8,128)(2,1)S(1)}, u32[]{:S(2)}, u32[]{:S(2)}) collective-permute-start(bf16[240,256]{0,1:T(8,128)(2,1)S(1)} %get-tuple-element.354), channel_id=1, source_target_pairs={{0,24},{4,28},{8,16},{12,20},{16,8},{20,12},{24,0},{28,4},{1,25},{... | collective-permute-start | bytes 368648 | tf_op jit(solution)/shard_map/ppermute | solution.py:389
  526.4 11.0 %collective-permute-start.61 = (bf16[240,256]{0,1:T(8,128)(2,1)S(1)}, bf16[240,256]{0,1:T(8,128)(2,1)S(1)}, u32[]{:S(2)}, u32[]{:S(2)}) collective-permute-start(bf16[240,256]{0,1:T(8,128)(2,1)S(1)} %get-tuple-element.355), channel_id=1, source_target_pairs={{0,16},{4,20},{8,24},{12,28},{16,0},{20,4},{24,8},{28,12},{1,17},{... | collective-permute-start | bytes 368648 | tf_op jit(solution)/shard_map/ppermute | solution.py:389
  540.0 17.9 %collective-permute-start.51 = (bf16[4,144,384]{2,1,0:T(8,128)(2,1)}, bf16[4,144,384]{2,1,0:T(8,128)(2,1)}, u32[]{:S(2)}, u32[]{:S(2)}) collective-permute-start(bf16[4,144,384]{2,1,0:T(8,128)(2,1)} %fusion.11), channel_id=1, source_target_pairs={{0,4},{4,0},{8,12},{12,8},{16,20},{20,16},{24,28},{28,24},{1,5},{5... | collective-permute-start | bytes 1327112 | tf_op jit(solution)/shard_map/ppermute | solution.py:389
  541.8 19.7 %collective-permute-start.52 = (bf16[4,144,384]{2,1,0:T(8,128)(2,1)}, bf16[4,144,384]{2,1,0:T(8,128)(2,1)S(1)}, u32[]{:S(2)}, u32[]{:S(2)}) collective-permute-start(bf16[4,144,384]{2,1,0:T(8,128)(2,1)} %get-tuple-element.364), channel_id=1, source_target_pairs={{0,2},{1,3},{2,0},{3,1},{4,6},{5,7},{6,4},{7,5},{8,10},{9,11},{10,... | collective-permute-start | bytes 1327112 | tf_op jit(solution)/shard_map/ppermute | solution.py:389
  543.3 18.2 %collective-permute-start.53 = (bf16[4,144,384]{2,1,0:T(8,128)(2,1)S(1)}, bf16[4,144,384]{2,1,0:T(8,128)(2,1)S(1)}, u32[]{:S(2)}, u32[]{:S(2)}) collective-permute-start(bf16[4,144,384]{2,1,0:T(8,128)(2,1)S(1)} %get-tuple-element.363), channel_id=1, source_target_pairs={{0,6},{1,7},{2,4},{3,5},{4,2},{5,3},{6,0},{7,1},{8,14},{9,15},{10,... | collective-permute-start | bytes 1327112 | tf_op jit(solution)/shard_map/ppermute | solution.py:405
  562.8 16.2 %collective-permute-start.54 = (bf16[144,384]{1,0:T(8,128)(2,1)S(1)}, bf16[144,384]{1,0:T(8,128)(2,1)S(1)}, u32[]{:S(2)}, u32[]{:S(2)}) collective-permute-start(bf16[144,384]{1,0:T(8,128)(2,1)S(1)} %get-tuple-element.362), channel_id=1, source_target_pairs={{0,8},{4,12},{8,0},{12,4},{16,24},{20,28},{24,16},{28,20},{1,9},{5... | collective-permute-start | bytes 331784 | tf_op jit(solution)/shard_map/ppermute | solution.py:389
  562.9 16.2 %collective-permute-start.55 = (bf16[144,384]{1,0:T(8,128)(2,1)S(1)}, bf16[144,384]{1,0:T(8,128)(2,1)S(1)}, u32[]{:S(2)}, u32[]{:S(2)}) collective-permute-start(bf16[144,384]{1,0:T(8,128)(2,1)S(1)} %get-tuple-element.361), channel_id=1, source_target_pairs={{0,16},{4,20},{8,24},{12,28},{16,0},{20,4},{24,8},{28,12},{1,17},{... | collective-permute-start | bytes 331784 | tf_op jit(solution)/shard_map/ppermute | solution.py:389
  565.8 13.3 %collective-permute-start.56 = (bf16[144,384]{1,0:T(8,128)(2,1)S(1)}, bf16[144,384]{1,0:T(8,128)(2,1)S(1)}, u32[]{:S(2)}, u32[]{:S(2)}) collective-permute-start(bf16[144,384]{1,0:T(8,128)(2,1)S(1)} %get-tuple-element.360), channel_id=1, source_target_pairs={{0,24},{4,28},{8,16},{12,20},{16,8},{20,12},{24,0},{28,4},{1,25},{... | collective-permute-start | bytes 331784 | tf_op jit(solution)/shard_map/ppermute | solution.py:389
  (96 other events, 754.2 us)

commit v3 on v2

--- a/solution.py
+++ b/solution.py
@@ -59,7 +59,7 @@
 
 
 def mixer_kernel(T, Q, R, x_ref, gain_ref, wx_ref, xpT_ref, wdt_ref, par_ref, a2_ref,
-                 nm_ref, in_ref, u_ref, dl_ref, pT_ref, y_ref, st_ref, state, bx, cx, du):
+                 nm_ref, in_ref, cv_ref, u_ref, dl_ref, pT_ref, y_ref, st_ref, state, bx, cx, du):
     c = pl.program_id(0)
     L, DI = nm_ref.shape[0], wx_ref.shape[1]
     taps = par_ref.shape[0] - 3
@@ -76,6 +76,7 @@
     par = par_ref[...]
     skip = par[taps + 2:taps + 3]
     conv = convolve(in_ref[pl.ds(pl.multiple_of(c * T, 8), T + 8)], par[:taps], par[taps:taps + 1], T)
+    cv_ref[0] = conv.reshape(T // 8, 8, DI)
     u = conv * sigmoid(conv)
     u_ref[0] = u.reshape(T // 8, 8, DI)
     pT = mm(xpT_ref[...], u.astype(jnp.bfloat16), NT)
@@ -122,7 +123,7 @@
     return jax.ShapeDtypeStruct(shape, dtype)
 
 
-def mixer_forward(x, gain, wx, xpT, wdt, par, a2, T, Q=3):
+def mixer_forward(x, gain, wx, xpT, wdt, par, a2, T, Q=6):
     L, D = x.shape
     DI = wx.shape[1]
     C, XP, R = L // T, xpT.shape[0], wdt.shape[0]
@@ -133,9 +134,9 @@
     return pl.pallas_call(
         functools.partial(mixer_kernel, T, Q, R), grid=(C,),
         in_specs=[whole_spec(a) for a in ins],
-        out_specs=[whole_spec(nm), whole_spec(inner), rows, rows, pl.BlockSpec((1, XP, T), lambda c: (c, 0, 0)), rows,
+        out_specs=[whole_spec(nm), whole_spec(inner), rows, rows, rows, pl.BlockSpec((1, XP, T), lambda c: (c, 0, 0)), rows,
                    pl.BlockSpec((1, NS, DI), lambda c: (c, 0, 0))],
-        out_shape=[nm, inner, big, big, sds((C, XP, T)), big, sds((C, NS, DI))],
+        out_shape=[nm, inner, big, big, big, sds((C, XP, T)), big, sds((C, NS, DI))],
         scratch_shapes=[pltpu.VMEM((NS, DI), F32), pltpu.VMEM((T, NS, 128), F32), pltpu.VMEM((T, NS, 128), F32),
                         pltpu.VMEM((T // 8, 8, DI), F32)],
         compiler_params=pltpu.CompilerParams(vmem_limit_bytes=48 << 20),
@@ -143,7 +144,7 @@
     )(*ins)
 
 
-def scan_back_kernel(T, Q, Q2, R, u_ref, dl_ref, gs_ref, in_ref, pT_ref, st_ref, xpT_ref, wdt_ref, par_ref, an_ref,
+def scan_back_kernel(T, Q, Q2, R, u_ref, dl_ref, gs_ref, cv_ref, in_ref, pT_ref, st_ref, xpT_ref, wdt_ref, par_ref, an_ref,
                      gi_ref, gxp_ref, gwd_ref, gpar_ref, carry, later, bx, cx, du, guc, gdt, hs, ds, gbp, gcp, sums):
     j = pl.program_id(0)
     c = pl.num_programs(0) - 1 - j
@@ -226,7 +227,7 @@
                 return (tuple(g_[q] for q in qs), tuple(ga[q] for q in qs), tuple(gbs), tuple(gsk))
             z8 = tuple(jnp.zeros((8, 128), F32) for q in qs)
             cr = lax.fori_loop(0, T // 8, rb, (tuple(carry[:, lanes[q]] for q in qs),
-                                               tuple(jnp.zeros((NS, 128), F32) for q in qs), z8, z8))
+                                               tuple(jnp.zeros((NS, 128), F32) for q in qs), z8, z8), unroll=2)
             for q in qs:
                 carry[:, lanes[q]] = cr[0][q - q0]
                 gpar_ref[taps + 2:taps + 2 + NS, lanes[q]] += cr[1][q - q0] * an[q]
@@ -243,18 +244,18 @@
     gxp_ref[...] += mm(gpT, u_ref[0].reshape(T, DI).astype(jnp.bfloat16))
     gu = guc[...].reshape(T, DI) + mm(gpT, xpT_ref[...], TN)
     par = par_ref[...]
-    ext = in_ref[pl.ds(pl.multiple_of(c * T, 8), T + 8)]
-    conv = convolve(ext, par[:taps], par[taps:taps + 1], T)
+    conv = cv_ref[0].reshape(T, DI)
     sig = sigmoid(conv)
     gconv = gu * (sig * (1.0 + conv * (1.0 - sig)))
     part = lambda v: jnp.sum(v.reshape(T // 8, 8, DI), axis=0)
     sums[taps] += part(gconv)
+    inner_x = in_ref[pl.ds(pl.multiple_of(c * T + 8, 8), T)]
+    both = jnp.concatenate([gconv, later[...]], axis=0)
+    gi = None
     for k in range(taps):
-        sums[k] += part(gconv * ext[9 - taps + k:9 - taps + k + T])
-    both = jnp.concatenate([gconv, later[...]], axis=0)
-    gi = par[0:1] * both[taps - 1:taps - 1 + T]
-    for k in range(1, taps):
-        gi = gi + par[k:k + 1] * both[taps - 1 - k:taps - 1 - k + T]
+        ahead = both[taps - 1 - k:taps - 1 - k + T]
+        sums[k] += part(ahead * inner_x)
+        gi = par[k:k + 1] * ahead if gi is None else gi + par[k:k + 1] * ahead
     gi_ref[...] = gi.astype(jnp.bfloat16)
     later[...] = gconv[:8]
 
@@ -265,7 +266,7 @@
         gpar_ref[taps + 2 + NS:taps + 3 + NS] = jnp.sum(sums[taps + 2], axis=0, keepdims=True)
 
 
-def scan_backward(u, dl, gs, inner, pT, st, xpT, wdt, par, an, Q=2, Q2=2):
+def scan_backward(u, dl, gs, conv, inner, pT, st, xpT, wdt, par, an, Q=3, Q2=3):
     C, T8, _, DI = u.shape
     T = T8 * 8
     XP, R = xpT.shape[0], wdt.shape[0]
@@ -276,14 +277,14 @@
     V = lambda *s: pltpu.VMEM(s, F32)
     return pl.pallas_call(
         functools.partial(scan_back_kernel, T, Q, Q2, R), grid=(C,),
-        in_specs=[rows, rows, rows, whole_spec(inner), rev(XP, T), rev(NS, DI)] + [whole_spec(a) for a in (xpT, wdt, par, an)],
+        in_specs=[rows, rows, rows, rows, whole_spec(inner), rev(XP, T), rev(NS, DI)] + [whole_spec(a) for a in (xpT, wdt, par, an)],
         out_specs=[pl.BlockSpec((T, DI), lambda j: (C - 1 - j, 0))] + [whole_spec(o) for o in outs[1:]],
         out_shape=outs,
         scratch_shapes=[V(NS, DI), V(8, DI), V(T, NS, 128), V(T, NS, 128), V(T8, 8, DI), V(T8, 8, DI), V(T8, 8, DI),
                         V(T, NS, Q * 128), V(T, NS, Q * 128), V(T, NS, 128), V(T, NS, 128), V(par.shape[0], 8, DI)],
         compiler_params=pltpu.CompilerParams(vmem_limit_bytes=52 << 20),
         cost_estimate=pl.CostEstimate(flops=80000000000, bytes_accessed=16 * C * T * DI, transcendentals=0),
-    )(u, dl, gs, inner, pT, st, xpT, wdt, par, an)
+    )(u, dl, gs, conv, inner, pT, st, xpT, wdt, par, an)
 
 
 def one_call(kernel, ins, outs, scalars=(), flops=0):
@@ -642,7 +643,7 @@
 
 def tiles_fit(w_in_x, w_xproj, w_out, conv_w):
     lanes = w_in_x.shape[1]
-    return (lanes % 128 == 0 and w_in_x.shape[0] % 32 == 0 and up_to(w_xproj.shape[0], 128) + 128 == lanes
+    return (lanes == 384 and w_in_x.shape[0] % 32 == 0 and up_to(w_xproj.shape[0], 128) + 128 == lanes
             and w_xproj.shape[1] <= 32 and conv_w.shape[1] <= 128 and w_out.shape[0] % 16 == 0
             and up_to(w_out.shape[1], 128) == 256)
 
@@ -653,7 +654,7 @@
     return jnp.where(match(i, j), 1.0, 0.0).astype(BF)
 
 
-def pack_kernel(wx, wdt, xp, cw, cb, db, al, ds, gx, gm, wo, wr, first, other, s_dt, s_xp, s_sm, s_out, s_r):
+def pack_kernel(wx, wdt, xp, cw, cb, db, al, ds, gx, gm, wz, wo, wr, first, other, s_dt, s_xp, s_sm, s_out, s_r):
     n = wx.shape[0]
     for s in (s_dt, s_xp, s_sm, s_out, s_r):
         s[...] = jnp.zeros_like(s)
@@ -669,22 +670,36 @@
         at += v.shape[0]
     first[n + 16:, wide:] = s_sm[...].astype(BF)
     s_out[:, :wo.shape[1]] = wo[...].astype(F32)
-    other[:wo.shape[0]] = s_out[...].astype(BF)
     s_r[:, :wr.shape[1]] = wr[...].astype(F32)
-    half = wr.shape[0] // 2
-    other[wo.shape[0]:, :128] = s_r[:half].astype(BF)
-    other[wo.shape[0]:, 128:] = s_r[half:].astype(BF)
-
-
-def pack_params(w_in_x, w_dt, w_xproj, conv_w, conv_b, dt_bias, a_log, d_skip, gain_mix, gain_moe, w_out, w_router):
+    put_other(lambda at, lane, v: store(other, at, lane, v), wz[:, :256], wz[:, 256:], s_out[...].astype(BF), s_r[...].astype(BF))
+
+
+def store(ref, at, lane, v):
+    ref[at:at + v.shape[0], lane:lane + v.shape[1]] = v
+
+
+def put_other(put, z_wide, z_rest, out, router):
+    n = z_wide.shape[-2]
+    put(0, 0, z_wide)
+    put(n, 0, z_rest[..., :n // 2, :])
+    put(n, 128, z_rest[..., n // 2:, :])
+    at = n + n // 2
+    put(at, 0, out)
+    at += out.shape[-2]
+    half = router.shape[-2] // 2
+    put(at, 0, router[..., :half, :])
+    put(at, 128, router[..., half:, :])
+
+
+def pack_params(w_in_x, w_dt, w_xproj, conv_w, conv_b, dt_bias, a_log, d_skip, gain_mix, gain_moe, w_in_z, w_out, w_router):
     n, lanes = w_in_x.shape
     ins = [w_in_x, w_dt, w_xproj, conv_w, conv_b[None], dt_bias[None], a_log, d_skip[None], gain_mix[None], gain_moe[None],
-           w_out, w_router]
+           w_in_z, w_out, w_router]
     vmem = pl.BlockSpec(memory_space=pltpu.VMEM)
     V = lambda *s: pltpu.VMEM(s, F32)
     return pl.pallas_call(
         pack_kernel, in_specs=[vmem] * len(ins), out_specs=[vmem] * 2,
-        out_shape=[sds((n + 48, lanes), BF), sds((w_out.shape[0] + w_router.shape[0] // 2, 256), BF)],
+        out_shape=[sds((n + 48, lanes), BF), sds((n + n // 2 + w_out.shape[0] + w_router.shape[0] // 2, 256), BF)],
         scratch_shapes=[V(16, lanes), V(32, lanes - 128), V(32, 128), V(w_out.shape[0], 256), V(w_router.shape[0], 128)],
     )(*ins)
 
@@ -730,15 +745,19 @@
 
 
 def unpack_other(masks, dims, me, *refs):
-    out_rows, out_lanes, r_cols, cols = dims
+    n, out_rows, out_lanes, r_cols, cols = dims
     count = len(masks)
     bufs = refs[:count]
-    fo, router, w_out, w_r = refs[count:]
-    half = bufs[0].shape[1] - out_rows
+    fz, fo, router, w_out, w_r = refs[count:]
+    half = n // 2
+    at = n + half
     for buf, i, r, c in each_block(masks, bufs, me[0], me[1]):
-        w_out[span(r, out_rows), span(c, 256)] = buf[i, :out_rows]
-        w_r[pl.ds(pl.multiple_of(r * (2 * half), half), half), span(c, 128)] = buf[i, out_rows:, :128]
-        w_r[pl.ds(pl.multiple_of(r * (2 * half) + half, half), half), span(c, 128)] = buf[i, out_rows:, 128:]
+        fz[span(r, n), pl.ds(pl.multiple_of(c * 384, 128), 256)] = buf[i, :n]
+        for j in range(2):
+            rows = pl.ds(pl.multiple_of(r * n + j * half, 16), half)
+            fz[rows, pl.ds(pl.multiple_of(c * 384 + 256, 128), 128)] = buf[i, n:at, j * 128:(j + 1) * 128]
+            w_r[rows, span(c, 128)] = buf[i, at + out_rows:, j * 128:(j + 1) * 128]
+        w_out[span(r, out_rows), span(c, 256)] = buf[i, at:at + out_rows]
     wide = w_out[...]
     fo[...] = jnp.concatenate([wide[:, c * 256:c * 256 + out_lanes] for c in range(cols)], axis=1)
     pick = one_hot((128 * cols, router.shape[1]), lambda i, j: (i % 128 < r_cols) & (i // 128 * r_cols + i % 128 == j))
@@ -763,10 +782,9 @@
     dt_rows, xp_cols, xp_rows, share, gshare, rows, cols = dims
     pairs = refs[:2 * count]
     gwd, gxp, gpar, gmix, gmoe = (refs[(2 + i) * count:(3 + i) * count] for i in range(5))
-    out, w_dt, w_xp, w_sm = refs[7 * count:]
+    keep, give, w_dt, w_xp, w_sm = refs[7 * count:]
     k = pl.program_id(0)
-    c = s_ref[0] ^ k
-    n, lanes = out.shape[2] - 48, out.shape[3]
+    n, lanes = keep.shape[2] - 48, keep.shape[3]
     wide = lanes - 128
     total = lambda vs: functools.reduce(lambda a, b: a + b, [v[...] for v in vs])
 
@@ -787,71 +805,153 @@
             w_sm[:m, p * 128:p * 128 + share] = par[:, p * share:(p + 1) * share]
             w_sm[m:m + 1, p * 128:p * 128 + gshare] = mix[:, p * gshare:(p + 1) * gshare]
             w_sm[m + 1:m + 2, p * 128:p * 128 + gshare] = moe[:, p * gshare:(p + 1) * gshare]
-    g = mm(pairs[0][...], pairs[1][...], TN)
-    for i in range(1, count):
-        g = g + mm(pairs[2 * i][...], pairs[2 * i + 1][...], TN)
-    out[0, :, :n] = g.astype(BF).reshape(rows, n, lanes)
-    for r in range(rows):
-        out[0, r, n:n + 16] = w_dt[r * 16:(r + 1) * 16, span(c, lanes)]
-        out[0, r, n + 16:, :wide] = w_xp[span(c, 32), r * wide:(r + 1) * wide]
-        out[0, r, n + 16:, wide:] = w_sm[:, span(r * cols + c, 128)].astype(BF)
+    for j, out in enumerate((keep, give)):
+        c = s_ref[0] ^ (2 * k + j)
+        g = sum_products(pairs, lambda r: r[:, span(c, lanes)])
+        out[0, :, :n] = g.astype(BF).reshape(rows, n, lanes)
+        for r in range(rows):
+            out[0, r, n:n + 16] = w_dt[r * 16:(r + 1) * 16, span(c, lanes)]
+            out[0, r, n + 16:, :wide] = w_xp[span(c, 32), r * wide:(r + 1) * wide]
+            out[0, r, n + 16:, wide:] = w_sm[:, span(r * cols + c, 128)].astype(BF)
+
+
+def sum_products(pairs, block):
+    return functools.reduce(lambda a, b: a + b, [mm(pairs[i][...], block(pairs[i + 1]), TN) for i in range(0, len(pairs), 2)])
+
+
+def grad_blocks(kernel, ins, scratch, block, rows, cols, my_col, flops):
+    out = sds((cols // 2, rows) + block, BF)
+    return list(pl.pallas_call(
+        kernel,
+        grid_spec=pltpu.PrefetchScalarGridSpec(
+            num_scalar_prefetch=1, grid=(cols // 2,), in_specs=[whole_spec(v) for v in ins],
+            out_specs=[pl.BlockSpec((1, rows) + block, lambda k, s: (k, 0, 0, 0))] * 2, scratch_shapes=scratch),
+        out_shape=[out, out],
+        compiler_params=pltpu.CompilerParams(vmem_limit_bytes=56 << 20),
+        cost_estimate=pl.CostEstimate(flops=flops, bytes_accessed=1 << 23, transcendentals=0),
+    )(my_col.reshape(1), *ins))
 
 
 def grad_x_blocks(pairs, smalls, dims, my_col):
     rows, cols = dims[-2:]
-    count = len(pairs)
     n, m = pairs[0][0].shape
-    lanes = pairs[0][1].shape[1] // cols
-    flat = [v for p in pairs for v in p]
-    specs = [pl.BlockSpec((n, m), lambda k, s: (0, 0)), pl.BlockSpec((n, lanes), lambda k, s: (0, s[0] ^ k))] * count
-    more = [g[name] for name in ("dt", "xproj", "chan", "gain_mix", "gain_moe") for g in smalls]
-    block = m // rows + 48
+    inner = pairs[0][1].shape[1]
+    lanes = inner // cols
+    ins = [v for p in pairs for v in p] + [g[name] for name in ("dt", "xproj", "chan", "gain_mix", "gain_moe") for g in smalls]
+    scratch = [pltpu.VMEM((16 * rows, inner), BF), pltpu.VMEM((32 * cols, (lanes - 128) * rows), BF), pltpu.VMEM((32, 128 * rows * cols), F32)]
+    return grad_blocks(functools.partial(grad_x_kernel, len(pairs), dims), ins, scratch, (m // rows + 48, lanes), rows, cols, my_col,
+                       2 * len(pairs) * n * m * inner)
+
+
+def grad_other_kernel(count, r_cols, s_ref, *refs):
+    zs, outs, routers = refs[:2 * count], refs[2 * count:4 * count], refs[4 * count:5 * count]
+    keep, give = refs[5 * count:]
+    rows = keep.shape[1]
+    k = pl.program_id(0)
+    r = functools.reduce(lambda a, b: a + b, [v[...] for v in routers]).astype(BF)
+    for j, out in enumerate((keep, give)):
+        c = s_ref[0] ^ (2 * k + j)
+        z = sum_products(zs, lambda v: v[:, pl.ds(pl.multiple_of(c * 384, 128), 384)]).astype(BF)
+        o = sum_products(outs, lambda v: v[:, span(2 * k + j, 256)]).astype(BF)
+        put = one_hot((r.shape[1], 128), lambda a, b: (b < r_cols) & (a == c * r_cols + b))
+        w = mm(r, put).astype(BF)
+        z, o, w = (v.reshape(rows, v.shape[0] // rows, v.shape[1]) for v in (z, o, w))
+
+        def put_block(at, lane, v):
+            out[0, :, at:at + v.shape[1], lane:lane + v.shape[2]] = v
+        put_other(put_block, z[..., :256], z[..., 256:], o, w)
+
+
+def grad_other_blocks(zs, outs, routers, block, rows, cols, r_cols, my_col):
+    ins = [v for p in zs for v in p] + [v for p in outs for v in p] + list(routers)
+    flops = 2 * sum(a.shape[0] * a.shape[1] * b.shape[1] for a, b in zs + outs)
+    return grad_blocks(functools.partial(grad_other_kernel, len(zs), r_cols), ins, [], block, rows, cols, my_col, flops)
+
+
+def split_near_kernel(plan, s_ref, keep, got, own, *gives):
+    for out, (ki, rm) in zip((own,) + gives, plan):
+        p = (s_ref[0] ^ rm) & 1
+        v = keep[ki, 0, p].astype(F32) + got[ki, 0, p].astype(F32)
+        out[0] = v.astype(out.dtype)
+
+
+def split_near(keep, got):
+    plane = stages()[1]
+    near, rows, n, lanes = keep.shape
+    plan = [(cm >> 1, rm) for rm, cm in plane]
+    view = (near, rows // 2, 2, n, lanes)
+    outs = [sds((rows // 2, n, lanes), F32 if i == 0 else BF) for i in range(len(plan))]
+    res = pl.pallas_call(
+        functools.partial(split_near_kernel, plan),
+        grid_spec=pltpu.PrefetchScalarGridSpec(
+            num_scalar_prefetch=1, grid=(rows // 2,),
+            in_specs=[pl.BlockSpec((near, 1, 2, n, lanes), lambda z, s: (0, z, 0, 0, 0))] * 2,
+            out_specs=[pl.BlockSpec((1, n, lanes), lambda z, s: (z, 0, 0))] * len(outs)),
+        out_shape=outs,
+        compiler_params=pltpu.CompilerParams(vmem_limit_bytes=32 << 20),
+        cost_estimate=pl.CostEstimate(flops=0, bytes_accessed=6 * keep.size, transcendentals=0),
+    )(lax.axis_index("row").reshape(1), keep.reshape(view), got.reshape(view))
+    return res[0], list(res[1:])
+
+
+def split_far_kernel(count, plan, s_ref, own, *refs):
+    gots, mine, gives = refs[:count], refs[count], refs[count + 1:]
+    for out, rm in zip((mine,) + gives, plan):
+        i = (s_ref[0] ^ rm) >> 1
+        v = own[i]
+        for g in gots:
+            v = v + g[i].astype(F32)
+        out[...] = v.astype(out.dtype)
+
+
+def split_far(own, gots):
+    plan = [rm for rm, _ in stages()[0]]
+    _, n, lanes = own.shape
+    outs = [sds((n, lanes), F32 if i == 0 else BF) for i in range(len(plan))]
+    res = one_call(functools.partial(split_far_kernel, len(gots), plan), [own] + gots, outs, [lax.axis_index("row").reshape(1)])
+    return res[0], list(res[1:])
+
+
+def total_of(refs):
+    return functools.reduce(lambda a, b: a + b[...].astype(F32), refs[1:], refs[0][...])
+
+
+def finish_x_kernel(count, *refs):
+    gx, gxp, gdt, gcw, gcb, gdb, gal, gds, gmix, gmoe, s = refs[count:]
+    s[...] = total_of(refs[:count])
+    n, lanes = gx.shape
+    gx[...] = s[:n]
+    gdt[...] = s[n:n + gdt.shape[0]]
+    wide = lanes - 128
+    gxp[...] = s[n + 16:, :wide].T[:gxp.shape[0], :gxp.shape[1]]
+    at = n + 16
+    for ref in (gcw, gcb, gdb, gal, gds, gmix, gmoe):
+        ref[...] = s[at:at + ref.shape[0], wide:wide + ref.shape[1]]
+        at += ref.shape[0]
+
+
+def finish_other_kernel(count, *refs):
+    gz, go, gr, s = refs[count:]
+    s[...] = total_of(refs[:count])
+    n = gz.shape[0]
+    half = n // 2
+    gz[:, :256] = s[:n]
+    gz[:half, 256:] = s[n:n + half, :128]
+    gz[half:, 256:] = s[n:n + half, 128:]
+    at = n + half
+    go[...] = s[at:at + go.shape[0], :go.shape[1]]
+    at += go.shape[0]
+    gr[:half] = s[at:, :gr.shape[1]]
+    gr[half:] = s[at:, 128:128 + gr.shape[1]]
+
+
+def finish(kernel, mine, gots, shapes):
+    ins = [mine] + gots
+    vmem = pl.BlockSpec(memory_space=pltpu.VMEM)
     return pl.pallas_call(
-        functools.partial(grad_x_kernel, count, dims),
-        grid_spec=pltpu.PrefetchScalarGridSpec(
-            num_scalar_prefetch=1, grid=(cols,), in_specs=specs + [whole_spec(v) for v in more],
-            out_specs=pl.BlockSpec((1, rows, block, lanes), lambda k, s: (k, 0, 0, 0)),
-            scratch_shapes=[pltpu.VMEM((16 * rows, lanes * cols), BF), pltpu.VMEM((32 * cols, (lanes - 128) * rows), BF),
-                            pltpu.VMEM((32, 128 * rows * cols), F32)]),
-        out_shape=sds((cols, rows, block, lanes), BF),
-        compiler_params=pltpu.CompilerParams(vmem_limit_bytes=48 << 20),
-        cost_estimate=pl.CostEstimate(flops=2 * count * n * m * lanes * cols, bytes_accessed=1 << 23, transcendentals=0),
-    )(my_col.reshape(1), *flat, *more)
-
-
-def grad_out_kernel(count, r_cols, s_ref, *refs):
-    pairs, routers, out = refs[:2 * count], refs[2 * count:3 * count], refs[3 * count]
-    c = s_ref[0] ^ pl.program_id(0)
-    rows = out.shape[1]
-    g = mm(pairs[0][...], pairs[1][...], TN)
-    r = routers[0][...]
-    for i in range(1, count):
-        g = g + mm(pairs[2 * i][...], pairs[2 * i + 1][...], TN)
-        r = r + routers[i][...]
-    n = g.shape[0] // rows
-    out[0, :, :n] = g.astype(BF).reshape(rows, n, 256)
-    put = one_hot((r.shape[1], 128), lambda i, j: (j < r_cols) & (i == c * r_cols + j))
-    w = mm(r.astype(BF), put).astype(BF).reshape(rows, r.shape[0] // rows, 128)
-    half = w.shape[1] // 2
-    out[0, :, n:, :128] = w[:, :half]
-    out[0, :, n:, 128:] = w[:, half:]
-
-
-def grad_out_blocks(pairs, routers, rows, cols, r_cols, my_col):
-    count = len(pairs)
-    n, m = pairs[0][0].shape
-    flat = [v for p in pairs for v in p]
-    specs = [pl.BlockSpec((n, m), lambda k, s: (0, 0)), pl.BlockSpec((n, 256), lambda k, s: (0, k))] * count
-    block = m // rows + routers[0].shape[0] // rows // 2
-    return pl.pallas_call(
-        functools.partial(grad_out_kernel, count, r_cols),
-        grid_spec=pltpu.PrefetchScalarGridSpec(
-            num_scalar_prefetch=1, grid=(cols,), in_specs=specs + [whole_spec(v) for v in routers],
-            out_specs=pl.BlockSpec((1, rows, block, 256), lambda k, s: (k, 0, 0, 0))),
-        out_shape=sds((cols, rows, block, 256), BF),
-        compiler_params=pltpu.CompilerParams(vmem_limit_bytes=48 << 20),
-        cost_estimate=pl.CostEstimate(flops=2 * count * n * m * 256 * cols, bytes_accessed=1 << 23, transcendentals=0),
-    )(my_col.reshape(1), *flat, *routers)
+        functools.partial(kernel, len(ins)), in_specs=[vmem] * len(ins), out_specs=[vmem] * len(shapes),
+        out_shape=[sds(s) for s in shapes], scratch_shapes=[pltpu.VMEM(mine.shape, F32)],
+    )(*ins)
 
 
 def weights_part_kernel(cols, sets, lead, *refs):
@@ -926,13 +1026,14 @@
     here, lanes = w_in_x.shape
     inner, width = lanes * cols, here * rows
     taps, share = conv_w.shape
-    packed, other = pack_params(w_in_x, w_dt, w_xproj, conv_w, conv_b, dt_bias, a_log, d_skip, gain_mix, gain_moe, w_out, w_router)
+    packed, other = pack_params(w_in_x, w_dt, w_xproj, conv_w, conv_b, dt_bias, a_log, d_skip, gain_mix, gain_moe, w_in_z,
+                                w_out, w_router)
     mine = gather_far(packed)
-    late_z, other, _ = lax.optimization_barrier((w_in_z, other, mine))
-    mine_z, mine_o = gather_far(late_z), gather_far(other)
+    other, _ = lax.optimization_barrier((other, mine))
+    mine_o = gather_far(other)
     near = gather_plane(mine)
-    mine_z, mine_o, _ = lax.optimization_barrier((mine_z, mine_o, near[-1]))
-    near_z, near_o = gather_plane(mine_z), gather_plane(mine_o)
+    mine_o, _ = lax.optimization_barrier((mine_o, near[-1]))
+    near_o = gather_plane(mine_o)
     first = gather_core(near)
     dims = (w_dt.shape[0], w_xproj.shape[1], w_xproj.shape[0], share, gain_mix.shape[0], taps, rows, cols)
     full_x, full_dt, full_xpT, par, a_neg, a_two, gx, gm = unpack_call(
@@ -942,11 +1043,11 @@
         [(16 * rows, inner), (32 * cols, (lanes - 128) * rows), (32, 128 * rows * cols)])
 
     def rest(done):
-        z, o, done = lax.optimization_barrier((near_z, near_o, done))
-        (full_z,) = assemble(gather_core(z), [((0, here, lanes), 0, put_block)], [(width, inner)])
-        full_out, router_f = unpack_call(
-            unpack_other, gather_core(o), (w_out.shape[0], w_out.shape[1], w_router.shape[1], cols),
-            [sds((inner, width), BF), sds((width, w_router.shape[1] * cols))], [(inner, 256 * cols), (width, 128 * cols)])
+        o, done = lax.optimization_barrier((near_o, done))
+        full_z, full_out, router_f = unpack_call(
+            unpack_other, gather_core(o), (here, w_out.shape[0], w_out.shape[1], w_router.shape[1], cols),
+            [sds((width, inner), BF), sds((inner, width), BF), sds((width, w_router.shape[1] * cols))],
+            [(inner, 256 * cols), (width, 128 * cols)])
         return full_z, full_out, router_f, done
     return rest, full_x, full_xpT, full_dt, par, a_neg, a_two, gx, gm
 
@@ -985,7 +1086,9 @@
     done = done[here:].reshape(-1)
     sm = done[cut[3]:cut[4]].reshape(-1, share)
     gm = gain_mix.shape[0]
-    small = (done[cut[0]:cut[1]].reshape(w_xproj.shape), done[cut[1]:cut[2]].reshape(w_dt.shape), sm[:-1], sm[-1, :gm], sm[-1, gm:],
+    taps = conv_w.shape[0]
+    chan = (sm[:taps], sm[taps], sm[taps + 1], sm[taps + 2:taps + 2 + NS], sm[taps + 2 + NS])
+    small = (done[cut[0]:cut[1]].reshape(w_xproj.shape), done[cut[1]:cut[2]].reshape(w_dt.shape), chan, sm[-1, :gm], sm[-1, gm:],
              done[cut[2]:cut[3]].reshape(w_router.shape))
     return (grad_x_block, grad_z_block, grad_out_block), small
 
@@ -1023,8 +1126,8 @@
     sort = (source[:, None] == jnp.arange(rows * message, dtype=jnp.int32)[None, :]).astype(BF)
 
     def mixer(x):
-        nm, inner_x, u, dl, pT, ssm, starts = mixer_forward(x, gain_mix_f, full_x, full_xpT, full_dt, par, a_two, QB)
-        return dict(x=x, nm=nm, inner=inner_x, u=u, dl=dl, pT=pT, ssm=ssm.reshape(length, inner), starts=starts)
+        nm, inner_x, conv, u, dl, pT, ssm, starts = mixer_forward(x, gain_mix_f, full_x, full_xpT, full_dt, par, a_two, QB)
+        return dict(x=x, nm=nm, inner=inner_x, conv=conv, u=u, dl=dl, pT=pT, ssm=ssm.reshape(length, inner), starts=starts)
 
     def router(k, route, n_live, grad):
         n_live = n_live.reshape(1)
@@ -1067,7 +1170,7 @@
         return dict(mixed_out=mixed_out, gh=gh, gs=gs.reshape(k["u"].shape), gz=gz, gm=gm, router=g_router, gain_moe=g_moe)
 
     def unscan(k, gs):
-        gi, g_xp, g_dt, g_chan = scan_backward(k["u"], k["dl"], gs, k["inner"], k["pT"], k["starts"], full_xpT, full_dt, par, a_neg)
+        gi, g_xp, g_dt, g_chan = scan_backward(k["u"], k["dl"], gs, k["conv"], k["inner"], k["pT"], k["starts"], full_xpT, full_dt, par, a_neg)
         return dict(gi=gi, xproj=g_xp, dt=g_dt, chan=g_chan)
 
     def unproject(k, g):
@@ -1085,25 +1188,26 @@
         k = mixer(x)
         if s == 0:
             full_z, full_out, router_f, k["ssm"] = rest_of(k["ssm"])
-        if last is not None:
-            own = arrive(home(last))
-            k["ssm"], own = after((k["ssm"], own))
-            owns.append(own)
-        last, k = router(k, routes[s], lengths[s], cotangent[s])
+        before, (last, k) = last, router(k, routes[s], lengths[s], cotangent[s])
         ks.append(k)
-    got = home(last)
+        if before is not None:
+            got, last = after((home(before), last))
+            owns.append(arrive(got))
+    owns.append(arrive(home(last)))
     sets, sent = [], []
     for s in range(seqs):
-        if s == seqs - 1:
-            if sets:
-                got, outs = after((got, outs))
-                sent[-1] = from_experts(outs)
-            owns.append(arrive(got))
         bufs = gather_cols(owns[s])
+        if s == seqs - 2:
+            bufs, owns[-1] = after((bufs, owns[-1]))
         outs, more = expert_both(bufs, w_up, w_down)
         sets.append((bufs, more))
         sent.append(from_experts(outs))
     backs = [home(v) for v in sent]
+    grads_w = []
+    for lead in (True, False):
+        ins, sent[0], _ = after(([b + [v[1 if lead else 0]] for b, v in sets], sent[0], grads_w))
+        grads_w.append(expert_weights_part(ins, lead, width, w_up.shape[2]))
+    backs[0], (grad_w_up, grad_w_down) = after((backs[0], grads_w))
     gs_ = []
     for s in range(seqs):
         g = unroute(ks[s], backs[s])
@@ -1115,47 +1219,42 @@
     g = gs_[-1]
     nms, gateds = [k["nm"] for k in ks], [k["gated"] for k in ks]
     if tiled:
-        out_parts = grad_out_blocks([(v, q["gm"]) for v, q in zip(gateds, gs_)], [q["router"] for q in gs_], rows, cols,
-                                    w_router.shape[1], my_col)
-        z_parts = column_blocks([(v, q["gz"]) for v, q in zip(nms, gs_)], cols, my_col)
-        z_sums, first = reduce_core([z_parts[k].reshape(rows, here, lanes) for k in range(cols)],
-                                    lambda give: unproject(ks[0], dict(gs_[0], gi=after((gs_[0]["gi"], give))[0])))
-        out_sums, _ = reduce_core([out_parts[k] for k in range(cols)])
-        z_own, z_give = reduce_plane_give(z_sums)
-        out_own, out_give = reduce_plane_give(out_sums)
-        g["gs"], z_give, out_give = after((g["gs"], z_give, out_give))
+        block = (here + here // 2 + out_rows + w_router.shape[0] // 2, 256)
+        keep, give = grad_other_blocks([(v, q["gz"]) for v, q in zip(nms, gs_)], [(v, q["gm"]) for v, q in zip(gateds, gs_)],
+                                       [q["router"] for q in gs_], block, rows, cols, w_router.shape[1], my_col)
+        far, plane, core = stages()
+
+        def first_tokens(v):
+            return unproject(ks[0], dict(gs_[0], gi=after((gs_[0]["gi"], v))[0]))
+        got, first = between(first_tokens, give, exchange(give, core))
+        if seqs > 1:
+            gs_[0].update(first)
+        own, gives = split_near(keep, got)
+        g["gs"], gives = after((g["gs"], gives))
+        gots = [exchange(v, p) for v, p in zip(gives, plane[1:])]
         g.update(unscan(ks[-1], g["gs"]))
-        z_total, _ = reduce_plane(z_own, z_give)
-        out_total, _ = reduce_plane(out_own, out_give)
-        z_total, out_total, g["gi"] = after((z_total, out_total, g["gi"]))
-        z_done, _ = reduce_far(z_total)
-        out_done, _ = reduce_far(out_total)
-        gs_[0].update(first)
-        for s in range(1, seqs - 1):
+        gots, g["gi"] = after((gots, g["gi"]))
+        mine, gives = split_far(own, gots)
+        g["gi"], gives = after((g["gi"], gives))
+        gots_o = [exchange(v, p) for v, p in zip(gives, far[1:])]
+        mine_o = mine
+        dims = (w_dt.shape[0], w_xproj.shape[1], w_xproj.shape[0], conv_w.shape[1], gain_mix.shape[0], rows, cols)
+        for s in range(1, seqs):
             gs_[s].update(unproject(ks[s], gs_[s]))
-        dims = (w_dt.shape[0], w_xproj.shape[1], w_xproj.shape[0], conv_w.shape[1], gain_mix.shape[0], rows, cols)
-        g.update(unproject(ks[-1], g))
-        x_parts = grad_x_blocks([(v, q["gi"]) for v, q in zip(nms, gs_)], gs_, dims, my_col)
-
-        def weights(lead):
-            def work(give):
-                ins, _ = after(([b + [m[1 if lead else 0]] for b, m in sets], give))
-                return expert_weights_part(ins, lead, width, w_up.shape[2])
-            return work
-        x_sums, _ = reduce_core([x_parts[k] for k in range(cols)])
-        x_own, x_give = reduce_plane_give(x_sums)
-        x_total, grad_w_up = reduce_plane(x_own, x_give, weights(True))
-        done, grad_w_down = reduce_far(x_total, weights(False))
-        xp = up_to(w_xproj.shape[0], 128)
-        sm = done[here + 16:, xp:]
-        share = conv_w.shape[1]
-        gm = gain_mix.shape[0]
-        chan = sm[:taps + 3 + NS, :share]
-        half = w_router.shape[0] // 2
-        router_done = jnp.concatenate([out_done[out_rows:, :w_router.shape[1]], out_done[out_rows:, 128:128 + w_router.shape[1]]], axis=0)
-        small = (done[here + 16:here + 16 + w_xproj.shape[1], :w_xproj.shape[0]].T, done[here:here + w_dt.shape[0]], chan,
-                 sm[taps + 3 + NS, :gm], sm[taps + 4 + NS, :gm], router_done)
-        blocks = (done[:here], z_done, out_done[:out_rows, :out_lanes])
+        keep, give = grad_x_blocks([(v, q["gi"]) for v, q in zip(nms, gs_)], gs_, dims, my_col)
+        own, gives = split_near(keep, exchange(give, core))
+        gots = [exchange(v, p) for v, p in zip(gives, plane[1:])]
+        gots_o, _ = after((gots_o, gives))
+        gz, go, g_router = finish(finish_other_kernel, mine_o, gots_o, [w_in_z.shape, w_out.shape, w_router.shape])
+        gots, gz, go, g_router = after((gots, gz, go, g_router))
+        mine, gives = split_far(own, gots)
+        gots = [exchange(v, p) for v, p in zip(gives, far[1:])]
+        share, gshare = conv_w.shape[1], gain_mix.shape[0]
+        gx, g_xproj, g_dt, gcw, gcb, gdb, gal, gds, g_mix, g_moe = finish(
+            finish_x_kernel, mine, gots,
+            [w_in_x.shape, w_xproj.shape, w_dt.shape, conv_w.shape, (1, share), (1, share), a_log.shape, (1, share), (1, gshare), (1, gshare)])
+        blocks = (gx, gz, go)
+        small = (g_xproj, g_dt, (gcw, gcb[0], gdb[0], gal, gds[0]), g_mix[0], g_moe[0], g_router)
     else:
         g.update(unscan(ks[-1], g["gs"]))
         for k, q in zip(ks, gs_):
@@ -1163,21 +1262,19 @@
         names = ("xproj", "dt", "chan", "gain_mix", "gain_moe", "router")
         total = {n: sum(q[n] for q in gs_) for n in names}
         blocks, small = grads_generic(nms, gateds, gs_, total, w_in_x, w_in_z, w_xproj, w_dt, w_out, w_router, gain_mix, conv_w)
-        grad_w_up = expert_weights_part([b + [m[1]] for b, m in sets], True, width, w_up.shape[2])
-        grad_w_down = expert_weights_part([b + [m[0]] for b, m in sets], False, width, w_up.shape[2])
-    g_xproj, g_dt, chan, g_mix, g_moe, g_router = small
+    g_xproj, g_dt, (gcw, gcb, gdb, gal, gds), g_mix, g_moe, g_router = small
     return (
         jnp.stack([q["mixed_out"] for q in gs_]),
         jnp.stack([q["tokens"] for q in gs_]),
         blocks[0],
         blocks[1],
-        chan[:taps],
-        chan[taps],
+        gcw,
+        gcb,
         g_xproj,
         g_dt,
-        chan[taps + 1],
-        chan[taps + 2:taps + 2 + NS],
-        chan[taps + 2 + NS],
+        gdb,
+        gal,
+        gds,
         blocks[2],
         g_mix,
         g_moe,

time: 592 us -> 530 us (0.90)
  local copies, waits for them, and re-layouts: 57.7 us -> 35.7 us
  waiting for transfers between devices: 139 us -> 118 us
  other arithmetic: 33.9 us -> 16.3 us
  Pallas kernels: 264 us -> 271 us
  starting transfers between devices: 77.9 us -> 71.3 us
    all_to_all x4, waiting for transfers between devices: 33.7 us -> 10.1 us  [home(): lax.all_to_all(rows_out, 'row', split_axis=0, concat_axis=0, tiled=True)]
    add x12 -> x0, other arithmetic: 10.5 us -> none  [the longest x3 6.06 us: reduce_plane(): return (functools.reduce(lambda t, v: t + v.astype(F32), got, own), result)]
    ppermute x57 -> x42, starting transfers between devices: 51 us -> 42.1 us  [swap(): return lax.ppermute(x, axis, [(i, i ^ bit) for i in range(n)])]
    slice x11 -> x1, local copies, waits for them, and re-layouts: 9.05 us -> 0.58 us  [on_device(): before, (last, k) = (last, router(k, routes[s], lengths[s], cotangent[s]))]
    pallas_call x2, Pallas kernels: 89.8 us -> 81.5 us  [scan_backward(): pl.pallas_call(functools.partial(scan_back_kernel, T, Q, Q2, R), grid=(C,...]
    pallas_call x4 -> x6, Pallas kernels: 17.1 us -> 24.7 us  [the longest x2 18.3 us: grad_blocks(): pl.pallas_call(kernel, grid_spec=pltpu.PrefetchScalarGridSpec(num_scalar_...]
    all_to_all x4, starting transfers between devices: 18.4 us -> 25.1 us  [home(): lax.all_to_all(rows_out, 'row', split_axis=0, concat_axis=0, tiled=True)]
    pallas_call x6 -> x8, Pallas kernels: 56.7 us -> 62.2 us  [one_call(): pl.pallas_call(kernel, in_specs=[smem] * len(scalars) + [vmem] * len(ins)...]
  transfers between devices with their start and end apart: 67 -> 50, of which waited for: 18 -> 19; matrix products, arithmetic and copies ran while one was open for 7% -> 5% of each run, Pallas kernels for 38% -> 40%
where the time goes in v3:
time: 530 us; the launch traced here: 522 us
  Pallas kernels  271 us (51%)
  waiting for transfers between devices  118 us (22%)
  starting transfers between devices  71.3 us (13%)
  local copies, waits for them, and re-layouts  35.7 us (7%)
  other arithmetic  16.3 us (3%)
  matrix products  8.7 us (2%)
    ppermute x42, waiting for transfers between devices, swap(): return lax.ppermute(x, axis, [(i, i ^ bit) for i in range(n)])  104 us
    pallas_call x2, Pallas kernels, scan_backward(): pl.pallas_call(functools.partial(scan_back_kernel, T, Q, Q2, R), grid=(C,...  81.5 us
    pallas_call x8, Pallas kernels, one_call(): pl.pallas_call(kernel, in_specs=[smem] * len(scalars) + [vmem] * len(ins)...  62.2 us
    pallas_call x4, Pallas kernels, per_expert(): pl.pallas_call(kernel, grid=(ins[0].shape[0],), in_specs=[tok(a) for a in...  51 us
    ppermute x42, starting transfers between devices, swap(): return lax.ppermute(x, axis, [(i, i ^ bit) for i in range(n)])  42.1 us
    pallas_call x2, Pallas kernels, mixer_forward(): pl.pallas_call(functools.partial(mixer_kernel, T, Q, R), grid=(C,), in_sp...  41 us
    unnamed x122, local copies, waits for them, and re-layouts  29.3 us
    all_to_all x4, starting transfers between devices, home(): lax.all_to_all(rows_out, 'row', split_axis=0, concat_axis=0, tiled=True)  25.1 us
  transfers between devices with their start and end apart: 50, of which 19 were waited for; matrix products, arithmetic and copies ran while one was open for 5% of the time, Pallas kernels for 40%

profile of v3, /device:TPU:0, one launch (start us, length us, event | category | flops | bytes accessed | tf_op | source)
XLA Modules:
  0.0 522.1 jit_solution(13189004556239508520)
XLA Ops:
  5.3 3.0 collective-permute-start
  8.4 2.6 collective-permute-start.1
  11.6 8.3 %collective-permute-done.1 = bf16[144,384]{1,0:T(8,128)(2,1)S(1)} collective-permute-done((bf16[144,384]{1,0:T(8,128)(2,1)}, bf16[144,384]{1,0:T(8,128)(2,1)S(1)}, u32[]{:S(2)}, u32[]{:S(2)}) %collective-permute-start.1) | collective-permute-done | bytes 110624 | tf_op jit(solution)/shard_map/ppermute | solution.py:390
  20.9 2.6 collective-permute-start.5
  27.6 4.7 collective-permute-done.10
  32.3 2.8 collective-permute-done.5.refs_3_
  35.0 6.3 %collective-permute-done.3.refs_1_ = bf16[4,144,384]{2,1,0:T(8,128)(2,1)} collective-permute-done((bf16[4,144,384]{2,1,0:T(8,128)(2,1)S(1)}, bf16[4,144,384]{2,1,0:T(8,128)(2,1)}, u32[]{:S(2)}, u32[]{:S(2)}) %collective-permute-start.3) | collective-permute-done | bytes 442400 | tf_op jit(solution)/shard_map/ppermute | solution.py:390
  41.9 2.5 collective-permute-start.12
  45.7 5.2 collective-permute-done.12
  54.5 3.2 shard_map.315
  58.2 20.6 %shard_map.316 = (bf16[320,768]{1,0:T(8,128)(2,1)S(1)}, f32[328,1536]{1,0:T(8,128)}, f32[5,8,8,1536]{3,2,1,0:T(8,128)S(1)}, f32[5,8,8,1536]{3,2,1,0:T(8,128)S(1)...) custom-call(bf16[320,768]{1,0:T(8,128)(2,1)S(1)} %get-tuple-element., ...), custom_call_target="tpu_custom_call" | custom-call | flops 40000000000 | bytes 7864320 | tf_op jit(solution)/shard_map/pallas_call | solution.py:134
  83.0 4.1 collective-permute-done.14.refs_2_
  91.2 2.9 slice_bitcast_fusion
  94.2 5.3 %shard_map.317 = (bf16[768,1536]{1,0:T(8,128)(2,1)}, bf16[1536,768]{1,0:T(8,128)(2,1)}, f32[768,32]{1,0:T(8,128)S(1)}) custom-call(s32[2]{0:T(128)S(1)} %pad_add_fusion.me, bf16[4,384,256]{2,1,0:T(8,128)(2,1)S(1)} %pad_maximum_fusion.2.refs_0_, bf16[4,384,256]{2,1,0:T(8,128)(2,1)S(1)} %collective-permute-done.13.refs_1_, ...), custom_call_target="tpu_custom_call" | custom-call | bytes 12582912 | tf_op jit(solution)/shard_map/pallas_call | solution.py:772
  100.3 10.0 %shard_map.318 = (f32[320,1536]{1,0:T(8,128)}, bf16[320,1536]{1,0:T(8,128)(2,1)}, f32[320,768]{1,0:T(8,128)}, bf16[320,448]{1,0:T(8,128)(2,1)}, bf16[448,1536]{1...) custom-call(s32[1]{0:T(128)} %get-tuple-element.419.live_ref, bf16[320,768]{1,0:T(8,128)(2,1)} %copy-done.2, ...), custom_call_target="tpu_custom_call" | custom-call | flops 2264924160 | bytes 14390784 | tf_op jit(solution)/shard_map/pallas_call | solution.py:294
  110.3 8.8 %all-to-all-start = ((bf16[8,56,1536]{2,1,0:T(8,128)(2,1)}), bf16[8,56,1536]{2,1,0:T(8,128)(2,1)}, u32[]{:S(2)}, u32[]{:S(2)}) async-start(bf16[8,56,1536]{2,1,0:T(8,128)(2,1)} %bitcast.82), calls=%async_computation | async-start | bytes 2752512 | tf_op jit(solution)/shard_map/all_to_all | solution.py:1145
  119.1 20.5 %shard_map.319 = (bf16[320,768]{1,0:T(8,128)(2,1)S(1)}, f32[328,1536]{1,0:T(8,128)}, f32[5,8,8,1536]{3,2,1,0:T(8,128)S(1)}, f32[5,8,8,1536]{3,2,1,0:T(8,128)S(1)...) custom-call(bf16[320,768]{1,0:T(8,128)(2,1)S(1)} %get-tuple-element., ...), custom_call_target="tpu_custom_call" | custom-call | flops 40000000000 | bytes 7864320 | tf_op jit(solution)/shard_map/pallas_call | solution.py:134
  143.9 10.0 %shard_map.320 = (f32[320,1536]{1,0:T(8,128)}, bf16[320,1536]{1,0:T(8,128)(2,1)}, f32[320,768]{1,0:T(8,128)}, bf16[320,448]{1,0:T(8,128)(2,1)}, bf16[448,1536]{1...) custom-call(s32[1]{0:T(128)} %get-tuple-element.420.live_ref, bf16[320,768]{1,0:T(8,128)(2,1)} %copy-done.1, ...), custom_call_target="tpu_custom_call" | custom-call | flops 2264924160 | bytes 14390784 | tf_op jit(solution)/shard_map/pallas_call | solution.py:294
  157.1 6.6 %all-to-all-start.1 = ((bf16[8,56,1536]{2,1,0:T(8,128)(2,1)}), bf16[8,56,1536]{2,1,0:T(8,128)(2,1)}, u32[]{:S(2)}, u32[]{:S(2)}) async-start(bf16[8,56,1536]{2,1,0:T(8,128)(2,1)} %bitcast.81), calls=%async_computation.1 | async-start | bytes 2752512 | tf_op jit(solution)/shard_map/all_to_all | solution.py:1145
  163.8 24.4 %collective-permute-done.20.refs_1_ = bf16[4,112,1536]{2,1,0:T(8,128)(2,1)} collective-permute-done((bf16[4,112,1536]{2,1,0:T(8,128)(2,1)S(1)}, bf16[4,112,1536]{2,1,0:T(8,128)(2,1)}, u32[]{:S(2)}, u32[]{:S(2)}) %collective-permute-start.20) | collective-permute-done | bytes 1376288 | tf_op jit(solution)/shard_map/ppermute | solution.py:390
  188.1 7.8 %all-to-all-done.1 = bf16[8,56,1536]{2,1,0:T(8,128)(2,1)} async-done(((bf16[8,56,1536]{2,1,0:T(8,128)(2,1)}), bf16[8,56,1536]{2,1,0:T(8,128)(2,1)}, u32[]{:S(2)}, u32[]{:S(2)}) %all-to-all-start.1) | async-done | bytes 1376288 | tf_op jit(solution)/shard_map/all_to_all | solution.py:1145
  199.5 13.7 %shard_map.321 = (bf16[4,112,1536]{2,1,0:T(8,128)(2,1)}, bf16[4,112,1536]{2,1,0:T(8,128)(2,1)}, bf16[4,112,1536]{2,1,0:T(8,128)(2,1)}, bf16[4,112,1536]{2,1,0:T(...) custom-call(bf16[4,112,1536]{2,1,0:T(8,128)(2,1)} %bitcast.72, ...), custom_call_target="tpu_custom_call" | custom-call | flops 8455716864 | bytes 25952256 | tf_op jit(solution)/shard_map/pallas_call | solution.py:612
  213.7 14.5 %collective-permute-done.26.refs_1_.refs_6_ = bf16[4,112,1536]{2,1,0:T(8,128)(2,1)S(1)} collective-permute-done((bf16[4,112,1536]{2,1,0:T(8,128)(2,1)S(1)}, bf16[4,112,1536]{2,1,0:T(8,128)(2,1)S(1)}, u32[]{:S(2)}, u32[]{:S(2)}) %collective-permute-start.26) | collective-permute-done | bytes 1376288 | tf_op jit(solution)/shard_map/ppermute | solution.py:390
  228.7 2.7 add_convert_fusion.4
  234.9 13.7 %shard_map.322 = (bf16[4,112,1536]{2,1,0:T(8,128)(2,1)}, bf16[4,112,1536]{2,1,0:T(8,128)(2,1)}, bf16[4,112,1536]{2,1,0:T(8,128)(2,1)}, bf16[4,112,1536]{2,1,0:T(...) custom-call(bf16[4,112,1536]{2,1,0:T(8,128)(2,1)} %bitcast.77, bf16[4,112,1536]{2,1,0:T(8,128)(2,1)} %copy-done.35, ...), custom_call_target="tpu_custom_call" | custom-call | flops 8455716864 | bytes 25952256 | tf_op jit(solution)/shard_map/pallas_call | solution.py:612
  248.6 15.3 %collective-permute-done.25 = bf16[4,112,1536]{2,1,0:T(8,128)(2,1)} collective-permute-done((bf16[4,112,1536]{2,1,0:T(8,128)(2,1)}, bf16[4,112,1536]{2,1,0:T(8,128)(2,1)}, u32[]{:S(2)}, u32[]{:S(2)}) %collective-permute-start.25) | collective-permute-done | bytes 1376288 | tf_op jit(solution)/shard_map/ppermute | solution.py:390
  263.9 2.7 add_convert_fusion.3
  268.7 5.9 %all-to-all-start.2 = ((bf16[8,56,1536]{2,1,0:T(8,128)(2,1)}), bf16[8,56,1536]{2,1,0:T(8,128)(2,1)S(1)}, u32[]{:S(2)}, u32[]{:S(2)}) async-start(bf16[8,56,1536]{2,1,0:T(8,128)(2,1)} %bitcast.80), calls=%async_computation.2 | async-start | bytes 2752512 | tf_op jit(solution)/shard_map/all_to_all | solution.py:1145
  274.7 3.2 add_convert_fusion.1
  280.8 11.8 %shard_map.323 = f32[4,768,768]{2,1,0:T(8,128)} custom-call(bf16[4,112,1536]{2,1,0:T(8,128)(2,1)} %bitcast.73, bf16[4,112,1536]{2,1,0:T(8,128)(2,1)} %collective-permute-done.20.refs_1_, bf16[4,112,1536]{2,1,0:T(8,128)(2,1)} %collective-permute-done.21.refs_2_, bf16[4,112,1536]{2,1,0:T(8,128)(2,1)} %collective-permute-done.22.refs_3_, ...), custom_call_target="tpu_custom_call" | custom-call | flops 4227858432 | bytes 25952256 | tf_op jit(solution)/shard_map/pallas_call | solution.py:612
  292.6 11.8 %shard_map.324 = f32[4,768,768]{2,1,0:T(8,128)} custom-call(bf16[4,112,1536]{2,1,0:T(8,128)(2,1)} %bitcast.74, bf16[4,112,1536]{2,1,0:T(8,128)(2,1)} %collective-permute-done.20.refs_1_, bf16[4,112,1536]{2,1,0:T(8,128)(2,1)} %collective-permute-done.21.refs_2_, bf16[4,112,1536]{2,1,0:T(8,128)(2,1)} %collective-permute-done.22.refs_3_, ...), custom_call_target="tpu_custom_call" | custom-call | flops 4227858432 | bytes 25952256 | tf_op jit(solution)/shard_map/pallas_call | solution.py:612
  307.8 12.1 %shard_map.325 = (bf16[320,768]{1,0:T(8,128)(2,1)}, f32[320,768]{1,0:T(8,128)}, f32[320,1536]{1,0:T(8,128)}, bf16[320,1536]{1,0:T(8,128)(2,1)}, bf16[320,1024]{1...) custom-call(s32[1]{0:T(128)} %get-tuple-element.419.live_ref, bf16[448,1536]{1,0:T(8,128)(2,1)} %bitcast.68, ...), custom_call_target="tpu_custom_call" | custom-call | flops 2264924160 | bytes 16818688 | tf_op jit(solution)/shard_map/pallas_call | solution.py:294
  324.2 3.9 all-to-all-start.3
  328.1 40.8 %shard_map.326 = (bf16[320,1536]{1,0:T(8,128)(2,1)}, f32[80,1536]{1,0:T(8,128)S(1)}, f32[48,1536]{1,0:T(8,128)S(1)}, f32[23,1536]{1,0:T(8,128)S(1)}) custom-call(f32[5,8,8,1536]{3,2,1,0:T(8,128)} %copy-done.28, f32[5,8,8,1536]{3,2,1,0:T(8,128)} %get-tuple-element.268.dl_ref, f32[5,8,8,1536]{3,2,1,0:T(8,128)} %bitcast.104, f32[5,8,8,1536]{3,2,1,0:T(8,128)} %copy-done.27, ...), custom_call_target="tpu_custom_call" | custom-call | flops 80000000000 | bytes 7864320 | tf_op jit(solution)/shard_map/pallas_call | solution.py:278
  372.1 12.1 %shard_map.327 = (bf16[320,768]{1,0:T(8,128)(2,1)}, f32[320,768]{1,0:T(8,128)}, f32[320,1536]{1,0:T(8,128)}, bf16[320,1536]{1,0:T(8,128)(2,1)}, bf16[320,1024]{1...) custom-call(s32[1]{0:T(128)} %get-tuple-element.420.live_ref, bf16[448,1536]{1,0:T(8,128)(2,1)} %bitcast.69, ...), custom_call_target="tpu_custom_call" | custom-call | flops 2264924160 | bytes 16818688 | tf_op jit(solution)/shard_map/pallas_call | solution.py:294
  384.2 11.0 %shard_map.328 = (bf16[2,8,384,256]{3,2,1,0:T(8,128)(2,1)}, bf16[2,8,384,256]{3,2,1,0:T(8,128)(2,1)}) custom-call(s32[1]{0:T(128)} %bitcast.3.s_ref, bf16[320,768]{1,0:T(8,128)(2,1)} %copy-done.7, bf16[320,1536]{1,0:T(8,128)(2,1)} %get-tuple-element.288.refs_1_.gz_ref, bf16[320,768]{1,0:T(8,128)(2,1)} %copy-done.8, ...), custom_call_target="tpu_custom_call" | custom-call | flops 3523215360 | bytes 8388608 | tf_op jit(solution)/shard_map/pallas_call | solution.py:824
  395.2 6.4 %shard_map.329 = (f32[320,768]{1,0:T(8,128)}, f32[1,768]{1,0:T(1,128)}) custom-call(bf16[320,1536]{1,0:T(8,128)(2,1)} %get-tuple-element.298.gi_ref.refs_1_, bf16[320,1536]{1,0:T(8,128)(2,1)} %get-tuple-element.288.refs_1_.gz_ref, bf16[768,1536]{1,0:T(8,128)(2,1)} %get-tuple-element.200.wx_ref, bf16[768,1536]{1,0:T(8,128)(2,1)} %get-tuple-element.215.wz_ref, ...), custom_call_target="tpu_custom_call" | custom-call | flops 1509949440 | bytes 9148416 | tf_op jit(solution)/shard_map/pallas_call | solution.py:294
  407.7 40.7 %shard_map.331 = (bf16[320,1536]{1,0:T(8,128)(2,1)}, f32[80,1536]{1,0:T(8,128)S(1)}, f32[48,1536]{1,0:T(8,128)S(1)}, f32[23,1536]{1,0:T(8,128)S(1)}) custom-call(f32[5,8,8,1536]{3,2,1,0:T(8,128)} %copy-done.26, f32[5,8,8,1536]{3,2,1,0:T(8,128)} %get-tuple-element.313.dl_ref, f32[5,8,8,1536]{3,2,1,0:T(8,128)} %bitcast.103, f32[5,8,8,1536]{3,2,1,0:T(8,128)} %copy-done.25, ...), custom_call_target="tpu_custom_call" | custom-call | flops 80000000000 | bytes 7864320 | tf_op jit(solution)/shard_map/pallas_call | solution.py:278
  452.1 3.2 shard_map.332
  455.2 6.2 %shard_map.333 = (f32[320,768]{1,0:T(8,128)}, f32[1,768]{1,0:T(1,128)}) custom-call(bf16[320,1536]{1,0:T(8,128)(2,1)} %get-tuple-element.328.gi_ref.refs_3_, bf16[320,1536]{1,0:T(8,128)(2,1)} %get-tuple-element.289.refs_3_.gz_ref, bf16[768,1536]{1,0:T(8,128)(2,1)} %get-tuple-element.200.wx_ref, bf16[768,1536]{1,0:T(8,128)(2,1)} %get-tuple-element.215.wz_ref, ...), custom_call_target="tpu_custom_call" | custom-call | flops 1509949440 | bytes 9148416 | tf_op jit(solution)/shard_map/pallas_call | solution.py:294
  461.4 7.3 %shard_map.334 = (bf16[2,8,144,384]{3,2,1,0:T(8,128)(2,1)}, bf16[2,8,144,384]{3,2,1,0:T(8,128)(2,1)}) custom-call(s32[1]{0:T(128)} %bitcast.3.s_ref, bf16[320,768]{1,0:T(8,128)(2,1)} %copy-done.7, bf16[320,1536]{1,0:T(8,128)(2,1)} %get-tuple-element.298.gi_ref.refs_1_, bf16[320,768]{1,0:T(8,128)(2,1)} %copy-done.8, ...), custom_call_target="tpu_custom_call" | custom-call | flops 1509949440 | bytes 8388608 | tf_op jit(solution)/shard_map/pallas_call | solution.py:824
  468.7 3.9 collective-permute-done.36
  483.8 5.9 %collective-permute-done.40.refs_1_ = bf16[384,256]{1,0:T(8,128)(2,1)S(1)} collective-permute-done((bf16[384,256]{1,0:T(8,128)(2,1)S(1)}, bf16[384,256]{1,0:T(8,128)(2,1)S(1)}, u32[]{:S(2)}, u32[]{:S(2)}) %collective-permute-start.40) | collective-permute-done | bytes 196640 | tf_op jit(solution)/shard_map/ppermute | solution.py:390
  489.7 2.7 collective-permute-start.42
  494.9 2.4 collective-permute-done.42.refs_3_
  500.1 2.4 shard_map.337
  502.5 4.1 collective-permute-start.43
  511.1 6.4 %collective-permute-done.44.refs_2_ = bf16[144,384]{1,0:T(8,128)(2,1)S(1)} collective-permute-done((bf16[144,384]{1,0:T(8,128)(2,1)}, bf16[144,384]{1,0:T(8,128)(2,1)S(1)}, u32[]{:S(2)}, u32[]{:S(2)}) %collective-permute-start.44) | collective-permute-done | bytes 110624 | tf_op jit(solution)/shard_map/ppermute | solution.py:390
  (221 shorter events, 91.9 us)
Async XLA Ops:
  5.3 6.3 %collective-permute-start = (bf16[144,384]{1,0:T(8,128)(2,1)}, bf16[144,384]{1,0:T(8,128)(2,1)S(1)}, u32[]{:S(2)}, u32[]{:S(2)}) collective-permute-start(bf16[144,384]{1,0:T(8,128)(2,1)} %get-tuple-element.198), channel_id=1, source_target_pairs={{0,8},{4,12},{8,0},{12,4},{16,24},{20,28},{24,16},{28,20},{1,9},{5... | collective-permute-start | bytes 331784 | tf_op jit(solution)/shard_map/ppermute | solution.py:390
  8.4 11.6 %collective-permute-start.1 = (bf16[144,384]{1,0:T(8,128)(2,1)}, bf16[144,384]{1,0:T(8,128)(2,1)S(1)}, u32[]{:S(2)}, u32[]{:S(2)}) collective-permute-start(bf16[144,384]{1,0:T(8,128)(2,1)} %get-tuple-element.198), channel_id=1, source_target_pairs={{0,16},{4,20},{8,24},{12,28},{16,0},{20,4},{24,8},{28,12},{1,17},{... | collective-permute-start | bytes 331784 | tf_op jit(solution)/shard_map/ppermute | solution.py:390
  10.9 9.0 %collective-permute-start.2 = (bf16[144,384]{1,0:T(8,128)(2,1)}, bf16[144,384]{1,0:T(8,128)(2,1)S(1)}, u32[]{:S(2)}, u32[]{:S(2)}) collective-permute-start(bf16[144,384]{1,0:T(8,128)(2,1)} %get-tuple-element.198), channel_id=1, source_target_pairs={{0,24},{4,28},{8,16},{12,20},{16,8},{20,12},{24,0},{28,4},{1,25},{... | collective-permute-start | bytes 331784 | tf_op jit(solution)/shard_map/ppermute | solution.py:390
  20.9 14.1 %collective-permute-start.5 = (bf16[4,144,384]{2,1,0:T(8,128)(2,1)S(1)}, bf16[4,144,384]{2,1,0:T(8,128)(2,1)S(1)}, u32[]{:S(2)}, u32[]{:S(2)}) collective-permute-start(bf16[4,144,384]{2,1,0:T(8,128)(2,1)S(1)} %pad_maximum_fusion.3.refs_0_), channel_id=1, source_target_pairs={{0,6},{1,7},{2,4},{3,5},{4,2},{5,3},{6,0},{7,1},{8,14},{9,15},{10,... | collective-permute-start | bytes 1327112 | tf_op jit(solution)/shard_map/ppermute | solution.py:406
  23.5 17.8 %collective-permute-start.3 = (bf16[4,144,384]{2,1,0:T(8,128)(2,1)S(1)}, bf16[4,144,384]{2,1,0:T(8,128)(2,1)}, u32[]{:S(2)}, u32[]{:S(2)}) collective-permute-start(bf16[4,144,384]{2,1,0:T(8,128)(2,1)S(1)} %pad_maximum_fusion.3.refs_0_), channel_id=1, source_target_pairs={{0,4},{4,0},{8,12},{12,8},{16,20},{20,16},{24,28},{28,24},{1,5},{5... | collective-permute-start | bytes 1327112 | tf_op jit(solution)/shard_map/ppermute | solution.py:390
  24.0 17.3 %collective-permute-start.4 = (bf16[4,144,384]{2,1,0:T(8,128)(2,1)S(1)}, bf16[4,144,384]{2,1,0:T(8,128)(2,1)}, u32[]{:S(2)}, u32[]{:S(2)}) collective-permute-start(bf16[4,144,384]{2,1,0:T(8,128)(2,1)S(1)} %pad_maximum_fusion.3.refs_0_), channel_id=1, source_target_pairs={{0,2},{1,3},{2,0},{3,1},{4,6},{5,7},{6,4},{7,5},{8,10},{9,11},{10,... | collective-permute-start | bytes 1327112 | tf_op jit(solution)/shard_map/ppermute | solution.py:390
  24.5 7.8 %collective-permute-start.10 = (bf16[384,256]{1,0:T(8,128)(2,1)}, bf16[384,256]{1,0:T(8,128)(2,1)S(1)}, u32[]{:S(2)}, u32[]{:S(2)}) collective-permute-start(bf16[384,256]{1,0:T(8,128)(2,1)} %get-tuple-element.207), channel_id=1, source_target_pairs={{0,8},{4,12},{8,0},{12,4},{16,24},{20,28},{24,16},{28,20},{1,9},{5... | collective-permute-start | bytes 589832 | tf_op jit(solution)/shard_map/ppermute | solution.py:390
  26.2 15.6 %collective-permute-start.11 = (bf16[384,256]{1,0:T(8,128)(2,1)}, bf16[384,256]{1,0:T(8,128)(2,1)S(1)}, u32[]{:S(2)}, u32[]{:S(2)}) collective-permute-start(bf16[384,256]{1,0:T(8,128)(2,1)} %get-tuple-element.207), channel_id=1, source_target_pairs={{0,16},{4,20},{8,24},{12,28},{16,0},{20,4},{24,8},{28,12},{1,17},{... | collective-permute-start | bytes 589832 | tf_op jit(solution)/shard_map/ppermute | solution.py:390
  32.3 20.2 %collective-permute-start.6 = (bf16[4,144,384]{2,1,0:T(8,128)(2,1)S(1)}, bf16[4,144,384]{2,1,0:T(8,128)(2,1)S(1)}, u32[]{:S(2)}, u32[]{:S(2)}) collective-permute-start(bf16[4,144,384]{2,1,0:T(8,128)(2,1)S(1)} %pad_maximum_fusion.3.refs_0_), channel_id=1, source_target_pairs={{0,1},{1,0},{2,3},{3,2},{4,5},{5,4},{6,7},{7,6},{8,9},{9,8},{10,11... | collective-permute-start | bytes 1327112 | tf_op jit(solution)/shard_map/ppermute | solution.py:390
  35.0 18.9 %collective-permute-start.9 = (bf16[4,144,384]{2,1,0:T(8,128)(2,1)S(1)}, bf16[4,144,384]{2,1,0:T(8,128)(2,1)S(1)}, u32[]{:S(2)}, u32[]{:S(2)}) collective-permute-start(bf16[4,144,384]{2,1,0:T(8,128)(2,1)S(1)} %collective-permute-done.5.refs_3_), channel_id=1, source_target_pairs={{0,1},{1,0},{2,3},{3,2},{4,5},{5,4},{6,7},{7,6},{8,9},{9,8},{10,11... | collective-permute-start | bytes 1327112 | tf_op jit(solution)/shard_map/ppermute | solution.py:390
  41.3 13.2 %collective-permute-start.7 = (bf16[4,144,384]{2,1,0:T(8,128)(2,1)}, bf16[4,144,384]{2,1,0:T(8,128)(2,1)S(1)}, u32[]{:S(2)}, u32[]{:S(2)}) collective-permute-start(bf16[4,144,384]{2,1,0:T(8,128)(2,1)} %collective-permute-done.3.refs_1_), channel_id=1, source_target_pairs={{0,1},{1,0},{2,3},{3,2},{4,5},{5,4},{6,7},{7,6},{8,9},{9,8},{10,11... | collective-permute-start | bytes 1327112 | tf_op jit(solution)/shard_map/ppermute | solution.py:390
  41.3 13.2 %collective-permute-start.8 = (bf16[4,144,384]{2,1,0:T(8,128)(2,1)}, bf16[4,144,384]{2,1,0:T(8,128)(2,1)S(1)}, u32[]{:S(2)}, u32[]{:S(2)}) collective-permute-start(bf16[4,144,384]{2,1,0:T(8,128)(2,1)} %collective-permute-done.4.refs_2_), channel_id=1, source_target_pairs={{0,1},{1,0},{2,3},{3,2},{4,5},{5,4},{6,7},{7,6},{8,9},{9,8},{10,11... | collective-permute-start | bytes 1327112 | tf_op jit(solution)/shard_map/ppermute | solution.py:390
  41.9 8.9 %collective-permute-start.12 = (bf16[384,256]{1,0:T(8,128)(2,1)}, bf16[384,256]{1,0:T(8,128)(2,1)S(1)}, u32[]{:S(2)}, u32[]{:S(2)}) collective-permute-start(bf16[384,256]{1,0:T(8,128)(2,1)} %get-tuple-element.207), channel_id=1, source_target_pairs={{0,24},{4,28},{8,16},{12,20},{16,8},{20,12},{24,0},{28,4},{1,25},{... | collective-permute-start | bytes 589832 | tf_op jit(solution)/shard_map/ppermute | solution.py:390
  50.9 32.1 %collective-permute-start.13 = (bf16[4,384,256]{2,1,0:T(8,128)(2,1)S(1)}, bf16[4,384,256]{2,1,0:T(8,128)(2,1)S(1)}, u32[]{:S(2)}, u32[]{:S(2)}) collective-permute-start(bf16[4,384,256]{2,1,0:T(8,128)(2,1)S(1)} %pad_maximum_fusion.2.refs_0_), channel_id=1, source_target_pairs={{0,4},{4,0},{8,12},{12,8},{16,20},{20,16},{24,28},{28,24},{1,5},{5... | collective-permute-start | bytes 2359304 | tf_op jit(solution)/shard_map/ppermute | solution.py:390
  52.5 34.6 %collective-permute-start.14 = (bf16[4,384,256]{2,1,0:T(8,128)(2,1)S(1)}, bf16[4,384,256]{2,1,0:T(8,128)(2,1)}, u32[]{:S(2)}, u32[]{:S(2)}) collective-permute-start(bf16[4,384,256]{2,1,0:T(8,128)(2,1)S(1)} %pad_maximum_fusion.2.refs_0_), channel_id=1, source_target_pairs={{0,2},{1,3},{2,0},{3,1},{4,6},{5,7},{6,4},{7,5},{8,10},{9,11},{10,... | collective-permute-start | bytes 2359304 | tf_op jit(solution)/shard_map/ppermute | solution.py:390
  53.9 34.0 %collective-permute-start.15 = (bf16[4,384,256]{2,1,0:T(8,128)(2,1)S(1)}, bf16[4,384,256]{2,1,0:T(8,128)(2,1)}, u32[]{:S(2)}, u32[]{:S(2)}) collective-permute-start(bf16[4,384,256]{2,1,0:T(8,128)(2,1)S(1)} %pad_maximum_fusion.2.refs_0_), channel_id=1, source_target_pairs={{0,6},{1,7},{2,4},{3,5},{4,2},{5,3},{6,0},{7,1},{8,14},{9,15},{10,... | collective-permute-start | bytes 2359304 | tf_op jit(solution)/shard_map/ppermute | solution.py:406
  87.9 6.2 %collective-permute-start.16 = (bf16[4,384,256]{2,1,0:T(8,128)(2,1)S(1)}, bf16[4,384,256]{2,1,0:T(8,128)(2,1)}, u32[]{:S(2)}, u32[]{:S(2)}) collective-permute-start(bf16[4,384,256]{2,1,0:T(8,128)(2,1)S(1)} %pad_maximum_fusion.2.refs_0_), channel_id=1, source_target_pairs={{0,1},{1,0},{2,3},{3,2},{4,5},{5,4},{6,7},{7,6},{8,9},{9,8},{10,11... | collective-permute-start | bytes 2359304 | tf_op jit(solution)/shard_map/ppermute | solution.py:390
  87.9 6.2 %collective-permute-start.17 = (bf16[4,384,256]{2,1,0:T(8,128)(2,1)S(1)}, bf16[4,384,256]{2,1,0:T(8,128)(2,1)}, u32[]{:S(2)}, u32[]{:S(2)}) collective-permute-start(bf16[4,384,256]{2,1,0:T(8,128)(2,1)S(1)} %collective-permute-done.13.refs_1_), channel_id=1, source_target_pairs={{0,1},{1,0},{2,3},{3,2},{4,5},{5,4},{6,7},{7,6},{8,9},{9,8},{10,11... | collective-permute-start | bytes 2359304 | tf_op jit(solution)/shard_map/ppermute | solution.py:390
  88.4 5.7 %collective-permute-start.18 = (bf16[4,384,256]{2,1,0:T(8,128)(2,1)}, bf16[4,384,256]{2,1,0:T(8,128)(2,1)}, u32[]{:S(2)}, u32[]{:S(2)}) collective-permute-start(bf16[4,384,256]{2,1,0:T(8,128)(2,1)} %collective-permute-done.14.refs_2_), channel_id=1, source_target_pairs={{0,1},{1,0},{2,3},{3,2},{4,5},{5,4},{6,7},{7,6},{8,9},{9,8},{10,11... | collective-permute-start | bytes 2359304 | tf_op jit(solution)/shard_map/ppermute | solution.py:390
  88.4 5.7 %collective-permute-start.19 = (bf16[4,384,256]{2,1,0:T(8,128)(2,1)}, bf16[4,384,256]{2,1,0:T(8,128)(2,1)}, u32[]{:S(2)}, u32[]{:S(2)}) collective-permute-start(bf16[4,384,256]{2,1,0:T(8,128)(2,1)} %collective-permute-done.15.refs_3_), channel_id=1, source_target_pairs={{0,1},{1,0},{2,3},{3,2},{4,5},{5,4},{6,7},{7,6},{8,9},{9,8},{10,11... | collective-permute-start | bytes 2359304 | tf_op jit(solution)/shard_map/ppermute | solution.py:390
  110.3 43.6 %all-to-all-start = ((bf16[8,56,1536]{2,1,0:T(8,128)(2,1)}), bf16[8,56,1536]{2,1,0:T(8,128)(2,1)}, u32[]{:S(2)}, u32[]{:S(2)}) async-start(bf16[8,56,1536]{2,1,0:T(8,128)(2,1)} %bitcast.82), calls=%async_computation | async-start | bytes 2752512 | tf_op jit(solution)/shard_map/all_to_all | solution.py:1145
  156.2 32.0 %collective-permute-start.20 = (bf16[4,112,1536]{2,1,0:T(8,128)(2,1)S(1)}, bf16[4,112,1536]{2,1,0:T(8,128)(2,1)}, u32[]{:S(2)}, u32[]{:S(2)}) collective-permute-start(bf16[4,112,1536]{2,1,0:T(8,128)(2,1)S(1)} %bitcast.70), channel_id=1, source_target_pairs={{0,2},{1,3},{2,0},{3,1},{4,6},{5,7},{6,4},{7,5},{8,10},{9,11},{10,... | collective-permute-start | bytes 4128776 | tf_op jit(solution)/shard_map/ppermute | solution.py:390
  157.1 38.9 %all-to-all-start.1 = ((bf16[8,56,1536]{2,1,0:T(8,128)(2,1)}), bf16[8,56,1536]{2,1,0:T(8,128)(2,1)}, u32[]{:S(2)}, u32[]{:S(2)}) async-start(bf16[8,56,1536]{2,1,0:T(8,128)(2,1)} %bitcast.81), calls=%async_computation.1 | async-start | bytes 2752512 | tf_op jit(solution)/shard_map/all_to_all | solution.py:1145
  163.7 34.5 %collective-permute-start.21 = (bf16[4,112,1536]{2,1,0:T(8,128)(2,1)S(1)}, bf16[4,112,1536]{2,1,0:T(8,128)(2,1)}, u32[]{:S(2)}, u32[]{:S(2)}) collective-permute-start(bf16[4,112,1536]{2,1,0:T(8,128)(2,1)S(1)} %bitcast.71), channel_id=1, source_target_pairs={{0,1},{1,0},{2,3},{3,2},{4,5},{5,4},{6,7},{7,6},{8,9},{9,8},{10,11... | collective-permute-start | bytes 4128776 | tf_op jit(solution)/shard_map/ppermute | solution.py:390
  188.1 10.1 %collective-permute-start.22 = (bf16[4,112,1536]{2,1,0:T(8,128)(2,1)}, bf16[4,112,1536]{2,1,0:T(8,128)(2,1)}, u32[]{:S(2)}, u32[]{:S(2)}) collective-permute-start(bf16[4,112,1536]{2,1,0:T(8,128)(2,1)} %collective-permute-done.20.refs_1_), channel_id=1, source_target_pairs={{0,1},{1,0},{2,3},{3,2},{4,5},{5,4},{6,7},{7,6},{8,9},{9,8},{10,11... | collective-permute-start | bytes 4128776 | tf_op jit(solution)/shard_map/ppermute | solution.py:390
  198.2 30.0 %collective-permute-start.26 = (bf16[4,112,1536]{2,1,0:T(8,128)(2,1)S(1)}, bf16[4,112,1536]{2,1,0:T(8,128)(2,1)S(1)}, u32[]{:S(2)}, u32[]{:S(2)}) collective-permute-start(bf16[4,112,1536]{2,1,0:T(8,128)(2,1)S(1)} %bitcast.75), channel_id=1, source_target_pairs={{0,2},{1,3},{2,0},{3,1},{4,6},{5,7},{6,4},{7,5},{8,10},{9,11},{10,... | collective-permute-start | bytes 4128776 | tf_op jit(solution)/shard_map/ppermute | solution.py:390
  213.2 15.6 %collective-permute-start.24 = (bf16[4,112,1536]{2,1,0:T(8,128)(2,1)}, bf16[4,112,1536]{2,1,0:T(8,128)(2,1)S(1)}, u32[]{:S(2)}, u32[]{:S(2)}) collective-permute-start(bf16[4,112,1536]{2,1,0:T(8,128)(2,1)} %get-tuple-element.234), channel_id=1, source_target_pairs={{0,1},{1,0},{2,3},{3,2},{4,5},{5,4},{6,7},{7,6},{8,9},{9,8},{10,11... | collective-permute-start | bytes 4128776 | tf_op jit(solution)/shard_map/ppermute | solution.py:390
  213.2 19.4 %collective-permute-start.27 = (bf16[4,112,1536]{2,1,0:T(8,128)(2,1)S(1)}, bf16[4,112,1536]{2,1,0:T(8,128)(2,1)S(1)}, u32[]{:S(2)}, u32[]{:S(2)}) collective-permute-start(bf16[4,112,1536]{2,1,0:T(8,128)(2,1)S(1)} %bitcast.76), channel_id=1, source_target_pairs={{0,1},{1,0},{2,3},{3,2},{4,5},{5,4},{6,7},{7,6},{8,9},{9,8},{10,11... | collective-permute-start | bytes 4128776 | tf_op jit(solution)/shard_map/ppermute | solution.py:390
  228.2 20.4 %collective-permute-start.23 = (bf16[4,112,1536]{2,1,0:T(8,128)(2,1)}, bf16[4,112,1536]{2,1,0:T(8,128)(2,1)}, u32[]{:S(2)}, u32[]{:S(2)}) collective-permute-start(bf16[4,112,1536]{2,1,0:T(8,128)(2,1)} %get-tuple-element.232), channel_id=1, source_target_pairs={{0,1},{1,0},{2,3},{3,2},{4,5},{5,4},{6,7},{7,6},{8,9},{9,8},{10,11... | collective-permute-start | bytes 4128776 | tf_op jit(solution)/shard_map/ppermute | solution.py:390
  231.5 32.4 %collective-permute-start.25 = (bf16[4,112,1536]{2,1,0:T(8,128)(2,1)}, bf16[4,112,1536]{2,1,0:T(8,128)(2,1)}, u32[]{:S(2)}, u32[]{:S(2)}) collective-permute-start(bf16[4,112,1536]{2,1,0:T(8,128)(2,1)} %add_convert_fusion.4), channel_id=1, source_target_pairs={{0,2},{1,3},{2,0},{3,1},{4,6},{5,7},{6,4},{7,5},{8,10},{9,11},{10,... | collective-permute-start | bytes 4128776 | tf_op jit(solution)/shard_map/ppermute | solution.py:390
  248.5 26.1 %collective-permute-start.30 = (bf16[4,112,1536]{2,1,0:T(8,128)(2,1)}, bf16[4,112,1536]{2,1,0:T(8,128)(2,1)}, u32[]{:S(2)}, u32[]{:S(2)}) collective-permute-start(bf16[4,112,1536]{2,1,0:T(8,128)(2,1)} %get-tuple-element.273), channel_id=1, source_target_pairs={{0,1},{1,0},{2,3},{3,2},{4,5},{5,4},{6,7},{7,6},{8,9},{9,8},{10,11... | collective-permute-start | bytes 4128776 | tf_op jit(solution)/shard_map/ppermute | solution.py:390
  268.7 38.1 %all-to-all-start.2 = ((bf16[8,56,1536]{2,1,0:T(8,128)(2,1)}), bf16[8,56,1536]{2,1,0:T(8,128)(2,1)S(1)}, u32[]{:S(2)}, u32[]{:S(2)}) async-start(bf16[8,56,1536]{2,1,0:T(8,128)(2,1)} %bitcast.80), calls=%async_computation.2 | async-start | bytes 2752512 | tf_op jit(solution)/shard_map/all_to_all | solution.py:1145
  274.6 45.3 %collective-permute-start.29 = (bf16[4,112,1536]{2,1,0:T(8,128)(2,1)}, bf16[4,112,1536]{2,1,0:T(8,128)(2,1)}, u32[]{:S(2)}, u32[]{:S(2)}) collective-permute-start(bf16[4,112,1536]{2,1,0:T(8,128)(2,1)} %get-tuple-element.271), channel_id=1, source_target_pairs={{0,1},{1,0},{2,3},{3,2},{4,5},{5,4},{6,7},{7,6},{8,9},{9,8},{10,11... | collective-permute-start | bytes 4128776 | tf_op jit(solution)/shard_map/ppermute | solution.py:390
  277.9 42.0 %collective-permute-start.31 = (bf16[4,112,1536]{2,1,0:T(8,128)(2,1)}, bf16[4,112,1536]{2,1,0:T(8,128)(2,1)}, u32[]{:S(2)}, u32[]{:S(2)}) collective-permute-start(bf16[4,112,1536]{2,1,0:T(8,128)(2,1)} %add_convert_fusion.1), channel_id=1, source_target_pairs={{0,2},{1,3},{2,0},{3,1},{4,6},{5,7},{6,4},{7,5},{8,10},{9,11},{10,... | collective-permute-start | bytes 4128776 | tf_op jit(solution)/shard_map/ppermute | solution.py:390
  324.2 46.8 %all-to-all-start.3 = ((bf16[8,56,1536]{2,1,0:T(8,128)(2,1)}), bf16[8,56,1536]{2,1,0:T(8,128)(2,1)S(1)}, u32[]{:S(2)}, u32[]{:S(2)}) async-start(bf16[8,56,1536]{2,1,0:T(8,128)(2,1)} %bitcast.83), calls=%async_computation.3 | async-start | bytes 2752512 | tf_op jit(solution)/shard_map/all_to_all | solution.py:1145
  395.2 6.4 %collective-permute-start.32 = (bf16[2,8,384,256]{3,2,1,0:T(8,128)(2,1)}, bf16[2,8,384,256]{3,2,1,0:T(8,128)(2,1)S(1)}, u32[]{:S(2)}, u32[]{:S(2)}) collective-permute-start(bf16[2,8,384,256]{3,2,1,0:T(8,128)(2,1)} %get-tuple-element.296), channel_id=1, source_target_pairs={{0,1},{1,0},{2,3},{3,2},{4,5},{5,4},{6,7},{7,6},{8,9},{9,8},{10,11... | collective-permute-start | bytes 9437192 | tf_op jit(solution)/shard_map/ppermute | solution.py:390
  404.3 46.4 %collective-permute-start.33 = (bf16[4,384,256]{2,1,0:T(8,128)(2,1)S(1)}, bf16[4,384,256]{2,1,0:T(8,128)(2,1)S(1)}, u32[]{:S(2)}, u32[]{:S(2)}) collective-permute-start(bf16[4,384,256]{2,1,0:T(8,128)(2,1)S(1)} %get-tuple-element.309), channel_id=1, source_target_pairs={{0,4},{4,0},{8,12},{12,8},{16,20},{20,16},{24,28},{28,24},{1,5},{5... | collective-permute-start | bytes 2359304 | tf_op jit(solution)/shard_map/ppermute | solution.py:390
  406.3 44.4 %collective-permute-start.34 = (bf16[4,384,256]{2,1,0:T(8,128)(2,1)S(1)}, bf16[4,384,256]{2,1,0:T(8,128)(2,1)S(1)}, u32[]{:S(2)}, u32[]{:S(2)}) collective-permute-start(bf16[4,384,256]{2,1,0:T(8,128)(2,1)S(1)} %get-tuple-element.310), channel_id=1, source_target_pairs={{0,2},{1,3},{2,0},{3,1},{4,6},{5,7},{6,4},{7,5},{8,10},{9,11},{10,... | collective-permute-start | bytes 2359304 | tf_op jit(solution)/shard_map/ppermute | solution.py:390
  407.3 43.4 %collective-permute-start.35 = (bf16[4,384,256]{2,1,0:T(8,128)(2,1)S(1)}, bf16[4,384,256]{2,1,0:T(8,128)(2,1)S(1)}, u32[]{:S(2)}, u32[]{:S(2)}) collective-permute-start(bf16[4,384,256]{2,1,0:T(8,128)(2,1)S(1)} %get-tuple-element.311), channel_id=1, source_target_pairs={{0,6},{1,7},{2,4},{3,5},{4,2},{5,3},{6,0},{7,1},{8,14},{9,15},{10,... | collective-permute-start | bytes 2359304 | tf_op jit(solution)/shard_map/ppermute | solution.py:406
  475.9 24.2 %collective-permute-start.37 = (bf16[4,144,384]{2,1,0:T(8,128)(2,1)S(1)}, bf16[4,144,384]{2,1,0:T(8,128)(2,1)}, u32[]{:S(2)}, u32[]{:S(2)}) collective-permute-start(bf16[4,144,384]{2,1,0:T(8,128)(2,1)S(1)} %get-tuple-element.344), channel_id=1, source_target_pairs={{0,4},{4,0},{8,12},{12,8},{16,20},{20,16},{24,28},{28,24},{1,5},{5... | collective-permute-start | bytes 1327112 | tf_op jit(solution)/shard_map/ppermute | solution.py:390
  477.9 22.1 %collective-permute-start.38 = (bf16[4,144,384]{2,1,0:T(8,128)(2,1)S(1)}, bf16[4,144,384]{2,1,0:T(8,128)(2,1)}, u32[]{:S(2)}, u32[]{:S(2)}) collective-permute-start(bf16[4,144,384]{2,1,0:T(8,128)(2,1)S(1)} %get-tuple-element.345), channel_id=1, source_target_pairs={{0,2},{1,3},{2,0},{3,1},{4,6},{5,7},{6,4},{7,5},{8,10},{9,11},{10,... | collective-permute-start | bytes 1327112 | tf_op jit(solution)/shard_map/ppermute | solution.py:390
  478.9 21.2 %collective-permute-start.39 = (bf16[4,144,384]{2,1,0:T(8,128)(2,1)S(1)}, bf16[4,144,384]{2,1,0:T(8,128)(2,1)}, u32[]{:S(2)}, u32[]{:S(2)}) collective-permute-start(bf16[4,144,384]{2,1,0:T(8,128)(2,1)S(1)} %get-tuple-element.346), channel_id=1, source_target_pairs={{0,6},{1,7},{2,4},{3,5},{4,2},{5,3},{6,0},{7,1},{8,14},{9,15},{10,... | collective-permute-start | bytes 1327112 | tf_op jit(solution)/shard_map/ppermute | solution.py:406
  479.4 10.3 %collective-permute-start.40 = (bf16[384,256]{1,0:T(8,128)(2,1)S(1)}, bf16[384,256]{1,0:T(8,128)(2,1)S(1)}, u32[]{:S(2)}, u32[]{:S(2)}) collective-permute-start(bf16[384,256]{1,0:T(8,128)(2,1)S(1)} %copy-done.58), channel_id=1, source_target_pairs={{0,8},{4,12},{8,0},{12,4},{16,24},{20,28},{24,16},{28,20},{1,9},{5... | collective-permute-start | bytes 589832 | tf_op jit(solution)/shard_map/ppermute | solution.py:390
  481.4 13.5 %collective-permute-start.41 = (bf16[384,256]{1,0:T(8,128)(2,1)S(1)}, bf16[384,256]{1,0:T(8,128)(2,1)S(1)}, u32[]{:S(2)}, u32[]{:S(2)}) collective-permute-start(bf16[384,256]{1,0:T(8,128)(2,1)S(1)} %copy-done.57), channel_id=1, source_target_pairs={{0,16},{4,20},{8,24},{12,28},{16,0},{20,4},{24,8},{28,12},{1,17},{... | collective-permute-start | bytes 589832 | tf_op jit(solution)/shard_map/ppermute | solution.py:390
  489.7 7.6 %collective-permute-start.42 = (bf16[384,256]{1,0:T(8,128)(2,1)S(1)}, bf16[384,256]{1,0:T(8,128)(2,1)S(1)}, u32[]{:S(2)}, u32[]{:S(2)}) collective-permute-start(bf16[384,256]{1,0:T(8,128)(2,1)S(1)} %copy-done.56), channel_id=1, source_target_pairs={{0,24},{4,28},{8,16},{12,20},{16,8},{20,12},{24,0},{28,4},{1,25},{... | collective-permute-start | bytes 589832 | tf_op jit(solution)/shard_map/ppermute | solution.py:390
  502.5 8.6 %collective-permute-start.43 = (bf16[144,384]{1,0:T(8,128)(2,1)}, bf16[144,384]{1,0:T(8,128)(2,1)S(1)}, u32[]{:S(2)}, u32[]{:S(2)}) collective-permute-start(bf16[144,384]{1,0:T(8,128)(2,1)} %get-tuple-element.361), channel_id=1, source_target_pairs={{0,8},{4,12},{8,0},{12,4},{16,24},{20,28},{24,16},{28,20},{1,9},{5... | collective-permute-start | bytes 331784 | tf_op jit(solution)/shard_map/ppermute | solution.py:390
  506.6 10.9 %collective-permute-start.44 = (bf16[144,384]{1,0:T(8,128)(2,1)}, bf16[144,384]{1,0:T(8,128)(2,1)S(1)}, u32[]{:S(2)}, u32[]{:S(2)}) collective-permute-start(bf16[144,384]{1,0:T(8,128)(2,1)} %get-tuple-element.362), channel_id=1, source_target_pairs={{0,16},{4,20},{8,24},{12,28},{16,0},{20,4},{24,8},{28,12},{1,17},{... | collective-permute-start | bytes 331784 | tf_op jit(solution)/shard_map/ppermute | solution.py:390
  507.6 10.0 %collective-permute-start.45 = (bf16[144,384]{1,0:T(8,128)(2,1)}, bf16[144,384]{1,0:T(8,128)(2,1)S(1)}, u32[]{:S(2)}, u32[]{:S(2)}) collective-permute-start(bf16[144,384]{1,0:T(8,128)(2,1)} %get-tuple-element.363), channel_id=1, source_target_pairs={{0,24},{4,28},{8,16},{12,20},{16,8},{20,12},{24,0},{28,4},{1,25},{... | collective-permute-start | bytes 331784 | tf_op jit(solution)/shard_map/ppermute | solution.py:390
  (61 other events, 547.6 us)

commit v4 on v3

--- a/solution.py
+++ b/solution.py
@@ -123,7 +123,7 @@
     return jax.ShapeDtypeStruct(shape, dtype)
 
 
-def mixer_forward(x, gain, wx, xpT, wdt, par, a2, T, Q=6):
+def mixer_forward(x, gain, wx, xpT, wdt, par, a2, T, limit, Q=6):
     L, D = x.shape
     DI = wx.shape[1]
     C, XP, R = L // T, xpT.shape[0], wdt.shape[0]
@@ -139,7 +139,7 @@
         out_shape=[nm, inner, big, big, big, sds((C, XP, T)), big, sds((C, NS, DI))],
         scratch_shapes=[pltpu.VMEM((NS, DI), F32), pltpu.VMEM((T, NS, 128), F32), pltpu.VMEM((T, NS, 128), F32),
                         pltpu.VMEM((T // 8, 8, DI), F32)],
-        compiler_params=pltpu.CompilerParams(vmem_limit_bytes=48 << 20),
+        compiler_params=pltpu.CompilerParams(vmem_limit_bytes=limit << 20),
         cost_estimate=pl.CostEstimate(flops=40000000000, bytes_accessed=16 * L * DI, transcendentals=0),
     )(*ins)
 
@@ -266,7 +266,7 @@
         gpar_ref[taps + 2 + NS:taps + 3 + NS] = jnp.sum(sums[taps + 2], axis=0, keepdims=True)
 
 
-def scan_backward(u, dl, gs, conv, inner, pT, st, xpT, wdt, par, an, Q=3, Q2=3):
+def scan_backward(u, dl, gs, conv, inner, pT, st, xpT, wdt, par, an, limit, Q=3, Q2=3):
     C, T8, _, DI = u.shape
     T = T8 * 8
     XP, R = xpT.shape[0], wdt.shape[0]
@@ -282,19 +282,19 @@
         out_shape=outs,
         scratch_shapes=[V(NS, DI), V(8, DI), V(T, NS, 128), V(T, NS, 128), V(T8, 8, DI), V(T8, 8, DI), V(T8, 8, DI),
                         V(T, NS, Q * 128), V(T, NS, Q * 128), V(T, NS, 128), V(T, NS, 128), V(par.shape[0], 8, DI)],
-        compiler_params=pltpu.CompilerParams(vmem_limit_bytes=52 << 20),
+        compiler_params=pltpu.CompilerParams(vmem_limit_bytes=limit << 20),
         cost_estimate=pl.CostEstimate(flops=80000000000, bytes_accessed=16 * C * T * DI, transcendentals=0),
     )(u, dl, gs, conv, inner, pT, st, xpT, wdt, par, an)
 
 
-def one_call(kernel, ins, outs, scalars=(), flops=0):
+def one_call(kernel, ins, outs, scalars=(), flops=0, limit=56):
     smem = pl.BlockSpec(memory_space=pltpu.SMEM)
     vmem = pl.BlockSpec(memory_space=pltpu.VMEM)
     size = sum(a.size * a.dtype.itemsize for a in list(ins) + list(outs))
     return pl.pallas_call(
         kernel,
         in_specs=[smem] * len(scalars) + [vmem] * len(ins), out_specs=[vmem] * len(outs), out_shape=list(outs),
-        compiler_params=pltpu.CompilerParams(vmem_limit_bytes=56 << 20),
+        compiler_params=pltpu.CompilerParams(vmem_limit_bytes=limit << 20),
         cost_estimate=pl.CostEstimate(flops=flops, bytes_accessed=size, transcendentals=0),
     )(*scalars, *ins)
 
@@ -303,7 +303,7 @@
                  z_ref, gated_ref, hid_ref, place_ref, out_ref, prob_ref, gate_ref):
     bf = jnp.bfloat16
     L = x_ref.shape[0]
-    E = wr_ref.shape[1]
+    E = wr_ref.shape[0]
     z = mm(nm_ref[...], wz_ref[...])
     z_ref[...] = z
     gated = (y_ref[...] * (z * sigmoid(z))).astype(bf)
@@ -311,7 +311,7 @@
     hid = x_ref[...].astype(F32) + mm(gated, wo_ref[...])
     hid_ref[...] = hid
     nmoe = hid * lax.rsqrt(jnp.mean(hid * hid, axis=-1, keepdims=True) + 1e-05) * gain_ref[...]
-    logits = mm(nmoe, wr_ref[...], precision=lax.Precision.HIGHEST)
+    logits = mm(nmoe, wr_ref[...], NT, precision=lax.Precision.HIGHEST)
     e = jnp.exp(logits - jnp.max(logits, axis=-1, keepdims=True))
     probs = e / jnp.sum(e, axis=-1, keepdims=True)
     prob_ref[...] = probs
@@ -340,7 +340,7 @@
     high = lax.Precision.HIGHEST
     hid, gain = hid_ref[...], gain_ref[...]
     L, D = hid.shape
-    E = wr_ref.shape[1]
+    E = wr_ref.shape[0]
     tok = mm(place_ref[...], home_ref[...])
     etok, gsent = tok[:, :D], tok[:, D:]
     live = lax.broadcasted_iota(jnp.int32, (L, 1), 0) < live_ref[0]
@@ -352,8 +352,8 @@
     glog = ggate * gate * (hot - probs)
     rms = lax.rsqrt(jnp.mean(hid * hid, axis=-1, keepdims=True) + 1e-05)
     hat = hid * rms
-    gr_ref[...] = mm(hat * gain, glog, TN, precision=high)
-    gnorm = gsent + mm(glog, wr_ref[...], NT, precision=high)
+    gr_ref[...] = mm(glog, hat * gain, TN, precision=high)
+    gnorm = gsent + mm(glog, wr_ref[...], precision=high)
     gg_ref[...] = jnp.sum(gnorm * hat, axis=0, keepdims=True)
     scaled = gnorm * gain
     gh = gy + rms * (scaled - hat * jnp.mean(scaled * hat, axis=-1, keepdims=True))
@@ -612,7 +612,7 @@
     return list(pl.pallas_call(
         kernel, grid=(ins[0].shape[0],),
         in_specs=[tok(a) for a in ins], out_specs=[tok(s) for s in shapes], out_shape=shapes,
-        compiler_params=pltpu.CompilerParams(vmem_limit_bytes=56 << 20),
+        compiler_params=pltpu.CompilerParams(vmem_limit_bytes=(44 if len(ins) <= 12 else 56) << 20),
         cost_estimate=pl.CostEstimate(flops=flops, bytes_accessed=size, transcendentals=0),
     )(*ins))
 
@@ -641,11 +641,10 @@
     return -(-n // m) * m
 
 
-def tiles_fit(w_in_x, w_xproj, w_out, conv_w):
-    lanes = w_in_x.shape[1]
-    return (lanes == 384 and w_in_x.shape[0] % 32 == 0 and up_to(w_xproj.shape[0], 128) + 128 == lanes
-            and w_xproj.shape[1] <= 32 and conv_w.shape[1] <= 128 and w_out.shape[0] % 16 == 0
-            and up_to(w_out.shape[1], 128) == 256)
+def tiles_fit(w_in_x, w_xproj, w_out, conv_w, w_dt, w_router):
+    return (w_in_x.shape == (96, 384) and w_xproj.shape[0] == 192 and w_xproj.shape[1] <= 26 and w_dt.shape[0] <= 6
+            and conv_w.shape[0] + NS + 5 <= 26 and conv_w.shape[1] <= 128 and w_out.shape == (192, 192)
+            and w_router.shape[0] <= 128 and w_router.shape[1] <= 16)
 
 
 def one_hot(shape, match):
@@ -654,41 +653,36 @@
     return jnp.where(match(i, j), 1.0, 0.0).astype(BF)
 
 
-def pack_kernel(wx, wdt, xp, cw, cb, db, al, ds, gx, gm, wz, wo, wr, first, other, s_dt, s_xp, s_sm, s_out, s_r):
+def pack_kernel(wx, wdt, xp, cw, cb, db, al, ds, gx, gm, wz, wo, wr, first, other, s_ex, s_r):
     n = wx.shape[0]
-    for s in (s_dt, s_xp, s_sm, s_out, s_r):
-        s[...] = jnp.zeros_like(s)
+    s_ex[...] = jnp.zeros_like(s_ex)
+    s_r[...] = jnp.zeros_like(s_r)
     first[:n] = wx[...]
-    s_dt[:wdt.shape[0]] = wdt[...].astype(F32)
-    first[n:n + 16] = s_dt[...].astype(BF)
-    s_xp[:xp.shape[1], :xp.shape[0]] = xp[...].astype(F32).T
-    wide = s_xp.shape[1]
-    first[n + 16:, :wide] = s_xp[...].astype(BF)
+    s_ex[:xp.shape[1], :xp.shape[0]] = xp[...].astype(F32).T
+    wide = s_ex.shape[1] - 128
     at = 0
     for v in (cw, cb, db, al, ds, gx, gm):
-        s_sm[at:at + v.shape[0], :v.shape[1]] = v[...].astype(F32)
+        s_ex[at:at + v.shape[0], wide:wide + v.shape[1]] = v[...].astype(F32)
         at += v.shape[0]
-    first[n + 16:, wide:] = s_sm[...].astype(BF)
-    s_out[:, :wo.shape[1]] = wo[...].astype(F32)
-    s_r[:, :wr.shape[1]] = wr[...].astype(F32)
-    put_other(lambda at, lane, v: store(other, at, lane, v), wz[:, :256], wz[:, 256:], s_out[...].astype(BF), s_r[...].astype(BF))
-
-
-def store(ref, at, lane, v):
-    ref[at:at + v.shape[0], lane:lane + v.shape[1]] = v
-
-
-def put_other(put, z_wide, z_rest, out, router):
-    n = z_wide.shape[-2]
-    put(0, 0, z_wide)
-    put(n, 0, z_rest[..., :n // 2, :])
-    put(n, 128, z_rest[..., n // 2:, :])
+    s_ex[26:26 + wdt.shape[0]] = wdt[...].astype(F32)
+    first[n:] = s_ex[...].astype(BF)
+    s_r[:wr.shape[1], :wr.shape[0]] = wr[...].astype(F32).T
+
+    def put(at, lane, v):
+        other[at:at + v.shape[0], lane:lane + v.shape[1]] = v
+    put_other(put, wz[...], wo[...])
+    other[other.shape[0] - 16:] = s_r[...].astype(BF)
+
+
+def put_other(put, z, out):
+    n, m = z.shape[-2], out.shape[-2]
+    put(0, 0, z[..., :256])
+    put(n, 0, z[..., :n // 2, 256:])
+    put(n, 128, z[..., n // 2:, 256:])
     at = n + n // 2
-    put(at, 0, out)
-    at += out.shape[-2]
-    half = router.shape[-2] // 2
-    put(at, 0, router[..., :half, :])
-    put(at, 128, router[..., half:, :])
+    put(at, 0, out[..., :m // 2, :128])
+    put(at, 128, out[..., m // 2:, :128])
+    put(at + m // 2, 0, jnp.concatenate([out[..., j * m // 4:(j + 1) * m // 4, 128:192] for j in range(4)], axis=-1))
 
 
 def pack_params(w_in_x, w_dt, w_xproj, conv_w, conv_b, dt_bias, a_log, d_skip, gain_mix, gain_moe, w_in_z, w_out, w_router):
@@ -699,8 +693,8 @@
     V = lambda *s: pltpu.VMEM(s, F32)
     return pl.pallas_call(
         pack_kernel, in_specs=[vmem] * len(ins), out_specs=[vmem] * 2,
-        out_shape=[sds((n + 48, lanes), BF), sds((n + n // 2 + w_out.shape[0] + w_router.shape[0] // 2, 256), BF)],
-        scratch_shapes=[V(16, lanes), V(32, lanes - 128), V(32, 128), V(w_out.shape[0], 256), V(w_router.shape[0], 128)],
+        out_shape=[sds((n + 32, lanes), BF), sds((n + n // 2 + w_out.shape[0] * 3 // 4 + 16, 256), BF)],
+        scratch_shapes=[V(32, lanes), V(16, 256)],
     )(*ins)
 
 
@@ -712,6 +706,11 @@
 
 def span(i, n):
     return pl.ds(pl.multiple_of(i * n, n), n)
+
+
+def dt_match(j, i, dt_rows):
+    k = j % 32 - 26
+    return (k >= 0) & (k < dt_rows) & (j // 32 * dt_rows + k == i)
 
 
 def unpack_first(masks, dims, me, *refs):
@@ -719,15 +718,15 @@
     count = len(masks)
     bufs = refs[:count]
     fx, dt, xpT, par, an, a2, gx, gm, w_dt, w_xp, w_sm = refs[count:]
-    n = bufs[0].shape[1] - 48
+    n = bufs[0].shape[1] - 32
     lanes = bufs[0].shape[2]
     wide = lanes - 128
     for buf, i, r, c in each_block(masks, bufs, me[0], me[1]):
         fx[span(r, n), span(c, lanes)] = buf[i, :n]
-        w_dt[span(r, 16), span(c, lanes)] = buf[i, n:n + 16]
-        w_xp[span(c, 32), span(r, wide)] = buf[i, n + 16:, :wide]
-        w_sm[:, span(r * cols + c, 128)] = buf[i, n + 16:, wide:]
-    pick = one_hot((dt.shape[0], 16 * rows), lambda i, j: (j % 16 < dt_rows) & (j // 16 * dt_rows + j % 16 == i))
+        w_dt[span(r, 32), span(c, lanes)] = buf[i, n:]
+        w_xp[span(c, 32), span(r, wide)] = buf[i, n:, :wide]
+        w_sm[:, span(r * cols + c, 128)] = buf[i, n:, wide:]
+    pick = one_hot((dt.shape[0], 32 * rows), lambda i, j: dt_match(j, i, dt_rows))
     dt[...] = mm(pick, w_dt[...]).astype(BF)
     pick = one_hot((xpT.shape[0], 32 * cols), lambda i, j: (j % 32 < xp_cols) & (j // 32 * xp_cols + j % 32 == i))
     t = mm(pick, w_xp[...])
@@ -751,17 +750,24 @@
     fz, fo, router, w_out, w_r = refs[count:]
     half = n // 2
     at = n + half
+    m = out_rows
     for buf, i, r, c in each_block(masks, bufs, me[0], me[1]):
         fz[span(r, n), pl.ds(pl.multiple_of(c * 384, 128), 256)] = buf[i, :n]
         for j in range(2):
             rows = pl.ds(pl.multiple_of(r * n + j * half, 16), half)
             fz[rows, pl.ds(pl.multiple_of(c * 384 + 256, 128), 128)] = buf[i, n:at, j * 128:(j + 1) * 128]
-            w_r[rows, span(c, 128)] = buf[i, at + out_rows:, j * 128:(j + 1) * 128]
-        w_out[span(r, out_rows), span(c, 256)] = buf[i, at:at + out_rows]
+            rows = pl.ds(pl.multiple_of(r * m + j * (m // 2), 16), m // 2)
+            w_out[rows, span(2 * c, 128)] = buf[i, at:at + m // 2, j * 128:(j + 1) * 128]
+        for j in range(4):
+            rows = pl.ds(pl.multiple_of(r * m + j * (m // 4), 16), m // 4)
+            w_out[rows, pl.ds(pl.multiple_of(c * 256 + 128, 128), 64)] = buf[i, at + m // 2:at + m * 3 // 4, j * 64:(j + 1) * 64]
+        w_r[span(c, 16), span(r, 128)] = buf[i, at + m * 3 // 4:, :128]
     wide = w_out[...]
     fo[...] = jnp.concatenate([wide[:, c * 256:c * 256 + out_lanes] for c in range(cols)], axis=1)
-    pick = one_hot((128 * cols, router.shape[1]), lambda i, j: (i % 128 < r_cols) & (i // 128 * r_cols + i % 128 == j))
-    router[...] = mm(w_r[...], pick)
+    pick = one_hot((router.shape[0], 16 * cols), lambda i, j: (j % 16 < r_cols) & (j // 16 * r_cols + j % 16 == i))
+    t = mm(pick, w_r[...])
+    r_rows = router.shape[1] // (t.shape[1] // 128)
+    router[...] = jnp.concatenate([t[:, r * 128:r * 128 + r_rows] for r in range(t.shape[1] // 128)], axis=1)
 
 
 def unpack_call(kernel, gathered, dims, outs, scratch):
@@ -773,7 +779,7 @@
         functools.partial(kernel, masks, dims),
         in_specs=[pl.BlockSpec(memory_space=pltpu.SMEM)] + [vmem] * len(bufs), out_specs=[vmem] * len(outs), out_shape=outs,
         scratch_shapes=[pltpu.VMEM(s, BF) for s in scratch],
-        compiler_params=pltpu.CompilerParams(vmem_limit_bytes=48 << 20),
+        compiler_params=pltpu.CompilerParams(vmem_limit_bytes=28 << 20),
         cost_estimate=pl.CostEstimate(flops=0, bytes_accessed=4 * sum(b.size for b in bufs), transcendentals=0),
     )(me, *bufs)
 
@@ -782,16 +788,17 @@
     dt_rows, xp_cols, xp_rows, share, gshare, rows, cols = dims
     pairs = refs[:2 * count]
     gwd, gxp, gpar, gmix, gmoe = (refs[(2 + i) * count:(3 + i) * count] for i in range(5))
-    keep, give, w_dt, w_xp, w_sm = refs[7 * count:]
+    keep, give, w_dt, w_xp, w_sm, full = refs[7 * count:]
     k = pl.program_id(0)
-    n, lanes = keep.shape[2] - 48, keep.shape[3]
+    n, lanes = keep.shape[2] - 32, keep.shape[3]
     wide = lanes - 128
     total = lambda vs: functools.reduce(lambda a, b: a + b, [v[...] for v in vs])
 
     @pl.when(k == 0)
     def _():
         g = total(gwd).astype(BF)
-        put = one_hot((16 * rows, g.shape[0]), lambda j, i: (j % 16 < dt_rows) & (j // 16 * dt_rows + j % 16 == i))
+        full[...] = sum_products(pairs)
+        put = one_hot((32 * rows, g.shape[0]), lambda j, i: dt_match(j, i, dt_rows))
         w_dt[...] = mm(put, g).astype(BF)
         g = total(gxp).astype(BF)
         put = one_hot((32 * cols, g.shape[0]), lambda j, i: (j % 32 < xp_cols) & (j // 32 * xp_cols + j % 32 == i))
@@ -807,16 +814,15 @@
             w_sm[m + 1:m + 2, p * 128:p * 128 + gshare] = moe[:, p * gshare:(p + 1) * gshare]
     for j, out in enumerate((keep, give)):
         c = s_ref[0] ^ (2 * k + j)
-        g = sum_products(pairs, lambda r: r[:, span(c, lanes)])
-        out[0, :, :n] = g.astype(BF).reshape(rows, n, lanes)
+        out[0, :, :n] = full[:, span(c, lanes)].astype(BF).reshape(rows, n, lanes)
         for r in range(rows):
-            out[0, r, n:n + 16] = w_dt[r * 16:(r + 1) * 16, span(c, lanes)]
-            out[0, r, n + 16:, :wide] = w_xp[span(c, 32), r * wide:(r + 1) * wide]
-            out[0, r, n + 16:, wide:] = w_sm[:, span(r * cols + c, 128)].astype(BF)
-
-
-def sum_products(pairs, block):
-    return functools.reduce(lambda a, b: a + b, [mm(pairs[i][...], block(pairs[i + 1]), TN) for i in range(0, len(pairs), 2)])
+            d = w_dt[r * 32:(r + 1) * 32, span(c, lanes)]
+            out[0, r, n:, :wide] = w_xp[span(c, 32), r * wide:(r + 1) * wide] + d[:, :wide]
+            out[0, r, n:, wide:] = (w_sm[:, span(r * cols + c, 128)] + d[:, wide:].astype(F32)).astype(BF)
+
+
+def sum_products(pairs):
+    return functools.reduce(lambda a, b: a + b, [mm(pairs[i][...], pairs[i + 1][...], TN) for i in range(0, len(pairs), 2)])
 
 
 def grad_blocks(kernel, ins, scratch, block, rows, cols, my_col, flops):
@@ -827,7 +833,7 @@
             num_scalar_prefetch=1, grid=(cols // 2,), in_specs=[whole_spec(v) for v in ins],
             out_specs=[pl.BlockSpec((1, rows) + block, lambda k, s: (k, 0, 0, 0))] * 2, scratch_shapes=scratch),
         out_shape=[out, out],
-        compiler_params=pltpu.CompilerParams(vmem_limit_bytes=56 << 20),
+        compiler_params=pltpu.CompilerParams(vmem_limit_bytes=44 << 20),
         cost_estimate=pl.CostEstimate(flops=flops, bytes_accessed=1 << 23, transcendentals=0),
     )(my_col.reshape(1), *ins))
 
@@ -838,34 +844,45 @@
     inner = pairs[0][1].shape[1]
     lanes = inner // cols
     ins = [v for p in pairs for v in p] + [g[name] for name in ("dt", "xproj", "chan", "gain_mix", "gain_moe") for g in smalls]
-    scratch = [pltpu.VMEM((16 * rows, inner), BF), pltpu.VMEM((32 * cols, (lanes - 128) * rows), BF), pltpu.VMEM((32, 128 * rows * cols), F32)]
-    return grad_blocks(functools.partial(grad_x_kernel, len(pairs), dims), ins, scratch, (m // rows + 48, lanes), rows, cols, my_col,
+    scratch = [pltpu.VMEM((32 * rows, inner), BF), pltpu.VMEM((32 * cols, (lanes - 128) * rows), BF), pltpu.VMEM((32, 128 * rows * cols), F32),
+               pltpu.VMEM((m, inner), F32)]
+    return grad_blocks(functools.partial(grad_x_kernel, len(pairs), dims), ins, scratch, (m // rows + 32, lanes), rows, cols, my_col,
                        2 * len(pairs) * n * m * inner)
 
 
 def grad_other_kernel(count, r_cols, s_ref, *refs):
     zs, outs, routers = refs[:2 * count], refs[2 * count:4 * count], refs[4 * count:5 * count]
-    keep, give = refs[5 * count:]
+    keep, give, full_z, full_o = refs[5 * count:]
     rows = keep.shape[1]
     k = pl.program_id(0)
+
+    @pl.when(k == 0)
+    def _():
+        full_z[...] = sum_products(zs)
+        full_o[...] = sum_products(outs)
     r = functools.reduce(lambda a, b: a + b, [v[...] for v in routers]).astype(BF)
+    r_rows = r.shape[1] // rows
     for j, out in enumerate((keep, give)):
         c = s_ref[0] ^ (2 * k + j)
-        z = sum_products(zs, lambda v: v[:, pl.ds(pl.multiple_of(c * 384, 128), 384)]).astype(BF)
-        o = sum_products(outs, lambda v: v[:, span(2 * k + j, 256)]).astype(BF)
-        put = one_hot((r.shape[1], 128), lambda a, b: (b < r_cols) & (a == c * r_cols + b))
-        w = mm(r, put).astype(BF)
-        z, o, w = (v.reshape(rows, v.shape[0] // rows, v.shape[1]) for v in (z, o, w))
+        z = full_z[:, pl.ds(pl.multiple_of(c * 384, 128), 384)].astype(BF)
+        o = full_o[:, span(2 * k + j, 256)].astype(BF)
+        z, o = (v.reshape(rows, v.shape[0] // rows, v.shape[1]) for v in (z, o))
 
         def put_block(at, lane, v):
             out[0, :, at:at + v.shape[1], lane:lane + v.shape[2]] = v
-        put_other(put_block, z[..., :256], z[..., 256:], o, w)
+        put_other(put_block, z, o)
+        w = mm(one_hot((16, r.shape[0]), lambda a, b: (a < r_cols) & (b == c * r_cols + a)), r).astype(BF)
+        at = out.shape[2] - 16
+        out[0, :, at:] = jnp.zeros((rows, 16, 256), BF)
+        for q in range(rows):
+            out[0, q, at:, :r_rows] = w[:, q * r_rows:(q + 1) * r_rows]
 
 
 def grad_other_blocks(zs, outs, routers, block, rows, cols, r_cols, my_col):
     ins = [v for p in zs for v in p] + [v for p in outs for v in p] + list(routers)
     flops = 2 * sum(a.shape[0] * a.shape[1] * b.shape[1] for a, b in zs + outs)
-    return grad_blocks(functools.partial(grad_other_kernel, len(zs), r_cols), ins, [], block, rows, cols, my_col, flops)
+    scratch = [pltpu.VMEM((a.shape[1], b.shape[1]), F32) for a, b in (zs[0], outs[0])]
+    return grad_blocks(functools.partial(grad_other_kernel, len(zs), r_cols), ins, scratch, block, rows, cols, my_col, flops)
 
 
 def split_near_kernel(plan, s_ref, keep, got, own, *gives):
@@ -888,7 +905,7 @@
             in_specs=[pl.BlockSpec((near, 1, 2, n, lanes), lambda z, s: (0, z, 0, 0, 0))] * 2,
             out_specs=[pl.BlockSpec((1, n, lanes), lambda z, s: (z, 0, 0))] * len(outs)),
         out_shape=outs,
-        compiler_params=pltpu.CompilerParams(vmem_limit_bytes=32 << 20),
+        compiler_params=pltpu.CompilerParams(vmem_limit_bytes=16 << 20),
         cost_estimate=pl.CostEstimate(flops=0, bytes_accessed=6 * keep.size, transcendentals=0),
     )(lax.axis_index("row").reshape(1), keep.reshape(view), got.reshape(view))
     return res[0], list(res[1:])
@@ -921,10 +938,10 @@
     s[...] = total_of(refs[:count])
     n, lanes = gx.shape
     gx[...] = s[:n]
-    gdt[...] = s[n:n + gdt.shape[0]]
+    gdt[...] = s[n + 26:n + 26 + gdt.shape[0]]
     wide = lanes - 128
-    gxp[...] = s[n + 16:, :wide].T[:gxp.shape[0], :gxp.shape[1]]
-    at = n + 16
+    gxp[...] = s[n:, :wide].T[:gxp.shape[0], :gxp.shape[1]]
+    at = n
     for ref in (gcw, gcb, gdb, gal, gds, gmix, gmoe):
         ref[...] = s[at:at + ref.shape[0], wide:wide + ref.shape[1]]
         at += ref.shape[0]
@@ -939,10 +956,12 @@
     gz[:half, 256:] = s[n:n + half, :128]
     gz[half:, 256:] = s[n:n + half, 128:]
     at = n + half
-    go[...] = s[at:at + go.shape[0], :go.shape[1]]
-    at += go.shape[0]
-    gr[:half] = s[at:, :gr.shape[1]]
-    gr[half:] = s[at:, 128:128 + gr.shape[1]]
+    m = go.shape[0]
+    for j in range(2):
+        go[j * m // 2:(j + 1) * m // 2, :128] = s[at:at + m // 2, j * 128:(j + 1) * 128]
+    for j in range(4):
+        go[j * m // 4:(j + 1) * m // 4, 128:] = s[at + m // 2:at + m * 3 // 4, j * 64:(j + 1) * 64]
+    gr[...] = s[at + m * 3 // 4:, :128].T[:gr.shape[0], :gr.shape[1]]
 
 
 def finish(kernel, mine, gots, shapes):
@@ -1009,7 +1028,7 @@
         cut.append(cut[-1] + n)
     full_xpT = whole(rest[:, :, cut[0]:cut[1]].reshape((rows, cols) + w_xproj.shape)).T
     full_dt = whole(rest[:, :, cut[1]:cut[2]].reshape((rows, cols) + w_dt.shape))
-    router_f = whole(rest[:, :, cut[2]:cut[3]].reshape((rows, cols) + w_router.shape)).astype(F32)
+    router_f = whole(rest[:, :, cut[2]:cut[3]].reshape((rows, cols) + w_router.shape)).astype(F32).T
     small = rest[:, :, cut[3]:cut[4]].reshape((parts,) + small.shape).transpose(1, 0, 2).astype(F32)
     chan = small[:-1].reshape(-1, inner)
     taps = conv_w.shape[0]
@@ -1040,14 +1059,14 @@
         unpack_first, first, dims,
         [sds((width, inner), BF), sds((w_dt.shape[0] * rows, inner), BF), sds((w_xproj.shape[1] * cols, inner), BF),
          sds((taps + 3, inner)), sds((NS, inner)), sds((NS, inner)), sds((1, width)), sds((1, width))],
-        [(16 * rows, inner), (32 * cols, (lanes - 128) * rows), (32, 128 * rows * cols)])
+        [(32 * rows, inner), (32 * cols, (lanes - 128) * rows), (32, 128 * rows * cols)])
 
     def rest(done):
         o, done = lax.optimization_barrier((near_o, done))
         full_z, full_out, router_f = unpack_call(
             unpack_other, gather_core(o), (here, w_out.shape[0], w_out.shape[1], w_router.shape[1], cols),
-            [sds((width, inner), BF), sds((inner, width), BF), sds((width, w_router.shape[1] * cols))],
-            [(inner, 256 * cols), (width, 128 * cols)])
+            [sds((width, inner), BF), sds((inner, width), BF), sds((w_router.shape[1] * cols, width))],
+            [(inner, 256 * cols), (16 * cols, 128 * rows)])
         return full_z, full_out, router_f, done
     return rest, full_x, full_xpT, full_dt, par, a_neg, a_two, gx, gm
 
@@ -1076,7 +1095,7 @@
     gsmall = total["chan"].astype(BF)
     ggain = jnp.concatenate([total["gain_mix"].reshape(parts, 1, -1), total["gain_moe"].reshape(parts, 1, -1)], axis=2)
     gsmall = jnp.concatenate([gsmall.reshape(-1, parts, share).transpose(1, 0, 2), ggain.astype(BF)], axis=1)
-    gflat = jnp.concatenate([blocks(total["xproj"].T, w_xproj), blocks(total["dt"], w_dt), blocks(total["router"], w_router),
+    gflat = jnp.concatenate([blocks(total["xproj"].T, w_xproj), blocks(total["dt"], w_dt), blocks(total["router"].T, w_router),
                              gsmall.reshape(rows, cols, -1)], axis=2)
     gflat = jnp.pad(gflat, ((0, 0), (0, 0), (0, extra * lanes - sum(sizes)))).reshape(rows, cols, extra, lanes)
     done = reduce_list([jnp.concatenate([grad_in_x[k].reshape(rows, here, lanes),
@@ -1106,7 +1125,7 @@
     xp = w_xproj.shape[1] * cols
     share = inner // parts
 
-    tiled = tiles_fit(w_in_x, w_xproj, w_out, conv_w)
+    tiled = tiles_fit(w_in_x, w_xproj, w_out, conv_w, w_dt, w_router)
     here, lanes = w_in_x.shape
     out_rows, out_lanes = w_out.shape
     wide = up_to(out_lanes, 128)
@@ -1125,8 +1144,8 @@
     source = jnp.where(there < rows * CAP, there // CAP * message + at // group * CAP + there % CAP, -1)
     sort = (source[:, None] == jnp.arange(rows * message, dtype=jnp.int32)[None, :]).astype(BF)
 
-    def mixer(x):
-        nm, inner_x, conv, u, dl, pT, ssm, starts = mixer_forward(x, gain_mix_f, full_x, full_xpT, full_dt, par, a_two, QB)
+    def mixer(x, limit):
+        nm, inner_x, conv, u, dl, pT, ssm, starts = mixer_forward(x, gain_mix_f, full_x, full_xpT, full_dt, par, a_two, QB, limit)
         return dict(x=x, nm=nm, inner=inner_x, conv=conv, u=u, dl=dl, pT=pT, ssm=ssm.reshape(length, inner), starts=starts)
 
     def router(k, route, n_live, grad):
@@ -1165,18 +1184,18 @@
             [back, k["place"], k["hidden"], k["probs"], k["gate"], k["route"], k["cot"], gain_moe_f, router_f, full_out, shifted,
              k["z"], k["ssm"]],
             [sds((length, width), BF), sds((length, width)), sds((length, inner)), sds((length, inner), BF),
-             sds((length, cols * wide), BF), sds((width, experts_all)), sds((1, width))],
+             sds((length, cols * wide), BF), sds((experts_all, width)), sds((1, width))],
             [k["n_live"]], 6 * length * inner * width)
         return dict(mixed_out=mixed_out, gh=gh, gs=gs.reshape(k["u"].shape), gz=gz, gm=gm, router=g_router, gain_moe=g_moe)
 
-    def unscan(k, gs):
-        gi, g_xp, g_dt, g_chan = scan_backward(k["u"], k["dl"], gs, k["conv"], k["inner"], k["pT"], k["starts"], full_xpT, full_dt, par, a_neg)
+    def unscan(k, gs, limit):
+        gi, g_xp, g_dt, g_chan = scan_backward(k["u"], k["dl"], gs, k["conv"], k["inner"], k["pT"], k["starts"], full_xpT, full_dt, par, a_neg, limit)
         return dict(gi=gi, xproj=g_xp, dt=g_dt, chan=g_chan)
 
     def unproject(k, g):
         grad_tokens, g_mix = one_call(
             token_kernel, [g["gi"], g["gz"], full_x, full_z, k["x"], g["gh"], gain_mix_f], [sds((length, width)), sds((1, width))], (),
-            4 * length * inner * width)
+            4 * length * inner * width, 24)
         return dict(tokens=grad_tokens, gain_mix=g_mix)
 
     after = lax.optimization_barrier
@@ -1185,7 +1204,7 @@
         x = tokens[s]
         if last is not None:
             x, last = after((x, last))
-        k = mixer(x)
+        k = mixer(x, 24 if s == 0 else 48)
         if s == 0:
             full_z, full_out, router_f, k["ssm"] = rest_of(k["ssm"])
         before, (last, k) = last, router(k, routes[s], lengths[s], cotangent[s])
@@ -1214,12 +1233,12 @@
         gs_.append(g)
         if s + 1 < seqs:
             g["gs"], sent[s + 1] = after((g["gs"], sent[s + 1]))
-            g.update(unscan(ks[s], g["gs"]))
+            g.update(unscan(ks[s], g["gs"], 52))
             g["gi"], backs[s + 1] = after((g["gi"], backs[s + 1]))
     g = gs_[-1]
     nms, gateds = [k["nm"] for k in ks], [k["gated"] for k in ks]
     if tiled:
-        block = (here + here // 2 + out_rows + w_router.shape[0] // 2, 256)
+        block = (here + here // 2 + out_rows * 3 // 4 + 16, 256)
         keep, give = grad_other_blocks([(v, q["gz"]) for v, q in zip(nms, gs_)], [(v, q["gm"]) for v, q in zip(gateds, gs_)],
                                        [q["router"] for q in gs_], block, rows, cols, w_router.shape[1], my_col)
         far, plane, core = stages()
@@ -1232,7 +1251,7 @@
         own, gives = split_near(keep, got)
         g["gs"], gives = after((g["gs"], gives))
         gots = [exchange(v, p) for v, p in zip(gives, plane[1:])]
-        g.update(unscan(ks[-1], g["gs"]))
+        g.update(unscan(ks[-1], g["gs"], 24))
         gots, g["gi"] = after((gots, g["gi"]))
         mine, gives = split_far(own, gots)
         g["gi"], gives = after((g["gi"], gives))
@@ -1256,7 +1275,7 @@
         blocks = (gx, gz, go)
         small = (g_xproj, g_dt, (gcw, gcb[0], gdb[0], gal, gds[0]), g_mix[0], g_moe[0], g_router)
     else:
-        g.update(unscan(ks[-1], g["gs"]))
+        g.update(unscan(ks[-1], g["gs"], 24))
         for k, q in zip(ks, gs_):
             q.update(unproject(k, q))
         names = ("xproj", "dt", "chan", "gain_mix", "gain_moe", "router")

time: 530 us -> 499 us (0.942)
  Pallas kernels: 271 us -> 237 us
  local copies, waits for them, and re-layouts: 35.7 us -> 54.6 us
  waiting for transfers between devices: 118 us -> 108 us
    unnamed x122 -> x236, local copies, waits for them, and re-layouts: 29.3 us -> 48.2 us
    pallas_call x8, Pallas kernels: 62.2 us -> 51.9 us  [one_call(): pl.pallas_call(kernel, in_specs=[smem] * len(scalars) + [vmem] * len(ins)...]
    ppermute x42, waiting for transfers between devices: 104 us -> 94.6 us  [swap(): return lax.ppermute(x, axis, [(i, i ^ bit) for i in range(n)])]
    pallas_call x4, Pallas kernels: 51 us -> 44.2 us  [per_expert(): pl.pallas_call(kernel, grid=(ins[0].shape[0],), in_specs=[tok(a) for a in...]
    pallas_call x2, Pallas kernels: 18.3 us -> 11.9 us  [grad_blocks(): pl.pallas_call(kernel, grid_spec=pltpu.PrefetchScalarGridSpec(num_scalar_...]
  transfers between devices with their start and end apart: 50 -> 50, of which waited for: 19 -> 16; matrix products, arithmetic and copies ran while one was open for 5% -> 4% of each run, Pallas kernels for 40% -> 38%
where the time goes in v4:
time: 499 us; the launch traced here: 491 us
  Pallas kernels  237 us (47%)
  waiting for transfers between devices  108 us (22%)
  starting transfers between devices  67.4 us (14%)
  local copies, waits for them, and re-layouts  54.6 us (11%)
  other arithmetic  13.8 us (3%)
  matrix products  7.35 us (1%)
    ppermute x42, waiting for transfers between devices, swap(): return lax.ppermute(x, axis, [(i, i ^ bit) for i in range(n)])  94.6 us
    pallas_call x2, Pallas kernels, scan_backward(): pl.pallas_call(functools.partial(scan_back_kernel, T, Q, Q2, R), grid=(C,...  78.3 us
    pallas_call x8, Pallas kernels, one_call(): pl.pallas_call(kernel, in_specs=[smem] * len(scalars) + [vmem] * len(ins)...  51.9 us
    unnamed x236, local copies, waits for them, and re-layouts  48.2 us
    pallas_call x4, Pallas kernels, per_expert(): pl.pallas_call(kernel, grid=(ins[0].shape[0],), in_specs=[tok(a) for a in...  44.2 us
    ppermute x42, starting transfers between devices, swap(): return lax.ppermute(x, axis, [(i, i ^ bit) for i in range(n)])  41 us
    pallas_call x2, Pallas kernels, mixer_forward(): pl.pallas_call(functools.partial(mixer_kernel, T, Q, R), grid=(C,), in_sp...  37.7 us
    all_to_all x4, starting transfers between devices, home(): lax.all_to_all(rows_out, 'row', split_axis=0, concat_axis=0, tiled=True)  22.4 us
  transfers between devices with their start and end apart: 50, of which 16 were waited for; matrix products, arithmetic and copies ran while one was open for 4% of the time, Pallas kernels for 38%

profile of v4, /device:TPU:0, one launch (start us, length us, event | category | flops | bytes accessed | tf_op | source)
XLA Modules:
  0.0 490.6 jit_solution(15757770068505391631)
XLA Ops:
  5.4 3.0 collective-permute-start
  8.4 2.6 collective-permute-start.1
  11.4 7.6 %collective-permute-done.1 = bf16[128,384]{1,0:T(8,128)(2,1)S(1)} collective-permute-done((bf16[128,384]{1,0:T(8,128)(2,1)}, bf16[128,384]{1,0:T(8,128)(2,1)S(1)}, u32[]{:S(2)}, u32[]{:S(2)}) %collective-permute-start.1) | collective-permute-done | bytes 98336 | tf_op jit(solution)/shard_map/ppermute | solution.py:390
  20.1 2.5 collective-permute-start.5
  26.6 3.2 collective-permute-done.10
  29.8 3.4 collective-permute-done.11
  33.2 2.5 collective-permute-start.12
  35.7 2.9 collective-permute-done.3.refs_1_
  53.3 17.3 %shard_map.316 = (bf16[320,768]{1,0:T(8,128)(2,1)S(1)}, f32[328,1536]{1,0:T(8,128)S(1)}, f32[5,8,8,1536]{3,2,1,0:T(8,128)S(1)}, f32[5,8,8,1536]{3,2,1,0:T(8,128)...) custom-call(bf16[320,768]{1,0:T(8,128)(2,1)S(1)} %get-tuple-element., ...), custom_call_target="tpu_custom_call" | custom-call | flops 40000000000 | bytes 7864320 | tf_op jit(solution)/shard_map/pallas_call | solution.py:134
  82.8 2.9 slice_bitcast_fusion
  85.7 3.3 shard_map.317
  92.5 9.9 %shard_map.318 = (f32[320,1536]{1,0:T(8,128)}, bf16[320,1536]{1,0:T(8,128)(2,1)}, f32[320,768]{1,0:T(8,128)}, bf16[320,448]{1,0:T(8,128)(2,1)}, bf16[448,1536]{1...) custom-call(s32[1]{0:T(128)} %get-tuple-element.419.live_ref, bf16[320,768]{1,0:T(8,128)(2,1)} %copy-done.14, ...), custom_call_target="tpu_custom_call" | custom-call | flops 2264924160 | bytes 14390784 | tf_op jit(solution)/shard_map/pallas_call | solution.py:294
  102.4 6.0 %all-to-all-start = ((bf16[8,56,1536]{2,1,0:T(8,128)(2,1)}), bf16[8,56,1536]{2,1,0:T(8,128)(2,1)S(1)}, u32[]{:S(2)}, u32[]{:S(2)}) async-start(bf16[8,56,1536]{2,1,0:T(8,128)(2,1)} %bitcast.84), calls=%async_computation | async-start | bytes 2752512 | tf_op jit(solution)/shard_map/all_to_all | solution.py:1164
  108.4 20.5 %shard_map.319 = (bf16[320,768]{1,0:T(8,128)(2,1)S(1)}, f32[328,1536]{1,0:T(8,128)}, f32[5,8,8,1536]{3,2,1,0:T(8,128)S(1)}, f32[5,8,8,1536]{3,2,1,0:T(8,128)S(1)...) custom-call(bf16[320,768]{1,0:T(8,128)(2,1)S(1)} %get-tuple-element., ...), custom_call_target="tpu_custom_call" | custom-call | flops 40000000000 | bytes 7864320 | tf_op jit(solution)/shard_map/pallas_call | solution.py:134
  133.1 9.9 %shard_map.320 = (f32[320,1536]{1,0:T(8,128)}, bf16[320,1536]{1,0:T(8,128)(2,1)}, f32[320,768]{1,0:T(8,128)}, bf16[320,448]{1,0:T(8,128)(2,1)}, bf16[448,1536]{1...) custom-call(s32[1]{0:T(128)} %get-tuple-element.420.live_ref, bf16[320,768]{1,0:T(8,128)(2,1)} %copy-done.12, ...), custom_call_target="tpu_custom_call" | custom-call | flops 2264924160 | bytes 14390784 | tf_op jit(solution)/shard_map/pallas_call | solution.py:294
  144.9 6.6 %all-to-all-start.1 = ((bf16[8,56,1536]{2,1,0:T(8,128)(2,1)}), bf16[8,56,1536]{2,1,0:T(8,128)(2,1)}, u32[]{:S(2)}, u32[]{:S(2)}) async-start(bf16[8,56,1536]{2,1,0:T(8,128)(2,1)} %bitcast.83), calls=%async_computation.1 | async-start | bytes 2752512 | tf_op jit(solution)/shard_map/all_to_all | solution.py:1164
  151.6 24.3 %collective-permute-done.20.refs_1_ = bf16[4,112,1536]{2,1,0:T(8,128)(2,1)S(1)} collective-permute-done((bf16[4,112,1536]{2,1,0:T(8,128)(2,1)S(1)}, bf16[4,112,1536]{2,1,0:T(8,128)(2,1)S(1)}, u32[]{:S(2)}, u32[]{:S(2)}) %collective-permute-start.20) | collective-permute-done | bytes 1376288 | tf_op jit(solution)/shard_map/ppermute | solution.py:390
  175.9 7.9 %all-to-all-done.1 = bf16[8,56,1536]{2,1,0:T(8,128)(2,1)} async-done(((bf16[8,56,1536]{2,1,0:T(8,128)(2,1)}), bf16[8,56,1536]{2,1,0:T(8,128)(2,1)}, u32[]{:S(2)}, u32[]{:S(2)}) %all-to-all-start.1) | async-done | bytes 1376288 | tf_op jit(solution)/shard_map/all_to_all | solution.py:1164
  183.8 2.3 convolution_convert_fusion.2
  187.3 11.9 %shard_map.321 = (bf16[4,112,1536]{2,1,0:T(8,128)(2,1)S(1)}, bf16[4,112,1536]{2,1,0:T(8,128)(2,1)S(1)}, bf16[4,112,1536]{2,1,0:T(8,128)(2,1)S(1)}, bf16[4,112,15...) custom-call(bf16[4,112,1536]{2,1,0:T(8,128)(2,1)S(1)} %bitcast.64, ...), custom_call_target="tpu_custom_call" | custom-call | flops 8455716864 | bytes 25952256 | tf_op jit(solution)/shard_map/pallas_call | solution.py:612
  199.6 16.5 %collective-permute-done.26.refs_1_.refs_6_ = bf16[4,112,1536]{2,1,0:T(8,128)(2,1)S(1)} collective-permute-done((bf16[4,112,1536]{2,1,0:T(8,128)(2,1)S(1)}, bf16[4,112,1536]{2,1,0:T(8,128)(2,1)S(1)}, u32[]{:S(2)}, u32[]{:S(2)}) %collective-permute-start.26) | collective-permute-done | bytes 1376288 | tf_op jit(solution)/shard_map/ppermute | solution.py:390
  220.4 12.1 %shard_map.322 = (bf16[4,112,1536]{2,1,0:T(8,128)(2,1)S(1)}, bf16[4,112,1536]{2,1,0:T(8,128)(2,1)S(1)}, bf16[4,112,1536]{2,1,0:T(8,128)(2,1)S(1)}, bf16[4,112,15...) custom-call(bf16[4,112,1536]{2,1,0:T(8,128)(2,1)S(1)} %bitcast.69, ...), custom_call_target="tpu_custom_call" | custom-call | flops 8455716864 | bytes 25952256 | tf_op jit(solution)/shard_map/pallas_call | solution.py:612
  232.7 17.6 %collective-permute-done.25 = bf16[4,112,1536]{2,1,0:T(8,128)(2,1)S(1)} collective-permute-done((bf16[4,112,1536]{2,1,0:T(8,128)(2,1)}, bf16[4,112,1536]{2,1,0:T(8,128)(2,1)S(1)}, u32[]{:S(2)}, u32[]{:S(2)}) %collective-permute-start.25) | collective-permute-done | bytes 1376288 | tf_op jit(solution)/shard_map/ppermute | solution.py:390
  253.0 5.9 %all-to-all-start.2 = ((bf16[8,56,1536]{2,1,0:T(8,128)(2,1)}), bf16[8,56,1536]{2,1,0:T(8,128)(2,1)}, u32[]{:S(2)}, u32[]{:S(2)}) async-start(bf16[8,56,1536]{2,1,0:T(8,128)(2,1)} %bitcast.82), calls=%async_computation.2 | async-start | bytes 2752512 | tf_op jit(solution)/shard_map/all_to_all | solution.py:1164
  259.0 3.3 add_convert_fusion.1
  265.1 10.1 %shard_map.323 = f32[4,768,768]{2,1,0:T(8,128)} custom-call(bf16[4,112,1536]{2,1,0:T(8,128)(2,1)S(1)} %bitcast.65, bf16[4,112,1536]{2,1,0:T(8,128)(2,1)S(1)} %collective-permute-done.20.refs_1_, bf16[4,112,1536]{2,1,0:T(8,128)(2,1)} %collective-permute-done.21.refs_2_, bf16[4,112,1536]{2,1,0:T(8,128)(2,1)} %collective-permute-done.22.refs_3_, ...), custom_call_target="tpu_custom_call" | custom-call | flops 4227858432 | bytes 25952256 | tf_op jit(solution)/shard_map/pallas_call | solution.py:612
  275.3 10.1 %shard_map.324 = f32[4,768,768]{2,1,0:T(8,128)} custom-call(bf16[4,112,1536]{2,1,0:T(8,128)(2,1)S(1)} %bitcast.66, bf16[4,112,1536]{2,1,0:T(8,128)(2,1)S(1)} %collective-permute-done.20.refs_1_, bf16[4,112,1536]{2,1,0:T(8,128)(2,1)} %collective-permute-done.21.refs_2_, bf16[4,112,1536]{2,1,0:T(8,128)(2,1)} %collective-permute-done.22.refs_3_, ...), custom_call_target="tpu_custom_call" | custom-call | flops 4227858432 | bytes 25952256 | tf_op jit(solution)/shard_map/pallas_call | solution.py:612
  285.4 5.7 %all-to-all-done.2 = bf16[8,56,1536]{2,1,0:T(8,128)(2,1)} async-done(((bf16[8,56,1536]{2,1,0:T(8,128)(2,1)}), bf16[8,56,1536]{2,1,0:T(8,128)(2,1)}, u32[]{:S(2)}, u32[]{:S(2)}) %all-to-all-start.2) | async-done | bytes 1376288 | tf_op jit(solution)/shard_map/all_to_all | solution.py:1164
  291.1 11.6 %shard_map.325 = (bf16[320,768]{1,0:T(8,128)(2,1)}, f32[320,768]{1,0:T(8,128)}, f32[320,1536]{1,0:T(8,128)}, bf16[320,1536]{1,0:T(8,128)(2,1)}, bf16[320,1024]{1...) custom-call(s32[1]{0:T(128)} %get-tuple-element.419.live_ref, bf16[448,1536]{1,0:T(8,128)(2,1)} %bitcast.31.home_ref, ...), custom_call_target="tpu_custom_call" | custom-call | flops 2264924160 | bytes 16818688 | tf_op jit(solution)/shard_map/pallas_call | solution.py:294
  302.7 2.3 add_convert_fusion
  305.0 2.1 convolution_convert_fusion
  307.1 3.9 all-to-all-start.3
  311.0 40.7 %shard_map.326 = (bf16[320,1536]{1,0:T(8,128)(2,1)}, f32[80,1536]{1,0:T(8,128)S(1)}, f32[48,1536]{1,0:T(8,128)S(1)}, f32[23,1536]{1,0:T(8,128)S(1)}) custom-call(f32[5,8,8,1536]{3,2,1,0:T(8,128)} %copy-done.87, f32[5,8,8,1536]{3,2,1,0:T(8,128)} %copy-done.88, f32[5,8,8,1536]{3,2,1,0:T(8,128)} %bitcast.104, f32[5,8,8,1536]{3,2,1,0:T(8,128)} %copy-done.86, ...), custom_call_target="tpu_custom_call" | custom-call | flops 80000000000 | bytes 7864320 | tf_op jit(solution)/shard_map/pallas_call | solution.py:278
  355.0 11.4 %shard_map.327 = (bf16[320,768]{1,0:T(8,128)(2,1)}, f32[320,768]{1,0:T(8,128)}, f32[320,1536]{1,0:T(8,128)}, bf16[320,1536]{1,0:T(8,128)(2,1)}, bf16[320,1024]{1...) custom-call(s32[1]{0:T(128)} %get-tuple-element.420.live_ref, bf16[448,1536]{1,0:T(8,128)(2,1)} %bitcast.81, ...), custom_call_target="tpu_custom_call" | custom-call | flops 2264924160 | bytes 16818688 | tf_op jit(solution)/shard_map/pallas_call | solution.py:294
  373.2 8.4 %shard_map.328 = (bf16[2,8,304,256]{3,2,1,0:T(8,128)(2,1)S(1)}, bf16[2,8,304,256]{3,2,1,0:T(8,128)(2,1)}) custom-call(s32[1]{0:T(128)} %bitcast.3.s_ref, bf16[320,768]{1,0:T(8,128)(2,1)S(1)} %copy-done.38, bf16[320,1536]{1,0:T(8,128)(2,1)S(1)} %copy-done.28, bf16[320,768]{1,0:T(8,128)(2,1)S(1)} %copy-done.41, bf16[320,1536]{1,0:T(8,128)(2,1)S(1)} %copy-done.25, ...), custom_call_target="tpu_custom_call" | custom-call | flops 3523215360 | bytes 8388608 | tf_op jit(solution)/shard_map/pallas_call | solution.py:830
  383.7 2.9 collective-permute-done.32
  391.2 37.6 %shard_map.331 = (bf16[320,1536]{1,0:T(8,128)(2,1)S(1)}, f32[80,1536]{1,0:T(8,128)S(1)}, f32[48,1536]{1,0:T(8,128)S(1)}, f32[23,1536]{1,0:T(8,128)S(1)}) custom-call(f32[5,8,8,1536]{3,2,1,0:T(8,128)S(1)} %copy-done.84, f32[5,8,8,1536]{3,2,1,0:T(8,128)S(1)} %copy-done.85, f32[5,8,8,1536]{3,2,1,0:T(8,128)S(1)} %bitcast.78, f32[5,8,8,1536]{3,2,1,0:T(8,128)S(1)} %copy-done.82, ...), custom_call_target="tpu_custom_call" | custom-call | flops 80000000000 | bytes 7864320 | tf_op jit(solution)/shard_map/pallas_call | solution.py:278
  433.2 3.0 shard_map.332
  440.5 3.5 shard_map.334
  444.1 3.4 collective-permute-done.36
  453.8 2.4 collective-permute-start.41
  456.2 3.5 collective-permute-done.40.refs_1_
  459.7 3.4 collective-permute-start.42
  464.2 3.2 collective-permute-done.41.refs_2_
  468.7 2.1 shard_map.336
  471.6 2.3 shard_map.337
  473.9 2.3 collective-permute-start.43
  480.6 5.5 %collective-permute-done.44.refs_2_ = bf16[128,384]{1,0:T(8,128)(2,1)S(1)} collective-permute-done((bf16[128,384]{1,0:T(8,128)(2,1)}, bf16[128,384]{1,0:T(8,128)(2,1)S(1)}, u32[]{:S(2)}, u32[]{:S(2)}) %collective-permute-start.44) | collective-permute-done | bytes 98336 | tf_op jit(solution)/shard_map/ppermute | solution.py:390
  (335 shorter events, 101.3 us)
Async XLA Ops:
  5.4 6.0 %collective-permute-start = (bf16[128,384]{1,0:T(8,128)(2,1)}, bf16[128,384]{1,0:T(8,128)(2,1)S(1)}, u32[]{:S(2)}, u32[]{:S(2)}) collective-permute-start(bf16[128,384]{1,0:T(8,128)(2,1)} %get-tuple-element.198), channel_id=1, source_target_pairs={{0,8},{4,12},{8,0},{12,4},{16,24},{20,28},{24,16},{28,20},{1,9},{5... | collective-permute-start | bytes 294920 | tf_op jit(solution)/shard_map/ppermute | solution.py:390
  8.4 10.6 %collective-permute-start.1 = (bf16[128,384]{1,0:T(8,128)(2,1)}, bf16[128,384]{1,0:T(8,128)(2,1)S(1)}, u32[]{:S(2)}, u32[]{:S(2)}) collective-permute-start(bf16[128,384]{1,0:T(8,128)(2,1)} %get-tuple-element.198), channel_id=1, source_target_pairs={{0,16},{4,20},{8,24},{12,28},{16,0},{20,4},{24,8},{28,12},{1,17},{... | collective-permute-start | bytes 294920 | tf_op jit(solution)/shard_map/ppermute | solution.py:390
  11.0 8.1 %collective-permute-start.2 = (bf16[128,384]{1,0:T(8,128)(2,1)}, bf16[128,384]{1,0:T(8,128)(2,1)S(1)}, u32[]{:S(2)}, u32[]{:S(2)}) collective-permute-start(bf16[128,384]{1,0:T(8,128)(2,1)} %get-tuple-element.198), channel_id=1, source_target_pairs={{0,24},{4,28},{8,16},{12,20},{16,8},{20,12},{24,0},{28,4},{1,25},{... | collective-permute-start | bytes 294920 | tf_op jit(solution)/shard_map/ppermute | solution.py:390
  20.1 15.6 %collective-permute-start.5 = (bf16[4,128,384]{2,1,0:T(8,128)(2,1)S(1)}, bf16[4,128,384]{2,1,0:T(8,128)(2,1)S(1)}, u32[]{:S(2)}, u32[]{:S(2)}) collective-permute-start(bf16[4,128,384]{2,1,0:T(8,128)(2,1)S(1)} %pad_maximum_fusion.3.refs_0_), channel_id=1, source_target_pairs={{0,6},{1,7},{2,4},{3,5},{4,2},{5,3},{6,0},{7,1},{8,14},{9,15},{10,... | collective-permute-start | bytes 1179656 | tf_op jit(solution)/shard_map/ppermute | solution.py:406
  22.6 16.0 %collective-permute-start.3 = (bf16[4,128,384]{2,1,0:T(8,128)(2,1)S(1)}, bf16[4,128,384]{2,1,0:T(8,128)(2,1)}, u32[]{:S(2)}, u32[]{:S(2)}) collective-permute-start(bf16[4,128,384]{2,1,0:T(8,128)(2,1)S(1)} %pad_maximum_fusion.3.refs_0_), channel_id=1, source_target_pairs={{0,4},{4,0},{8,12},{12,8},{16,20},{20,16},{24,28},{28,24},{1,5},{5... | collective-permute-start | bytes 1179656 | tf_op jit(solution)/shard_map/ppermute | solution.py:390
  23.1 15.5 %collective-permute-start.4 = (bf16[4,128,384]{2,1,0:T(8,128)(2,1)S(1)}, bf16[4,128,384]{2,1,0:T(8,128)(2,1)}, u32[]{:S(2)}, u32[]{:S(2)}) collective-permute-start(bf16[4,128,384]{2,1,0:T(8,128)(2,1)S(1)} %pad_maximum_fusion.3.refs_0_), channel_id=1, source_target_pairs={{0,2},{1,3},{2,0},{3,1},{4,6},{5,7},{6,4},{7,5},{8,10},{9,11},{10,... | collective-permute-start | bytes 1179656 | tf_op jit(solution)/shard_map/ppermute | solution.py:390
  23.6 6.2 %collective-permute-start.10 = (bf16[304,256]{1,0:T(8,128)(2,1)}, bf16[304,256]{1,0:T(8,128)(2,1)S(1)}, u32[]{:S(2)}, u32[]{:S(2)}) collective-permute-start(bf16[304,256]{1,0:T(8,128)(2,1)} %get-tuple-element.207), channel_id=1, source_target_pairs={{0,8},{4,12},{8,0},{12,4},{16,24},{20,28},{24,16},{28,20},{1,9},{5... | collective-permute-start | bytes 466952 | tf_op jit(solution)/shard_map/ppermute | solution.py:390
  25.2 8.0 %collective-permute-start.11 = (bf16[304,256]{1,0:T(8,128)(2,1)}, bf16[304,256]{1,0:T(8,128)(2,1)S(1)}, u32[]{:S(2)}, u32[]{:S(2)}) collective-permute-start(bf16[304,256]{1,0:T(8,128)(2,1)} %get-tuple-element.207), channel_id=1, source_target_pairs={{0,16},{4,20},{8,24},{12,28},{16,0},{20,4},{24,8},{28,12},{1,17},{... | collective-permute-start | bytes 466952 | tf_op jit(solution)/shard_map/ppermute | solution.py:390
  29.8 13.2 %collective-permute-start.6 = (bf16[4,128,384]{2,1,0:T(8,128)(2,1)S(1)}, bf16[4,128,384]{2,1,0:T(8,128)(2,1)S(1)}, u32[]{:S(2)}, u32[]{:S(2)}) collective-permute-start(bf16[4,128,384]{2,1,0:T(8,128)(2,1)S(1)} %pad_maximum_fusion.3.refs_0_), channel_id=1, source_target_pairs={{0,1},{1,0},{2,3},{3,2},{4,5},{5,4},{6,7},{7,6},{8,9},{9,8},{10,11... | collective-permute-start | bytes 1179656 | tf_op jit(solution)/shard_map/ppermute | solution.py:390
  33.2 7.2 %collective-permute-start.12 = (bf16[304,256]{1,0:T(8,128)(2,1)}, bf16[304,256]{1,0:T(8,128)(2,1)S(1)}, u32[]{:S(2)}, u32[]{:S(2)}) collective-permute-start(bf16[304,256]{1,0:T(8,128)(2,1)} %get-tuple-element.207), channel_id=1, source_target_pairs={{0,24},{4,28},{8,16},{12,20},{16,8},{20,12},{24,0},{28,4},{1,25},{... | collective-permute-start | bytes 466952 | tf_op jit(solution)/shard_map/ppermute | solution.py:390
  35.7 9.5 %collective-permute-start.9 = (bf16[4,128,384]{2,1,0:T(8,128)(2,1)S(1)}, bf16[4,128,384]{2,1,0:T(8,128)(2,1)S(1)}, u32[]{:S(2)}, u32[]{:S(2)}) collective-permute-start(bf16[4,128,384]{2,1,0:T(8,128)(2,1)S(1)} %collective-permute-done.5.refs_3_), channel_id=1, source_target_pairs={{0,1},{1,0},{2,3},{3,2},{4,5},{5,4},{6,7},{7,6},{8,9},{9,8},{10,11... | collective-permute-start | bytes 1179656 | tf_op jit(solution)/shard_map/ppermute | solution.py:390
  38.6 7.9 %collective-permute-start.7 = (bf16[4,128,384]{2,1,0:T(8,128)(2,1)}, bf16[4,128,384]{2,1,0:T(8,128)(2,1)}, u32[]{:S(2)}, u32[]{:S(2)}) collective-permute-start(bf16[4,128,384]{2,1,0:T(8,128)(2,1)} %collective-permute-done.3.refs_1_), channel_id=1, source_target_pairs={{0,1},{1,0},{2,3},{3,2},{4,5},{5,4},{6,7},{7,6},{8,9},{9,8},{10,11... | collective-permute-start | bytes 1179656 | tf_op jit(solution)/shard_map/ppermute | solution.py:390
  38.6 7.9 %collective-permute-start.8 = (bf16[4,128,384]{2,1,0:T(8,128)(2,1)}, bf16[4,128,384]{2,1,0:T(8,128)(2,1)}, u32[]{:S(2)}, u32[]{:S(2)}) collective-permute-start(bf16[4,128,384]{2,1,0:T(8,128)(2,1)} %collective-permute-done.4.refs_2_), channel_id=1, source_target_pairs={{0,1},{1,0},{2,3},{3,2},{4,5},{5,4},{6,7},{7,6},{8,9},{9,8},{10,11... | collective-permute-start | bytes 1179656 | tf_op jit(solution)/shard_map/ppermute | solution.py:390
  41.5 37.9 %collective-permute-start.13 = (bf16[4,304,256]{2,1,0:T(8,128)(2,1)}, bf16[4,304,256]{2,1,0:T(8,128)(2,1)S(1)}, u32[]{:S(2)}, u32[]{:S(2)}) collective-permute-start(bf16[4,304,256]{2,1,0:T(8,128)(2,1)} %pad_maximum_fusion.2.refs_0_), channel_id=1, source_target_pairs={{0,4},{4,0},{8,12},{12,8},{16,20},{20,16},{24,28},{28,24},{1,5},{5... | collective-permute-start | bytes 1867784 | tf_op jit(solution)/shard_map/ppermute | solution.py:390
  43.8 35.6 %collective-permute-start.14 = (bf16[4,304,256]{2,1,0:T(8,128)(2,1)}, bf16[4,304,256]{2,1,0:T(8,128)(2,1)S(1)}, u32[]{:S(2)}, u32[]{:S(2)}) collective-permute-start(bf16[4,304,256]{2,1,0:T(8,128)(2,1)} %pad_maximum_fusion.2.refs_0_), channel_id=1, source_target_pairs={{0,2},{1,3},{2,0},{3,1},{4,6},{5,7},{6,4},{7,5},{8,10},{9,11},{10,... | collective-permute-start | bytes 1867784 | tf_op jit(solution)/shard_map/ppermute | solution.py:390
  45.9 33.5 %collective-permute-start.15 = (bf16[4,304,256]{2,1,0:T(8,128)(2,1)}, bf16[4,304,256]{2,1,0:T(8,128)(2,1)S(1)}, u32[]{:S(2)}, u32[]{:S(2)}) collective-permute-start(bf16[4,304,256]{2,1,0:T(8,128)(2,1)} %pad_maximum_fusion.2.refs_0_), channel_id=1, source_target_pairs={{0,6},{1,7},{2,4},{3,5},{4,2},{5,3},{6,0},{7,1},{8,14},{9,15},{10,... | collective-permute-start | bytes 1867784 | tf_op jit(solution)/shard_map/ppermute | solution.py:406
  79.4 6.3 %collective-permute-start.16 = (bf16[4,304,256]{2,1,0:T(8,128)(2,1)}, bf16[4,304,256]{2,1,0:T(8,128)(2,1)S(1)}, u32[]{:S(2)}, u32[]{:S(2)}) collective-permute-start(bf16[4,304,256]{2,1,0:T(8,128)(2,1)} %pad_maximum_fusion.2.refs_0_), channel_id=1, source_target_pairs={{0,1},{1,0},{2,3},{3,2},{4,5},{5,4},{6,7},{7,6},{8,9},{9,8},{10,11... | collective-permute-start | bytes 1867784 | tf_op jit(solution)/shard_map/ppermute | solution.py:390
  79.5 6.2 %collective-permute-start.17 = (bf16[4,304,256]{2,1,0:T(8,128)(2,1)S(1)}, bf16[4,304,256]{2,1,0:T(8,128)(2,1)}, u32[]{:S(2)}, u32[]{:S(2)}) collective-permute-start(bf16[4,304,256]{2,1,0:T(8,128)(2,1)S(1)} %collective-permute-done.13.refs_1_), channel_id=1, source_target_pairs={{0,1},{1,0},{2,3},{3,2},{4,5},{5,4},{6,7},{7,6},{8,9},{9,8},{10,11... | collective-permute-start | bytes 1867784 | tf_op jit(solution)/shard_map/ppermute | solution.py:390
  80.0 5.7 %collective-permute-start.18 = (bf16[4,304,256]{2,1,0:T(8,128)(2,1)S(1)}, bf16[4,304,256]{2,1,0:T(8,128)(2,1)}, u32[]{:S(2)}, u32[]{:S(2)}) collective-permute-start(bf16[4,304,256]{2,1,0:T(8,128)(2,1)S(1)} %collective-permute-done.14.refs_2_), channel_id=1, source_target_pairs={{0,1},{1,0},{2,3},{3,2},{4,5},{5,4},{6,7},{7,6},{8,9},{9,8},{10,11... | collective-permute-start | bytes 1867784 | tf_op jit(solution)/shard_map/ppermute | solution.py:390
  80.1 5.6 %collective-permute-start.19 = (bf16[4,304,256]{2,1,0:T(8,128)(2,1)S(1)}, bf16[4,304,256]{2,1,0:T(8,128)(2,1)}, u32[]{:S(2)}, u32[]{:S(2)}) collective-permute-start(bf16[4,304,256]{2,1,0:T(8,128)(2,1)S(1)} %collective-permute-done.15.refs_3_), channel_id=1, source_target_pairs={{0,1},{1,0},{2,3},{3,2},{4,5},{5,4},{6,7},{7,6},{8,9},{9,8},{10,11... | collective-permute-start | bytes 1867784 | tf_op jit(solution)/shard_map/ppermute | solution.py:390
  102.4 40.6 %all-to-all-start = ((bf16[8,56,1536]{2,1,0:T(8,128)(2,1)}), bf16[8,56,1536]{2,1,0:T(8,128)(2,1)S(1)}, u32[]{:S(2)}, u32[]{:S(2)}) async-start(bf16[8,56,1536]{2,1,0:T(8,128)(2,1)} %bitcast.84), calls=%async_computation | async-start | bytes 2752512 | tf_op jit(solution)/shard_map/all_to_all | solution.py:1164
  143.9 32.0 %collective-permute-start.20 = (bf16[4,112,1536]{2,1,0:T(8,128)(2,1)S(1)}, bf16[4,112,1536]{2,1,0:T(8,128)(2,1)S(1)}, u32[]{:S(2)}, u32[]{:S(2)}) collective-permute-start(bf16[4,112,1536]{2,1,0:T(8,128)(2,1)S(1)} %bitcast.62), channel_id=1, source_target_pairs={{0,2},{1,3},{2,0},{3,1},{4,6},{5,7},{6,4},{7,5},{8,10},{9,11},{10,... | collective-permute-start | bytes 4128776 | tf_op jit(solution)/shard_map/ppermute | solution.py:390
  144.9 38.9 %all-to-all-start.1 = ((bf16[8,56,1536]{2,1,0:T(8,128)(2,1)}), bf16[8,56,1536]{2,1,0:T(8,128)(2,1)}, u32[]{:S(2)}, u32[]{:S(2)}) async-start(bf16[8,56,1536]{2,1,0:T(8,128)(2,1)} %bitcast.83), calls=%async_computation.1 | async-start | bytes 2752512 | tf_op jit(solution)/shard_map/all_to_all | solution.py:1164
  151.5 34.6 %collective-permute-start.21 = (bf16[4,112,1536]{2,1,0:T(8,128)(2,1)S(1)}, bf16[4,112,1536]{2,1,0:T(8,128)(2,1)}, u32[]{:S(2)}, u32[]{:S(2)}) collective-permute-start(bf16[4,112,1536]{2,1,0:T(8,128)(2,1)S(1)} %bitcast.63), channel_id=1, source_target_pairs={{0,1},{1,0},{2,3},{3,2},{4,5},{5,4},{6,7},{7,6},{8,9},{9,8},{10,11... | collective-permute-start | bytes 4128776 | tf_op jit(solution)/shard_map/ppermute | solution.py:390
  175.9 10.2 %collective-permute-start.22 = (bf16[4,112,1536]{2,1,0:T(8,128)(2,1)S(1)}, bf16[4,112,1536]{2,1,0:T(8,128)(2,1)}, u32[]{:S(2)}, u32[]{:S(2)}) collective-permute-start(bf16[4,112,1536]{2,1,0:T(8,128)(2,1)S(1)} %collective-permute-done.20.refs_1_), channel_id=1, source_target_pairs={{0,1},{1,0},{2,3},{3,2},{4,5},{5,4},{6,7},{7,6},{8,9},{9,8},{10,11... | collective-permute-start | bytes 4128776 | tf_op jit(solution)/shard_map/ppermute | solution.py:390
  186.1 30.0 %collective-permute-start.26 = (bf16[4,112,1536]{2,1,0:T(8,128)(2,1)S(1)}, bf16[4,112,1536]{2,1,0:T(8,128)(2,1)S(1)}, u32[]{:S(2)}, u32[]{:S(2)}) collective-permute-start(bf16[4,112,1536]{2,1,0:T(8,128)(2,1)S(1)} %bitcast.67), channel_id=1, source_target_pairs={{0,2},{1,3},{2,0},{3,1},{4,6},{5,7},{6,4},{7,5},{8,10},{9,11},{10,... | collective-permute-start | bytes 4128776 | tf_op jit(solution)/shard_map/ppermute | solution.py:390
  199.1 17.5 %collective-permute-start.24 = (bf16[4,112,1536]{2,1,0:T(8,128)(2,1)S(1)}, bf16[4,112,1536]{2,1,0:T(8,128)(2,1)S(1)}, u32[]{:S(2)}, u32[]{:S(2)}) collective-permute-start(bf16[4,112,1536]{2,1,0:T(8,128)(2,1)S(1)} %get-tuple-element.234), channel_id=1, source_target_pairs={{0,1},{1,0},{2,3},{3,2},{4,5},{5,4},{6,7},{7,6},{8,9},{9,8},{10,11... | collective-permute-start | bytes 4128776 | tf_op jit(solution)/shard_map/ppermute | solution.py:390
  199.1 20.0 %collective-permute-start.27 = (bf16[4,112,1536]{2,1,0:T(8,128)(2,1)S(1)}, bf16[4,112,1536]{2,1,0:T(8,128)(2,1)S(1)}, u32[]{:S(2)}, u32[]{:S(2)}) collective-permute-start(bf16[4,112,1536]{2,1,0:T(8,128)(2,1)S(1)} %bitcast.68), channel_id=1, source_target_pairs={{0,1},{1,0},{2,3},{3,2},{4,5},{5,4},{6,7},{7,6},{8,9},{9,8},{10,11... | collective-permute-start | bytes 4128776 | tf_op jit(solution)/shard_map/ppermute | solution.py:390
  216.1 16.6 %collective-permute-start.23 = (bf16[4,112,1536]{2,1,0:T(8,128)(2,1)S(1)}, bf16[4,112,1536]{2,1,0:T(8,128)(2,1)S(1)}, u32[]{:S(2)}, u32[]{:S(2)}) collective-permute-start(bf16[4,112,1536]{2,1,0:T(8,128)(2,1)S(1)} %get-tuple-element.232), channel_id=1, source_target_pairs={{0,1},{1,0},{2,3},{3,2},{4,5},{5,4},{6,7},{7,6},{8,9},{9,8},{10,11... | collective-permute-start | bytes 4128776 | tf_op jit(solution)/shard_map/ppermute | solution.py:390
  218.0 32.3 %collective-permute-start.25 = (bf16[4,112,1536]{2,1,0:T(8,128)(2,1)}, bf16[4,112,1536]{2,1,0:T(8,128)(2,1)S(1)}, u32[]{:S(2)}, u32[]{:S(2)}) collective-permute-start(bf16[4,112,1536]{2,1,0:T(8,128)(2,1)} %add_convert_fusion.4), channel_id=1, source_target_pairs={{0,2},{1,3},{2,0},{3,1},{4,6},{5,7},{6,4},{7,5},{8,10},{9,11},{10,... | collective-permute-start | bytes 4128776 | tf_op jit(solution)/shard_map/ppermute | solution.py:390
  232.6 26.3 %collective-permute-start.30 = (bf16[4,112,1536]{2,1,0:T(8,128)(2,1)}, bf16[4,112,1536]{2,1,0:T(8,128)(2,1)}, u32[]{:S(2)}, u32[]{:S(2)}) collective-permute-start(bf16[4,112,1536]{2,1,0:T(8,128)(2,1)} %get-tuple-element.273), channel_id=1, source_target_pairs={{0,1},{1,0},{2,3},{3,2},{4,5},{5,4},{6,7},{7,6},{8,9},{9,8},{10,11... | collective-permute-start | bytes 4128776 | tf_op jit(solution)/shard_map/ppermute | solution.py:390
  253.0 38.2 %all-to-all-start.2 = ((bf16[8,56,1536]{2,1,0:T(8,128)(2,1)}), bf16[8,56,1536]{2,1,0:T(8,128)(2,1)}, u32[]{:S(2)}, u32[]{:S(2)}) async-start(bf16[8,56,1536]{2,1,0:T(8,128)(2,1)} %bitcast.82), calls=%async_computation.2 | async-start | bytes 2752512 | tf_op jit(solution)/shard_map/all_to_all | solution.py:1164
  258.9 43.8 %collective-permute-start.29 = (bf16[4,112,1536]{2,1,0:T(8,128)(2,1)}, bf16[4,112,1536]{2,1,0:T(8,128)(2,1)}, u32[]{:S(2)}, u32[]{:S(2)}) collective-permute-start(bf16[4,112,1536]{2,1,0:T(8,128)(2,1)} %copy-done.51), channel_id=1, source_target_pairs={{0,1},{1,0},{2,3},{3,2},{4,5},{5,4},{6,7},{7,6},{8,9},{9,8},{10,11... | collective-permute-start | bytes 4128776 | tf_op jit(solution)/shard_map/ppermute | solution.py:390
  262.3 40.4 %collective-permute-start.31 = (bf16[4,112,1536]{2,1,0:T(8,128)(2,1)}, bf16[4,112,1536]{2,1,0:T(8,128)(2,1)}, u32[]{:S(2)}, u32[]{:S(2)}) collective-permute-start(bf16[4,112,1536]{2,1,0:T(8,128)(2,1)} %add_convert_fusion.1), channel_id=1, source_target_pairs={{0,2},{1,3},{2,0},{3,1},{4,6},{5,7},{6,4},{7,5},{8,10},{9,11},{10,... | collective-permute-start | bytes 4128776 | tf_op jit(solution)/shard_map/ppermute | solution.py:390
  307.1 46.8 %all-to-all-start.3 = ((bf16[8,56,1536]{2,1,0:T(8,128)(2,1)}), bf16[8,56,1536]{2,1,0:T(8,128)(2,1)S(1)}, u32[]{:S(2)}, u32[]{:S(2)}) async-start(bf16[8,56,1536]{2,1,0:T(8,128)(2,1)} %bitcast.86), calls=%async_computation.3 | async-start | bytes 2752512 | tf_op jit(solution)/shard_map/all_to_all | solution.py:1164
  381.6 5.0 %collective-permute-start.32 = (bf16[2,8,304,256]{3,2,1,0:T(8,128)(2,1)}, bf16[2,8,304,256]{3,2,1,0:T(8,128)(2,1)S(1)}, u32[]{:S(2)}, u32[]{:S(2)}) collective-permute-start(bf16[2,8,304,256]{3,2,1,0:T(8,128)(2,1)} %get-tuple-element.296), channel_id=1, source_target_pairs={{0,1},{1,0},{2,3},{3,2},{4,5},{5,4},{6,7},{7,6},{8,9},{9,8},{10,11... | collective-permute-start | bytes 7471112 | tf_op jit(solution)/shard_map/ppermute | solution.py:390
  387.6 44.4 %collective-permute-start.33 = (bf16[4,304,256]{2,1,0:T(8,128)(2,1)S(1)}, bf16[4,304,256]{2,1,0:T(8,128)(2,1)S(1)}, u32[]{:S(2)}, u32[]{:S(2)}) collective-permute-start(bf16[4,304,256]{2,1,0:T(8,128)(2,1)S(1)} %get-tuple-element.309), channel_id=1, source_target_pairs={{0,4},{4,0},{8,12},{12,8},{16,20},{20,16},{24,28},{28,24},{1,5},{5... | collective-permute-start | bytes 1867784 | tf_op jit(solution)/shard_map/ppermute | solution.py:390
  389.6 42.4 %collective-permute-start.34 = (bf16[4,304,256]{2,1,0:T(8,128)(2,1)S(1)}, bf16[4,304,256]{2,1,0:T(8,128)(2,1)S(1)}, u32[]{:S(2)}, u32[]{:S(2)}) collective-permute-start(bf16[4,304,256]{2,1,0:T(8,128)(2,1)S(1)} %get-tuple-element.310), channel_id=1, source_target_pairs={{0,2},{1,3},{2,0},{3,1},{4,6},{5,7},{6,4},{7,5},{8,10},{9,11},{10,... | collective-permute-start | bytes 1867784 | tf_op jit(solution)/shard_map/ppermute | solution.py:390
  390.7 41.3 %collective-permute-start.35 = (bf16[4,304,256]{2,1,0:T(8,128)(2,1)S(1)}, bf16[4,304,256]{2,1,0:T(8,128)(2,1)S(1)}, u32[]{:S(2)}, u32[]{:S(2)}) collective-permute-start(bf16[4,304,256]{2,1,0:T(8,128)(2,1)S(1)} %get-tuple-element.311), channel_id=1, source_target_pairs={{0,6},{1,7},{2,4},{3,5},{4,2},{5,3},{6,0},{7,1},{8,14},{9,15},{10,... | collective-permute-start | bytes 1867784 | tf_op jit(solution)/shard_map/ppermute | solution.py:406
  448.3 22.5 %collective-permute-start.37 = (bf16[4,128,384]{2,1,0:T(8,128)(2,1)S(1)}, bf16[4,128,384]{2,1,0:T(8,128)(2,1)S(1)}, u32[]{:S(2)}, u32[]{:S(2)}) collective-permute-start(bf16[4,128,384]{2,1,0:T(8,128)(2,1)S(1)} %get-tuple-element.344), channel_id=1, source_target_pairs={{0,4},{4,0},{8,12},{12,8},{16,20},{20,16},{24,28},{28,24},{1,5},{5... | collective-permute-start | bytes 1179656 | tf_op jit(solution)/shard_map/ppermute | solution.py:390
  450.3 20.5 %collective-permute-start.38 = (bf16[4,128,384]{2,1,0:T(8,128)(2,1)S(1)}, bf16[4,128,384]{2,1,0:T(8,128)(2,1)}, u32[]{:S(2)}, u32[]{:S(2)}) collective-permute-start(bf16[4,128,384]{2,1,0:T(8,128)(2,1)S(1)} %get-tuple-element.345), channel_id=1, source_target_pairs={{0,2},{1,3},{2,0},{3,1},{4,6},{5,7},{6,4},{7,5},{8,10},{9,11},{10,... | collective-permute-start | bytes 1179656 | tf_op jit(solution)/shard_map/ppermute | solution.py:390
  451.4 19.4 %collective-permute-start.39 = (bf16[4,128,384]{2,1,0:T(8,128)(2,1)S(1)}, bf16[4,128,384]{2,1,0:T(8,128)(2,1)}, u32[]{:S(2)}, u32[]{:S(2)}) collective-permute-start(bf16[4,128,384]{2,1,0:T(8,128)(2,1)S(1)} %get-tuple-element.346), channel_id=1, source_target_pairs={{0,6},{1,7},{2,4},{3,5},{4,2},{5,3},{6,0},{7,1},{8,14},{9,15},{10,... | collective-permute-start | bytes 1179656 | tf_op jit(solution)/shard_map/ppermute | solution.py:406
  451.9 7.8 %collective-permute-start.40 = (bf16[304,256]{1,0:T(8,128)(2,1)S(1)}, bf16[304,256]{1,0:T(8,128)(2,1)}, u32[]{:S(2)}, u32[]{:S(2)}) collective-permute-start(bf16[304,256]{1,0:T(8,128)(2,1)S(1)} %copy-done.115), channel_id=1, source_target_pairs={{0,8},{4,12},{8,0},{12,4},{16,24},{20,28},{24,16},{28,20},{1,9},{5... | collective-permute-start | bytes 466952 | tf_op jit(solution)/shard_map/ppermute | solution.py:390
  453.8 13.5 %collective-permute-start.41 = (bf16[304,256]{1,0:T(8,128)(2,1)S(1)}, bf16[304,256]{1,0:T(8,128)(2,1)S(1)}, u32[]{:S(2)}, u32[]{:S(2)}) collective-permute-start(bf16[304,256]{1,0:T(8,128)(2,1)S(1)} %copy-done.114), channel_id=1, source_target_pairs={{0,16},{4,20},{8,24},{12,28},{16,0},{20,4},{24,8},{28,12},{1,17},{... | collective-permute-start | bytes 466952 | tf_op jit(solution)/shard_map/ppermute | solution.py:390
  459.7 7.6 %collective-permute-start.42 = (bf16[304,256]{1,0:T(8,128)(2,1)S(1)}, bf16[304,256]{1,0:T(8,128)(2,1)S(1)}, u32[]{:S(2)}, u32[]{:S(2)}) collective-permute-start(bf16[304,256]{1,0:T(8,128)(2,1)S(1)} %copy-done.113), channel_id=1, source_target_pairs={{0,24},{4,28},{8,16},{12,20},{16,8},{20,12},{24,0},{28,4},{1,25},{... | collective-permute-start | bytes 466952 | tf_op jit(solution)/shard_map/ppermute | solution.py:390
  473.9 6.7 %collective-permute-start.43 = (bf16[128,384]{1,0:T(8,128)(2,1)}, bf16[128,384]{1,0:T(8,128)(2,1)S(1)}, u32[]{:S(2)}, u32[]{:S(2)}) collective-permute-start(bf16[128,384]{1,0:T(8,128)(2,1)} %get-tuple-element.361), channel_id=1, source_target_pairs={{0,8},{4,12},{8,0},{12,4},{16,24},{20,28},{24,16},{28,20},{1,9},{5... | collective-permute-start | bytes 294920 | tf_op jit(solution)/shard_map/ppermute | solution.py:390
  476.2 9.9 %collective-permute-start.44 = (bf16[128,384]{1,0:T(8,128)(2,1)}, bf16[128,384]{1,0:T(8,128)(2,1)S(1)}, u32[]{:S(2)}, u32[]{:S(2)}) collective-permute-start(bf16[128,384]{1,0:T(8,128)(2,1)} %get-tuple-element.362), channel_id=1, source_target_pairs={{0,16},{4,20},{8,24},{12,28},{16,0},{20,4},{24,8},{28,12},{1,17},{... | collective-permute-start | bytes 294920 | tf_op jit(solution)/shard_map/ppermute | solution.py:390
  477.0 9.0 %collective-permute-start.45 = (bf16[128,384]{1,0:T(8,128)(2,1)}, bf16[128,384]{1,0:T(8,128)(2,1)S(1)}, u32[]{:S(2)}, u32[]{:S(2)}) collective-permute-start(bf16[128,384]{1,0:T(8,128)(2,1)} %get-tuple-element.363), channel_id=1, source_target_pairs={{0,24},{4,28},{8,16},{12,20},{16,8},{20,12},{24,0},{28,4},{1,25},{... | collective-permute-start | bytes 294920 | tf_op jit(solution)/shard_map/ppermute | solution.py:390
  (118 other events, 799.4 us)

commit v5 on v4

--- a/solution.py
+++ b/solution.py
@@ -299,10 +299,10 @@
     )(*scalars, *ins)
 
 
-def route_kernel(cap, here, message, live_ref, x_ref, nm_ref, y_ref, wz_ref, wo_ref, gain_ref, wr_ref, route_ref, cot_ref,
+def route_kernel(cap, here, message, s, live_ref, x_ref, nm_ref, y_ref, wz_ref, wo_ref, gain_ref, wr_ref, route_ref, cot_ref,
                  z_ref, gated_ref, hid_ref, place_ref, out_ref, prob_ref, gate_ref):
     bf = jnp.bfloat16
-    L = x_ref.shape[0]
+    L = nm_ref.shape[0]
     E = wr_ref.shape[0]
     z = mm(nm_ref[...], wz_ref[...])
     z_ref[...] = z
@@ -329,12 +329,12 @@
     place = jnp.where(target == lax.broadcasted_iota(jnp.int32, (L, slots), 1), 1.0, 0.0).astype(bf)
     place_ref[...] = place
     D = hid.shape[1]
-    gy = jnp.where(live, cot_ref[...], 0.0)
+    gy = jnp.where(live, cot_ref[s], 0.0)
     out_ref[:, :D] = mm(place, nmoe.astype(bf), TN).astype(bf)
     out_ref[:, D:] = mm(place, (gy * gate).astype(bf), TN).astype(bf)
 
 
-def unroute_kernel(live_ref, home_ref, place_ref, hid_ref, prob_ref, gate_ref, route_ref, cot_ref, gain_ref, wr_ref, wo_ref, sh_ref,
+def unroute_kernel(s, live_ref, home_ref, place_ref, hid_ref, prob_ref, gate_ref, route_ref, cot_ref, gain_ref, wr_ref, wo_ref, sh_ref,
                    z_ref, y_ref, mix_ref, gh_ref, gs_ref, gz_ref, gm_ref, gr_ref, gg_ref):
     bf = jnp.bfloat16
     high = lax.Precision.HIGHEST
@@ -346,7 +346,7 @@
     live = lax.broadcasted_iota(jnp.int32, (L, 1), 0) < live_ref[0]
     gate, probs = gate_ref[...], prob_ref[...]
     mix_ref[...] = jnp.where(live, hid + gate * etok, 0.0).astype(bf)
-    gy = jnp.where(live, cot_ref[...], 0.0)
+    gy = jnp.where(live, cot_ref[s], 0.0)
     ggate = jnp.sum(gy * etok, axis=-1, keepdims=True)
     hot = jnp.where(route_ref[...] == lax.broadcasted_iota(jnp.int32, (L, E), 1), 1.0, 0.0)
     glog = ggate * gate * (hot - probs)
@@ -658,7 +658,7 @@
     s_ex[...] = jnp.zeros_like(s_ex)
     s_r[...] = jnp.zeros_like(s_r)
     first[:n] = wx[...]
-    s_ex[:xp.shape[1], :xp.shape[0]] = xp[...].astype(F32).T
+    s_ex[:xp.shape[0], :xp.shape[1]] = xp[...].astype(F32)
     wide = s_ex.shape[1] - 128
     at = 0
     for v in (cw, cb, db, al, ds, gx, gm):
@@ -666,7 +666,7 @@
         at += v.shape[0]
     s_ex[26:26 + wdt.shape[0]] = wdt[...].astype(F32)
     first[n:] = s_ex[...].astype(BF)
-    s_r[:wr.shape[1], :wr.shape[0]] = wr[...].astype(F32).T
+    s_r[:wr.shape[0], :wr.shape[1]] = wr[...].astype(F32)
 
     def put(at, lane, v):
         other[at:at + v.shape[0], lane:lane + v.shape[1]] = v
@@ -687,8 +687,8 @@
 
 def pack_params(w_in_x, w_dt, w_xproj, conv_w, conv_b, dt_bias, a_log, d_skip, gain_mix, gain_moe, w_in_z, w_out, w_router):
     n, lanes = w_in_x.shape
-    ins = [w_in_x, w_dt, w_xproj, conv_w, conv_b[None], dt_bias[None], a_log, d_skip[None], gain_mix[None], gain_moe[None],
-           w_in_z, w_out, w_router]
+    ins = [w_in_x, w_dt, w_xproj.T, conv_w, conv_b[None], dt_bias[None], a_log, d_skip[None], gain_mix[None], gain_moe[None],
+           w_in_z, w_out, w_router.T]
     vmem = pl.BlockSpec(memory_space=pltpu.VMEM)
     V = lambda *s: pltpu.VMEM(s, F32)
     return pl.pallas_call(
@@ -825,7 +825,7 @@
     return functools.reduce(lambda a, b: a + b, [mm(pairs[i][...], pairs[i + 1][...], TN) for i in range(0, len(pairs), 2)])
 
 
-def grad_blocks(kernel, ins, scratch, block, rows, cols, my_col, flops):
+def grad_blocks(kernel, ins, scratch, block, rows, cols, my_col, flops, limit):
     out = sds((cols // 2, rows) + block, BF)
     return list(pl.pallas_call(
         kernel,
@@ -833,7 +833,7 @@
             num_scalar_prefetch=1, grid=(cols // 2,), in_specs=[whole_spec(v) for v in ins],
             out_specs=[pl.BlockSpec((1, rows) + block, lambda k, s: (k, 0, 0, 0))] * 2, scratch_shapes=scratch),
         out_shape=[out, out],
-        compiler_params=pltpu.CompilerParams(vmem_limit_bytes=44 << 20),
+        compiler_params=pltpu.CompilerParams(vmem_limit_bytes=limit << 20),
         cost_estimate=pl.CostEstimate(flops=flops, bytes_accessed=1 << 23, transcendentals=0),
     )(my_col.reshape(1), *ins))
 
@@ -847,7 +847,7 @@
     scratch = [pltpu.VMEM((32 * rows, inner), BF), pltpu.VMEM((32 * cols, (lanes - 128) * rows), BF), pltpu.VMEM((32, 128 * rows * cols), F32),
                pltpu.VMEM((m, inner), F32)]
     return grad_blocks(functools.partial(grad_x_kernel, len(pairs), dims), ins, scratch, (m // rows + 32, lanes), rows, cols, my_col,
-                       2 * len(pairs) * n * m * inner)
+                       2 * len(pairs) * n * m * inner, 44)
 
 
 def grad_other_kernel(count, r_cols, s_ref, *refs):
@@ -882,7 +882,7 @@
     ins = [v for p in zs for v in p] + [v for p in outs for v in p] + list(routers)
     flops = 2 * sum(a.shape[0] * a.shape[1] * b.shape[1] for a, b in zs + outs)
     scratch = [pltpu.VMEM((a.shape[1], b.shape[1]), F32) for a, b in (zs[0], outs[0])]
-    return grad_blocks(functools.partial(grad_other_kernel, len(zs), r_cols), ins, scratch, block, rows, cols, my_col, flops)
+    return grad_blocks(functools.partial(grad_other_kernel, len(zs), r_cols), ins, scratch, block, rows, cols, my_col, flops, 56)
 
 
 def split_near_kernel(plan, s_ref, keep, got, own, *gives):
@@ -940,7 +940,7 @@
     gx[...] = s[:n]
     gdt[...] = s[n + 26:n + 26 + gdt.shape[0]]
     wide = lanes - 128
-    gxp[...] = s[n:, :wide].T[:gxp.shape[0], :gxp.shape[1]]
+    gxp[...] = s[n:n + gxp.shape[0], :gxp.shape[1]]
     at = n
     for ref in (gcw, gcb, gdb, gal, gds, gmix, gmoe):
         ref[...] = s[at:at + ref.shape[0], wide:wide + ref.shape[1]]
@@ -961,7 +961,8 @@
         go[j * m // 2:(j + 1) * m // 2, :128] = s[at:at + m // 2, j * 128:(j + 1) * 128]
     for j in range(4):
         go[j * m // 4:(j + 1) * m // 4, 128:] = s[at + m // 2:at + m * 3 // 4, j * 64:(j + 1) * 64]
-    gr[...] = s[at + m * 3 // 4:, :128].T[:gr.shape[0], :gr.shape[1]]
+    at += m * 3 // 4
+    gr[...] = s[at:at + gr.shape[0], :gr.shape[1]]
 
 
 def finish(kernel, mine, gots, shapes):
@@ -1144,15 +1145,15 @@
     source = jnp.where(there < rows * CAP, there // CAP * message + at // group * CAP + there % CAP, -1)
     sort = (source[:, None] == jnp.arange(rows * message, dtype=jnp.int32)[None, :]).astype(BF)
 
-    def mixer(x, limit):
+    def mixer(s, x, limit):
         nm, inner_x, conv, u, dl, pT, ssm, starts = mixer_forward(x, gain_mix_f, full_x, full_xpT, full_dt, par, a_two, QB, limit)
-        return dict(x=x, nm=nm, inner=inner_x, conv=conv, u=u, dl=dl, pT=pT, ssm=ssm.reshape(length, inner), starts=starts)
+        return dict(x=x, s=s, nm=nm, inner=inner_x, conv=conv, u=u, dl=dl, pT=pT, ssm=ssm.reshape(length, inner), starts=starts)
 
     def router(k, route, n_live, grad):
         n_live = n_live.reshape(1)
         slots = rows * message
         z, gated, hidden, place, outgoing, probs, gate = one_call(
-            functools.partial(route_kernel, CAP, experts_here, message),
+            functools.partial(route_kernel, CAP, experts_here, message, k["s"]),
             [k["x"], k["nm"], k["ssm"], full_z, full_out, gain_moe_f, router_f, route, grad],
             [sds((length, inner)), sds((length, inner), BF), sds((length, width)), sds((length, slots), BF),
              sds((slots, 2 * width), BF), sds((length, experts_all)), sds((length, 1))],
@@ -1180,7 +1181,7 @@
 
     def unroute(k, back):
         mixed_out, gh, gs, gz, gm, g_router, g_moe = one_call(
-            unroute_kernel,
+            functools.partial(unroute_kernel, k["s"]),
             [back, k["place"], k["hidden"], k["probs"], k["gate"], k["route"], k["cot"], gain_moe_f, router_f, full_out, shifted,
              k["z"], k["ssm"]],
             [sds((length, width), BF), sds((length, width)), sds((length, inner)), sds((length, inner), BF),
@@ -1204,10 +1205,10 @@
         x = tokens[s]
         if last is not None:
             x, last = after((x, last))
-        k = mixer(x, 24 if s == 0 else 48)
+        k = mixer(s, x, 24 if s == 0 else 48)
         if s == 0:
             full_z, full_out, router_f, k["ssm"] = rest_of(k["ssm"])
-        before, (last, k) = last, router(k, routes[s], lengths[s], cotangent[s])
+        before, (last, k) = last, router(k, routes[s], lengths[s], cotangent)
         ks.append(k)
         if before is not None:
             got, last = after((home(before), last))
@@ -1264,16 +1265,16 @@
         own, gives = split_near(keep, exchange(give, core))
         gots = [exchange(v, p) for v, p in zip(gives, plane[1:])]
         gots_o, _ = after((gots_o, gives))
-        gz, go, g_router = finish(finish_other_kernel, mine_o, gots_o, [w_in_z.shape, w_out.shape, w_router.shape])
+        gz, go, g_router = finish(finish_other_kernel, mine_o, gots_o, [w_in_z.shape, w_out.shape, w_router.shape[::-1]])
         gots, gz, go, g_router = after((gots, gz, go, g_router))
         mine, gives = split_far(own, gots)
         gots = [exchange(v, p) for v, p in zip(gives, far[1:])]
         share, gshare = conv_w.shape[1], gain_mix.shape[0]
         gx, g_xproj, g_dt, gcw, gcb, gdb, gal, gds, g_mix, g_moe = finish(
             finish_x_kernel, mine, gots,
-            [w_in_x.shape, w_xproj.shape, w_dt.shape, conv_w.shape, (1, share), (1, share), a_log.shape, (1, share), (1, gshare), (1, gshare)])
+            [w_in_x.shape, w_xproj.shape[::-1], w_dt.shape, conv_w.shape, (1, share), (1, share), a_log.shape, (1, share), (1, gshare), (1, gshare)])
         blocks = (gx, gz, go)
-        small = (g_xproj, g_dt, (gcw, gcb[0], gdb[0], gal, gds[0]), g_mix[0], g_moe[0], g_router)
+        small = (g_xproj.T, g_dt, (gcw, gcb[0], gdb[0], gal, gds[0]), g_mix[0], g_moe[0], g_router.T)
     else:
         g.update(unscan(ks[-1], g["gs"], 24))
         for k, q in zip(ks, gs_):

time: 499 us -> 494 us (0.990)
  local copies, waits for them, and re-layouts: 54.6 us -> 42 us
  Pallas kernels: 237 us -> 242 us
    unnamed x236 -> x222, local copies, waits for them, and re-layouts: 48.2 us -> 38.6 us
  transfers between devices with their start and end apart: 50 -> 50, of which waited for: 16 -> 18; matrix products, arithmetic and copies ran while one was open for 4% -> 4% of each run, Pallas kernels for 38% -> 39%
where the time goes in v5:
time: 494 us; the launch traced here: 486 us
  Pallas kernels  242 us (49%)
  waiting for transfers between devices  110 us (22%)
  starting transfers between devices  67.4 us (14%)
  local copies, waits for them, and re-layouts  42 us (9%)
  other arithmetic  14 us (3%)
  matrix products  7.38 us (1%)
    ppermute x42, waiting for transfers between devices, swap(): return lax.ppermute(x, axis, [(i, i ^ bit) for i in range(n)])  96.5 us
    pallas_call x2, Pallas kernels, scan_backward(): pl.pallas_call(functools.partial(scan_back_kernel, T, Q, Q2, R), grid=(C,...  78.7 us
    pallas_call x8, Pallas kernels, one_call(): pl.pallas_call(kernel, in_specs=[smem] * len(scalars) + [vmem] * len(ins)...  53.1 us
    pallas_call x4, Pallas kernels, per_expert(): pl.pallas_call(kernel, grid=(ins[0].shape[0],), in_specs=[tok(a) for a in...  44.5 us
    ppermute x42, starting transfers between devices, swap(): return lax.ppermute(x, axis, [(i, i ^ bit) for i in range(n)])  41 us
    unnamed x222, local copies, waits for them, and re-layouts  38.6 us
    pallas_call x2, Pallas kernels, mixer_forward(): pl.pallas_call(functools.partial(mixer_kernel, T, Q, R), grid=(C,), in_sp...  38 us
    all_to_all x4, starting transfers between devices, home(): lax.all_to_all(rows_out, 'row', split_axis=0, concat_axis=0, tiled=True)  22.4 us
  transfers between devices with their start and end apart: 50, of which 18 were waited for; matrix products, arithmetic and copies ran while one was open for 4% of the time, Pallas kernels for 39%

profile of v5, /device:TPU:0, one launch (start us, length us, event | category | flops | bytes accessed | tf_op | source)
XLA Modules:
  0.0 485.6 jit_solution(17618138017980490710)
XLA Ops:
  2.5 3.0 collective-permute-start
  5.5 2.6 collective-permute-start.1
  8.5 7.6 %collective-permute-done.1 = bf16[128,384]{1,0:T(8,128)(2,1)S(1)} collective-permute-done((bf16[128,384]{1,0:T(8,128)(2,1)}, bf16[128,384]{1,0:T(8,128)(2,1)S(1)}, u32[]{:S(2)}, u32[]{:S(2)}) %collective-permute-start.1) | collective-permute-done | bytes 98336 | tf_op jit(solution)/shard_map/ppermute | solution.py:390
  17.2 2.5 collective-permute-start.5
  23.7 3.2 collective-permute-done.10
  26.9 3.4 collective-permute-done.11
  30.3 2.5 collective-permute-start.12
  32.8 2.9 collective-permute-done.3.refs_1_
  47.6 2.1 shard_map.315
  50.4 17.4 %shard_map.316 = (bf16[320,768]{1,0:T(8,128)(2,1)S(1)}, f32[328,1536]{1,0:T(8,128)S(1)}, f32[5,8,8,1536]{3,2,1,0:T(8,128)S(1)}, f32[5,8,8,1536]{3,2,1,0:T(8,128)...) custom-call(bf16[320,768]{1,0:T(8,128)(2,1)S(1)} %get-tuple-element., ...), custom_call_target="tpu_custom_call" | custom-call | flops 40000000000 | bytes 7864320 | tf_op jit(solution)/shard_map/pallas_call | solution.py:134
  81.6 3.3 shard_map.317
  88.3 10.2 %shard_map.318 = (f32[320,1536]{1,0:T(8,128)}, bf16[320,1536]{1,0:T(8,128)(2,1)}, f32[320,768]{1,0:T(8,128)}, bf16[320,448]{1,0:T(8,128)(2,1)}, bf16[448,1536]{1...) custom-call(s32[1]{0:T(128)} %get-tuple-element.383.live_ref, bf16[320,768]{1,0:T(8,128)(2,1)} %copy-done.14, ...), custom_call_target="tpu_custom_call" | custom-call | flops 2264924160 | bytes 15373824 | tf_op jit(solution)/shard_map/pallas_call | solution.py:294
  98.6 6.0 %all-to-all-start = ((bf16[8,56,1536]{2,1,0:T(8,128)(2,1)}), bf16[8,56,1536]{2,1,0:T(8,128)(2,1)S(1)}, u32[]{:S(2)}, u32[]{:S(2)}) async-start(bf16[8,56,1536]{2,1,0:T(8,128)(2,1)} %bitcast.84), calls=%async_computation | async-start | bytes 2752512 | tf_op jit(solution)/shard_map/all_to_all | solution.py:1165
  104.6 20.6 %shard_map.319 = (bf16[320,768]{1,0:T(8,128)(2,1)S(1)}, f32[328,1536]{1,0:T(8,128)}, f32[5,8,8,1536]{3,2,1,0:T(8,128)S(1)}, f32[5,8,8,1536]{3,2,1,0:T(8,128)S(1)...) custom-call(bf16[320,768]{1,0:T(8,128)(2,1)S(1)} %get-tuple-element., ...), custom_call_target="tpu_custom_call" | custom-call | flops 40000000000 | bytes 7864320 | tf_op jit(solution)/shard_map/pallas_call | solution.py:134
  129.5 10.2 %shard_map.320 = (f32[320,1536]{1,0:T(8,128)}, bf16[320,1536]{1,0:T(8,128)(2,1)}, f32[320,768]{1,0:T(8,128)}, bf16[320,448]{1,0:T(8,128)(2,1)}, bf16[448,1536]{1...) custom-call(s32[1]{0:T(128)} %get-tuple-element.384.live_ref, bf16[320,768]{1,0:T(8,128)(2,1)} %copy-done.12, ...), custom_call_target="tpu_custom_call" | custom-call | flops 2264924160 | bytes 15373824 | tf_op jit(solution)/shard_map/pallas_call | solution.py:294
  141.7 6.6 %all-to-all-start.1 = ((bf16[8,56,1536]{2,1,0:T(8,128)(2,1)}), bf16[8,56,1536]{2,1,0:T(8,128)(2,1)}, u32[]{:S(2)}, u32[]{:S(2)}) async-start(bf16[8,56,1536]{2,1,0:T(8,128)(2,1)} %bitcast.83), calls=%async_computation.1 | async-start | bytes 2752512 | tf_op jit(solution)/shard_map/all_to_all | solution.py:1165
  148.3 24.4 %collective-permute-done.20.refs_1_ = bf16[4,112,1536]{2,1,0:T(8,128)(2,1)S(1)} collective-permute-done((bf16[4,112,1536]{2,1,0:T(8,128)(2,1)S(1)}, bf16[4,112,1536]{2,1,0:T(8,128)(2,1)S(1)}, u32[]{:S(2)}, u32[]{:S(2)}) %collective-permute-start.20) | collective-permute-done | bytes 1376288 | tf_op jit(solution)/shard_map/ppermute | solution.py:390
  172.7 7.9 %all-to-all-done.1 = bf16[8,56,1536]{2,1,0:T(8,128)(2,1)} async-done(((bf16[8,56,1536]{2,1,0:T(8,128)(2,1)}), bf16[8,56,1536]{2,1,0:T(8,128)(2,1)}, u32[]{:S(2)}, u32[]{:S(2)}) %all-to-all-start.1) | async-done | bytes 1376288 | tf_op jit(solution)/shard_map/all_to_all | solution.py:1165
  180.6 2.3 convolution_convert_fusion.2
  184.0 11.9 %shard_map.321 = (bf16[4,112,1536]{2,1,0:T(8,128)(2,1)S(1)}, bf16[4,112,1536]{2,1,0:T(8,128)(2,1)S(1)}, bf16[4,112,1536]{2,1,0:T(8,128)(2,1)S(1)}, bf16[4,112,15...) custom-call(bf16[4,112,1536]{2,1,0:T(8,128)(2,1)S(1)} %bitcast.64, ...), custom_call_target="tpu_custom_call" | custom-call | flops 8455716864 | bytes 25952256 | tf_op jit(solution)/shard_map/pallas_call | solution.py:612
  196.5 16.4 %collective-permute-done.26.refs_1_.refs_6_ = bf16[4,112,1536]{2,1,0:T(8,128)(2,1)S(1)} collective-permute-done((bf16[4,112,1536]{2,1,0:T(8,128)(2,1)S(1)}, bf16[4,112,1536]{2,1,0:T(8,128)(2,1)S(1)}, u32[]{:S(2)}, u32[]{:S(2)}) %collective-permute-start.26) | collective-permute-done | bytes 1376288 | tf_op jit(solution)/shard_map/ppermute | solution.py:390
  217.2 12.3 %shard_map.322 = (bf16[4,112,1536]{2,1,0:T(8,128)(2,1)S(1)}, bf16[4,112,1536]{2,1,0:T(8,128)(2,1)S(1)}, bf16[4,112,1536]{2,1,0:T(8,128)(2,1)S(1)}, bf16[4,112,15...) custom-call(bf16[4,112,1536]{2,1,0:T(8,128)(2,1)S(1)} %bitcast.69, ...), custom_call_target="tpu_custom_call" | custom-call | flops 8455716864 | bytes 25952256 | tf_op jit(solution)/shard_map/pallas_call | solution.py:612
  229.7 17.5 %collective-permute-done.25 = bf16[4,112,1536]{2,1,0:T(8,128)(2,1)S(1)} collective-permute-done((bf16[4,112,1536]{2,1,0:T(8,128)(2,1)}, bf16[4,112,1536]{2,1,0:T(8,128)(2,1)S(1)}, u32[]{:S(2)}, u32[]{:S(2)}) %collective-permute-start.25) | collective-permute-done | bytes 1376288 | tf_op jit(solution)/shard_map/ppermute | solution.py:390
  249.8 5.9 %all-to-all-start.2 = ((bf16[8,56,1536]{2,1,0:T(8,128)(2,1)}), bf16[8,56,1536]{2,1,0:T(8,128)(2,1)}, u32[]{:S(2)}, u32[]{:S(2)}) async-start(bf16[8,56,1536]{2,1,0:T(8,128)(2,1)} %bitcast.82), calls=%async_computation.2 | async-start | bytes 2752512 | tf_op jit(solution)/shard_map/all_to_all | solution.py:1165
  255.8 3.3 add_convert_fusion.1
  262.0 10.1 %shard_map.323 = f32[4,768,768]{2,1,0:T(8,128)} custom-call(bf16[4,112,1536]{2,1,0:T(8,128)(2,1)S(1)} %bitcast.65, bf16[4,112,1536]{2,1,0:T(8,128)(2,1)S(1)} %collective-permute-done.20.refs_1_, bf16[4,112,1536]{2,1,0:T(8,128)(2,1)} %collective-permute-done.21.refs_2_, bf16[4,112,1536]{2,1,0:T(8,128)(2,1)} %collective-permute-done.22.refs_3_, ...), custom_call_target="tpu_custom_call" | custom-call | flops 4227858432 | bytes 25952256 | tf_op jit(solution)/shard_map/pallas_call | solution.py:612
  272.1 10.1 %shard_map.324 = f32[4,768,768]{2,1,0:T(8,128)} custom-call(bf16[4,112,1536]{2,1,0:T(8,128)(2,1)S(1)} %bitcast.66, bf16[4,112,1536]{2,1,0:T(8,128)(2,1)S(1)} %collective-permute-done.20.refs_1_, bf16[4,112,1536]{2,1,0:T(8,128)(2,1)} %collective-permute-done.21.refs_2_, bf16[4,112,1536]{2,1,0:T(8,128)(2,1)} %collective-permute-done.22.refs_3_, ...), custom_call_target="tpu_custom_call" | custom-call | flops 4227858432 | bytes 25952256 | tf_op jit(solution)/shard_map/pallas_call | solution.py:612
  282.3 5.7 %all-to-all-done.2 = bf16[8,56,1536]{2,1,0:T(8,128)(2,1)} async-done(((bf16[8,56,1536]{2,1,0:T(8,128)(2,1)}), bf16[8,56,1536]{2,1,0:T(8,128)(2,1)}, u32[]{:S(2)}, u32[]{:S(2)}) %all-to-all-start.2) | async-done | bytes 1376288 | tf_op jit(solution)/shard_map/all_to_all | solution.py:1165
  288.0 11.7 %shard_map.325 = (bf16[320,768]{1,0:T(8,128)(2,1)}, f32[320,768]{1,0:T(8,128)}, f32[320,1536]{1,0:T(8,128)}, bf16[320,1536]{1,0:T(8,128)(2,1)}, bf16[320,1024]{1...) custom-call(s32[1]{0:T(128)} %get-tuple-element.383.live_ref, bf16[448,1536]{1,0:T(8,128)(2,1)} %bitcast.31.home_ref, ...), custom_call_target="tpu_custom_call" | custom-call | flops 2264924160 | bytes 17801728 | tf_op jit(solution)/shard_map/pallas_call | solution.py:294
  299.8 2.4 add_convert_fusion
  302.2 2.1 convolution_convert_fusion
  304.3 3.9 all-to-all-start.3
  308.2 40.9 %shard_map.326 = (bf16[320,1536]{1,0:T(8,128)(2,1)}, f32[80,1536]{1,0:T(8,128)S(1)}, f32[48,1536]{1,0:T(8,128)S(1)}, f32[23,1536]{1,0:T(8,128)S(1)}) custom-call(f32[5,8,8,1536]{3,2,1,0:T(8,128)} %copy-done.83, f32[5,8,8,1536]{3,2,1,0:T(8,128)} %copy-done.84, f32[5,8,8,1536]{3,2,1,0:T(8,128)} %bitcast.105, f32[5,8,8,1536]{3,2,1,0:T(8,128)} %copy-done.82, ...), custom_call_target="tpu_custom_call" | custom-call | flops 80000000000 | bytes 7864320 | tf_op jit(solution)/shard_map/pallas_call | solution.py:278
  352.4 11.7 %shard_map.327 = (bf16[320,768]{1,0:T(8,128)(2,1)}, f32[320,768]{1,0:T(8,128)}, f32[320,1536]{1,0:T(8,128)}, bf16[320,1536]{1,0:T(8,128)(2,1)}, bf16[320,1024]{1...) custom-call(s32[1]{0:T(128)} %get-tuple-element.384.live_ref, bf16[448,1536]{1,0:T(8,128)(2,1)} %bitcast.81, ...), custom_call_target="tpu_custom_call" | custom-call | flops 2264924160 | bytes 17801728 | tf_op jit(solution)/shard_map/pallas_call | solution.py:294
  364.1 11.7 %shard_map.328 = (bf16[2,8,304,256]{3,2,1,0:T(8,128)(2,1)}, bf16[2,8,304,256]{3,2,1,0:T(8,128)(2,1)}) custom-call(s32[1]{0:T(128)} %bitcast.3.s_ref, bf16[320,768]{1,0:T(8,128)(2,1)} %copy-done.37, bf16[320,1536]{1,0:T(8,128)(2,1)} %get-tuple-element.288.refs_1_.gz_ref, bf16[320,768]{1,0:T(8,128)(2,1)} %copy-done.39, ...), custom_call_target="tpu_custom_call" | custom-call | flops 3523215360 | bytes 8388608 | tf_op jit(solution)/shard_map/pallas_call | solution.py:830
  378.1 2.8 collective-permute-done.32
  387.6 37.8 %shard_map.331 = (bf16[320,1536]{1,0:T(8,128)(2,1)S(1)}, f32[80,1536]{1,0:T(8,128)S(1)}, f32[48,1536]{1,0:T(8,128)S(1)}, f32[23,1536]{1,0:T(8,128)S(1)}) custom-call(f32[5,8,8,1536]{3,2,1,0:T(8,128)S(1)} %copy-done.80, f32[5,8,8,1536]{3,2,1,0:T(8,128)S(1)} %copy-done.81, f32[5,8,8,1536]{3,2,1,0:T(8,128)S(1)} %bitcast.78, f32[5,8,8,1536]{3,2,1,0:T(8,128)S(1)} %copy-done.78, ...), custom_call_target="tpu_custom_call" | custom-call | flops 80000000000 | bytes 7864320 | tf_op jit(solution)/shard_map/pallas_call | solution.py:278
  429.8 3.0 shard_map.332
  437.1 3.5 shard_map.334
  440.7 3.4 collective-permute-done.36
  450.4 2.4 collective-permute-start.41
  452.8 3.5 collective-permute-done.40.refs_1_
  456.3 3.4 collective-permute-start.42
  460.8 3.1 collective-permute-done.41.refs_2_
  465.3 2.1 shard_map.336
  468.1 2.3 shard_map.337
  470.4 2.3 collective-permute-start.43
  476.5 6.1 %collective-permute-done.44.refs_2_ = bf16[128,384]{1,0:T(8,128)(2,1)S(1)} collective-permute-done((bf16[128,384]{1,0:T(8,128)(2,1)}, bf16[128,384]{1,0:T(8,128)(2,1)S(1)}, u32[]{:S(2)}, u32[]{:S(2)}) %collective-permute-start.44) | collective-permute-done | bytes 98336 | tf_op jit(solution)/shard_map/ppermute | solution.py:390
  (320 shorter events, 91.2 us)
Async XLA Ops:
  2.5 6.0 %collective-permute-start = (bf16[128,384]{1,0:T(8,128)(2,1)}, bf16[128,384]{1,0:T(8,128)(2,1)S(1)}, u32[]{:S(2)}, u32[]{:S(2)}) collective-permute-start(bf16[128,384]{1,0:T(8,128)(2,1)} %get-tuple-element.198), channel_id=1, source_target_pairs={{0,8},{4,12},{8,0},{12,4},{16,24},{20,28},{24,16},{28,20},{1,9},{5... | collective-permute-start | bytes 294920 | tf_op jit(solution)/shard_map/ppermute | solution.py:390
  5.5 10.6 %collective-permute-start.1 = (bf16[128,384]{1,0:T(8,128)(2,1)}, bf16[128,384]{1,0:T(8,128)(2,1)S(1)}, u32[]{:S(2)}, u32[]{:S(2)}) collective-permute-start(bf16[128,384]{1,0:T(8,128)(2,1)} %get-tuple-element.198), channel_id=1, source_target_pairs={{0,16},{4,20},{8,24},{12,28},{16,0},{20,4},{24,8},{28,12},{1,17},{... | collective-permute-start | bytes 294920 | tf_op jit(solution)/shard_map/ppermute | solution.py:390
  8.1 8.1 %collective-permute-start.2 = (bf16[128,384]{1,0:T(8,128)(2,1)}, bf16[128,384]{1,0:T(8,128)(2,1)S(1)}, u32[]{:S(2)}, u32[]{:S(2)}) collective-permute-start(bf16[128,384]{1,0:T(8,128)(2,1)} %get-tuple-element.198), channel_id=1, source_target_pairs={{0,24},{4,28},{8,16},{12,20},{16,8},{20,12},{24,0},{28,4},{1,25},{... | collective-permute-start | bytes 294920 | tf_op jit(solution)/shard_map/ppermute | solution.py:390
  17.2 15.6 %collective-permute-start.5 = (bf16[4,128,384]{2,1,0:T(8,128)(2,1)S(1)}, bf16[4,128,384]{2,1,0:T(8,128)(2,1)S(1)}, u32[]{:S(2)}, u32[]{:S(2)}) collective-permute-start(bf16[4,128,384]{2,1,0:T(8,128)(2,1)S(1)} %pad_maximum_fusion.3.refs_0_), channel_id=1, source_target_pairs={{0,6},{1,7},{2,4},{3,5},{4,2},{5,3},{6,0},{7,1},{8,14},{9,15},{10,... | collective-permute-start | bytes 1179656 | tf_op jit(solution)/shard_map/ppermute | solution.py:406
  19.7 16.0 %collective-permute-start.3 = (bf16[4,128,384]{2,1,0:T(8,128)(2,1)S(1)}, bf16[4,128,384]{2,1,0:T(8,128)(2,1)}, u32[]{:S(2)}, u32[]{:S(2)}) collective-permute-start(bf16[4,128,384]{2,1,0:T(8,128)(2,1)S(1)} %pad_maximum_fusion.3.refs_0_), channel_id=1, source_target_pairs={{0,4},{4,0},{8,12},{12,8},{16,20},{20,16},{24,28},{28,24},{1,5},{5... | collective-permute-start | bytes 1179656 | tf_op jit(solution)/shard_map/ppermute | solution.py:390
  20.2 15.5 %collective-permute-start.4 = (bf16[4,128,384]{2,1,0:T(8,128)(2,1)S(1)}, bf16[4,128,384]{2,1,0:T(8,128)(2,1)}, u32[]{:S(2)}, u32[]{:S(2)}) collective-permute-start(bf16[4,128,384]{2,1,0:T(8,128)(2,1)S(1)} %pad_maximum_fusion.3.refs_0_), channel_id=1, source_target_pairs={{0,2},{1,3},{2,0},{3,1},{4,6},{5,7},{6,4},{7,5},{8,10},{9,11},{10,... | collective-permute-start | bytes 1179656 | tf_op jit(solution)/shard_map/ppermute | solution.py:390
  20.7 6.2 %collective-permute-start.10 = (bf16[304,256]{1,0:T(8,128)(2,1)}, bf16[304,256]{1,0:T(8,128)(2,1)S(1)}, u32[]{:S(2)}, u32[]{:S(2)}) collective-permute-start(bf16[304,256]{1,0:T(8,128)(2,1)} %get-tuple-element.207), channel_id=1, source_target_pairs={{0,8},{4,12},{8,0},{12,4},{16,24},{20,28},{24,16},{28,20},{1,9},{5... | collective-permute-start | bytes 466952 | tf_op jit(solution)/shard_map/ppermute | solution.py:390
  22.3 8.0 %collective-permute-start.11 = (bf16[304,256]{1,0:T(8,128)(2,1)}, bf16[304,256]{1,0:T(8,128)(2,1)S(1)}, u32[]{:S(2)}, u32[]{:S(2)}) collective-permute-start(bf16[304,256]{1,0:T(8,128)(2,1)} %get-tuple-element.207), channel_id=1, source_target_pairs={{0,16},{4,20},{8,24},{12,28},{16,0},{20,4},{24,8},{28,12},{1,17},{... | collective-permute-start | bytes 466952 | tf_op jit(solution)/shard_map/ppermute | solution.py:390
  26.9 13.2 %collective-permute-start.6 = (bf16[4,128,384]{2,1,0:T(8,128)(2,1)S(1)}, bf16[4,128,384]{2,1,0:T(8,128)(2,1)S(1)}, u32[]{:S(2)}, u32[]{:S(2)}) collective-permute-start(bf16[4,128,384]{2,1,0:T(8,128)(2,1)S(1)} %pad_maximum_fusion.3.refs_0_), channel_id=1, source_target_pairs={{0,1},{1,0},{2,3},{3,2},{4,5},{5,4},{6,7},{7,6},{8,9},{9,8},{10,11... | collective-permute-start | bytes 1179656 | tf_op jit(solution)/shard_map/ppermute | solution.py:390
  30.3 7.2 %collective-permute-start.12 = (bf16[304,256]{1,0:T(8,128)(2,1)}, bf16[304,256]{1,0:T(8,128)(2,1)S(1)}, u32[]{:S(2)}, u32[]{:S(2)}) collective-permute-start(bf16[304,256]{1,0:T(8,128)(2,1)} %get-tuple-element.207), channel_id=1, source_target_pairs={{0,24},{4,28},{8,16},{12,20},{16,8},{20,12},{24,0},{28,4},{1,25},{... | collective-permute-start | bytes 466952 | tf_op jit(solution)/shard_map/ppermute | solution.py:390
  32.8 9.5 %collective-permute-start.9 = (bf16[4,128,384]{2,1,0:T(8,128)(2,1)S(1)}, bf16[4,128,384]{2,1,0:T(8,128)(2,1)S(1)}, u32[]{:S(2)}, u32[]{:S(2)}) collective-permute-start(bf16[4,128,384]{2,1,0:T(8,128)(2,1)S(1)} %collective-permute-done.5.refs_3_), channel_id=1, source_target_pairs={{0,1},{1,0},{2,3},{3,2},{4,5},{5,4},{6,7},{7,6},{8,9},{9,8},{10,11... | collective-permute-start | bytes 1179656 | tf_op jit(solution)/shard_map/ppermute | solution.py:390
  35.7 7.9 %collective-permute-start.7 = (bf16[4,128,384]{2,1,0:T(8,128)(2,1)}, bf16[4,128,384]{2,1,0:T(8,128)(2,1)}, u32[]{:S(2)}, u32[]{:S(2)}) collective-permute-start(bf16[4,128,384]{2,1,0:T(8,128)(2,1)} %collective-permute-done.3.refs_1_), channel_id=1, source_target_pairs={{0,1},{1,0},{2,3},{3,2},{4,5},{5,4},{6,7},{7,6},{8,9},{9,8},{10,11... | collective-permute-start | bytes 1179656 | tf_op jit(solution)/shard_map/ppermute | solution.py:390
  35.7 7.9 %collective-permute-start.8 = (bf16[4,128,384]{2,1,0:T(8,128)(2,1)}, bf16[4,128,384]{2,1,0:T(8,128)(2,1)}, u32[]{:S(2)}, u32[]{:S(2)}) collective-permute-start(bf16[4,128,384]{2,1,0:T(8,128)(2,1)} %collective-permute-done.4.refs_2_), channel_id=1, source_target_pairs={{0,1},{1,0},{2,3},{3,2},{4,5},{5,4},{6,7},{7,6},{8,9},{9,8},{10,11... | collective-permute-start | bytes 1179656 | tf_op jit(solution)/shard_map/ppermute | solution.py:390
  38.6 38.0 %collective-permute-start.13 = (bf16[4,304,256]{2,1,0:T(8,128)(2,1)}, bf16[4,304,256]{2,1,0:T(8,128)(2,1)S(1)}, u32[]{:S(2)}, u32[]{:S(2)}) collective-permute-start(bf16[4,304,256]{2,1,0:T(8,128)(2,1)} %pad_maximum_fusion.2.refs_0_), channel_id=1, source_target_pairs={{0,4},{4,0},{8,12},{12,8},{16,20},{20,16},{24,28},{28,24},{1,5},{5... | collective-permute-start | bytes 1867784 | tf_op jit(solution)/shard_map/ppermute | solution.py:390
  40.9 35.8 %collective-permute-start.14 = (bf16[4,304,256]{2,1,0:T(8,128)(2,1)}, bf16[4,304,256]{2,1,0:T(8,128)(2,1)S(1)}, u32[]{:S(2)}, u32[]{:S(2)}) collective-permute-start(bf16[4,304,256]{2,1,0:T(8,128)(2,1)} %pad_maximum_fusion.2.refs_0_), channel_id=1, source_target_pairs={{0,2},{1,3},{2,0},{3,1},{4,6},{5,7},{6,4},{7,5},{8,10},{9,11},{10,... | collective-permute-start | bytes 1867784 | tf_op jit(solution)/shard_map/ppermute | solution.py:390
  43.0 33.6 %collective-permute-start.15 = (bf16[4,304,256]{2,1,0:T(8,128)(2,1)}, bf16[4,304,256]{2,1,0:T(8,128)(2,1)S(1)}, u32[]{:S(2)}, u32[]{:S(2)}) collective-permute-start(bf16[4,304,256]{2,1,0:T(8,128)(2,1)} %pad_maximum_fusion.2.refs_0_), channel_id=1, source_target_pairs={{0,6},{1,7},{2,4},{3,5},{4,2},{5,3},{6,0},{7,1},{8,14},{9,15},{10,... | collective-permute-start | bytes 1867784 | tf_op jit(solution)/shard_map/ppermute | solution.py:406
  76.7 3.3 collective-permute-start.16
  77.3 3.5 collective-permute-start.18
  77.3 4.3 collective-permute-start.19
  98.6 41.1 %all-to-all-start = ((bf16[8,56,1536]{2,1,0:T(8,128)(2,1)}), bf16[8,56,1536]{2,1,0:T(8,128)(2,1)S(1)}, u32[]{:S(2)}, u32[]{:S(2)}) async-start(bf16[8,56,1536]{2,1,0:T(8,128)(2,1)} %bitcast.84), calls=%async_computation | async-start | bytes 2752512 | tf_op jit(solution)/shard_map/all_to_all | solution.py:1165
  140.7 32.0 %collective-permute-start.20 = (bf16[4,112,1536]{2,1,0:T(8,128)(2,1)S(1)}, bf16[4,112,1536]{2,1,0:T(8,128)(2,1)S(1)}, u32[]{:S(2)}, u32[]{:S(2)}) collective-permute-start(bf16[4,112,1536]{2,1,0:T(8,128)(2,1)S(1)} %bitcast.62), channel_id=1, source_target_pairs={{0,2},{1,3},{2,0},{3,1},{4,6},{5,7},{6,4},{7,5},{8,10},{9,11},{10,... | collective-permute-start | bytes 4128776 | tf_op jit(solution)/shard_map/ppermute | solution.py:390
  141.7 38.9 %all-to-all-start.1 = ((bf16[8,56,1536]{2,1,0:T(8,128)(2,1)}), bf16[8,56,1536]{2,1,0:T(8,128)(2,1)}, u32[]{:S(2)}, u32[]{:S(2)}) async-start(bf16[8,56,1536]{2,1,0:T(8,128)(2,1)} %bitcast.83), calls=%async_computation.1 | async-start | bytes 2752512 | tf_op jit(solution)/shard_map/all_to_all | solution.py:1165
  148.2 34.6 %collective-permute-start.21 = (bf16[4,112,1536]{2,1,0:T(8,128)(2,1)S(1)}, bf16[4,112,1536]{2,1,0:T(8,128)(2,1)}, u32[]{:S(2)}, u32[]{:S(2)}) collective-permute-start(bf16[4,112,1536]{2,1,0:T(8,128)(2,1)S(1)} %bitcast.63), channel_id=1, source_target_pairs={{0,1},{1,0},{2,3},{3,2},{4,5},{5,4},{6,7},{7,6},{8,9},{9,8},{10,11... | collective-permute-start | bytes 4128776 | tf_op jit(solution)/shard_map/ppermute | solution.py:390
  172.7 10.2 %collective-permute-start.22 = (bf16[4,112,1536]{2,1,0:T(8,128)(2,1)S(1)}, bf16[4,112,1536]{2,1,0:T(8,128)(2,1)}, u32[]{:S(2)}, u32[]{:S(2)}) collective-permute-start(bf16[4,112,1536]{2,1,0:T(8,128)(2,1)S(1)} %collective-permute-done.20.refs_1_), channel_id=1, source_target_pairs={{0,1},{1,0},{2,3},{3,2},{4,5},{5,4},{6,7},{7,6},{8,9},{9,8},{10,11... | collective-permute-start | bytes 4128776 | tf_op jit(solution)/shard_map/ppermute | solution.py:390
  182.9 30.0 %collective-permute-start.26 = (bf16[4,112,1536]{2,1,0:T(8,128)(2,1)S(1)}, bf16[4,112,1536]{2,1,0:T(8,128)(2,1)S(1)}, u32[]{:S(2)}, u32[]{:S(2)}) collective-permute-start(bf16[4,112,1536]{2,1,0:T(8,128)(2,1)S(1)} %bitcast.67), channel_id=1, source_target_pairs={{0,2},{1,3},{2,0},{3,1},{4,6},{5,7},{6,4},{7,5},{8,10},{9,11},{10,... | collective-permute-start | bytes 4128776 | tf_op jit(solution)/shard_map/ppermute | solution.py:390
  196.0 17.5 %collective-permute-start.24 = (bf16[4,112,1536]{2,1,0:T(8,128)(2,1)S(1)}, bf16[4,112,1536]{2,1,0:T(8,128)(2,1)S(1)}, u32[]{:S(2)}, u32[]{:S(2)}) collective-permute-start(bf16[4,112,1536]{2,1,0:T(8,128)(2,1)S(1)} %get-tuple-element.234), channel_id=1, source_target_pairs={{0,1},{1,0},{2,3},{3,2},{4,5},{5,4},{6,7},{7,6},{8,9},{9,8},{10,11... | collective-permute-start | bytes 4128776 | tf_op jit(solution)/shard_map/ppermute | solution.py:390
  196.0 20.0 %collective-permute-start.27 = (bf16[4,112,1536]{2,1,0:T(8,128)(2,1)S(1)}, bf16[4,112,1536]{2,1,0:T(8,128)(2,1)S(1)}, u32[]{:S(2)}, u32[]{:S(2)}) collective-permute-start(bf16[4,112,1536]{2,1,0:T(8,128)(2,1)S(1)} %bitcast.68), channel_id=1, source_target_pairs={{0,1},{1,0},{2,3},{3,2},{4,5},{5,4},{6,7},{7,6},{8,9},{9,8},{10,11... | collective-permute-start | bytes 4128776 | tf_op jit(solution)/shard_map/ppermute | solution.py:390
  212.9 16.7 %collective-permute-start.23 = (bf16[4,112,1536]{2,1,0:T(8,128)(2,1)S(1)}, bf16[4,112,1536]{2,1,0:T(8,128)(2,1)S(1)}, u32[]{:S(2)}, u32[]{:S(2)}) collective-permute-start(bf16[4,112,1536]{2,1,0:T(8,128)(2,1)S(1)} %get-tuple-element.232), channel_id=1, source_target_pairs={{0,1},{1,0},{2,3},{3,2},{4,5},{5,4},{6,7},{7,6},{8,9},{9,8},{10,11... | collective-permute-start | bytes 4128776 | tf_op jit(solution)/shard_map/ppermute | solution.py:390
  214.9 32.3 %collective-permute-start.25 = (bf16[4,112,1536]{2,1,0:T(8,128)(2,1)}, bf16[4,112,1536]{2,1,0:T(8,128)(2,1)S(1)}, u32[]{:S(2)}, u32[]{:S(2)}) collective-permute-start(bf16[4,112,1536]{2,1,0:T(8,128)(2,1)} %add_convert_fusion.4), channel_id=1, source_target_pairs={{0,2},{1,3},{2,0},{3,1},{4,6},{5,7},{6,4},{7,5},{8,10},{9,11},{10,... | collective-permute-start | bytes 4128776 | tf_op jit(solution)/shard_map/ppermute | solution.py:390
  229.5 26.3 %collective-permute-start.30 = (bf16[4,112,1536]{2,1,0:T(8,128)(2,1)}, bf16[4,112,1536]{2,1,0:T(8,128)(2,1)}, u32[]{:S(2)}, u32[]{:S(2)}) collective-permute-start(bf16[4,112,1536]{2,1,0:T(8,128)(2,1)} %get-tuple-element.273), channel_id=1, source_target_pairs={{0,1},{1,0},{2,3},{3,2},{4,5},{5,4},{6,7},{7,6},{8,9},{9,8},{10,11... | collective-permute-start | bytes 4128776 | tf_op jit(solution)/shard_map/ppermute | solution.py:390
  249.8 38.2 %all-to-all-start.2 = ((bf16[8,56,1536]{2,1,0:T(8,128)(2,1)}), bf16[8,56,1536]{2,1,0:T(8,128)(2,1)}, u32[]{:S(2)}, u32[]{:S(2)}) async-start(bf16[8,56,1536]{2,1,0:T(8,128)(2,1)} %bitcast.82), calls=%async_computation.2 | async-start | bytes 2752512 | tf_op jit(solution)/shard_map/all_to_all | solution.py:1165
  255.7 44.0 %collective-permute-start.29 = (bf16[4,112,1536]{2,1,0:T(8,128)(2,1)}, bf16[4,112,1536]{2,1,0:T(8,128)(2,1)}, u32[]{:S(2)}, u32[]{:S(2)}) collective-permute-start(bf16[4,112,1536]{2,1,0:T(8,128)(2,1)} %copy-done.49), channel_id=1, source_target_pairs={{0,1},{1,0},{2,3},{3,2},{4,5},{5,4},{6,7},{7,6},{8,9},{9,8},{10,11... | collective-permute-start | bytes 4128776 | tf_op jit(solution)/shard_map/ppermute | solution.py:390
  259.2 40.6 %collective-permute-start.31 = (bf16[4,112,1536]{2,1,0:T(8,128)(2,1)}, bf16[4,112,1536]{2,1,0:T(8,128)(2,1)}, u32[]{:S(2)}, u32[]{:S(2)}) collective-permute-start(bf16[4,112,1536]{2,1,0:T(8,128)(2,1)} %add_convert_fusion.1), channel_id=1, source_target_pairs={{0,2},{1,3},{2,0},{3,1},{4,6},{5,7},{6,4},{7,5},{8,10},{9,11},{10,... | collective-permute-start | bytes 4128776 | tf_op jit(solution)/shard_map/ppermute | solution.py:390
  304.3 47.1 %all-to-all-start.3 = ((bf16[8,56,1536]{2,1,0:T(8,128)(2,1)}), bf16[8,56,1536]{2,1,0:T(8,128)(2,1)S(1)}, u32[]{:S(2)}, u32[]{:S(2)}) async-start(bf16[8,56,1536]{2,1,0:T(8,128)(2,1)} %bitcast.35), calls=%async_computation.3 | async-start | bytes 2752512 | tf_op jit(solution)/shard_map/all_to_all | solution.py:1165
  375.9 5.0 %collective-permute-start.32 = (bf16[2,8,304,256]{3,2,1,0:T(8,128)(2,1)}, bf16[2,8,304,256]{3,2,1,0:T(8,128)(2,1)S(1)}, u32[]{:S(2)}, u32[]{:S(2)}) collective-permute-start(bf16[2,8,304,256]{3,2,1,0:T(8,128)(2,1)} %get-tuple-element.296), channel_id=1, source_target_pairs={{0,1},{1,0},{2,3},{3,2},{4,5},{5,4},{6,7},{7,6},{8,9},{9,8},{10,11... | collective-permute-start | bytes 7471112 | tf_op jit(solution)/shard_map/ppermute | solution.py:390
  383.0 45.5 %collective-permute-start.33 = (bf16[4,304,256]{2,1,0:T(8,128)(2,1)S(1)}, bf16[4,304,256]{2,1,0:T(8,128)(2,1)S(1)}, u32[]{:S(2)}, u32[]{:S(2)}) collective-permute-start(bf16[4,304,256]{2,1,0:T(8,128)(2,1)S(1)} %get-tuple-element.309), channel_id=1, source_target_pairs={{0,4},{4,0},{8,12},{12,8},{16,20},{20,16},{24,28},{28,24},{1,5},{5... | collective-permute-start | bytes 1867784 | tf_op jit(solution)/shard_map/ppermute | solution.py:390
  385.0 43.5 %collective-permute-start.34 = (bf16[4,304,256]{2,1,0:T(8,128)(2,1)S(1)}, bf16[4,304,256]{2,1,0:T(8,128)(2,1)S(1)}, u32[]{:S(2)}, u32[]{:S(2)}) collective-permute-start(bf16[4,304,256]{2,1,0:T(8,128)(2,1)S(1)} %get-tuple-element.310), channel_id=1, source_target_pairs={{0,2},{1,3},{2,0},{3,1},{4,6},{5,7},{6,4},{7,5},{8,10},{9,11},{10,... | collective-permute-start | bytes 1867784 | tf_op jit(solution)/shard_map/ppermute | solution.py:390
  386.1 42.4 %collective-permute-start.35 = (bf16[4,304,256]{2,1,0:T(8,128)(2,1)S(1)}, bf16[4,304,256]{2,1,0:T(8,128)(2,1)S(1)}, u32[]{:S(2)}, u32[]{:S(2)}) collective-permute-start(bf16[4,304,256]{2,1,0:T(8,128)(2,1)S(1)} %get-tuple-element.311), channel_id=1, source_target_pairs={{0,6},{1,7},{2,4},{3,5},{4,2},{5,3},{6,0},{7,1},{8,14},{9,15},{10,... | collective-permute-start | bytes 1867784 | tf_op jit(solution)/shard_map/ppermute | solution.py:406
  440.6 3.5 collective-permute-start.36
  444.9 22.5 %collective-permute-start.37 = (bf16[4,128,384]{2,1,0:T(8,128)(2,1)S(1)}, bf16[4,128,384]{2,1,0:T(8,128)(2,1)S(1)}, u32[]{:S(2)}, u32[]{:S(2)}) collective-permute-start(bf16[4,128,384]{2,1,0:T(8,128)(2,1)S(1)} %get-tuple-element.344), channel_id=1, source_target_pairs={{0,4},{4,0},{8,12},{12,8},{16,20},{20,16},{24,28},{28,24},{1,5},{5... | collective-permute-start | bytes 1179656 | tf_op jit(solution)/shard_map/ppermute | solution.py:390
  446.9 20.4 %collective-permute-start.38 = (bf16[4,128,384]{2,1,0:T(8,128)(2,1)S(1)}, bf16[4,128,384]{2,1,0:T(8,128)(2,1)}, u32[]{:S(2)}, u32[]{:S(2)}) collective-permute-start(bf16[4,128,384]{2,1,0:T(8,128)(2,1)S(1)} %get-tuple-element.345), channel_id=1, source_target_pairs={{0,2},{1,3},{2,0},{3,1},{4,6},{5,7},{6,4},{7,5},{8,10},{9,11},{10,... | collective-permute-start | bytes 1179656 | tf_op jit(solution)/shard_map/ppermute | solution.py:390
  448.0 19.4 %collective-permute-start.39 = (bf16[4,128,384]{2,1,0:T(8,128)(2,1)S(1)}, bf16[4,128,384]{2,1,0:T(8,128)(2,1)}, u32[]{:S(2)}, u32[]{:S(2)}) collective-permute-start(bf16[4,128,384]{2,1,0:T(8,128)(2,1)S(1)} %get-tuple-element.346), channel_id=1, source_target_pairs={{0,6},{1,7},{2,4},{3,5},{4,2},{5,3},{6,0},{7,1},{8,14},{9,15},{10,... | collective-permute-start | bytes 1179656 | tf_op jit(solution)/shard_map/ppermute | solution.py:406
  448.5 7.9 %collective-permute-start.40 = (bf16[304,256]{1,0:T(8,128)(2,1)S(1)}, bf16[304,256]{1,0:T(8,128)(2,1)}, u32[]{:S(2)}, u32[]{:S(2)}) collective-permute-start(bf16[304,256]{1,0:T(8,128)(2,1)S(1)} %copy-done.110), channel_id=1, source_target_pairs={{0,8},{4,12},{8,0},{12,4},{16,24},{20,28},{24,16},{28,20},{1,9},{5... | collective-permute-start | bytes 466952 | tf_op jit(solution)/shard_map/ppermute | solution.py:390
  450.4 13.5 %collective-permute-start.41 = (bf16[304,256]{1,0:T(8,128)(2,1)S(1)}, bf16[304,256]{1,0:T(8,128)(2,1)S(1)}, u32[]{:S(2)}, u32[]{:S(2)}) collective-permute-start(bf16[304,256]{1,0:T(8,128)(2,1)S(1)} %copy-done.109), channel_id=1, source_target_pairs={{0,16},{4,20},{8,24},{12,28},{16,0},{20,4},{24,8},{28,12},{1,17},{... | collective-permute-start | bytes 466952 | tf_op jit(solution)/shard_map/ppermute | solution.py:390
  456.3 7.6 %collective-permute-start.42 = (bf16[304,256]{1,0:T(8,128)(2,1)S(1)}, bf16[304,256]{1,0:T(8,128)(2,1)S(1)}, u32[]{:S(2)}, u32[]{:S(2)}) collective-permute-start(bf16[304,256]{1,0:T(8,128)(2,1)S(1)} %copy-done.108), channel_id=1, source_target_pairs={{0,24},{4,28},{8,16},{12,20},{16,8},{20,12},{24,0},{28,4},{1,25},{... | collective-permute-start | bytes 466952 | tf_op jit(solution)/shard_map/ppermute | solution.py:390
  470.4 6.1 %collective-permute-start.43 = (bf16[128,384]{1,0:T(8,128)(2,1)}, bf16[128,384]{1,0:T(8,128)(2,1)S(1)}, u32[]{:S(2)}, u32[]{:S(2)}) collective-permute-start(bf16[128,384]{1,0:T(8,128)(2,1)} %get-tuple-element.361), channel_id=1, source_target_pairs={{0,8},{4,12},{8,0},{12,4},{16,24},{20,28},{24,16},{28,20},{1,9},{5... | collective-permute-start | bytes 294920 | tf_op jit(solution)/shard_map/ppermute | solution.py:390
  472.7 9.9 %collective-permute-start.44 = (bf16[128,384]{1,0:T(8,128)(2,1)}, bf16[128,384]{1,0:T(8,128)(2,1)S(1)}, u32[]{:S(2)}, u32[]{:S(2)}) collective-permute-start(bf16[128,384]{1,0:T(8,128)(2,1)} %get-tuple-element.362), channel_id=1, source_target_pairs={{0,16},{4,20},{8,24},{12,28},{16,0},{20,4},{24,8},{28,12},{1,17},{... | collective-permute-start | bytes 294920 | tf_op jit(solution)/shard_map/ppermute | solution.py:390
  473.6 9.0 %collective-permute-start.45 = (bf16[128,384]{1,0:T(8,128)(2,1)}, bf16[128,384]{1,0:T(8,128)(2,1)S(1)}, u32[]{:S(2)}, u32[]{:S(2)}) collective-permute-start(bf16[128,384]{1,0:T(8,128)(2,1)} %get-tuple-element.363), channel_id=1, source_target_pairs={{0,24},{4,28},{8,16},{12,20},{16,8},{20,12},{24,0},{28,4},{1,25},{... | collective-permute-start | bytes 294920 | tf_op jit(solution)/shard_map/ppermute | solution.py:390
  (113 other events, 774.2 us)

commit v6 on v5

--- a/solution.py
+++ b/solution.py
@@ -300,7 +300,7 @@
 
 
 def route_kernel(cap, here, message, s, live_ref, x_ref, nm_ref, y_ref, wz_ref, wo_ref, gain_ref, wr_ref, route_ref, cot_ref,
-                 z_ref, gated_ref, hid_ref, place_ref, out_ref, prob_ref, gate_ref):
+                 z_ref, gated_ref, hid_ref, target_ref, out_ref, prob_ref, gate_ref):
     bf = jnp.bfloat16
     L = nm_ref.shape[0]
     E = wr_ref.shape[0]
@@ -323,26 +323,55 @@
     hits = jnp.where(hot & live, 1.0, 0.0)
     before = lax.broadcasted_iota(jnp.int32, (L, L), 0) > lax.broadcasted_iota(jnp.int32, (L, L), 1)
     slot = jnp.sum(mm(jnp.where(before, 1.0, 0.0).astype(bf), hits.astype(bf)) * hits, axis=-1, keepdims=True).astype(jnp.int32)
-    slots = place_ref.shape[1]
+    slots = out_ref.shape[0]
     target = route // here * message + route % here * cap + slot
-    target = jnp.where(live & (slot < cap), target, slots)
-    place = jnp.where(target == lax.broadcasted_iota(jnp.int32, (L, slots), 1), 1.0, 0.0).astype(bf)
-    place_ref[...] = place
-    D = hid.shape[1]
+    target = jnp.where(live & (slot < cap), target, -slots)
+    target_ref[...] = target
     gy = jnp.where(live, cot_ref[s], 0.0)
-    out_ref[:, :D] = mm(place, nmoe.astype(bf), TN).astype(bf)
-    out_ref[:, D:] = mm(place, (gy * gate).astype(bf), TN).astype(bf)
-
-
-def unroute_kernel(s, live_ref, home_ref, place_ref, hid_ref, prob_ref, gate_ref, route_ref, cot_ref, gain_ref, wr_ref, wo_ref, sh_ref,
+    first, second = places(target, slots, here * cap)
+    out_ref[...] = (mm(first, nmoe.astype(bf), TN) + mm(second, (gy * gate).astype(bf), TN)).astype(bf)
+
+
+def places(target, slots, half):
+    at = lax.broadcasted_iota(jnp.int32, (target.shape[0], slots), 1)
+    return (jnp.where(at == target, 1.0, 0.0).astype(jnp.bfloat16), jnp.where(at == target + half, 1.0, 0.0).astype(jnp.bfloat16))
+
+
+def sort_kernel(cap, message, half, group, got_ref, out_ref):
+    n, slots = out_ref.shape[0], got_ref.shape[0]
+    i = lax.broadcasted_iota(jnp.int32, (n, 1), 0)
+    there = i % group
+    src = jnp.where(there < slots // message * cap, there // cap * message + i // group * cap + there % cap, -slots)
+    at = lax.broadcasted_iota(jnp.int32, (n, slots), 1)
+    got = got_ref[...]
+    D = got.shape[1]
+    out_ref[:, :D] = mm(jnp.where(at == src, 1.0, 0.0).astype(jnp.bfloat16), got).astype(jnp.bfloat16)
+    out_ref[:, D:] = mm(jnp.where(at == src + half, 1.0, 0.0).astype(jnp.bfloat16), got).astype(jnp.bfloat16)
+
+
+def unsort_kernel(cap, message, half, group, buf_ref, out_ref):
+    slots, n = out_ref.shape[0], buf_ref.shape[0]
+    q = lax.broadcasted_iota(jnp.int32, (slots, 1), 0)
+    w = q % message
+    second = w >= half
+    v = jnp.where(second, w - half, w)
+    dst = jnp.where(w < 2 * half, v // cap * group + q // message * cap + v % cap, -1)
+    at = lax.broadcasted_iota(jnp.int32, (slots, n), 1)
+    D = out_ref.shape[1]
+    one = jnp.where(at == jnp.where(second, -1, dst), 1.0, 0.0).astype(jnp.bfloat16)
+    two = jnp.where(at == jnp.where(second, dst, -1), 1.0, 0.0).astype(jnp.bfloat16)
+    out_ref[...] = (mm(one, buf_ref[:, :D]) + mm(two, buf_ref[:, D:])).astype(jnp.bfloat16)
+
+
+def unroute_kernel(s, half, live_ref, home_ref, target_ref, hid_ref, prob_ref, gate_ref, route_ref, cot_ref, gain_ref, wr_ref, wo_ref, sh_ref,
                    z_ref, y_ref, mix_ref, gh_ref, gs_ref, gz_ref, gm_ref, gr_ref, gg_ref):
     bf = jnp.bfloat16
     high = lax.Precision.HIGHEST
     hid, gain = hid_ref[...], gain_ref[...]
     L, D = hid.shape
     E = wr_ref.shape[0]
-    tok = mm(place_ref[...], home_ref[...])
-    etok, gsent = tok[:, :D], tok[:, D:]
+    first, second = places(target_ref[...], home_ref.shape[0], half)
+    etok, gsent = mm(first, home_ref[...]), mm(second, home_ref[...])
     live = lax.broadcasted_iota(jnp.int32, (L, 1), 0) < live_ref[0]
     gate, probs = gate_ref[...], prob_ref[...]
     mix_ref[...] = jnp.where(live, hid + gate * etok, 0.0).astype(bf)
@@ -1138,12 +1167,10 @@
     shifted = jnp.where(lane_of % wide < out_lanes, (lane_of // wide ^ my_col) * out_lanes + lane_of % wide, -1)
     shifted = (jnp.arange(width, dtype=jnp.int32)[:, None] == shifted[None, :]).astype(BF)
 
-    message = -(-experts_here * CAP // 8) * 8
+    half = experts_here * CAP
+    message = -(-2 * half // 8) * 8
     group = -(-rows * CAP // 16) * 16
-    at = jnp.arange(experts_here * group, dtype=jnp.int32)
-    there = at % group
-    source = jnp.where(there < rows * CAP, there // CAP * message + at // group * CAP + there % CAP, -1)
-    sort = (source[:, None] == jnp.arange(rows * message, dtype=jnp.int32)[None, :]).astype(BF)
+    slots = rows * message
 
     def mixer(s, x, limit):
         nm, inner_x, conv, u, dl, pT, ssm, starts = mixer_forward(x, gain_mix_f, full_x, full_xpT, full_dt, par, a_two, QB, limit)
@@ -1151,21 +1178,22 @@
 
     def router(k, route, n_live, grad):
         n_live = n_live.reshape(1)
-        slots = rows * message
-        z, gated, hidden, place, outgoing, probs, gate = one_call(
+        z, gated, hidden, target, outgoing, probs, gate = one_call(
             functools.partial(route_kernel, CAP, experts_here, message, k["s"]),
             [k["x"], k["nm"], k["ssm"], full_z, full_out, gain_moe_f, router_f, route, grad],
-            [sds((length, inner)), sds((length, inner), BF), sds((length, width)), sds((length, slots), BF),
-             sds((slots, 2 * width), BF), sds((length, experts_all)), sds((length, 1))],
+            [sds((length, inner)), sds((length, inner), BF), sds((length, width)), sds((length, 1), jnp.int32),
+             sds((slots, width), BF), sds((length, experts_all)), sds((length, 1))],
             [n_live], 6 * length * inner * width)
-        kept = dict(k, z=z, gated=gated, hidden=hidden, place=place, probs=probs, gate=gate, route=route, n_live=n_live, cot=grad)
+        kept = dict(k, z=z, gated=gated, hidden=hidden, target=target, probs=probs, gate=gate, route=route, n_live=n_live, cot=grad)
         return outgoing, kept
 
     def home(rows_out):
         return lax.all_to_all(rows_out, "row", split_axis=0, concat_axis=0, tiled=True)
 
     def arrive(got):
-        return mm(sort, got).astype(BF).reshape(experts_here, group, 2 * width)
+        (out,) = one_call(functools.partial(sort_kernel, CAP, message, half, group), [got], [sds((experts_here * group, 2 * width), BF)],
+                          (), 4 * slots * experts_here * group * width, 24)
+        return out.reshape(experts_here, group, 2 * width)
 
     def gather_cols(own):
         bufs = [own]
@@ -1175,14 +1203,16 @@
 
     def from_experts(bufs):
         for bit in bits_of("col"):
-            half = len(bufs) // 2
-            bufs = [(a.astype(F32) + swap(b, "col", bit).astype(F32)).astype(BF) for a, b in zip(bufs[:half], bufs[half:])]
-        return mm(sort, bufs[0].reshape(experts_here * group, 2 * width), ((0,), (0,))).astype(BF)
+            mid = len(bufs) // 2
+            bufs = [(a.astype(F32) + swap(b, "col", bit).astype(F32)).astype(BF) for a, b in zip(bufs[:mid], bufs[mid:])]
+        (out,) = one_call(functools.partial(unsort_kernel, CAP, message, half, group), [bufs[0].reshape(experts_here * group, 2 * width)],
+                          [sds((slots, width), BF)], (), 4 * slots * experts_here * group * width, 24)
+        return out
 
     def unroute(k, back):
         mixed_out, gh, gs, gz, gm, g_router, g_moe = one_call(
-            functools.partial(unroute_kernel, k["s"]),
-            [back, k["place"], k["hidden"], k["probs"], k["gate"], k["route"], k["cot"], gain_moe_f, router_f, full_out, shifted,
+            functools.partial(unroute_kernel, k["s"], half),
+            [back, k["target"], k["hidden"], k["probs"], k["gate"], k["route"], k["cot"], gain_moe_f, router_f, full_out, shifted,
              k["z"], k["ssm"]],
             [sds((length, width), BF), sds((length, width)), sds((length, inner)), sds((length, inner), BF),
              sds((length, cols * wide), BF), sds((experts_all, width)), sds((1, width))],
@@ -1253,16 +1283,16 @@
         g["gs"], gives = after((g["gs"], gives))
         gots = [exchange(v, p) for v, p in zip(gives, plane[1:])]
         g.update(unscan(ks[-1], g["gs"], 24))
-        gots, g["gi"] = after((gots, g["gi"]))
-        mine, gives = split_far(own, gots)
-        g["gi"], gives = after((g["gi"], gives))
-        gots_o = [exchange(v, p) for v, p in zip(gives, far[1:])]
-        mine_o = mine
         dims = (w_dt.shape[0], w_xproj.shape[1], w_xproj.shape[0], conv_w.shape[1], gain_mix.shape[0], rows, cols)
         for s in range(1, seqs):
             gs_[s].update(unproject(ks[s], gs_[s]))
         keep, give = grad_x_blocks([(v, q["gi"]) for v, q in zip(nms, gs_)], gs_, dims, my_col)
-        own, gives = split_near(keep, exchange(give, core))
+        gots, give = after((gots, give))
+        got = exchange(give, core)
+        mine_o, gives = split_far(own, gots)
+        got, gives = after((got, gives))
+        gots_o = [exchange(v, p) for v, p in zip(gives, far[1:])]
+        own, gives = split_near(keep, got)
         gots = [exchange(v, p) for v, p in zip(gives, plane[1:])]
         gots_o, _ = after((gots_o, gives))
         gz, go, g_router = finish(finish_other_kernel, mine_o, gots_o, [w_in_z.shape, w_out.shape, w_router.shape[::-1]])

time: 494 us -> 487 us (0.986)
  Pallas kernels: 242 us -> 256 us
  waiting for transfers between devices: 110 us -> 102 us
  matrix products: 7.38 us -> 0 us
  local copies, waits for them, and re-layouts: 42 us -> 36.5 us
    pallas_call x8 -> x12, Pallas kernels: 53.1 us -> 67.8 us  [one_call(): pl.pallas_call(kernel, in_specs=[smem] * len(scalars) + [vmem] * len(ins)...]
    dot_general x4 -> x0, matrix products: 7.38 us -> none  [mm(): lax.dot_general(a, b, (dims, ((), ())), preferred_element_type=F32, **kw)]
    unnamed x222 -> x198, local copies, waits for them, and re-layouts: 38.6 us -> 33.1 us
  transfers between devices with their start and end apart: 50 -> 50, of which waited for: 18 -> 18; matrix products, arithmetic and copies ran while one was open for 4% -> 3% of each run, Pallas kernels for 39% -> 43%
where the time goes in v6:
time: 487 us; the launch traced here: 478 us
  Pallas kernels  256 us (53%)
  waiting for transfers between devices  102 us (21%)
  starting transfers between devices  66.8 us (14%)
  local copies, waits for them, and re-layouts  36.5 us (7%)
  other arithmetic  13.8 us (3%)
    ppermute x42, waiting for transfers between devices, swap(): return lax.ppermute(x, axis, [(i, i ^ bit) for i in range(n)])  93 us
    pallas_call x2, Pallas kernels, scan_backward(): pl.pallas_call(functools.partial(scan_back_kernel, T, Q, Q2, R), grid=(C,...  78.4 us
    pallas_call x12, Pallas kernels, one_call(): pl.pallas_call(kernel, in_specs=[smem] * len(scalars) + [vmem] * len(ins)...  67.8 us
    pallas_call x4, Pallas kernels, per_expert(): pl.pallas_call(kernel, grid=(ins[0].shape[0],), in_specs=[tok(a) for a in...  44.2 us
    ppermute x42, starting transfers between devices, swap(): return lax.ppermute(x, axis, [(i, i ^ bit) for i in range(n)])  40.7 us
    pallas_call x2, Pallas kernels, mixer_forward(): pl.pallas_call(functools.partial(mixer_kernel, T, Q, R), grid=(C,), in_sp...  37.8 us
    unnamed x198, local copies, waits for them, and re-layouts  33.1 us
    all_to_all x4, starting transfers between devices, home(): lax.all_to_all(rows_out, 'row', split_axis=0, concat_axis=0, tiled=True)  22 us
  transfers between devices with their start and end apart: 50, of which 18 were waited for; matrix products, arithmetic and copies ran while one was open for 3% of the time, Pallas kernels for 43%

profile of v6, /device:TPU:0, one launch (start us, length us, event | category | flops | bytes accessed | tf_op | source)
XLA Modules:
  0.0 478.2 jit_solution(17518292646618359947)
XLA Ops:
  2.5 3.0 collective-permute-start
  5.5 2.6 collective-permute-start.1
  8.5 7.6 %collective-permute-done.1 = bf16[128,384]{1,0:T(8,128)(2,1)S(1)} collective-permute-done((bf16[128,384]{1,0:T(8,128)(2,1)}, bf16[128,384]{1,0:T(8,128)(2,1)S(1)}, u32[]{:S(2)}, u32[]{:S(2)}) %collective-permute-start.1) | collective-permute-done | bytes 98336 | tf_op jit(solution)/shard_map/ppermute | solution.py:419
  17.1 2.5 collective-permute-start.5
  23.7 3.2 collective-permute-done.10
  26.9 3.4 collective-permute-done.11
  30.3 2.5 collective-permute-start.12
  32.8 2.9 collective-permute-done.3.refs_1_
  47.6 2.1 shard_map.315
  50.3 17.3 %shard_map.316 = (bf16[320,768]{1,0:T(8,128)(2,1)S(1)}, f32[328,1536]{1,0:T(8,128)S(1)}, f32[5,8,8,1536]{3,2,1,0:T(8,128)S(1)}, f32[5,8,8,1536]{3,2,1,0:T(8,128)...) custom-call(bf16[320,768]{1,0:T(8,128)(2,1)S(1)} %get-tuple-element., ...), custom_call_target="tpu_custom_call" | custom-call | flops 40000000000 | bytes 7864320 | tf_op jit(solution)/shard_map/pallas_call | solution.py:134
  81.5 3.3 shard_map.317
  88.2 11.6 %shard_map.318 = (f32[320,1536]{1,0:T(8,128)}, bf16[320,1536]{1,0:T(8,128)(2,1)}, f32[320,768]{1,0:T(8,128)}, s32[320,1]{1,0:T(8,128)}, bf16[832,768]{1,0:T(8,12...) custom-call(s32[1]{0:T(128)} %get-tuple-element.383.live_ref, bf16[320,768]{1,0:T(8,128)(2,1)} %copy-done.14, ...), custom_call_target="tpu_custom_call" | custom-call | flops 2264924160 | bytes 14990080 | tf_op jit(solution)/shard_map/pallas_call | solution.py:294
  99.8 5.9 %all-to-all-start = ((bf16[8,104,768]{2,1,0:T(8,128)(2,1)}), bf16[8,104,768]{2,1,0:T(8,128)(2,1)S(1)}, u32[]{:S(2)}, u32[]{:S(2)}) async-start(bf16[8,104,768]{2,1,0:T(8,128)(2,1)} %bitcast.83), calls=%async_computation | async-start | bytes 2555904 | tf_op jit(solution)/shard_map/all_to_all | solution.py:1191
  105.7 20.5 %shard_map.319 = (bf16[320,768]{1,0:T(8,128)(2,1)S(1)}, f32[328,1536]{1,0:T(8,128)}, f32[5,8,8,1536]{3,2,1,0:T(8,128)S(1)}, f32[5,8,8,1536]{3,2,1,0:T(8,128)S(1)...) custom-call(bf16[320,768]{1,0:T(8,128)(2,1)S(1)} %get-tuple-element., ...), custom_call_target="tpu_custom_call" | custom-call | flops 40000000000 | bytes 7864320 | tf_op jit(solution)/shard_map/pallas_call | solution.py:134
  130.5 11.6 %shard_map.320 = (f32[320,1536]{1,0:T(8,128)}, bf16[320,1536]{1,0:T(8,128)(2,1)}, f32[320,768]{1,0:T(8,128)}, s32[320,1]{1,0:T(8,128)}, bf16[832,768]{1,0:T(8,12...) custom-call(s32[1]{0:T(128)} %get-tuple-element.384.live_ref, bf16[320,768]{1,0:T(8,128)(2,1)} %copy-done.12, ...), custom_call_target="tpu_custom_call" | custom-call | flops 2264924160 | bytes 14990080 | tf_op jit(solution)/shard_map/pallas_call | solution.py:294
  144.9 6.5 %all-to-all-start.1 = ((bf16[8,104,768]{2,1,0:T(8,128)(2,1)}), bf16[8,104,768]{2,1,0:T(8,128)(2,1)}, u32[]{:S(2)}, u32[]{:S(2)}) async-start(bf16[8,104,768]{2,1,0:T(8,128)(2,1)} %bitcast.82), calls=%async_computation.1 | async-start | bytes 2555904 | tf_op jit(solution)/shard_map/all_to_all | solution.py:1191
  151.5 24.5 %collective-permute-done.20.refs_1_ = bf16[4,112,1536]{2,1,0:T(8,128)(2,1)S(1)} collective-permute-done((bf16[4,112,1536]{2,1,0:T(8,128)(2,1)S(1)}, bf16[4,112,1536]{2,1,0:T(8,128)(2,1)S(1)}, u32[]{:S(2)}, u32[]{:S(2)}) %collective-permute-start.20) | collective-permute-done | bytes 1376288 | tf_op jit(solution)/shard_map/ppermute | solution.py:419
  175.9 5.8 %all-to-all-done.1 = bf16[8,104,768]{2,1,0:T(8,128)(2,1)} async-done(((bf16[8,104,768]{2,1,0:T(8,128)(2,1)}), bf16[8,104,768]{2,1,0:T(8,128)(2,1)}, u32[]{:S(2)}, u32[]{:S(2)}) %all-to-all-start.1) | async-done | bytes 1277984 | tf_op jit(solution)/shard_map/all_to_all | solution.py:1191
  181.7 3.1 shard_map.322
  186.0 11.8 %shard_map.323 = (bf16[4,112,1536]{2,1,0:T(8,128)(2,1)S(1)}, bf16[4,112,1536]{2,1,0:T(8,128)(2,1)S(1)}, bf16[4,112,1536]{2,1,0:T(8,128)(2,1)S(1)}, bf16[4,112,15...) custom-call(bf16[4,112,1536]{2,1,0:T(8,128)(2,1)S(1)} %bitcast.60, ...), custom_call_target="tpu_custom_call" | custom-call | flops 8455716864 | bytes 25952256 | tf_op jit(solution)/shard_map/pallas_call | solution.py:641
  198.3 16.6 %collective-permute-done.26.refs_1_.refs_6_ = bf16[4,112,1536]{2,1,0:T(8,128)(2,1)S(1)} collective-permute-done((bf16[4,112,1536]{2,1,0:T(8,128)(2,1)S(1)}, bf16[4,112,1536]{2,1,0:T(8,128)(2,1)S(1)}, u32[]{:S(2)}, u32[]{:S(2)}) %collective-permute-start.26) | collective-permute-done | bytes 1376288 | tf_op jit(solution)/shard_map/ppermute | solution.py:419
  219.3 12.1 %shard_map.325 = (bf16[4,112,1536]{2,1,0:T(8,128)(2,1)S(1)}, bf16[4,112,1536]{2,1,0:T(8,128)(2,1)S(1)}, bf16[4,112,1536]{2,1,0:T(8,128)(2,1)S(1)}, bf16[4,112,15...) custom-call(bf16[4,112,1536]{2,1,0:T(8,128)(2,1)S(1)} %bitcast.65, ...), custom_call_target="tpu_custom_call" | custom-call | flops 8455716864 | bytes 25952256 | tf_op jit(solution)/shard_map/pallas_call | solution.py:641
  231.5 17.7 %collective-permute-done.25 = bf16[4,112,1536]{2,1,0:T(8,128)(2,1)S(1)} collective-permute-done((bf16[4,112,1536]{2,1,0:T(8,128)(2,1)}, bf16[4,112,1536]{2,1,0:T(8,128)(2,1)S(1)}, u32[]{:S(2)}, u32[]{:S(2)}) %collective-permute-start.25) | collective-permute-done | bytes 1376288 | tf_op jit(solution)/shard_map/ppermute | solution.py:419
  249.7 2.1 shard_map.324
  252.9 5.7 %all-to-all-start.2 = ((bf16[8,104,768]{2,1,0:T(8,128)(2,1)}), bf16[8,104,768]{2,1,0:T(8,128)(2,1)}, u32[]{:S(2)}, u32[]{:S(2)}) async-start(bf16[8,104,768]{2,1,0:T(8,128)(2,1)} %bitcast.74), calls=%async_computation.2 | async-start | bytes 2555904 | tf_op jit(solution)/shard_map/all_to_all | solution.py:1191
  258.8 3.3 add_convert_fusion.1
  265.0 10.1 %shard_map.326 = f32[4,768,768]{2,1,0:T(8,128)} custom-call(bf16[4,112,1536]{2,1,0:T(8,128)(2,1)S(1)} %bitcast.61, bf16[4,112,1536]{2,1,0:T(8,128)(2,1)S(1)} %collective-permute-done.20.refs_1_, bf16[4,112,1536]{2,1,0:T(8,128)(2,1)} %collective-permute-done.21.refs_2_, bf16[4,112,1536]{2,1,0:T(8,128)(2,1)} %collective-permute-done.22.refs_3_, ...), custom_call_target="tpu_custom_call" | custom-call | flops 4227858432 | bytes 25952256 | tf_op jit(solution)/shard_map/pallas_call | solution.py:641
  275.1 10.1 %shard_map.327 = f32[4,768,768]{2,1,0:T(8,128)} custom-call(bf16[4,112,1536]{2,1,0:T(8,128)(2,1)S(1)} %bitcast.62, bf16[4,112,1536]{2,1,0:T(8,128)(2,1)S(1)} %collective-permute-done.20.refs_1_, bf16[4,112,1536]{2,1,0:T(8,128)(2,1)} %collective-permute-done.21.refs_2_, bf16[4,112,1536]{2,1,0:T(8,128)(2,1)} %collective-permute-done.22.refs_3_, ...), custom_call_target="tpu_custom_call" | custom-call | flops 4227858432 | bytes 25952256 | tf_op jit(solution)/shard_map/pallas_call | solution.py:641
  285.3 3.7 all-to-all-done.2
  288.9 12.8 %shard_map.328 = (bf16[320,768]{1,0:T(8,128)(2,1)}, f32[320,768]{1,0:T(8,128)}, f32[320,1536]{1,0:T(8,128)}, bf16[320,1536]{1,0:T(8,128)(2,1)}, bf16[320,1024]{1...) custom-call(s32[1]{0:T(128)} %get-tuple-element.383.live_ref, bf16[832,768]{1,0:T(8,128)(2,1)} %bitcast.31.home_ref, ...), custom_call_target="tpu_custom_call" | custom-call | flops 2264924160 | bytes 17417984 | tf_op jit(solution)/shard_map/pallas_call | solution.py:294
  301.8 2.3 add_convert_fusion
  304.0 3.2 shard_map.329
  307.2 3.9 all-to-all-start.3
  311.1 40.7 %shard_map.330 = (bf16[320,1536]{1,0:T(8,128)(2,1)}, f32[80,1536]{1,0:T(8,128)S(1)}, f32[48,1536]{1,0:T(8,128)S(1)}, f32[23,1536]{1,0:T(8,128)S(1)}) custom-call(f32[5,8,8,1536]{3,2,1,0:T(8,128)} %copy-done.72, f32[5,8,8,1536]{3,2,1,0:T(8,128)} %copy-done.73, f32[5,8,8,1536]{3,2,1,0:T(8,128)} %bitcast.101, f32[5,8,8,1536]{3,2,1,0:T(8,128)} %copy-done.71, ...), custom_call_target="tpu_custom_call" | custom-call | flops 80000000000 | bytes 7864320 | tf_op jit(solution)/shard_map/pallas_call | solution.py:278
  354.4 12.6 %shard_map.331 = (bf16[320,768]{1,0:T(8,128)(2,1)}, f32[320,768]{1,0:T(8,128)}, f32[320,1536]{1,0:T(8,128)}, bf16[320,1536]{1,0:T(8,128)(2,1)}, bf16[320,1024]{1...) custom-call(s32[1]{0:T(128)} %get-tuple-element.384.live_ref, bf16[832,768]{1,0:T(8,128)(2,1)} %bitcast.81, ...), custom_call_target="tpu_custom_call" | custom-call | flops 2264924160 | bytes 17417984 | tf_op jit(solution)/shard_map/pallas_call | solution.py:294
  367.1 11.8 %shard_map.332 = (bf16[2,8,304,256]{3,2,1,0:T(8,128)(2,1)}, bf16[2,8,304,256]{3,2,1,0:T(8,128)(2,1)}) custom-call(s32[1]{0:T(128)} %bitcast.3.s_ref, bf16[320,768]{1,0:T(8,128)(2,1)} %copy-done.33, bf16[320,1536]{1,0:T(8,128)(2,1)} %get-tuple-element.288.refs_1_.gz_ref, bf16[320,768]{1,0:T(8,128)(2,1)} %copy-done.35, ...), custom_call_target="tpu_custom_call" | custom-call | flops 3523215360 | bytes 8388608 | tf_op jit(solution)/shard_map/pallas_call | solution.py:859
  380.9 2.9 collective-permute-done.32
  390.5 37.6 %shard_map.335 = (bf16[320,1536]{1,0:T(8,128)(2,1)S(1)}, f32[80,1536]{1,0:T(8,128)S(1)}, f32[48,1536]{1,0:T(8,128)S(1)}, f32[23,1536]{1,0:T(8,128)S(1)}) custom-call(f32[5,8,8,1536]{3,2,1,0:T(8,128)S(1)} %copy-done.69, f32[5,8,8,1536]{3,2,1,0:T(8,128)S(1)} %copy-done.70, f32[5,8,8,1536]{3,2,1,0:T(8,128)S(1)} %bitcast.78, f32[5,8,8,1536]{3,2,1,0:T(8,128)S(1)} %copy-done.67, ...), custom_call_target="tpu_custom_call" | custom-call | flops 80000000000 | bytes 7864320 | tf_op jit(solution)/shard_map/pallas_call | solution.py:278
  428.3 2.0 shard_map.336
  430.3 3.8 shard_map.337
  435.4 2.8 shard_map.338
  445.4 2.4 collective-permute-start.41
  447.8 2.9 collective-permute-done.40.refs_1_
  450.6 3.6 collective-permute-start.42
  455.3 3.4 collective-permute-done.41.refs_2_
  461.3 2.3 shard_map.341
  463.6 2.0 collective-permute-start.43
  469.5 5.7 %collective-permute-done.44.refs_2_ = bf16[128,384]{1,0:T(8,128)(2,1)S(1)} collective-permute-done((bf16[128,384]{1,0:T(8,128)(2,1)}, bf16[128,384]{1,0:T(8,128)(2,1)S(1)}, u32[]{:S(2)}, u32[]{:S(2)}) %collective-permute-start.44) | collective-permute-done | bytes 98336 | tf_op jit(solution)/shard_map/ppermute | solution.py:419
  (295 shorter events, 84.3 us)
Async XLA Ops:
  2.5 6.0 %collective-permute-start = (bf16[128,384]{1,0:T(8,128)(2,1)}, bf16[128,384]{1,0:T(8,128)(2,1)S(1)}, u32[]{:S(2)}, u32[]{:S(2)}) collective-permute-start(bf16[128,384]{1,0:T(8,128)(2,1)} %get-tuple-element.198), channel_id=1, source_target_pairs={{0,8},{4,12},{8,0},{12,4},{16,24},{20,28},{24,16},{28,20},{1,9},{5... | collective-permute-start | bytes 294920 | tf_op jit(solution)/shard_map/ppermute | solution.py:419
  5.5 10.6 %collective-permute-start.1 = (bf16[128,384]{1,0:T(8,128)(2,1)}, bf16[128,384]{1,0:T(8,128)(2,1)S(1)}, u32[]{:S(2)}, u32[]{:S(2)}) collective-permute-start(bf16[128,384]{1,0:T(8,128)(2,1)} %get-tuple-element.198), channel_id=1, source_target_pairs={{0,16},{4,20},{8,24},{12,28},{16,0},{20,4},{24,8},{28,12},{1,17},{... | collective-permute-start | bytes 294920 | tf_op jit(solution)/shard_map/ppermute | solution.py:419
  8.1 8.1 %collective-permute-start.2 = (bf16[128,384]{1,0:T(8,128)(2,1)}, bf16[128,384]{1,0:T(8,128)(2,1)S(1)}, u32[]{:S(2)}, u32[]{:S(2)}) collective-permute-start(bf16[128,384]{1,0:T(8,128)(2,1)} %get-tuple-element.198), channel_id=1, source_target_pairs={{0,24},{4,28},{8,16},{12,20},{16,8},{20,12},{24,0},{28,4},{1,25},{... | collective-permute-start | bytes 294920 | tf_op jit(solution)/shard_map/ppermute | solution.py:419
  17.1 15.6 %collective-permute-start.5 = (bf16[4,128,384]{2,1,0:T(8,128)(2,1)S(1)}, bf16[4,128,384]{2,1,0:T(8,128)(2,1)S(1)}, u32[]{:S(2)}, u32[]{:S(2)}) collective-permute-start(bf16[4,128,384]{2,1,0:T(8,128)(2,1)S(1)} %pad_maximum_fusion.3.refs_0_), channel_id=1, source_target_pairs={{0,6},{1,7},{2,4},{3,5},{4,2},{5,3},{6,0},{7,1},{8,14},{9,15},{10,... | collective-permute-start | bytes 1179656 | tf_op jit(solution)/shard_map/ppermute | solution.py:435
  19.6 16.0 %collective-permute-start.3 = (bf16[4,128,384]{2,1,0:T(8,128)(2,1)S(1)}, bf16[4,128,384]{2,1,0:T(8,128)(2,1)}, u32[]{:S(2)}, u32[]{:S(2)}) collective-permute-start(bf16[4,128,384]{2,1,0:T(8,128)(2,1)S(1)} %pad_maximum_fusion.3.refs_0_), channel_id=1, source_target_pairs={{0,4},{4,0},{8,12},{12,8},{16,20},{20,16},{24,28},{28,24},{1,5},{5... | collective-permute-start | bytes 1179656 | tf_op jit(solution)/shard_map/ppermute | solution.py:419
  20.2 15.5 %collective-permute-start.4 = (bf16[4,128,384]{2,1,0:T(8,128)(2,1)S(1)}, bf16[4,128,384]{2,1,0:T(8,128)(2,1)}, u32[]{:S(2)}, u32[]{:S(2)}) collective-permute-start(bf16[4,128,384]{2,1,0:T(8,128)(2,1)S(1)} %pad_maximum_fusion.3.refs_0_), channel_id=1, source_target_pairs={{0,2},{1,3},{2,0},{3,1},{4,6},{5,7},{6,4},{7,5},{8,10},{9,11},{10,... | collective-permute-start | bytes 1179656 | tf_op jit(solution)/shard_map/ppermute | solution.py:419
  20.7 6.2 %collective-permute-start.10 = (bf16[304,256]{1,0:T(8,128)(2,1)}, bf16[304,256]{1,0:T(8,128)(2,1)S(1)}, u32[]{:S(2)}, u32[]{:S(2)}) collective-permute-start(bf16[304,256]{1,0:T(8,128)(2,1)} %get-tuple-element.207), channel_id=1, source_target_pairs={{0,8},{4,12},{8,0},{12,4},{16,24},{20,28},{24,16},{28,20},{1,9},{5... | collective-permute-start | bytes 466952 | tf_op jit(solution)/shard_map/ppermute | solution.py:419
  22.3 8.0 %collective-permute-start.11 = (bf16[304,256]{1,0:T(8,128)(2,1)}, bf16[304,256]{1,0:T(8,128)(2,1)S(1)}, u32[]{:S(2)}, u32[]{:S(2)}) collective-permute-start(bf16[304,256]{1,0:T(8,128)(2,1)} %get-tuple-element.207), channel_id=1, source_target_pairs={{0,16},{4,20},{8,24},{12,28},{16,0},{20,4},{24,8},{28,12},{1,17},{... | collective-permute-start | bytes 466952 | tf_op jit(solution)/shard_map/ppermute | solution.py:419
  26.9 13.2 %collective-permute-start.6 = (bf16[4,128,384]{2,1,0:T(8,128)(2,1)S(1)}, bf16[4,128,384]{2,1,0:T(8,128)(2,1)S(1)}, u32[]{:S(2)}, u32[]{:S(2)}) collective-permute-start(bf16[4,128,384]{2,1,0:T(8,128)(2,1)S(1)} %pad_maximum_fusion.3.refs_0_), channel_id=1, source_target_pairs={{0,1},{1,0},{2,3},{3,2},{4,5},{5,4},{6,7},{7,6},{8,9},{9,8},{10,11... | collective-permute-start | bytes 1179656 | tf_op jit(solution)/shard_map/ppermute | solution.py:419
  30.3 7.2 %collective-permute-start.12 = (bf16[304,256]{1,0:T(8,128)(2,1)}, bf16[304,256]{1,0:T(8,128)(2,1)S(1)}, u32[]{:S(2)}, u32[]{:S(2)}) collective-permute-start(bf16[304,256]{1,0:T(8,128)(2,1)} %get-tuple-element.207), channel_id=1, source_target_pairs={{0,24},{4,28},{8,16},{12,20},{16,8},{20,12},{24,0},{28,4},{1,25},{... | collective-permute-start | bytes 466952 | tf_op jit(solution)/shard_map/ppermute | solution.py:419
  32.8 9.5 %collective-permute-start.9 = (bf16[4,128,384]{2,1,0:T(8,128)(2,1)S(1)}, bf16[4,128,384]{2,1,0:T(8,128)(2,1)S(1)}, u32[]{:S(2)}, u32[]{:S(2)}) collective-permute-start(bf16[4,128,384]{2,1,0:T(8,128)(2,1)S(1)} %collective-permute-done.5.refs_3_), channel_id=1, source_target_pairs={{0,1},{1,0},{2,3},{3,2},{4,5},{5,4},{6,7},{7,6},{8,9},{9,8},{10,11... | collective-permute-start | bytes 1179656 | tf_op jit(solution)/shard_map/ppermute | solution.py:419
  35.7 7.9 %collective-permute-start.7 = (bf16[4,128,384]{2,1,0:T(8,128)(2,1)}, bf16[4,128,384]{2,1,0:T(8,128)(2,1)}, u32[]{:S(2)}, u32[]{:S(2)}) collective-permute-start(bf16[4,128,384]{2,1,0:T(8,128)(2,1)} %collective-permute-done.3.refs_1_), channel_id=1, source_target_pairs={{0,1},{1,0},{2,3},{3,2},{4,5},{5,4},{6,7},{7,6},{8,9},{9,8},{10,11... | collective-permute-start | bytes 1179656 | tf_op jit(solution)/shard_map/ppermute | solution.py:419
  35.7 7.9 %collective-permute-start.8 = (bf16[4,128,384]{2,1,0:T(8,128)(2,1)}, bf16[4,128,384]{2,1,0:T(8,128)(2,1)}, u32[]{:S(2)}, u32[]{:S(2)}) collective-permute-start(bf16[4,128,384]{2,1,0:T(8,128)(2,1)} %collective-permute-done.4.refs_2_), channel_id=1, source_target_pairs={{0,1},{1,0},{2,3},{3,2},{4,5},{5,4},{6,7},{7,6},{8,9},{9,8},{10,11... | collective-permute-start | bytes 1179656 | tf_op jit(solution)/shard_map/ppermute | solution.py:419
  38.6 37.9 %collective-permute-start.13 = (bf16[4,304,256]{2,1,0:T(8,128)(2,1)}, bf16[4,304,256]{2,1,0:T(8,128)(2,1)S(1)}, u32[]{:S(2)}, u32[]{:S(2)}) collective-permute-start(bf16[4,304,256]{2,1,0:T(8,128)(2,1)} %pad_maximum_fusion.2.refs_0_), channel_id=1, source_target_pairs={{0,4},{4,0},{8,12},{12,8},{16,20},{20,16},{24,28},{28,24},{1,5},{5... | collective-permute-start | bytes 1867784 | tf_op jit(solution)/shard_map/ppermute | solution.py:419
  40.8 35.7 %collective-permute-start.14 = (bf16[4,304,256]{2,1,0:T(8,128)(2,1)}, bf16[4,304,256]{2,1,0:T(8,128)(2,1)S(1)}, u32[]{:S(2)}, u32[]{:S(2)}) collective-permute-start(bf16[4,304,256]{2,1,0:T(8,128)(2,1)} %pad_maximum_fusion.2.refs_0_), channel_id=1, source_target_pairs={{0,2},{1,3},{2,0},{3,1},{4,6},{5,7},{6,4},{7,5},{8,10},{9,11},{10,... | collective-permute-start | bytes 1867784 | tf_op jit(solution)/shard_map/ppermute | solution.py:419
  43.0 33.6 %collective-permute-start.15 = (bf16[4,304,256]{2,1,0:T(8,128)(2,1)}, bf16[4,304,256]{2,1,0:T(8,128)(2,1)S(1)}, u32[]{:S(2)}, u32[]{:S(2)}) collective-permute-start(bf16[4,304,256]{2,1,0:T(8,128)(2,1)} %pad_maximum_fusion.2.refs_0_), channel_id=1, source_target_pairs={{0,6},{1,7},{2,4},{3,5},{4,2},{5,3},{6,0},{7,1},{8,14},{9,15},{10,... | collective-permute-start | bytes 1867784 | tf_op jit(solution)/shard_map/ppermute | solution.py:435
  76.5 3.3 collective-permute-start.16
  77.1 3.5 collective-permute-start.18
  77.2 4.3 collective-permute-start.19
  99.8 42.3 %all-to-all-start = ((bf16[8,104,768]{2,1,0:T(8,128)(2,1)}), bf16[8,104,768]{2,1,0:T(8,128)(2,1)S(1)}, u32[]{:S(2)}, u32[]{:S(2)}) async-start(bf16[8,104,768]{2,1,0:T(8,128)(2,1)} %bitcast.83), calls=%async_computation | async-start | bytes 2555904 | tf_op jit(solution)/shard_map/all_to_all | solution.py:1191
  143.9 32.0 %collective-permute-start.20 = (bf16[4,112,1536]{2,1,0:T(8,128)(2,1)S(1)}, bf16[4,112,1536]{2,1,0:T(8,128)(2,1)S(1)}, u32[]{:S(2)}, u32[]{:S(2)}) collective-permute-start(bf16[4,112,1536]{2,1,0:T(8,128)(2,1)S(1)} %bitcast.58), channel_id=1, source_target_pairs={{0,2},{1,3},{2,0},{3,1},{4,6},{5,7},{6,4},{7,5},{8,10},{9,11},{10,... | collective-permute-start | bytes 4128776 | tf_op jit(solution)/shard_map/ppermute | solution.py:419
  144.9 36.8 %all-to-all-start.1 = ((bf16[8,104,768]{2,1,0:T(8,128)(2,1)}), bf16[8,104,768]{2,1,0:T(8,128)(2,1)}, u32[]{:S(2)}, u32[]{:S(2)}) async-start(bf16[8,104,768]{2,1,0:T(8,128)(2,1)} %bitcast.82), calls=%async_computation.1 | async-start | bytes 2555904 | tf_op jit(solution)/shard_map/all_to_all | solution.py:1191
  151.4 33.4 %collective-permute-start.21 = (bf16[4,112,1536]{2,1,0:T(8,128)(2,1)S(1)}, bf16[4,112,1536]{2,1,0:T(8,128)(2,1)}, u32[]{:S(2)}, u32[]{:S(2)}) collective-permute-start(bf16[4,112,1536]{2,1,0:T(8,128)(2,1)S(1)} %bitcast.59), channel_id=1, source_target_pairs={{0,1},{1,0},{2,3},{3,2},{4,5},{5,4},{6,7},{7,6},{8,9},{9,8},{10,11... | collective-permute-start | bytes 4128776 | tf_op jit(solution)/shard_map/ppermute | solution.py:419
  175.9 8.9 %collective-permute-start.22 = (bf16[4,112,1536]{2,1,0:T(8,128)(2,1)S(1)}, bf16[4,112,1536]{2,1,0:T(8,128)(2,1)}, u32[]{:S(2)}, u32[]{:S(2)}) collective-permute-start(bf16[4,112,1536]{2,1,0:T(8,128)(2,1)S(1)} %collective-permute-done.20.refs_1_), channel_id=1, source_target_pairs={{0,1},{1,0},{2,3},{3,2},{4,5},{5,4},{6,7},{7,6},{8,9},{9,8},{10,11... | collective-permute-start | bytes 4128776 | tf_op jit(solution)/shard_map/ppermute | solution.py:419
  184.8 30.1 %collective-permute-start.26 = (bf16[4,112,1536]{2,1,0:T(8,128)(2,1)S(1)}, bf16[4,112,1536]{2,1,0:T(8,128)(2,1)S(1)}, u32[]{:S(2)}, u32[]{:S(2)}) collective-permute-start(bf16[4,112,1536]{2,1,0:T(8,128)(2,1)S(1)} %bitcast.63), channel_id=1, source_target_pairs={{0,2},{1,3},{2,0},{3,1},{4,6},{5,7},{6,4},{7,5},{8,10},{9,11},{10,... | collective-permute-start | bytes 4128776 | tf_op jit(solution)/shard_map/ppermute | solution.py:419
  197.8 17.7 %collective-permute-start.24 = (bf16[4,112,1536]{2,1,0:T(8,128)(2,1)S(1)}, bf16[4,112,1536]{2,1,0:T(8,128)(2,1)S(1)}, u32[]{:S(2)}, u32[]{:S(2)}) collective-permute-start(bf16[4,112,1536]{2,1,0:T(8,128)(2,1)S(1)} %get-tuple-element.234), channel_id=1, source_target_pairs={{0,1},{1,0},{2,3},{3,2},{4,5},{5,4},{6,7},{7,6},{8,9},{9,8},{10,11... | collective-permute-start | bytes 4128776 | tf_op jit(solution)/shard_map/ppermute | solution.py:419
  197.8 20.2 %collective-permute-start.27 = (bf16[4,112,1536]{2,1,0:T(8,128)(2,1)S(1)}, bf16[4,112,1536]{2,1,0:T(8,128)(2,1)S(1)}, u32[]{:S(2)}, u32[]{:S(2)}) collective-permute-start(bf16[4,112,1536]{2,1,0:T(8,128)(2,1)S(1)} %bitcast.64), channel_id=1, source_target_pairs={{0,1},{1,0},{2,3},{3,2},{4,5},{5,4},{6,7},{7,6},{8,9},{9,8},{10,11... | collective-permute-start | bytes 4128776 | tf_op jit(solution)/shard_map/ppermute | solution.py:419
  215.0 16.6 %collective-permute-start.23 = (bf16[4,112,1536]{2,1,0:T(8,128)(2,1)S(1)}, bf16[4,112,1536]{2,1,0:T(8,128)(2,1)S(1)}, u32[]{:S(2)}, u32[]{:S(2)}) collective-permute-start(bf16[4,112,1536]{2,1,0:T(8,128)(2,1)S(1)} %get-tuple-element.232), channel_id=1, source_target_pairs={{0,1},{1,0},{2,3},{3,2},{4,5},{5,4},{6,7},{7,6},{8,9},{9,8},{10,11... | collective-permute-start | bytes 4128776 | tf_op jit(solution)/shard_map/ppermute | solution.py:419
  216.9 32.3 %collective-permute-start.25 = (bf16[4,112,1536]{2,1,0:T(8,128)(2,1)}, bf16[4,112,1536]{2,1,0:T(8,128)(2,1)S(1)}, u32[]{:S(2)}, u32[]{:S(2)}) collective-permute-start(bf16[4,112,1536]{2,1,0:T(8,128)(2,1)} %add_convert_fusion.4), channel_id=1, source_target_pairs={{0,2},{1,3},{2,0},{3,1},{4,6},{5,7},{6,4},{7,5},{8,10},{9,11},{10,... | collective-permute-start | bytes 4128776 | tf_op jit(solution)/shard_map/ppermute | solution.py:419
  231.5 27.3 %collective-permute-start.30 = (bf16[4,112,1536]{2,1,0:T(8,128)(2,1)}, bf16[4,112,1536]{2,1,0:T(8,128)(2,1)}, u32[]{:S(2)}, u32[]{:S(2)}) collective-permute-start(bf16[4,112,1536]{2,1,0:T(8,128)(2,1)} %get-tuple-element.273), channel_id=1, source_target_pairs={{0,1},{1,0},{2,3},{3,2},{4,5},{5,4},{6,7},{7,6},{8,9},{9,8},{10,11... | collective-permute-start | bytes 4128776 | tf_op jit(solution)/shard_map/ppermute | solution.py:419
  252.9 36.0 %all-to-all-start.2 = ((bf16[8,104,768]{2,1,0:T(8,128)(2,1)}), bf16[8,104,768]{2,1,0:T(8,128)(2,1)}, u32[]{:S(2)}, u32[]{:S(2)}) async-start(bf16[8,104,768]{2,1,0:T(8,128)(2,1)} %bitcast.74), calls=%async_computation.2 | async-start | bytes 2555904 | tf_op jit(solution)/shard_map/all_to_all | solution.py:1191
  258.7 43.0 %collective-permute-start.29 = (bf16[4,112,1536]{2,1,0:T(8,128)(2,1)}, bf16[4,112,1536]{2,1,0:T(8,128)(2,1)}, u32[]{:S(2)}, u32[]{:S(2)}) collective-permute-start(bf16[4,112,1536]{2,1,0:T(8,128)(2,1)} %copy-done.45), channel_id=1, source_target_pairs={{0,1},{1,0},{2,3},{3,2},{4,5},{5,4},{6,7},{7,6},{8,9},{9,8},{10,11... | collective-permute-start | bytes 4128776 | tf_op jit(solution)/shard_map/ppermute | solution.py:419
  262.1 39.6 %collective-permute-start.31 = (bf16[4,112,1536]{2,1,0:T(8,128)(2,1)}, bf16[4,112,1536]{2,1,0:T(8,128)(2,1)}, u32[]{:S(2)}, u32[]{:S(2)}) collective-permute-start(bf16[4,112,1536]{2,1,0:T(8,128)(2,1)} %add_convert_fusion.1), channel_id=1, source_target_pairs={{0,2},{1,3},{2,0},{3,1},{4,6},{5,7},{6,4},{7,5},{8,10},{9,11},{10,... | collective-permute-start | bytes 4128776 | tf_op jit(solution)/shard_map/ppermute | solution.py:419
  307.2 46.2 %all-to-all-start.3 = ((bf16[8,104,768]{2,1,0:T(8,128)(2,1)}), bf16[8,104,768]{2,1,0:T(8,128)(2,1)S(1)}, u32[]{:S(2)}, u32[]{:S(2)}) async-start(bf16[8,104,768]{2,1,0:T(8,128)(2,1)} %bitcast.35), calls=%async_computation.3 | async-start | bytes 2555904 | tf_op jit(solution)/shard_map/all_to_all | solution.py:1191
  378.9 4.9 %collective-permute-start.32 = (bf16[2,8,304,256]{3,2,1,0:T(8,128)(2,1)}, bf16[2,8,304,256]{3,2,1,0:T(8,128)(2,1)S(1)}, u32[]{:S(2)}, u32[]{:S(2)}) collective-permute-start(bf16[2,8,304,256]{3,2,1,0:T(8,128)(2,1)} %get-tuple-element.296), channel_id=1, source_target_pairs={{0,1},{1,0},{2,3},{3,2},{4,5},{5,4},{6,7},{7,6},{8,9},{9,8},{10,11... | collective-permute-start | bytes 7471112 | tf_op jit(solution)/shard_map/ppermute | solution.py:419
  385.9 48.2 %collective-permute-start.33 = (bf16[4,304,256]{2,1,0:T(8,128)(2,1)S(1)}, bf16[4,304,256]{2,1,0:T(8,128)(2,1)S(1)}, u32[]{:S(2)}, u32[]{:S(2)}) collective-permute-start(bf16[4,304,256]{2,1,0:T(8,128)(2,1)S(1)} %get-tuple-element.330), channel_id=1, source_target_pairs={{0,4},{4,0},{8,12},{12,8},{16,20},{20,16},{24,28},{28,24},{1,5},{5... | collective-permute-start | bytes 1867784 | tf_op jit(solution)/shard_map/ppermute | solution.py:419
  387.9 46.3 %collective-permute-start.34 = (bf16[4,304,256]{2,1,0:T(8,128)(2,1)S(1)}, bf16[4,304,256]{2,1,0:T(8,128)(2,1)S(1)}, u32[]{:S(2)}, u32[]{:S(2)}) collective-permute-start(bf16[4,304,256]{2,1,0:T(8,128)(2,1)S(1)} %get-tuple-element.331), channel_id=1, source_target_pairs={{0,2},{1,3},{2,0},{3,1},{4,6},{5,7},{6,4},{7,5},{8,10},{9,11},{10,... | collective-permute-start | bytes 1867784 | tf_op jit(solution)/shard_map/ppermute | solution.py:419
  388.9 45.2 %collective-permute-start.35 = (bf16[4,304,256]{2,1,0:T(8,128)(2,1)S(1)}, bf16[4,304,256]{2,1,0:T(8,128)(2,1)S(1)}, u32[]{:S(2)}, u32[]{:S(2)}) collective-permute-start(bf16[4,304,256]{2,1,0:T(8,128)(2,1)S(1)} %get-tuple-element.332), channel_id=1, source_target_pairs={{0,6},{1,7},{2,4},{3,5},{4,2},{5,3},{6,0},{7,1},{8,14},{9,15},{10,... | collective-permute-start | bytes 1867784 | tf_op jit(solution)/shard_map/ppermute | solution.py:435
  434.2 4.0 collective-permute-start.36
  439.9 21.4 %collective-permute-start.37 = (bf16[4,128,384]{2,1,0:T(8,128)(2,1)S(1)}, bf16[4,128,384]{2,1,0:T(8,128)(2,1)}, u32[]{:S(2)}, u32[]{:S(2)}) collective-permute-start(bf16[4,128,384]{2,1,0:T(8,128)(2,1)S(1)} %get-tuple-element.344), channel_id=1, source_target_pairs={{0,4},{4,0},{8,12},{12,8},{16,20},{20,16},{24,28},{28,24},{1,5},{5... | collective-permute-start | bytes 1179656 | tf_op jit(solution)/shard_map/ppermute | solution.py:419
  441.9 19.5 %collective-permute-start.38 = (bf16[4,128,384]{2,1,0:T(8,128)(2,1)S(1)}, bf16[4,128,384]{2,1,0:T(8,128)(2,1)}, u32[]{:S(2)}, u32[]{:S(2)}) collective-permute-start(bf16[4,128,384]{2,1,0:T(8,128)(2,1)S(1)} %get-tuple-element.345), channel_id=1, source_target_pairs={{0,2},{1,3},{2,0},{3,1},{4,6},{5,7},{6,4},{7,5},{8,10},{9,11},{10,... | collective-permute-start | bytes 1179656 | tf_op jit(solution)/shard_map/ppermute | solution.py:419
  443.0 18.4 %collective-permute-start.39 = (bf16[4,128,384]{2,1,0:T(8,128)(2,1)S(1)}, bf16[4,128,384]{2,1,0:T(8,128)(2,1)}, u32[]{:S(2)}, u32[]{:S(2)}) collective-permute-start(bf16[4,128,384]{2,1,0:T(8,128)(2,1)S(1)} %get-tuple-element.346), channel_id=1, source_target_pairs={{0,6},{1,7},{2,4},{3,5},{4,2},{5,3},{6,0},{7,1},{8,14},{9,15},{10,... | collective-permute-start | bytes 1179656 | tf_op jit(solution)/shard_map/ppermute | solution.py:435
  443.4 7.2 %collective-permute-start.40 = (bf16[304,256]{1,0:T(8,128)(2,1)S(1)}, bf16[304,256]{1,0:T(8,128)(2,1)S(1)}, u32[]{:S(2)}, u32[]{:S(2)}) collective-permute-start(bf16[304,256]{1,0:T(8,128)(2,1)S(1)} %copy-done.98), channel_id=1, source_target_pairs={{0,8},{4,12},{8,0},{12,4},{16,24},{20,28},{24,16},{28,20},{1,9},{5... | collective-permute-start | bytes 466952 | tf_op jit(solution)/shard_map/ppermute | solution.py:419
  445.4 13.3 %collective-permute-start.41 = (bf16[304,256]{1,0:T(8,128)(2,1)S(1)}, bf16[304,256]{1,0:T(8,128)(2,1)S(1)}, u32[]{:S(2)}, u32[]{:S(2)}) collective-permute-start(bf16[304,256]{1,0:T(8,128)(2,1)S(1)} %copy-done.97), channel_id=1, source_target_pairs={{0,16},{4,20},{8,24},{12,28},{16,0},{20,4},{24,8},{28,12},{1,17},{... | collective-permute-start | bytes 466952 | tf_op jit(solution)/shard_map/ppermute | solution.py:419
  450.6 8.1 %collective-permute-start.42 = (bf16[304,256]{1,0:T(8,128)(2,1)S(1)}, bf16[304,256]{1,0:T(8,128)(2,1)}, u32[]{:S(2)}, u32[]{:S(2)}) collective-permute-start(bf16[304,256]{1,0:T(8,128)(2,1)S(1)} %copy-done.96), channel_id=1, source_target_pairs={{0,24},{4,28},{8,16},{12,20},{16,8},{20,12},{24,0},{28,4},{1,25},{... | collective-permute-start | bytes 466952 | tf_op jit(solution)/shard_map/ppermute | solution.py:419
  463.6 5.9 %collective-permute-start.43 = (bf16[128,384]{1,0:T(8,128)(2,1)}, bf16[128,384]{1,0:T(8,128)(2,1)S(1)}, u32[]{:S(2)}, u32[]{:S(2)}) collective-permute-start(bf16[128,384]{1,0:T(8,128)(2,1)} %get-tuple-element.361), channel_id=1, source_target_pairs={{0,8},{4,12},{8,0},{12,4},{16,24},{20,28},{24,16},{28,20},{1,9},{5... | collective-permute-start | bytes 294920 | tf_op jit(solution)/shard_map/ppermute | solution.py:419
  465.6 9.6 %collective-permute-start.44 = (bf16[128,384]{1,0:T(8,128)(2,1)}, bf16[128,384]{1,0:T(8,128)(2,1)S(1)}, u32[]{:S(2)}, u32[]{:S(2)}) collective-permute-start(bf16[128,384]{1,0:T(8,128)(2,1)} %get-tuple-element.362), channel_id=1, source_target_pairs={{0,16},{4,20},{8,24},{12,28},{16,0},{20,4},{24,8},{28,12},{1,17},{... | collective-permute-start | bytes 294920 | tf_op jit(solution)/shard_map/ppermute | solution.py:419
  466.9 8.3 %collective-permute-start.45 = (bf16[128,384]{1,0:T(8,128)(2,1)}, bf16[128,384]{1,0:T(8,128)(2,1)S(1)}, u32[]{:S(2)}, u32[]{:S(2)}) collective-permute-start(bf16[128,384]{1,0:T(8,128)(2,1)} %get-tuple-element.363), channel_id=1, source_target_pairs={{0,24},{4,28},{8,16},{12,20},{16,8},{20,12},{24,0},{28,4},{1,25},{... | collective-permute-start | bytes 294920 | tf_op jit(solution)/shard_map/ppermute | solution.py:419
  (101 other events, 1109.5 us)

commit v7 on v6

--- a/solution.py
+++ b/solution.py
@@ -227,7 +227,7 @@
                 return (tuple(g_[q] for q in qs), tuple(ga[q] for q in qs), tuple(gbs), tuple(gsk))
             z8 = tuple(jnp.zeros((8, 128), F32) for q in qs)
             cr = lax.fori_loop(0, T // 8, rb, (tuple(carry[:, lanes[q]] for q in qs),
-                                               tuple(jnp.zeros((NS, 128), F32) for q in qs), z8, z8), unroll=2)
+                                               tuple(jnp.zeros((NS, 128), F32) for q in qs), z8, z8), unroll=4)
             for q in qs:
                 carry[:, lanes[q]] = cr[0][q - q0]
                 gpar_ref[taps + 2:taps + 2 + NS, lanes[q]] += cr[1][q - q0] * an[q]

time: 487 us -> 486 us (level)
  no operation moved by 1% of the time
where the time goes in v7:
time: 486 us; the launch traced here: 477 us
  Pallas kernels  255 us (52%)
  waiting for transfers between devices  102 us (21%)
  starting transfers between devices  66.9 us (14%)
  local copies, waits for them, and re-layouts  36.5 us (8%)
  other arithmetic  13.8 us (3%)
    ppermute x42, waiting for transfers between devices, swap(): return lax.ppermute(x, axis, [(i, i ^ bit) for i in range(n)])  93 us
    pallas_call x2, Pallas kernels, scan_backward(): pl.pallas_call(functools.partial(scan_back_kernel, T, Q, Q2, R), grid=(C,...  76.8 us
    pallas_call x12, Pallas kernels, one_call(): pl.pallas_call(kernel, in_specs=[smem] * len(scalars) + [vmem] * len(ins)...  67.8 us
    pallas_call x4, Pallas kernels, per_expert(): pl.pallas_call(kernel, grid=(ins[0].shape[0],), in_specs=[tok(a) for a in...  44.2 us
    ppermute x42, starting transfers between devices, swap(): return lax.ppermute(x, axis, [(i, i ^ bit) for i in range(n)])  40.8 us
    pallas_call x2, Pallas kernels, mixer_forward(): pl.pallas_call(functools.partial(mixer_kernel, T, Q, R), grid=(C,), in_sp...  37.8 us
    unnamed x198, local copies, waits for them, and re-layouts  33.1 us
    all_to_all x4, starting transfers between devices, home(): lax.all_to_all(rows_out, 'row', split_axis=0, concat_axis=0, tiled=True)  22 us
  transfers between devices with their start and end apart: 50, of which 18 were waited for; matrix products, arithmetic and copies ran while one was open for 3% of the time, Pallas kernels for 43%

profile of v7, /device:TPU:0, one launch (start us, length us, event | category | flops | bytes accessed | tf_op | source)
XLA Modules:
  0.0 476.7 jit_solution(14927392272813947231)
XLA Ops:
  2.5 3.0 collective-permute-start
  5.5 2.6 collective-permute-start.1
  8.5 7.6 %collective-permute-done.1 = bf16[128,384]{1,0:T(8,128)(2,1)S(1)} collective-permute-done((bf16[128,384]{1,0:T(8,128)(2,1)}, bf16[128,384]{1,0:T(8,128)(2,1)S(1)}, u32[]{:S(2)}, u32[]{:S(2)}) %collective-permute-start.1) | collective-permute-done | bytes 98336 | tf_op jit(solution)/shard_map/ppermute | solution.py:419
  17.1 2.5 collective-permute-start.5
  23.7 3.2 collective-permute-done.10
  26.9 3.4 collective-permute-done.11
  30.3 2.5 collective-permute-start.12
  32.8 2.9 collective-permute-done.3.refs_1_
  47.6 2.1 shard_map.315
  50.3 17.3 %shard_map.316 = (bf16[320,768]{1,0:T(8,128)(2,1)S(1)}, f32[328,1536]{1,0:T(8,128)S(1)}, f32[5,8,8,1536]{3,2,1,0:T(8,128)S(1)}, f32[5,8,8,1536]{3,2,1,0:T(8,128)...) custom-call(bf16[320,768]{1,0:T(8,128)(2,1)S(1)} %get-tuple-element., ...), custom_call_target="tpu_custom_call" | custom-call | flops 40000000000 | bytes 7864320 | tf_op jit(solution)/shard_map/pallas_call | solution.py:134
  81.5 3.3 shard_map.317
  88.2 11.6 %shard_map.318 = (f32[320,1536]{1,0:T(8,128)}, bf16[320,1536]{1,0:T(8,128)(2,1)}, f32[320,768]{1,0:T(8,128)}, s32[320,1]{1,0:T(8,128)}, bf16[832,768]{1,0:T(8,12...) custom-call(s32[1]{0:T(128)} %get-tuple-element.383.live_ref, bf16[320,768]{1,0:T(8,128)(2,1)} %copy-done.14, ...), custom_call_target="tpu_custom_call" | custom-call | flops 2264924160 | bytes 14990080 | tf_op jit(solution)/shard_map/pallas_call | solution.py:294
  99.8 5.9 %all-to-all-start = ((bf16[8,104,768]{2,1,0:T(8,128)(2,1)}), bf16[8,104,768]{2,1,0:T(8,128)(2,1)S(1)}, u32[]{:S(2)}, u32[]{:S(2)}) async-start(bf16[8,104,768]{2,1,0:T(8,128)(2,1)} %bitcast.83), calls=%async_computation | async-start | bytes 2555904 | tf_op jit(solution)/shard_map/all_to_all | solution.py:1191
  105.7 20.5 %shard_map.319 = (bf16[320,768]{1,0:T(8,128)(2,1)S(1)}, f32[328,1536]{1,0:T(8,128)}, f32[5,8,8,1536]{3,2,1,0:T(8,128)S(1)}, f32[5,8,8,1536]{3,2,1,0:T(8,128)S(1)...) custom-call(bf16[320,768]{1,0:T(8,128)(2,1)S(1)} %get-tuple-element., ...), custom_call_target="tpu_custom_call" | custom-call | flops 40000000000 | bytes 7864320 | tf_op jit(solution)/shard_map/pallas_call | solution.py:134
  130.5 11.6 %shard_map.320 = (f32[320,1536]{1,0:T(8,128)}, bf16[320,1536]{1,0:T(8,128)(2,1)}, f32[320,768]{1,0:T(8,128)}, s32[320,1]{1,0:T(8,128)}, bf16[832,768]{1,0:T(8,12...) custom-call(s32[1]{0:T(128)} %get-tuple-element.384.live_ref, bf16[320,768]{1,0:T(8,128)(2,1)} %copy-done.12, ...), custom_call_target="tpu_custom_call" | custom-call | flops 2264924160 | bytes 14990080 | tf_op jit(solution)/shard_map/pallas_call | solution.py:294
  144.9 6.5 %all-to-all-start.1 = ((bf16[8,104,768]{2,1,0:T(8,128)(2,1)}), bf16[8,104,768]{2,1,0:T(8,128)(2,1)}, u32[]{:S(2)}, u32[]{:S(2)}) async-start(bf16[8,104,768]{2,1,0:T(8,128)(2,1)} %bitcast.82), calls=%async_computation.1 | async-start | bytes 2555904 | tf_op jit(solution)/shard_map/all_to_all | solution.py:1191
  151.5 24.5 %collective-permute-done.20.refs_1_ = bf16[4,112,1536]{2,1,0:T(8,128)(2,1)S(1)} collective-permute-done((bf16[4,112,1536]{2,1,0:T(8,128)(2,1)S(1)}, bf16[4,112,1536]{2,1,0:T(8,128)(2,1)S(1)}, u32[]{:S(2)}, u32[]{:S(2)}) %collective-permute-start.20) | collective-permute-done | bytes 1376288 | tf_op jit(solution)/shard_map/ppermute | solution.py:419
  175.9 5.8 %all-to-all-done.1 = bf16[8,104,768]{2,1,0:T(8,128)(2,1)} async-done(((bf16[8,104,768]{2,1,0:T(8,128)(2,1)}), bf16[8,104,768]{2,1,0:T(8,128)(2,1)}, u32[]{:S(2)}, u32[]{:S(2)}) %all-to-all-start.1) | async-done | bytes 1277984 | tf_op jit(solution)/shard_map/all_to_all | solution.py:1191
  181.7 3.1 shard_map.322
  186.0 11.8 %shard_map.323 = (bf16[4,112,1536]{2,1,0:T(8,128)(2,1)S(1)}, bf16[4,112,1536]{2,1,0:T(8,128)(2,1)S(1)}, bf16[4,112,1536]{2,1,0:T(8,128)(2,1)S(1)}, bf16[4,112,15...) custom-call(bf16[4,112,1536]{2,1,0:T(8,128)(2,1)S(1)} %bitcast.60, ...), custom_call_target="tpu_custom_call" | custom-call | flops 8455716864 | bytes 25952256 | tf_op jit(solution)/shard_map/pallas_call | solution.py:641
  198.3 16.6 %collective-permute-done.26.refs_1_.refs_6_ = bf16[4,112,1536]{2,1,0:T(8,128)(2,1)S(1)} collective-permute-done((bf16[4,112,1536]{2,1,0:T(8,128)(2,1)S(1)}, bf16[4,112,1536]{2,1,0:T(8,128)(2,1)S(1)}, u32[]{:S(2)}, u32[]{:S(2)}) %collective-permute-start.26) | collective-permute-done | bytes 1376288 | tf_op jit(solution)/shard_map/ppermute | solution.py:419
  219.3 12.1 %shard_map.325 = (bf16[4,112,1536]{2,1,0:T(8,128)(2,1)S(1)}, bf16[4,112,1536]{2,1,0:T(8,128)(2,1)S(1)}, bf16[4,112,1536]{2,1,0:T(8,128)(2,1)S(1)}, bf16[4,112,15...) custom-call(bf16[4,112,1536]{2,1,0:T(8,128)(2,1)S(1)} %bitcast.65, ...), custom_call_target="tpu_custom_call" | custom-call | flops 8455716864 | bytes 25952256 | tf_op jit(solution)/shard_map/pallas_call | solution.py:641
  231.5 17.7 %collective-permute-done.25 = bf16[4,112,1536]{2,1,0:T(8,128)(2,1)S(1)} collective-permute-done((bf16[4,112,1536]{2,1,0:T(8,128)(2,1)}, bf16[4,112,1536]{2,1,0:T(8,128)(2,1)S(1)}, u32[]{:S(2)}, u32[]{:S(2)}) %collective-permute-start.25) | collective-permute-done | bytes 1376288 | tf_op jit(solution)/shard_map/ppermute | solution.py:419
  249.7 2.1 shard_map.324
  252.9 5.7 %all-to-all-start.2 = ((bf16[8,104,768]{2,1,0:T(8,128)(2,1)}), bf16[8,104,768]{2,1,0:T(8,128)(2,1)}, u32[]{:S(2)}, u32[]{:S(2)}) async-start(bf16[8,104,768]{2,1,0:T(8,128)(2,1)} %bitcast.74), calls=%async_computation.2 | async-start | bytes 2555904 | tf_op jit(solution)/shard_map/all_to_all | solution.py:1191
  258.8 3.3 add_convert_fusion.1
  265.0 10.1 %shard_map.326 = f32[4,768,768]{2,1,0:T(8,128)} custom-call(bf16[4,112,1536]{2,1,0:T(8,128)(2,1)S(1)} %bitcast.61, bf16[4,112,1536]{2,1,0:T(8,128)(2,1)S(1)} %collective-permute-done.20.refs_1_, bf16[4,112,1536]{2,1,0:T(8,128)(2,1)} %collective-permute-done.21.refs_2_, bf16[4,112,1536]{2,1,0:T(8,128)(2,1)} %collective-permute-done.22.refs_3_, ...), custom_call_target="tpu_custom_call" | custom-call | flops 4227858432 | bytes 25952256 | tf_op jit(solution)/shard_map/pallas_call | solution.py:641
  275.1 10.1 %shard_map.327 = f32[4,768,768]{2,1,0:T(8,128)} custom-call(bf16[4,112,1536]{2,1,0:T(8,128)(2,1)S(1)} %bitcast.62, bf16[4,112,1536]{2,1,0:T(8,128)(2,1)S(1)} %collective-permute-done.20.refs_1_, bf16[4,112,1536]{2,1,0:T(8,128)(2,1)} %collective-permute-done.21.refs_2_, bf16[4,112,1536]{2,1,0:T(8,128)(2,1)} %collective-permute-done.22.refs_3_, ...), custom_call_target="tpu_custom_call" | custom-call | flops 4227858432 | bytes 25952256 | tf_op jit(solution)/shard_map/pallas_call | solution.py:641
  285.3 3.7 all-to-all-done.2
  288.9 12.8 %shard_map.328 = (bf16[320,768]{1,0:T(8,128)(2,1)}, f32[320,768]{1,0:T(8,128)}, f32[320,1536]{1,0:T(8,128)}, bf16[320,1536]{1,0:T(8,128)(2,1)}, bf16[320,1024]{1...) custom-call(s32[1]{0:T(128)} %get-tuple-element.383.live_ref, bf16[832,768]{1,0:T(8,128)(2,1)} %bitcast.31.home_ref, ...), custom_call_target="tpu_custom_call" | custom-call | flops 2264924160 | bytes 17417984 | tf_op jit(solution)/shard_map/pallas_call | solution.py:294
  301.8 2.3 add_convert_fusion
  304.0 3.2 shard_map.329
  307.2 3.9 all-to-all-start.3
  311.1 40.0 %shard_map.330 = (bf16[320,1536]{1,0:T(8,128)(2,1)}, f32[80,1536]{1,0:T(8,128)S(1)}, f32[48,1536]{1,0:T(8,128)S(1)}, f32[23,1536]{1,0:T(8,128)S(1)}) custom-call(f32[5,8,8,1536]{3,2,1,0:T(8,128)} %copy-done.72, f32[5,8,8,1536]{3,2,1,0:T(8,128)} %copy-done.73, f32[5,8,8,1536]{3,2,1,0:T(8,128)} %bitcast.101, f32[5,8,8,1536]{3,2,1,0:T(8,128)} %copy-done.71, ...), custom_call_target="tpu_custom_call" | custom-call | flops 80000000000 | bytes 7864320 | tf_op jit(solution)/shard_map/pallas_call | solution.py:278
  353.7 12.6 %shard_map.331 = (bf16[320,768]{1,0:T(8,128)(2,1)}, f32[320,768]{1,0:T(8,128)}, f32[320,1536]{1,0:T(8,128)}, bf16[320,1536]{1,0:T(8,128)(2,1)}, bf16[320,1024]{1...) custom-call(s32[1]{0:T(128)} %get-tuple-element.384.live_ref, bf16[832,768]{1,0:T(8,128)(2,1)} %bitcast.81, ...), custom_call_target="tpu_custom_call" | custom-call | flops 2264924160 | bytes 17417984 | tf_op jit(solution)/shard_map/pallas_call | solution.py:294
  366.4 11.8 %shard_map.332 = (bf16[2,8,304,256]{3,2,1,0:T(8,128)(2,1)}, bf16[2,8,304,256]{3,2,1,0:T(8,128)(2,1)}) custom-call(s32[1]{0:T(128)} %bitcast.3.s_ref, bf16[320,768]{1,0:T(8,128)(2,1)} %copy-done.33, bf16[320,1536]{1,0:T(8,128)(2,1)} %get-tuple-element.288.refs_1_.gz_ref, bf16[320,768]{1,0:T(8,128)(2,1)} %copy-done.35, ...), custom_call_target="tpu_custom_call" | custom-call | flops 3523215360 | bytes 8388608 | tf_op jit(solution)/shard_map/pallas_call | solution.py:859
  380.2 2.9 collective-permute-done.32
  389.8 36.8 %shard_map.335 = (bf16[320,1536]{1,0:T(8,128)(2,1)S(1)}, f32[80,1536]{1,0:T(8,128)S(1)}, f32[48,1536]{1,0:T(8,128)S(1)}, f32[23,1536]{1,0:T(8,128)S(1)}) custom-call(f32[5,8,8,1536]{3,2,1,0:T(8,128)S(1)} %copy-done.69, f32[5,8,8,1536]{3,2,1,0:T(8,128)S(1)} %copy-done.70, f32[5,8,8,1536]{3,2,1,0:T(8,128)S(1)} %bitcast.78, f32[5,8,8,1536]{3,2,1,0:T(8,128)S(1)} %copy-done.67, ...), custom_call_target="tpu_custom_call" | custom-call | flops 80000000000 | bytes 7864320 | tf_op jit(solution)/shard_map/pallas_call | solution.py:278
  428.8 3.8 shard_map.337
  433.8 2.8 shard_map.338
  441.9 2.0 collective-permute-start.40
  443.9 2.4 collective-permute-start.41
  446.3 2.8 collective-permute-done.40.refs_1_
  449.1 3.6 collective-permute-start.42
  453.8 3.4 collective-permute-done.41.refs_2_
  459.8 2.3 shard_map.341
  462.1 2.0 collective-permute-start.43
  468.0 5.7 %collective-permute-done.44.refs_2_ = bf16[128,384]{1,0:T(8,128)(2,1)S(1)} collective-permute-done((bf16[128,384]{1,0:T(8,128)(2,1)}, bf16[128,384]{1,0:T(8,128)(2,1)S(1)}, u32[]{:S(2)}, u32[]{:S(2)}) %collective-permute-start.44) | collective-permute-done | bytes 98336 | tf_op jit(solution)/shard_map/ppermute | solution.py:419
  (295 shorter events, 84.2 us)
Async XLA Ops:
  2.5 6.0 %collective-permute-start = (bf16[128,384]{1,0:T(8,128)(2,1)}, bf16[128,384]{1,0:T(8,128)(2,1)S(1)}, u32[]{:S(2)}, u32[]{:S(2)}) collective-permute-start(bf16[128,384]{1,0:T(8,128)(2,1)} %get-tuple-element.198), channel_id=1, source_target_pairs={{0,8},{4,12},{8,0},{12,4},{16,24},{20,28},{24,16},{28,20},{1,9},{5... | collective-permute-start | bytes 294920 | tf_op jit(solution)/shard_map/ppermute | solution.py:419
  5.5 10.6 %collective-permute-start.1 = (bf16[128,384]{1,0:T(8,128)(2,1)}, bf16[128,384]{1,0:T(8,128)(2,1)S(1)}, u32[]{:S(2)}, u32[]{:S(2)}) collective-permute-start(bf16[128,384]{1,0:T(8,128)(2,1)} %get-tuple-element.198), channel_id=1, source_target_pairs={{0,16},{4,20},{8,24},{12,28},{16,0},{20,4},{24,8},{28,12},{1,17},{... | collective-permute-start | bytes 294920 | tf_op jit(solution)/shard_map/ppermute | solution.py:419
  8.1 8.1 %collective-permute-start.2 = (bf16[128,384]{1,0:T(8,128)(2,1)}, bf16[128,384]{1,0:T(8,128)(2,1)S(1)}, u32[]{:S(2)}, u32[]{:S(2)}) collective-permute-start(bf16[128,384]{1,0:T(8,128)(2,1)} %get-tuple-element.198), channel_id=1, source_target_pairs={{0,24},{4,28},{8,16},{12,20},{16,8},{20,12},{24,0},{28,4},{1,25},{... | collective-permute-start | bytes 294920 | tf_op jit(solution)/shard_map/ppermute | solution.py:419
  17.1 15.6 %collective-permute-start.5 = (bf16[4,128,384]{2,1,0:T(8,128)(2,1)S(1)}, bf16[4,128,384]{2,1,0:T(8,128)(2,1)S(1)}, u32[]{:S(2)}, u32[]{:S(2)}) collective-permute-start(bf16[4,128,384]{2,1,0:T(8,128)(2,1)S(1)} %pad_maximum_fusion.3.refs_0_), channel_id=1, source_target_pairs={{0,6},{1,7},{2,4},{3,5},{4,2},{5,3},{6,0},{7,1},{8,14},{9,15},{10,... | collective-permute-start | bytes 1179656 | tf_op jit(solution)/shard_map/ppermute | solution.py:435
  19.6 16.0 %collective-permute-start.3 = (bf16[4,128,384]{2,1,0:T(8,128)(2,1)S(1)}, bf16[4,128,384]{2,1,0:T(8,128)(2,1)}, u32[]{:S(2)}, u32[]{:S(2)}) collective-permute-start(bf16[4,128,384]{2,1,0:T(8,128)(2,1)S(1)} %pad_maximum_fusion.3.refs_0_), channel_id=1, source_target_pairs={{0,4},{4,0},{8,12},{12,8},{16,20},{20,16},{24,28},{28,24},{1,5},{5... | collective-permute-start | bytes 1179656 | tf_op jit(solution)/shard_map/ppermute | solution.py:419
  20.2 15.5 %collective-permute-start.4 = (bf16[4,128,384]{2,1,0:T(8,128)(2,1)S(1)}, bf16[4,128,384]{2,1,0:T(8,128)(2,1)}, u32[]{:S(2)}, u32[]{:S(2)}) collective-permute-start(bf16[4,128,384]{2,1,0:T(8,128)(2,1)S(1)} %pad_maximum_fusion.3.refs_0_), channel_id=1, source_target_pairs={{0,2},{1,3},{2,0},{3,1},{4,6},{5,7},{6,4},{7,5},{8,10},{9,11},{10,... | collective-permute-start | bytes 1179656 | tf_op jit(solution)/shard_map/ppermute | solution.py:419
  20.7 6.2 %collective-permute-start.10 = (bf16[304,256]{1,0:T(8,128)(2,1)}, bf16[304,256]{1,0:T(8,128)(2,1)S(1)}, u32[]{:S(2)}, u32[]{:S(2)}) collective-permute-start(bf16[304,256]{1,0:T(8,128)(2,1)} %get-tuple-element.207), channel_id=1, source_target_pairs={{0,8},{4,12},{8,0},{12,4},{16,24},{20,28},{24,16},{28,20},{1,9},{5... | collective-permute-start | bytes 466952 | tf_op jit(solution)/shard_map/ppermute | solution.py:419
  22.3 8.0 %collective-permute-start.11 = (bf16[304,256]{1,0:T(8,128)(2,1)}, bf16[304,256]{1,0:T(8,128)(2,1)S(1)}, u32[]{:S(2)}, u32[]{:S(2)}) collective-permute-start(bf16[304,256]{1,0:T(8,128)(2,1)} %get-tuple-element.207), channel_id=1, source_target_pairs={{0,16},{4,20},{8,24},{12,28},{16,0},{20,4},{24,8},{28,12},{1,17},{... | collective-permute-start | bytes 466952 | tf_op jit(solution)/shard_map/ppermute | solution.py:419
  26.9 13.2 %collective-permute-start.6 = (bf16[4,128,384]{2,1,0:T(8,128)(2,1)S(1)}, bf16[4,128,384]{2,1,0:T(8,128)(2,1)S(1)}, u32[]{:S(2)}, u32[]{:S(2)}) collective-permute-start(bf16[4,128,384]{2,1,0:T(8,128)(2,1)S(1)} %pad_maximum_fusion.3.refs_0_), channel_id=1, source_target_pairs={{0,1},{1,0},{2,3},{3,2},{4,5},{5,4},{6,7},{7,6},{8,9},{9,8},{10,11... | collective-permute-start | bytes 1179656 | tf_op jit(solution)/shard_map/ppermute | solution.py:419
  30.3 7.2 %collective-permute-start.12 = (bf16[304,256]{1,0:T(8,128)(2,1)}, bf16[304,256]{1,0:T(8,128)(2,1)S(1)}, u32[]{:S(2)}, u32[]{:S(2)}) collective-permute-start(bf16[304,256]{1,0:T(8,128)(2,1)} %get-tuple-element.207), channel_id=1, source_target_pairs={{0,24},{4,28},{8,16},{12,20},{16,8},{20,12},{24,0},{28,4},{1,25},{... | collective-permute-start | bytes 466952 | tf_op jit(solution)/shard_map/ppermute | solution.py:419
  32.8 9.5 %collective-permute-start.9 = (bf16[4,128,384]{2,1,0:T(8,128)(2,1)S(1)}, bf16[4,128,384]{2,1,0:T(8,128)(2,1)S(1)}, u32[]{:S(2)}, u32[]{:S(2)}) collective-permute-start(bf16[4,128,384]{2,1,0:T(8,128)(2,1)S(1)} %collective-permute-done.5.refs_3_), channel_id=1, source_target_pairs={{0,1},{1,0},{2,3},{3,2},{4,5},{5,4},{6,7},{7,6},{8,9},{9,8},{10,11... | collective-permute-start | bytes 1179656 | tf_op jit(solution)/shard_map/ppermute | solution.py:419
  35.7 7.9 %collective-permute-start.7 = (bf16[4,128,384]{2,1,0:T(8,128)(2,1)}, bf16[4,128,384]{2,1,0:T(8,128)(2,1)}, u32[]{:S(2)}, u32[]{:S(2)}) collective-permute-start(bf16[4,128,384]{2,1,0:T(8,128)(2,1)} %collective-permute-done.3.refs_1_), channel_id=1, source_target_pairs={{0,1},{1,0},{2,3},{3,2},{4,5},{5,4},{6,7},{7,6},{8,9},{9,8},{10,11... | collective-permute-start | bytes 1179656 | tf_op jit(solution)/shard_map/ppermute | solution.py:419
  35.7 7.9 %collective-permute-start.8 = (bf16[4,128,384]{2,1,0:T(8,128)(2,1)}, bf16[4,128,384]{2,1,0:T(8,128)(2,1)}, u32[]{:S(2)}, u32[]{:S(2)}) collective-permute-start(bf16[4,128,384]{2,1,0:T(8,128)(2,1)} %collective-permute-done.4.refs_2_), channel_id=1, source_target_pairs={{0,1},{1,0},{2,3},{3,2},{4,5},{5,4},{6,7},{7,6},{8,9},{9,8},{10,11... | collective-permute-start | bytes 1179656 | tf_op jit(solution)/shard_map/ppermute | solution.py:419
  38.6 37.9 %collective-permute-start.13 = (bf16[4,304,256]{2,1,0:T(8,128)(2,1)}, bf16[4,304,256]{2,1,0:T(8,128)(2,1)S(1)}, u32[]{:S(2)}, u32[]{:S(2)}) collective-permute-start(bf16[4,304,256]{2,1,0:T(8,128)(2,1)} %pad_maximum_fusion.2.refs_0_), channel_id=1, source_target_pairs={{0,4},{4,0},{8,12},{12,8},{16,20},{20,16},{24,28},{28,24},{1,5},{5... | collective-permute-start | bytes 1867784 | tf_op jit(solution)/shard_map/ppermute | solution.py:419
  40.8 35.7 %collective-permute-start.14 = (bf16[4,304,256]{2,1,0:T(8,128)(2,1)}, bf16[4,304,256]{2,1,0:T(8,128)(2,1)S(1)}, u32[]{:S(2)}, u32[]{:S(2)}) collective-permute-start(bf16[4,304,256]{2,1,0:T(8,128)(2,1)} %pad_maximum_fusion.2.refs_0_), channel_id=1, source_target_pairs={{0,2},{1,3},{2,0},{3,1},{4,6},{5,7},{6,4},{7,5},{8,10},{9,11},{10,... | collective-permute-start | bytes 1867784 | tf_op jit(solution)/shard_map/ppermute | solution.py:419
  43.0 33.6 %collective-permute-start.15 = (bf16[4,304,256]{2,1,0:T(8,128)(2,1)}, bf16[4,304,256]{2,1,0:T(8,128)(2,1)S(1)}, u32[]{:S(2)}, u32[]{:S(2)}) collective-permute-start(bf16[4,304,256]{2,1,0:T(8,128)(2,1)} %pad_maximum_fusion.2.refs_0_), channel_id=1, source_target_pairs={{0,6},{1,7},{2,4},{3,5},{4,2},{5,3},{6,0},{7,1},{8,14},{9,15},{10,... | collective-permute-start | bytes 1867784 | tf_op jit(solution)/shard_map/ppermute | solution.py:435
  76.5 3.3 collective-permute-start.16
  77.1 3.5 collective-permute-start.18
  77.2 4.3 collective-permute-start.19
  99.8 42.3 %all-to-all-start = ((bf16[8,104,768]{2,1,0:T(8,128)(2,1)}), bf16[8,104,768]{2,1,0:T(8,128)(2,1)S(1)}, u32[]{:S(2)}, u32[]{:S(2)}) async-start(bf16[8,104,768]{2,1,0:T(8,128)(2,1)} %bitcast.83), calls=%async_computation | async-start | bytes 2555904 | tf_op jit(solution)/shard_map/all_to_all | solution.py:1191
  143.9 32.0 %collective-permute-start.20 = (bf16[4,112,1536]{2,1,0:T(8,128)(2,1)S(1)}, bf16[4,112,1536]{2,1,0:T(8,128)(2,1)S(1)}, u32[]{:S(2)}, u32[]{:S(2)}) collective-permute-start(bf16[4,112,1536]{2,1,0:T(8,128)(2,1)S(1)} %bitcast.58), channel_id=1, source_target_pairs={{0,2},{1,3},{2,0},{3,1},{4,6},{5,7},{6,4},{7,5},{8,10},{9,11},{10,... | collective-permute-start | bytes 4128776 | tf_op jit(solution)/shard_map/ppermute | solution.py:419
  144.9 36.8 %all-to-all-start.1 = ((bf16[8,104,768]{2,1,0:T(8,128)(2,1)}), bf16[8,104,768]{2,1,0:T(8,128)(2,1)}, u32[]{:S(2)}, u32[]{:S(2)}) async-start(bf16[8,104,768]{2,1,0:T(8,128)(2,1)} %bitcast.82), calls=%async_computation.1 | async-start | bytes 2555904 | tf_op jit(solution)/shard_map/all_to_all | solution.py:1191
  151.4 33.4 %collective-permute-start.21 = (bf16[4,112,1536]{2,1,0:T(8,128)(2,1)S(1)}, bf16[4,112,1536]{2,1,0:T(8,128)(2,1)}, u32[]{:S(2)}, u32[]{:S(2)}) collective-permute-start(bf16[4,112,1536]{2,1,0:T(8,128)(2,1)S(1)} %bitcast.59), channel_id=1, source_target_pairs={{0,1},{1,0},{2,3},{3,2},{4,5},{5,4},{6,7},{7,6},{8,9},{9,8},{10,11... | collective-permute-start | bytes 4128776 | tf_op jit(solution)/shard_map/ppermute | solution.py:419
  175.9 8.9 %collective-permute-start.22 = (bf16[4,112,1536]{2,1,0:T(8,128)(2,1)S(1)}, bf16[4,112,1536]{2,1,0:T(8,128)(2,1)}, u32[]{:S(2)}, u32[]{:S(2)}) collective-permute-start(bf16[4,112,1536]{2,1,0:T(8,128)(2,1)S(1)} %collective-permute-done.20.refs_1_), channel_id=1, source_target_pairs={{0,1},{1,0},{2,3},{3,2},{4,5},{5,4},{6,7},{7,6},{8,9},{9,8},{10,11... | collective-permute-start | bytes 4128776 | tf_op jit(solution)/shard_map/ppermute | solution.py:419
  184.8 30.1 %collective-permute-start.26 = (bf16[4,112,1536]{2,1,0:T(8,128)(2,1)S(1)}, bf16[4,112,1536]{2,1,0:T(8,128)(2,1)S(1)}, u32[]{:S(2)}, u32[]{:S(2)}) collective-permute-start(bf16[4,112,1536]{2,1,0:T(8,128)(2,1)S(1)} %bitcast.63), channel_id=1, source_target_pairs={{0,2},{1,3},{2,0},{3,1},{4,6},{5,7},{6,4},{7,5},{8,10},{9,11},{10,... | collective-permute-start | bytes 4128776 | tf_op jit(solution)/shard_map/ppermute | solution.py:419
  197.8 17.7 %collective-permute-start.24 = (bf16[4,112,1536]{2,1,0:T(8,128)(2,1)S(1)}, bf16[4,112,1536]{2,1,0:T(8,128)(2,1)S(1)}, u32[]{:S(2)}, u32[]{:S(2)}) collective-permute-start(bf16[4,112,1536]{2,1,0:T(8,128)(2,1)S(1)} %get-tuple-element.234), channel_id=1, source_target_pairs={{0,1},{1,0},{2,3},{3,2},{4,5},{5,4},{6,7},{7,6},{8,9},{9,8},{10,11... | collective-permute-start | bytes 4128776 | tf_op jit(solution)/shard_map/ppermute | solution.py:419
  197.8 20.2 %collective-permute-start.27 = (bf16[4,112,1536]{2,1,0:T(8,128)(2,1)S(1)}, bf16[4,112,1536]{2,1,0:T(8,128)(2,1)S(1)}, u32[]{:S(2)}, u32[]{:S(2)}) collective-permute-start(bf16[4,112,1536]{2,1,0:T(8,128)(2,1)S(1)} %bitcast.64), channel_id=1, source_target_pairs={{0,1},{1,0},{2,3},{3,2},{4,5},{5,4},{6,7},{7,6},{8,9},{9,8},{10,11... | collective-permute-start | bytes 4128776 | tf_op jit(solution)/shard_map/ppermute | solution.py:419
  215.0 16.6 %collective-permute-start.23 = (bf16[4,112,1536]{2,1,0:T(8,128)(2,1)S(1)}, bf16[4,112,1536]{2,1,0:T(8,128)(2,1)S(1)}, u32[]{:S(2)}, u32[]{:S(2)}) collective-permute-start(bf16[4,112,1536]{2,1,0:T(8,128)(2,1)S(1)} %get-tuple-element.232), channel_id=1, source_target_pairs={{0,1},{1,0},{2,3},{3,2},{4,5},{5,4},{6,7},{7,6},{8,9},{9,8},{10,11... | collective-permute-start | bytes 4128776 | tf_op jit(solution)/shard_map/ppermute | solution.py:419
  216.9 32.3 %collective-permute-start.25 = (bf16[4,112,1536]{2,1,0:T(8,128)(2,1)}, bf16[4,112,1536]{2,1,0:T(8,128)(2,1)S(1)}, u32[]{:S(2)}, u32[]{:S(2)}) collective-permute-start(bf16[4,112,1536]{2,1,0:T(8,128)(2,1)} %add_convert_fusion.4), channel_id=1, source_target_pairs={{0,2},{1,3},{2,0},{3,1},{4,6},{5,7},{6,4},{7,5},{8,10},{9,11},{10,... | collective-permute-start | bytes 4128776 | tf_op jit(solution)/shard_map/ppermute | solution.py:419
  231.5 27.3 %collective-permute-start.30 = (bf16[4,112,1536]{2,1,0:T(8,128)(2,1)}, bf16[4,112,1536]{2,1,0:T(8,128)(2,1)}, u32[]{:S(2)}, u32[]{:S(2)}) collective-permute-start(bf16[4,112,1536]{2,1,0:T(8,128)(2,1)} %get-tuple-element.273), channel_id=1, source_target_pairs={{0,1},{1,0},{2,3},{3,2},{4,5},{5,4},{6,7},{7,6},{8,9},{9,8},{10,11... | collective-permute-start | bytes 4128776 | tf_op jit(solution)/shard_map/ppermute | solution.py:419
  252.9 36.0 %all-to-all-start.2 = ((bf16[8,104,768]{2,1,0:T(8,128)(2,1)}), bf16[8,104,768]{2,1,0:T(8,128)(2,1)}, u32[]{:S(2)}, u32[]{:S(2)}) async-start(bf16[8,104,768]{2,1,0:T(8,128)(2,1)} %bitcast.74), calls=%async_computation.2 | async-start | bytes 2555904 | tf_op jit(solution)/shard_map/all_to_all | solution.py:1191
  258.7 43.0 %collective-permute-start.29 = (bf16[4,112,1536]{2,1,0:T(8,128)(2,1)}, bf16[4,112,1536]{2,1,0:T(8,128)(2,1)}, u32[]{:S(2)}, u32[]{:S(2)}) collective-permute-start(bf16[4,112,1536]{2,1,0:T(8,128)(2,1)} %copy-done.45), channel_id=1, source_target_pairs={{0,1},{1,0},{2,3},{3,2},{4,5},{5,4},{6,7},{7,6},{8,9},{9,8},{10,11... | collective-permute-start | bytes 4128776 | tf_op jit(solution)/shard_map/ppermute | solution.py:419
  262.1 39.6 %collective-permute-start.31 = (bf16[4,112,1536]{2,1,0:T(8,128)(2,1)}, bf16[4,112,1536]{2,1,0:T(8,128)(2,1)}, u32[]{:S(2)}, u32[]{:S(2)}) collective-permute-start(bf16[4,112,1536]{2,1,0:T(8,128)(2,1)} %add_convert_fusion.1), channel_id=1, source_target_pairs={{0,2},{1,3},{2,0},{3,1},{4,6},{5,7},{6,4},{7,5},{8,10},{9,11},{10,... | collective-permute-start | bytes 4128776 | tf_op jit(solution)/shard_map/ppermute | solution.py:419
  307.2 45.4 %all-to-all-start.3 = ((bf16[8,104,768]{2,1,0:T(8,128)(2,1)}), bf16[8,104,768]{2,1,0:T(8,128)(2,1)S(1)}, u32[]{:S(2)}, u32[]{:S(2)}) async-start(bf16[8,104,768]{2,1,0:T(8,128)(2,1)} %bitcast.35), calls=%async_computation.3 | async-start | bytes 2555904 | tf_op jit(solution)/shard_map/all_to_all | solution.py:1191
  378.2 4.9 %collective-permute-start.32 = (bf16[2,8,304,256]{3,2,1,0:T(8,128)(2,1)}, bf16[2,8,304,256]{3,2,1,0:T(8,128)(2,1)S(1)}, u32[]{:S(2)}, u32[]{:S(2)}) collective-permute-start(bf16[2,8,304,256]{3,2,1,0:T(8,128)(2,1)} %get-tuple-element.296), channel_id=1, source_target_pairs={{0,1},{1,0},{2,3},{3,2},{4,5},{5,4},{6,7},{7,6},{8,9},{9,8},{10,11... | collective-permute-start | bytes 7471112 | tf_op jit(solution)/shard_map/ppermute | solution.py:419
  385.2 47.4 %collective-permute-start.33 = (bf16[4,304,256]{2,1,0:T(8,128)(2,1)S(1)}, bf16[4,304,256]{2,1,0:T(8,128)(2,1)S(1)}, u32[]{:S(2)}, u32[]{:S(2)}) collective-permute-start(bf16[4,304,256]{2,1,0:T(8,128)(2,1)S(1)} %get-tuple-element.330), channel_id=1, source_target_pairs={{0,4},{4,0},{8,12},{12,8},{16,20},{20,16},{24,28},{28,24},{1,5},{5... | collective-permute-start | bytes 1867784 | tf_op jit(solution)/shard_map/ppermute | solution.py:419
  387.1 45.4 %collective-permute-start.34 = (bf16[4,304,256]{2,1,0:T(8,128)(2,1)S(1)}, bf16[4,304,256]{2,1,0:T(8,128)(2,1)S(1)}, u32[]{:S(2)}, u32[]{:S(2)}) collective-permute-start(bf16[4,304,256]{2,1,0:T(8,128)(2,1)S(1)} %get-tuple-element.331), channel_id=1, source_target_pairs={{0,2},{1,3},{2,0},{3,1},{4,6},{5,7},{6,4},{7,5},{8,10},{9,11},{10,... | collective-permute-start | bytes 1867784 | tf_op jit(solution)/shard_map/ppermute | solution.py:419
  388.2 44.4 %collective-permute-start.35 = (bf16[4,304,256]{2,1,0:T(8,128)(2,1)S(1)}, bf16[4,304,256]{2,1,0:T(8,128)(2,1)S(1)}, u32[]{:S(2)}, u32[]{:S(2)}) collective-permute-start(bf16[4,304,256]{2,1,0:T(8,128)(2,1)S(1)} %get-tuple-element.332), channel_id=1, source_target_pairs={{0,6},{1,7},{2,4},{3,5},{4,2},{5,3},{6,0},{7,1},{8,14},{9,15},{10,... | collective-permute-start | bytes 1867784 | tf_op jit(solution)/shard_map/ppermute | solution.py:435
  432.6 4.0 collective-permute-start.36
  438.4 21.4 %collective-permute-start.37 = (bf16[4,128,384]{2,1,0:T(8,128)(2,1)S(1)}, bf16[4,128,384]{2,1,0:T(8,128)(2,1)}, u32[]{:S(2)}, u32[]{:S(2)}) collective-permute-start(bf16[4,128,384]{2,1,0:T(8,128)(2,1)S(1)} %get-tuple-element.344), channel_id=1, source_target_pairs={{0,4},{4,0},{8,12},{12,8},{16,20},{20,16},{24,28},{28,24},{1,5},{5... | collective-permute-start | bytes 1179656 | tf_op jit(solution)/shard_map/ppermute | solution.py:419
  440.4 19.4 %collective-permute-start.38 = (bf16[4,128,384]{2,1,0:T(8,128)(2,1)S(1)}, bf16[4,128,384]{2,1,0:T(8,128)(2,1)}, u32[]{:S(2)}, u32[]{:S(2)}) collective-permute-start(bf16[4,128,384]{2,1,0:T(8,128)(2,1)S(1)} %get-tuple-element.345), channel_id=1, source_target_pairs={{0,2},{1,3},{2,0},{3,1},{4,6},{5,7},{6,4},{7,5},{8,10},{9,11},{10,... | collective-permute-start | bytes 1179656 | tf_op jit(solution)/shard_map/ppermute | solution.py:419
  441.4 18.4 %collective-permute-start.39 = (bf16[4,128,384]{2,1,0:T(8,128)(2,1)S(1)}, bf16[4,128,384]{2,1,0:T(8,128)(2,1)}, u32[]{:S(2)}, u32[]{:S(2)}) collective-permute-start(bf16[4,128,384]{2,1,0:T(8,128)(2,1)S(1)} %get-tuple-element.346), channel_id=1, source_target_pairs={{0,6},{1,7},{2,4},{3,5},{4,2},{5,3},{6,0},{7,1},{8,14},{9,15},{10,... | collective-permute-start | bytes 1179656 | tf_op jit(solution)/shard_map/ppermute | solution.py:435
  441.9 7.2 %collective-permute-start.40 = (bf16[304,256]{1,0:T(8,128)(2,1)S(1)}, bf16[304,256]{1,0:T(8,128)(2,1)S(1)}, u32[]{:S(2)}, u32[]{:S(2)}) collective-permute-start(bf16[304,256]{1,0:T(8,128)(2,1)S(1)} %copy-done.98), channel_id=1, source_target_pairs={{0,8},{4,12},{8,0},{12,4},{16,24},{20,28},{24,16},{28,20},{1,9},{5... | collective-permute-start | bytes 466952 | tf_op jit(solution)/shard_map/ppermute | solution.py:419
  443.9 13.3 %collective-permute-start.41 = (bf16[304,256]{1,0:T(8,128)(2,1)S(1)}, bf16[304,256]{1,0:T(8,128)(2,1)S(1)}, u32[]{:S(2)}, u32[]{:S(2)}) collective-permute-start(bf16[304,256]{1,0:T(8,128)(2,1)S(1)} %copy-done.97), channel_id=1, source_target_pairs={{0,16},{4,20},{8,24},{12,28},{16,0},{20,4},{24,8},{28,12},{1,17},{... | collective-permute-start | bytes 466952 | tf_op jit(solution)/shard_map/ppermute | solution.py:419
  449.1 8.1 %collective-permute-start.42 = (bf16[304,256]{1,0:T(8,128)(2,1)S(1)}, bf16[304,256]{1,0:T(8,128)(2,1)}, u32[]{:S(2)}, u32[]{:S(2)}) collective-permute-start(bf16[304,256]{1,0:T(8,128)(2,1)S(1)} %copy-done.96), channel_id=1, source_target_pairs={{0,24},{4,28},{8,16},{12,20},{16,8},{20,12},{24,0},{28,4},{1,25},{... | collective-permute-start | bytes 466952 | tf_op jit(solution)/shard_map/ppermute | solution.py:419
  462.1 5.9 %collective-permute-start.43 = (bf16[128,384]{1,0:T(8,128)(2,1)}, bf16[128,384]{1,0:T(8,128)(2,1)S(1)}, u32[]{:S(2)}, u32[]{:S(2)}) collective-permute-start(bf16[128,384]{1,0:T(8,128)(2,1)} %get-tuple-element.361), channel_id=1, source_target_pairs={{0,8},{4,12},{8,0},{12,4},{16,24},{20,28},{24,16},{28,20},{1,9},{5... | collective-permute-start | bytes 294920 | tf_op jit(solution)/shard_map/ppermute | solution.py:419
  464.1 9.6 %collective-permute-start.44 = (bf16[128,384]{1,0:T(8,128)(2,1)}, bf16[128,384]{1,0:T(8,128)(2,1)S(1)}, u32[]{:S(2)}, u32[]{:S(2)}) collective-permute-start(bf16[128,384]{1,0:T(8,128)(2,1)} %get-tuple-element.362), channel_id=1, source_target_pairs={{0,16},{4,20},{8,24},{12,28},{16,0},{20,4},{24,8},{28,12},{1,17},{... | collective-permute-start | bytes 294920 | tf_op jit(solution)/shard_map/ppermute | solution.py:419
  465.3 8.4 %collective-permute-start.45 = (bf16[128,384]{1,0:T(8,128)(2,1)}, bf16[128,384]{1,0:T(8,128)(2,1)S(1)}, u32[]{:S(2)}, u32[]{:S(2)}) collective-permute-start(bf16[128,384]{1,0:T(8,128)(2,1)} %get-tuple-element.363), channel_id=1, source_target_pairs={{0,24},{4,28},{8,16},{12,20},{16,8},{20,12},{24,0},{28,4},{1,25},{... | collective-permute-start | bytes 294920 | tf_op jit(solution)/shard_map/ppermute | solution.py:419
  (101 other events, 1107.2 us)
